TPU v7x, 256 devices: a whole 4x4x8 slice. The times are simulated.
256 devices in a mesh: dp: 32 (over z_hi, x, core), token: 8 (over z_lo, y).
Axes of the slice: x: 4, y: 4, z: 8 (z_hi: 4, z_lo: 2; z = z_hi * 2 + z_lo), core: 2. Of those that a mesh axis runs over, the one named last changes fastest.
Arguments:
- block_input: bfloat16 [8192, 8, 1536], P('dp', 'token'), may hold values from -6 to 6
- out_cotangent: bfloat16 [8192, 8, 1536], P('dp', 'token'), may hold values from -6 to 6
- w_in: bfloat16 [8, 1536, 2, 1024], P('token'), may hold values from -0.15625 to 0.15625
- w_out: bfloat16 [8, 1536, 1024], P('token'), may hold values from -0.1875 to 0.1875
Outputs:
- input_grad: bfloat16 [8192, 8, 1536], P('dp', 'token')
- w_in_grad: bfloat16 [8, 1536, 2, 1024], P('token', 'dp')
- w_out_grad: bfloat16 [8, 1536, 1024], P('token', 'dp')
All inputs are finite; a program needn't handle non-finite values.
Results may differ from a plain program's by a relative error of at most 0.022.
Values may be sent and summed in bfloat16 or wider, within the bound.
No kernel may reach another device: no remote copies, remote signals or barrier semaphores. Data moves between devices by JAX's collectives and lax.ppermute only.
A program may use at most 128 MiB of HBM per device.

v0:
```python
import jax
import jax.numpy as jnp
from jax import lax
from jax.sharding import PartitionSpec as P

eps = 1e-06


def contract(left, right, dims_left, dims_right):
    return lax.dot_general(
        left, right, ((dims_left, dims_right), ((), ())), preferred_element_type=jnp.float32
    )


def normalize(values):
    scale = lax.rsqrt(jnp.mean(values * values, axis=-1, keepdims=True) + eps)
    return (values * scale, scale)


def norm_back(normed, scale, grads):
    return scale * (grads - normed * jnp.mean(grads * normed, axis=-1, keepdims=True))


def local(block_input, out_cotangent, w_in, w_out):
    samples = block_input.shape[0]
    width = block_input.shape[2]
    count = lax.axis_size("token")
    head = width // count
    hidden_units = w_out.shape[2]
    own_rows = width // lax.axis_size("dp")
    mixed = lax.all_to_all(
        block_input.reshape(samples, count, 1, head),
        "token",
        split_axis=1,
        concat_axis=2,
        tiled=True,
    )
    pre_norm = block_input[:, 0].astype(jnp.float32) + mixed.reshape(samples, width).astype(
        jnp.float32
    )
    normed, scale_one = normalize(pre_norm)
    state = normed.astype(jnp.bfloat16)
    flat_in = w_in[0].reshape(width, 2 * hidden_units)
    weight_out = w_out[0]
    both = contract(state, flat_in, (1,), (0,)).reshape(samples, 2, hidden_units)
    gate = both[:, 0]
    up_part = both[:, 1]
    sigma = jax.nn.sigmoid(gate)
    silu_gate = gate * sigma
    hidden = (silu_gate * up_part).astype(jnp.bfloat16)
    ffn_sum = contract(hidden, weight_out, (1,), (1,)) + state.astype(jnp.float32)
    out_normed, scale_two = normalize(ffn_sum)
    out_grad = norm_back(out_normed, scale_two, out_cotangent[:, 0].astype(jnp.float32))
    out_grad16 = out_grad.astype(jnp.bfloat16)
    hidden_grad = contract(out_grad16, weight_out, (1,), (0,))
    gate_grad = hidden_grad * up_part * sigma * (1.0 + gate * (1.0 - sigma))
    up_grad = hidden_grad * silu_gate
    inner_grad = (
        jnp.stack([gate_grad, up_grad], axis=1)
        .astype(jnp.bfloat16)
        .reshape(samples, 2 * hidden_units)
    )
    state_grad = contract(inner_grad, flat_in, (1,), (1,)) + out_grad
    pre_grad = norm_back(normed, scale_one, state_grad)
    returned = lax.all_to_all(
        pre_grad.reshape(samples, 1, count, head).astype(jnp.bfloat16),
        "token",
        split_axis=2,
        concat_axis=1,
        tiled=True,
    ).astype(jnp.float32)
    input_grad = (pre_grad + returned.reshape(samples, width)).astype(jnp.bfloat16)[:, None, :]
    columns = out_grad16
    down_grad = lax.psum_scatter(
        contract(columns, hidden, (0,), (0,)).astype(jnp.bfloat16),
        "dp",
        scatter_dimension=0,
        tiled=True,
    )
    columns = state
    in_grad = lax.psum_scatter(
        contract(columns, inner_grad, (0,), (0,))
        .reshape(own_rows * lax.axis_size("dp"), 2, hidden_units)
        .astype(jnp.bfloat16),
        "dp",
        scatter_dimension=0,
        tiled=True,
    )
    return (input_grad, in_grad[None], down_grad[None])


def solution(mesh):
    placed = (
        P("dp", "token", None),
        P("dp", "token", None),
        P("token", None, None, None),
        P("token", None, None),
    )
    return jax.shard_map(
        local,
        mesh=mesh,
        in_specs=placed,
        out_specs=(P("dp", "token", None), P("token", "dp", None, None), P("token", "dp", None)),
        check_vma=False,
    )
```

profile of v0, /device:TPU:8, one launch (start us, length us, event | category | flops | bytes accessed | tf_op | source)
XLA Modules:
  0.0 279.8 jit_solution(7272724064130774858)
XLA Ops:
  7.2 0.0 copy-start
  7.2 2.4 copy.19
  9.6 6.3 %all-to-all-start = ((bf16[256,8,1,192]{0,3,2,1:T(8,128)(2,1)}), bf16[256,8,1,192]{0,3,2,1:T(8,128)(2,1)}, u32[]{:S(2)}, u32[]{:S(2)}) async-start(bf16[256,8,1,192]{0,3,2,1:T(8,128)(2,1)} %bitcast.127), calls=%async_computation | async-start | bytes 1572864 | tf_op jit(solution)/shard_map/all_to_all | solution.py:31
  15.9 0.0 reduce-scatter.3.cloned.1.call-start
  15.9 8.0 %copy.34 = bf16[192,8,2,1024]{3,1,2,0:T(8,128)(2,1)} copy(bf16[192,8,2,1024]{3,2,1,0:T(2,128)(2,1)} %bitcast.125) | data formatting | bytes 12582912
  24.0 8.6 %copy.24 = bf16[2048,1536]{1,0:T(8,128)(2,1)} copy(bf16[2048,1536]{0,1:T(8,128)(2,1)} %bitcast.120) | data formatting | bytes 12582912 | tf_op jit(solution)/shard_map/dot_general | solution.py:10
  32.6 0.0 all-to-all-done
  32.6 2.5 bitcast_convert_fusion.1
  35.0 3.1 %copy.22 = f32[256,1536]{1,0:T(8,128)} copy(f32[256,1536]{0,1:T(8,128)} %bitcast.122) | data formatting | bytes 3145728 | tf_op jit(solution)/shard_map/convert_element_type | solution.py:38
  38.1 1.9 multiply_reduce_fusion.2
  40.0 3.0 %copy.23 = f32[256,1,1536]{2,0,1:T(8,128)} copy(f32[256,1,1536]{0,2,1:T(8,128)} %bitcast.123) | data formatting | bytes 3145728 | tf_op jit(solution)/shard_map/convert_element_type | solution.py:38
  43.0 1.8 fusion.23
  44.8 0.0 copy-start.8
  44.9 0.0 copy-start.1
  44.9 0.0 copy-start.3
  44.9 4.9 %fusion.31 = f32[256,2,1024]{2,0,1:T(8,128)S(1)} fusion(bf16[256,1536,1]{1,0,2:T(8,128)(2,1)S(1)} %fusion.23, bf16[2,1024,1536]{2,1,0:T(8,128)(2,1)} %bitcast.126), kind=kOutput, calls=%fused_computation.53 | convolution fusion | flops 1610612736 | bytes 9175040 | tf_op jit(solution)/shard_map/dot_general | solution.py:10
  49.8 0.0 copy-done.8
  49.8 0.0 copy-done
  49.9 0.0 copy-done.1
  49.9 0.0 copy-done.3
  49.9 0.0 copy-start.10
  49.9 0.0 copy-start.7
  49.9 1.3 multiply_reduce_fusion.1
  51.2 0.0 copy-start.5
  51.2 0.4 copy-done.7
  51.6 0.3 fusion.10
  51.9 0.4 fusion.21
  52.3 0.0 copy-done.10
  52.3 0.0 copy-done.5
  52.3 0.0 copy-start.9
  52.3 1.3 fusion.18
  53.7 0.0 copy-done.9
  53.7 1.1 maximum_convert_fusion
  54.8 2.3 copy.25
  57.1 6.0 %convolution_convert_fusion = bf16[1536,2,1024]{2,0,1:T(8,128)(2,1)} fusion(bf16[256,1536,1]{1,0,2:T(8,128)(2,1)} %copy-done.8, bf16[256,2,1024]{0,2,1:T(8,128)(2,1)} %copy.25), kind=kOutput, calls=%fused_computation | convolution fusion | flops 1613758464 | bytes 8126464 | tf_op jit(solution)/shard_map/dot_general | solution.py:10
  63.0 0.0 reduce-scatter.3.cloned.1.call-update
  63.1 0.2 reduce-scatter.5.cloned.1.call-start
  63.3 4.5 %convolution_convert_fusion.1 = bf16[1536,1024]{1,0:T(8,128)(2,1)} fusion(bf16[256,1536]{1,0:T(8,128)(2,1)} %copy-done.9, f32[256,2,1024]{2,0,1:T(8,128)} %copy-done.10), kind=kOutput, calls=%fused_computation.1 | convolution fusion | flops 808452096 | bytes 6029312 | tf_op jit(solution)/shard_map/dot_general | solution.py:10
  67.8 0.0 reduce-scatter.5.cloned.1.call-update
  67.8 0.0 copy-start.2
  67.9 0.0 copy-start.4
  67.9 6.9 %multiply_reduce_fusion = (f32[256]{0:T(256)S(1)}, f32[256,1536]{1,0:T(8,128)S(1)}) fusion(f32[256]{0:T(256)S(1)} %add_rsqrt_fusion.1, f32[256,1536]{1,0:T(8,128)} %copy.22, bf16[256,1,1536]{2,0,1:T(8,128)(2,1)} %param.4, f32[256]{0:T(256)S(1)} %broadcast_multiply_fusion.1, f32[256,1536]{1,0:T(8,128)} %copy-done.5, bf16[256,1,1536]{2,0,1:T(8,128)(2,1)} %param.5, ...), kind=kOutput, calls=%fused_computation.20 | convolution fusion | flops 1614937856 | bytes 13635584 | tf_op jit(solution)/shard_map/dot_general | solution.py:10
  74.7 0.0 copy-start.6
  74.8 1.1 copy-done.6
  75.9 0.0 copy-done.2
  75.9 0.0 copy-done.4
  75.9 1.3 fusion.28
  77.1 2.3 copy.26
  79.5 16.1 %all_to_all.8 = bf16[256,1,8,192]{0,3,1,2:T(8,128)(2,1)S(1)} all-to-all(bf16[256,1,8,192]{0,3,1,2:T(8,128)(2,1)} %bitcast.128), channel_id=1, replica_groups=mesh['dp'=32,'token'=8] {'token'}, dimensions={2} | all-to-all | bytes 1572864 | tf_op jit(solution)/shard_map/all_to_all | solution.py:65
  95.6 1.3 bitcast_convert_fusion
  96.9 3.1 %copy.29 = f32[256,1536]{1,0:T(8,128)} copy(f32[256,1536]{0,1:T(8,128)} %bitcast_convert_fusion) | data formatting | bytes 3145728 | tf_op jit(solution)/shard_map/convert_element_type | solution.py:71
  100.0 4.1 %fusion.22 = bf16[256,1,1536]{2,0,1:T(8,128)(2,1)} fusion(f32[256,1536]{1,0:T(8,128)} %copy.29, f32[256,1536]{1,0:T(8,128)} %copy-done.6, f32[256]{0:T(256)S(1)} %broadcast_multiply_fusion, f32[256,1536]{1,0:T(8,128)} %copy.22, bf16[256,1,1536]{2,0,1:T(8,128)(2,1)} %param.4, f32[256]{0:T(256)S(1)} %add_rsqrt_fusion.1), kind=kLoop, calls=%fused_computation.41 | loop fusion | flops 3145728 | bytes 6293504 | tf_op jit(solution)/shard_map/broadcast_in_dim | solution.py:72
  104.1 70.5 %reduce-scatter.3.cloned.1.call-done = bf16[48,2,1024]{2,0,1:T(8,128)(2,1)} async-done(((bf16[1536,2,1024]{2,0,1:T(8,128)(2,1)}), bf16[48,2,1024]{2,0,1:T(8,128)(2,1)}) %reduce-scatter.3.cloned.1.call-update) | async-done | bytes 196624 | tf_op jit(solution)/shard_map/reduce_scatter | solution.py:81
  174.5 1.8 copy.31
  176.3 96.6 %reduce-scatter.5.cloned.1.call-done = bf16[48,1024]{1,0:T(8,128)(2,1)} async-done(((bf16[1536,1024]{1,0:T(8,128)(2,1)}), bf16[48,1024]{1,0:T(8,128)(2,1)}) %reduce-scatter.5.cloned.1.call-update) | async-done | bytes 98320 | tf_op jit(solution)/shard_map/reduce_scatter | solution.py:74
  (4 shorter events, 0.0 us)
Async XLA Ops:
  7.2 42.7 %copy-start = (bf16[1,1536,1024]{2,1,0:T(8,128)(2,1)S(1)}, bf16[1,1536,1024]{2,1,0:T(8,128)(2,1)}, u32[]{:S(2)}) copy-start(bf16[1,1536,1024]{2,1,0:T(8,128)(2,1)} %param.7) | copy-start | bytes 9437188
  9.6 23.0 %all-to-all-start = ((bf16[256,8,1,192]{0,3,2,1:T(8,128)(2,1)}), bf16[256,8,1,192]{0,3,2,1:T(8,128)(2,1)}, u32[]{:S(2)}, u32[]{:S(2)}) async-start(bf16[256,8,1,192]{0,3,2,1:T(8,128)(2,1)} %bitcast.127), calls=%async_computation | async-start | bytes 1572864 | tf_op jit(solution)/shard_map/all_to_all | solution.py:31
  15.9 158.6 %reduce-scatter.3.cloned.1.call-start = ((), (), s32[]{:S(2)}) async-start(), calls=%async_computation.4 | async-start | bytes 6488064 | tf_op jit(solution)/shard_map/reduce_scatter | solution.py:81
  44.8 5.0 %copy-start.8 = (bf16[256,1536,1]{1,0,2:T(8,128)(2,1)}, bf16[256,1536,1]{1,0,2:T(8,128)(2,1)S(1)}, u32[]{:S(2)}) copy-start(bf16[256,1536,1]{1,0,2:T(8,128)(2,1)S(1)} %fusion.23) | copy-start | bytes 2359300
  44.9 5.0 %copy-start.1 = (f32[256,1536]{1,0:T(8,128)S(1)}, f32[256,1536]{1,0:T(8,128)}, u32[]{:S(2)}) copy-start(f32[256,1536]{1,0:T(8,128)} %copy.22) | copy-start | bytes 4718596
  44.9 5.0 %copy-start.3 = (bf16[256,1,1536]{2,0,1:T(8,128)(2,1)S(1)}, bf16[256,1,1536]{2,0,1:T(8,128)(2,1)}, u32[]{:S(2)}) copy-start(bf16[256,1,1536]{2,0,1:T(8,128)(2,1)} %param.4) | copy-start | bytes 2359300
  49.9 2.4 copy-start.10
  49.9 1.7 copy-start.7
  51.2 1.1 copy-start.5
  52.3 1.3 copy-start.9
  63.1 209.9 %reduce-scatter.5.cloned.1.call-start = ((), (), s32[]{:S(2)}) async-start(), calls=%async_computation.5 | async-start | bytes 3244032 | tf_op jit(solution)/shard_map/reduce_scatter | solution.py:74
  67.8 8.0 %copy-start.2 = (f32[256,1536]{1,0:T(8,128)S(1)}, f32[256,1536]{1,0:T(8,128)}, u32[]{:S(2)}) copy-start(f32[256,1536]{1,0:T(8,128)} %copy.22) | copy-start | bytes 4718596
  67.9 8.0 %copy-start.4 = (bf16[256,1,1536]{2,0,1:T(8,128)(2,1)S(1)}, bf16[256,1,1536]{2,0,1:T(8,128)(2,1)}, u32[]{:S(2)}) copy-start(bf16[256,1,1536]{2,0,1:T(8,128)(2,1)} %param.4) | copy-start | bytes 2359300
  74.7 1.1 copy-start.6
Sparse Core Ops, SparseCore 0:
  63.2 111.3 reduce-scatter.2
  179.5 93.3 reduce-scatter.4
where the time goes:
time: 281 us; the launch traced here: 280 us
  waiting for transfers between devices  167 us (59%)
  local copies, waits for them, and re-layouts  36.3 us (13%)
  matrix products  24.9 us (9%)
  blocking collectives  16.1 us (6%)
  other arithmetic  14.6 us (5%)
  between operations  14.2 us (5%)
  starting transfers between devices  6.51 us (2%)
    reduce_scatter x1, waiting for transfers between devices, local(): lax.psum_scatter(contract(columns, hidden, (0,), (0,)).astype(jnp.bfloat1...  96.6 us
    reduce_scatter x1, waiting for transfers between devices, local(): lax.psum_scatter(contract(columns, inner_grad, (0,), (0,)).reshape(own_ro...  70.5 us
    dot_general x6, matrix products, contract(): lax.dot_general(left, right, ((dims_left, dims_right), ((), ())), preferr...  24.9 us
    all_to_all x1, blocking collectives, local(): lax.all_to_all(pre_grad.reshape(samples, 1, count, head).astype(jnp.bfloa...  16.1 us
    unnamed x25, local copies, waits for them, and re-layouts  13.9 us
    dot_general x1, local copies, waits for them, and re-layouts, contract(): lax.dot_general(left, right, ((dims_left, dims_right), ((), ())), preferr...  8.62 us
    all_to_all x1, starting transfers between devices, local(): lax.all_to_all(block_input.reshape(samples, count, 1, head), 'token', spl...  6.29 us
    convert_element_type x2, local copies, waits for them, and re-layouts, local(): mixed.reshape(samples, width).astype(jnp.float32)  6.08 us
  transfers between devices with their start and end apart: 3, of which 2 were waited for; matrix products, arithmetic and copies ran while one was open for 15% of the time, Pallas kernels for 0%

commit v1 on v0

v1 whole, which is shorter than its diff:
```python
import functools

import jax
import jax.numpy as jnp
from jax import lax
from jax.experimental import pallas as pl
from jax.experimental.pallas import tpu as pltpu
from jax.sharding import PartitionSpec as P

EPS = 1e-06
TOK = 8
F32 = jnp.float32
BF16 = jnp.bfloat16
VMEM_LIMIT = 56 * 1024 * 1024


def low_lanes(rows):
    return lax.broadcasted_iota(jnp.int32, (rows, 128), 1) < 64


def turn(values):
    return pltpu.roll(values, 64, 1)


def pack(read, packed_ref):
    samples = packed_ref.shape[1] * 2 // 3
    half = samples // 2
    low, low_half = low_lanes(samples), low_lanes(half)
    for pair in range(TOK // 2):
        first, middle, last = read(3 * pair), read(3 * pair + 1), read(3 * pair + 2)
        even, odd = packed_ref.at[2 * pair], packed_ref.at[2 * pair + 1]
        even[:samples] = first.astype(BF16)
        even[samples:] = jnp.where(low_half, middle[:half], turn(middle[half:])).astype(BF16)
        odd[:samples] = turn(jnp.where(low, last, middle)).astype(BF16)
        odd[samples:] = jnp.where(low_half, turn(last[:half]), last[half:]).astype(BF16)


def unpack(packed_ref, write):
    samples = packed_ref.shape[1] * 2 // 3
    low = low_lanes(samples)
    for pair in range(TOK // 2):
        even, odd = packed_ref.at[2 * pair], packed_ref.at[2 * pair + 1]
        turned = turn(odd[:samples].astype(F32))
        rest = even[samples:].astype(F32)
        rest = jnp.concatenate([rest, turn(rest)], axis=0)
        rest_odd = odd[samples:].astype(F32)
        rest_odd = jnp.concatenate([turn(rest_odd), rest_odd], axis=0)
        write(3 * pair, even[:samples].astype(F32))
        write(3 * pair + 1, jnp.where(low, rest, turned))
        write(3 * pair + 2, jnp.where(low, turned, rest_odd))


def tile(t):
    return slice(128 * t, 128 * t + 128)


def pack_kernel(x_ref, packed_ref):
    pack(lambda t: x_ref[:, tile(t)].astype(F32), packed_ref)


def nn(a, b):
    return lax.dot_general(a, b, (((1,), (0,)), ((), ())), preferred_element_type=F32)


def nt(a, b):
    return lax.dot_general(a, b, (((1,), (1,)), ((), ())), preferred_element_type=F32)


def forward_kernel(
    index_ref, x_ref, recv_ref, cot_ref, w_in_hbm, w_out_hbm,
    own_ref, send_ref, normed_ref, scale_ref, grad_ref, grad16_ref, slope_ref, silu_ref,
    w_in, w_out, state, hidden, turned, in_sem, out_sem,
):
    samples, width = x_ref.shape
    ff = w_out.shape[1]
    wide = 256
    steps = ff // wide
    half = width // 2

    def w_in_copy(j, c):
        cols = pl.ds(c * ff + j * wide, wide)
        return pltpu.make_async_copy(w_in_hbm.at[:, cols], w_in.at[:, cols], in_sem.at[2 * j + c])

    for j in range(steps):
        w_in_copy(j, 0).start()
        w_in_copy(j, 1).start()
    out_copy = pltpu.make_async_copy(w_out_hbm, w_out, out_sem)
    out_copy.start()

    rank = index_ref[0]

    def spread(at):
        for b in range(16):
            place = slice(at + 48 * b, at + 48 * b + 48)
            own_ref[place, :] = turned[pl.ds(pl.multiple_of((rank ^ (2 * b)) * 48, 48), 48), :]
            send_ref[place, :] = turned[pl.ds(pl.multiple_of((rank ^ (2 * b + 1)) * 48, 48), 48), :]

    def add_mixed(t, mixed):
        normed_ref[:, tile(t)] = x_ref[:, tile(t)].astype(F32) + mixed

    unpack(recv_ref, add_mixed)
    squares = jnp.zeros((samples, 128), F32)
    for t in range(width // 128):
        v = normed_ref[:, tile(t)]
        squares = squares + v * v
    scale = lax.rsqrt(jnp.sum(squares, axis=1, keepdims=True) / width + EPS)
    scale_ref[...] = jnp.broadcast_to(scale, scale_ref.shape)
    for t in range(width // 128):
        v = normed_ref[:, tile(t)] * scale
        normed_ref[:, tile(t)] = v
        state[:, tile(t)] = v.astype(BF16)

    for j in range(steps):
        cols = slice(wide * j, wide * j + wide)
        w_in_copy(j, 0).wait()
        gate = nn(state[...], w_in[:, cols])
        w_in_copy(j, 1).wait()
        up = nn(state[...], w_in[:, ff + wide * j : ff + wide * j + wide])
        sigma = jax.nn.sigmoid(gate)
        silu_gate = gate * sigma
        part = (silu_gate * up).astype(BF16)
        hidden[:, cols] = part
        send_ref[width + wide * j : width + wide * j + wide, :] = part
        silu_ref[:, cols] = silu_gate
        slope_ref[:, cols] = up * sigma * (1.0 + gate * (1.0 - sigma))

    for t in range(width // 128):
        turned[tile(t), :] = state[:, tile(t)].T
    spread(half)

    out_copy.wait()
    for d in range(width // wide):
        cols = slice(wide * d, wide * d + wide)
        grad_ref[:, cols] = nt(hidden[...], w_out[cols, :]) + state[:, cols].astype(F32)
    squares = jnp.zeros((samples, 128), F32)
    products = jnp.zeros((samples, 128), F32)
    for t in range(width // 128):
        v = grad_ref[:, tile(t)]
        squares = squares + v * v
        products = products + v * cot_ref[:, tile(t)].astype(F32)
    scale_two = lax.rsqrt(jnp.sum(squares, axis=1, keepdims=True) / width + EPS)
    mean = scale_two * jnp.sum(products, axis=1, keepdims=True) / width
    for t in range(width // 128):
        out_normed = grad_ref[:, tile(t)] * scale_two
        g = scale_two * (cot_ref[:, tile(t)].astype(F32) - out_normed * mean)
        grad_ref[:, tile(t)] = g
        g16 = g.astype(BF16)
        grad16_ref[:, tile(t)] = g16
        turned[tile(t), :] = g16.T
    spread(0)


def inner_kernel(grad16_ref, slope_ref, silu_ref, w_out_ref, inner_ref):
    ff = w_out_ref.shape[1]
    wide = 256
    for j in range(ff // wide):
        cols = slice(wide * j, wide * j + wide)
        hidden_grad = nn(grad16_ref[...], w_out_ref[:, cols])
        inner_ref[cols, :] = (hidden_grad * slope_ref[:, cols]).astype(BF16)
        inner_ref[ff + wide * j : ff + wide * j + wide, :] = (hidden_grad * silu_ref[:, cols]).astype(BF16)


def input_kernel(
    inner_ref, w_in_hbm, normed_ref, scale_ref, grad_ref, after_ref, pre_ref, packed_ref, w_in, inner, sem
):
    del after_ref
    samples, width = normed_ref.shape
    wide = 256

    def copy(d):
        rows = pl.ds(d * wide, wide)
        return pltpu.make_async_copy(w_in_hbm.at[rows], w_in.at[rows], sem.at[d])

    for d in range(width // wide):
        copy(d).start()
    for j in range(inner.shape[1] // samples):
        inner[:, samples * j : samples * j + samples] = inner_ref[samples * j : samples * j + samples, :]
    products = jnp.zeros((samples, 128), F32)
    for d in range(width // wide):
        copy(d).wait()
        cols = slice(wide * d, wide * d + wide)
        g = nt(inner[...], w_in[cols, :]) + grad_ref[:, cols]
        pre_ref[:, cols] = g
        p = g * normed_ref[:, cols]
        products = products + p[:, :128] + p[:, 128:]
    mean = jnp.sum(products, axis=1, keepdims=True) / width
    scale = scale_ref[:, :1]
    for t in range(width // 128):
        pre_ref[:, tile(t)] = scale * (pre_ref[:, tile(t)] - normed_ref[:, tile(t)] * mean)
    pack(lambda t: pre_ref[:, tile(t)], packed_ref)


def final_kernel(pre_ref, recv_ref, out_ref):
    def write(t, returned):
        out_ref[:, tile(t)] = (pre_ref[:, tile(t)] + returned).astype(BF16)

    unpack(recv_ref, write)


KEEP_FIRST = ((0, 3, 1, 2), (0, 1, 3, 2))
PARTNERS = ((1, 3), (3, 1))


def grad_kernel(x_first, at, block, own_ref, recv_ref, right_ref, right_recv_ref, after_ref, *outs):
    del after_ref
    rows = own_ref.shape[0] // 2
    wide = 256
    per = outs[0].shape[1] // wide
    for k in range(2 * per):
        flavour, col = divmod(k, per)
        keep, send = outs[2 * flavour], outs[2 * flavour + 1]
        order = KEEP_FIRST[flavour]
        place = slice(block + wide * k, block + wide * k + wide)
        g = nn(own_ref[at : at + rows, :], right_ref[place, :])
        g = (g + nn(recv_ref[at : at + rows, :], right_recv_ref[place, :])).astype(BF16)
        for b in range(16):
            rz, rx = order.index(b // 4), order.index(b % 4)
            to = rx * 4 + rz if x_first else rz * 4 + rx
            target = keep if to < 8 else send
            to = (to % 8) * 48
            target[to : to + 48, wide * col : wide * col + wide] = g[48 * b : 48 * b + 48]


def params():
    return pltpu.CompilerParams(vmem_limit_bytes=VMEM_LIMIT)


VMEM = pl.BlockSpec(memory_space=pltpu.VMEM)
SMEM = pl.BlockSpec(memory_space=pltpu.SMEM)
ANY = pl.BlockSpec(memory_space=pl.ANY)


def cost(flops, moved):
    return pl.CostEstimate(flops=int(flops), bytes_accessed=int(moved), transcendentals=0)


def shape(dims, dtype=BF16):
    return jax.ShapeDtypeStruct(dims, dtype)


def swap(values, distance):
    return lax.ppermute(values, "dp", [(i, i ^ distance) for i in range(32)])


def gradients(x_first, at, block, columns, own, recv, right, right_recv, after, name):
    piece = shape((384, columns // 2))
    moved = (own.size + recv.size + 2 * right.size + 768 * columns) * 2
    return pl.pallas_call(
        functools.partial(grad_kernel, x_first, at, block),
        out_shape=[piece] * 4,
        in_specs=[VMEM] * 4 + [ANY],
        out_specs=[VMEM] * 4,
        compiler_params=params(),
        cost_estimate=cost(2 * 768 * 512 * columns, moved),
        name=name,
    )(own, recv, right, right_recv, after)


def reduce_step(scales, step, keep, send):
    kept, sent = [], []
    for flavour in range(2):
        scale = scales[step // 2]
        got = swap(send[flavour], PARTNERS[flavour][step % 2] * scale)
        total = keep[flavour].astype(F32) + got.astype(F32)
        if step == 3:
            kept.append(total.astype(BF16))
            continue
        half = total.shape[0] // 2
        kept.append(total[:half].astype(BF16))
        sent.append(total[half:].astype(BF16))
    return kept, sent


def local(block_input, out_cotangent, w_in, w_out):
    samples, _, width = block_input.shape
    ff = w_out.shape[2]
    x = block_input[:, 0]
    cotangent = out_cotangent[:, 0]
    flat_in = w_in[0].reshape(width, 2 * ff)
    weight_out = w_out[0]
    packed_shape = shape((TOK, samples * 3 // 2, 128))
    index = lax.axis_index("dp").astype(jnp.int32).reshape(1)

    packed = pl.pallas_call(
        pack_kernel, out_shape=packed_shape, in_specs=[VMEM], out_specs=VMEM, compiler_params=params(),
        cost_estimate=cost(samples * width, 4 * samples * width), name="pack",
    )(x)
    recv = lax.all_to_all(packed, "token", split_axis=0, concat_axis=0, tiled=True)

    full = shape((samples, width), F32)
    gates = shape((samples, ff), F32)
    own, out_send, normed, scale, out_grad, out_grad16, slope, silu = pl.pallas_call(
        forward_kernel,
        out_shape=[
            shape((width, samples)), shape((width + ff, samples)), full, shape((samples, 128), F32), full,
            shape((samples, width)), gates, gates,
        ],
        in_specs=[SMEM, VMEM, VMEM, VMEM, ANY, ANY],
        out_specs=[VMEM] * 8,
        scratch_shapes=[
            pltpu.VMEM((width, 2 * ff), BF16),
            pltpu.VMEM((width, ff), BF16),
            pltpu.VMEM((samples, width), BF16),
            pltpu.VMEM((samples, ff), BF16),
            pltpu.VMEM((width, samples), BF16),
            pltpu.SemaphoreType.DMA((8,)),
            pltpu.SemaphoreType.DMA,
        ],
        compiler_params=params(),
        cost_estimate=cost(6 * samples * width * ff, 18e6),
        name="forward",
    )(index, x, recv, cotangent, flat_in, weight_out)
    out_recv = swap(out_send, 1)

    inner = pl.pallas_call(
        inner_kernel,
        out_shape=shape((2 * ff, samples)),
        in_specs=[VMEM] * 4,
        out_specs=VMEM,
        compiler_params=params(),
        cost_estimate=cost(2 * samples * width * ff, 8e6),
        name="inner",
    )(out_grad16, slope, silu, weight_out)
    inner_recv = swap(inner, 1)

    down = gradients(False, 0, width, ff, own, out_recv, out_send, out_recv, inner, "down_grads")
    up = gradients(True, width // 2, 0, 2 * ff, own, out_recv, inner, inner_recv, down[1], "in_grads")

    pre_grad, back = pl.pallas_call(
        input_kernel,
        out_shape=[full, packed_shape],
        in_specs=[VMEM, ANY, VMEM, VMEM, VMEM, ANY],
        out_specs=[VMEM] * 2,
        scratch_shapes=[
            pltpu.VMEM((width, 2 * ff), BF16),
            pltpu.VMEM((samples, 2 * ff), BF16),
            pltpu.SemaphoreType.DMA((width // 256,)),
        ],
        compiler_params=params(),
        cost_estimate=cost(4 * samples * width * ff, 14e6),
        name="input",
    )(inner, flat_in, normed, scale, out_grad, up[1])
    returned = lax.all_to_all(back, "token", split_axis=0, concat_axis=0, tiled=True)

    down_keep, down_send = down[0::2], down[1::2]
    up_keep, up_send = up[0::2], up[1::2]
    for step in range(4):
        down_keep, down_send = reduce_step((8, 2), step, down_keep, down_send)
        up_keep, up_send = reduce_step((2, 8), step, up_keep, up_send)

    input_grad = pl.pallas_call(
        final_kernel, out_shape=shape((samples, width)), in_specs=[VMEM] * 2, out_specs=VMEM,
        compiler_params=params(), cost_estimate=cost(samples * width, 8 * samples * width), name="final",
    )(pre_grad, returned)
    return (
        input_grad[:, None, :],
        jnp.stack(up_keep, axis=1)[None],
        jnp.concatenate(down_keep, axis=1)[None],
    )


def solution(mesh):
    placed = (
        P("dp", "token", None),
        P("dp", "token", None),
        P("token", None, None, None),
        P("token", None, None),
    )
    return jax.shard_map(
        local,
        mesh=mesh,
        in_specs=placed,
        out_specs=(P("dp", "token", None), P("token", "dp", None, None), P("token", "dp", None)),
        check_vma=False,
    )
```

time: 281 us -> 132 us (0.47)
  waiting for transfers between devices: 167 us -> 39 us
  Pallas kernels: 0 us -> 40.7 us
  starting transfers between devices: 6.51 us -> 35.3 us
  matrix products: 24.9 us -> 0 us
  local copies, waits for them, and re-layouts: 36.3 us -> 12.9 us
  blocking collectives: 16.1 us -> 0 us
  between operations: 14.2 us -> 0.94 us
  other arithmetic: 14.6 us -> 3.07 us
    reduce_scatter x2 -> x0, waiting for transfers between devices: 167 us -> none  [the longest x1 96.6 us: local(): lax.psum_scatter(contract(columns, hidden, (0,), (0,)).astype(jnp.bfloat1...]
    pallas_call x0 -> x7, Pallas kernels: none -> 40.7 us  [the longest x1 12 us: local(): pl.pallas_call(forward_kernel, out_shape=[shape((width, samples)), shape(...]
    ppermute x0 -> x18, waiting for transfers between devices: none -> 36.2 us  [swap(): return lax.ppermute(values, 'dp', [(i, i ^ distance) for i in range(32)])]
    dot_general x6 -> x0, matrix products: 24.9 us -> none  [contract(): lax.dot_general(left, right, ((dims_left, dims_right), ((), ())), preferr...]
    ppermute x0 -> x18, starting transfers between devices: none -> 24.1 us  [swap(): return lax.ppermute(values, 'dp', [(i, i ^ distance) for i in range(32)])]
    all_to_all x1 -> x0, blocking collectives: 16.1 us -> none  [local(): lax.all_to_all(pre_grad.reshape(samples, 1, count, head).astype(jnp.bfloa...]
    convert_element_type x5 -> x0, local copies, waits for them, and re-layouts: 13.8 us -> none  [the longest x2 6.08 us: local(): mixed.reshape(samples, width).astype(jnp.float32)]
    dot_general x1 -> x0, local copies, waits for them, and re-layouts: 8.62 us -> none  [contract(): lax.dot_general(left, right, ((dims_left, dims_right), ((), ())), preferr...]
  transfers between devices with their start and end apart: 3 -> 20, of which waited for: 2 -> 9; matrix products, arithmetic and copies ran while one was open for 15% -> 8% of each run, Pallas kernels for 0% -> 20%
where the time goes in v1:
time: 132 us
  Pallas kernels  40.7 us (31%)
  waiting for transfers between devices  39 us (30%)
  starting transfers between devices  35.3 us (27%)
  local copies, waits for them, and re-layouts  12.9 us (10%)
  other arithmetic  3.07 us (2%)
    ppermute x18, waiting for transfers between devices, swap(): return lax.ppermute(values, 'dp', [(i, i ^ distance) for i in range(32)])  36.2 us
    ppermute x18, starting transfers between devices, swap(): return lax.ppermute(values, 'dp', [(i, i ^ distance) for i in range(32)])  24.1 us
    unnamed x18, local copies, waits for them, and re-layouts  12.8 us
    pallas_call x1, Pallas kernels, local(): pl.pallas_call(forward_kernel, out_shape=[shape((width, samples)), shape(...  12 us
    pallas_call x1, Pallas kernels, local(): pl.pallas_call(input_kernel, out_shape=[full, packed_shape], in_specs=[VM...  9.65 us
    pallas_call x2, Pallas kernels, gradients(): pl.pallas_call(functools.partial(grad_kernel, x_first, at, block), out_sh...  9.21 us
    all_to_all x1, starting transfers between devices, local(): lax.all_to_all(packed, 'token', split_axis=0, concat_axis=0, tiled=True)  6.27 us
    all_to_all x1, starting transfers between devices, local(): lax.all_to_all(back, 'token', split_axis=0, concat_axis=0, tiled=True)  4.93 us
  transfers between devices with their start and end apart: 20, of which 9 were waited for; matrix products, arithmetic and copies ran while one was open for 8% of the time, Pallas kernels for 20%

profile of v1, /device:TPU:8, one launch (start us, length us, event | category | flops | bytes accessed | tf_op | source)
XLA Modules:
  0.0 131.9 jit_solution(7856782610193709651)
XLA Ops:
  0.6 2.3 %pack.1 = bf16[8,384,128]{2,1,0:T(8,128)(2,1)} custom-call(bf16[256,1536]{1,0:T(8,128)(2,1)} %bitcast.21), custom_call_target="tpu_custom_call" | custom-call | flops 393216 | bytes 1572864 | tf_op jit(solution)/shard_map/pack/pallas_call | solution.py:284
  2.9 6.3 %all-to-all-start = ((bf16[8,384,128]{2,1,0:T(8,128)(2,1)}), bf16[8,384,128]{2,1,0:T(8,128)(2,1)S(1)}, u32[]{:S(2)}, u32[]{:S(2)}) async-start(bf16[8,384,128]{2,1,0:T(8,128)(2,1)} %pack.1), calls=%async_computation | async-start | bytes 1572864 | tf_op jit(solution)/shard_map/all_to_all | solution.py:288
  9.2 8.0 %copy.8 = bf16[192,8,2,1024]{3,1,2,0:T(8,128)(2,1)} copy(bf16[192,8,2,1024]{3,2,1,0:T(2,128)(2,1)} %bitcast.20) | data formatting | bytes 12582912
  17.2 2.8 %all-to-all-done.recv_ref = bf16[8,384,128]{2,1,0:T(8,128)(2,1)S(1)} async-done(((bf16[8,384,128]{2,1,0:T(8,128)(2,1)}), bf16[8,384,128]{2,1,0:T(8,128)(2,1)S(1)}, u32[]{:S(2)}, u32[]{:S(2)}) %all-to-all-start) | async-done | bytes 786464 | tf_op jit(solution)/shard_map/all_to_all | solution.py:288
  20.0 0.9 copy-done.1
  20.9 12.0 %forward.1 = (bf16[1536,256]{1,0:T(8,128)(2,1)}, bf16[2560,256]{1,0:T(8,128)(2,1)}, f32[256,1536]{1,0:T(8,128)}, f32[256,128]{1,0:T(8,128)}, f32[256,1536]{1,0:T...) custom-call(s32[1]{0:T(128)} %bitcast.index_ref, bf16[256,1536]{1,0:T(8,128)(2,1)} %bitcast.22, ...), custom_call_target="tpu_custom_call" | custom-call | flops 2415919104 | bytes 18000000 | tf_op jit(solution)/shard_map/forward/pallas_call | solution.py:292
  32.9 0.1 collective-permute-start
  33.0 4.8 %inner.1.after_ref.right_ref.inner_ref = bf16[2048,256]{1,0:T(8,128)(2,1)} custom-call(bf16[256,1536]{1,0:T(8,128)(2,1)} %get-tuple-element.21.grad16_ref, f32[256,1024]{1,0:T(8,128)} %get-tuple-element.22.slope_ref, f32[256,1024]{1,0:T(8,128)} %get-tuple-element.23.silu_ref, bf16[1536,1024]{1,0:T(8,128)(2,1)} %bitcast.19), custom_call_target="tpu_custom_call" | custom-call | flops 805306368 | bytes 8000000 | tf_op jit(solution)/shard_map/inner/pallas_call | solution.py:315
  37.8 0.5 collective-permute-start.1
  38.3 0.0 collective-permute-done.recv_ref.right_recv_ref
  38.3 1.1 copy-done
  39.4 4.1 %down_grads.1 = (bf16[384,512]{1,0:T(8,128)(2,1)}, bf16[384,512]{1,0:T(8,128)(2,1)}, bf16[384,512]{1,0:T(8,128)(2,1)}, bf16[384,512]{1,0:T(8,128)(2,1)}) custom-call(bf16[1536,256]{1,0:T(8,128)(2,1)} %get-tuple-element.27.own_ref, bf16[2560,256]{1,0:T(8,128)(2,1)} %copy-done, bf16[2560,256]{1,0:T(8,128)(2,1)} %get-tuple-element.28.right_ref, ...), custom_call_target="tpu_custom_call" | custom-call | flops 805306368 | bytes 6291456 | tf_op jit(solution)/shard_map/down_grads/pallas_call | solution.py:248
  43.5 3.3 %collective-permute-start.10 = (bf16[384,512]{1,0:T(8,128)(2,1)}, bf16[384,512]{1,0:T(8,128)(2,1)}, u32[]{:S(2)}, u32[]{:S(2)}) collective-permute-start(bf16[384,512]{1,0:T(8,128)(2,1)} %get-tuple-element.29.after_ref), channel_id=1, source_target_pairs={{0,64},{8,72},{16,80},{24,88},{32,96},{40,104},{48,112},{56,120},{... | collective-permute-start | bytes 1179656 | tf_op jit(solution)/shard_map/ppermute | solution.py:242
  46.7 3.6 %collective-permute-start.14 = (bf16[384,512]{1,0:T(8,128)(2,1)}, bf16[384,512]{1,0:T(8,128)(2,1)S(1)}, u32[]{:S(2)}, u32[]{:S(2)}) collective-permute-start(bf16[384,512]{1,0:T(8,128)(2,1)} %get-tuple-element.38), channel_id=1, source_target_pairs={{0,192},{8,200},{16,208},{24,216},{32,224},{40,232},{48,240},{56,2... | collective-permute-start | bytes 1179656 | tf_op jit(solution)/shard_map/ppermute | solution.py:242
  50.3 0.0 collective-permute-done.1.right_recv_ref
  50.3 1.0 copy-done.7
  51.3 5.1 %in_grads.1 = (bf16[384,1024]{1,0:T(8,128)(2,1)}, bf16[384,1024]{1,0:T(8,128)(2,1)}, bf16[384,1024]{1,0:T(8,128)(2,1)}, bf16[384,1024]{1,0:T(8,128)(2,1)}) custom-call(bf16[1536,256]{1,0:T(8,128)(2,1)} %get-tuple-element.27.own_ref, bf16[2560,256]{1,0:T(8,128)(2,1)} %copy-done, bf16[2048,256]{1,0:T(8,128)(2,1)} %inner.1.after_ref.right_ref.inner_ref, ...), custom_call_target="tpu_custom_call" | custom-call | flops 1610612736 | bytes 7340032 | tf_op jit(solution)/shard_map/in_grads/pallas_call | solution.py:248
  56.4 1.5 %collective-permute-start.2 = (bf16[384,1024]{1,0:T(8,128)(2,1)}, bf16[384,1024]{1,0:T(8,128)(2,1)S(1)}, u32[]{:S(2)}, u32[]{:S(2)}) collective-permute-start(bf16[384,1024]{1,0:T(8,128)(2,1)} %get-tuple-element.30.after_ref), channel_id=1, source_target_pairs={{0,16},{8,24},{16,0},{24,8},{32,48},{40,56},{48,32},{56,40},{64,80... | collective-permute-start | bytes 2359304 | tf_op jit(solution)/shard_map/ppermute | solution.py:242
  57.9 2.1 %collective-permute-start.6 = (bf16[384,1024]{1,0:T(8,128)(2,1)}, bf16[384,1024]{1,0:T(8,128)(2,1)S(1)}, u32[]{:S(2)}, u32[]{:S(2)}) collective-permute-start(bf16[384,1024]{1,0:T(8,128)(2,1)} %get-tuple-element.35), channel_id=1, source_target_pairs={{0,48},{8,56},{16,32},{24,40},{32,16},{40,24},{48,0},{56,8},{64,11... | collective-permute-start | bytes 2359304 | tf_op jit(solution)/shard_map/ppermute | solution.py:242
  60.0 9.6 %input.1 = (f32[256,1536]{1,0:T(8,128)}, bf16[8,384,128]{2,1,0:T(8,128)(2,1)}) custom-call(bf16[2048,256]{1,0:T(8,128)(2,1)} %inner.1.after_ref.right_ref.inner_ref, bf16[1536,2048]{1,0:T(8,128)(2,1)} %bitcast.17, f32[256,1536]{1,0:T(8,128)} %get-tuple-element.24.normed_ref, f32[256,128]{1,0:T(8,128)} %get-tuple-element.25.scale_ref, ...), custom_call_target="tpu_custom_call" | custom-call | flops 1610612736 | bytes 14000000 | tf_op jit(solution)/shard_map/input/pallas_call | solution.py:329
  69.7 4.9 %all-to-all-start.1 = ((bf16[8,384,128]{2,1,0:T(8,128)(2,1)}), bf16[8,384,128]{2,1,0:T(8,128)(2,1)S(1)}, u32[]{:S(2)}, u32[]{:S(2)}) async-start(bf16[8,384,128]{2,1,0:T(8,128)(2,1)} %get-tuple-element.32), calls=%async_computation.1 | async-start | bytes 1572864 | tf_op jit(solution)/shard_map/all_to_all | solution.py:343
  74.6 0.0 collective-permute-done.10
  74.6 1.1 add_convert_fusion.3
  75.7 0.6 collective-permute-start.11
  76.4 0.0 collective-permute-done.14
  76.4 0.0 copy-done.5
  76.4 0.1 add_convert_fusion.2
  76.5 0.0 copy-start.4
  76.5 1.0 collective-permute-start.15
  77.6 14.0 %collective-permute-done.11 = bf16[192,512]{1,0:T(8,128)(2,1)S(1)} collective-permute-done((bf16[192,512]{1,0:T(8,128)(2,1)S(1)}, bf16[192,512]{1,0:T(8,128)(2,1)S(1)}, u32[]{:S(2)}, u32[]{:S(2)}) %collective-permute-start.11) | collective-permute-done | bytes 196640 | tf_op jit(solution)/shard_map/ppermute | solution.py:242
  91.6 0.1 add_convert_fusion.7
  91.6 0.7 collective-permute-start.12
  92.3 0.0 collective-permute-done.15
  92.3 0.1 add_convert_fusion.6
  92.4 1.0 collective-permute-start.16
  93.3 3.0 %collective-permute-done.12 = bf16[96,512]{1,0:T(8,128)(2,1)S(1)} collective-permute-done((bf16[96,512]{1,0:T(8,128)(2,1)S(1)}, bf16[96,512]{1,0:T(8,128)(2,1)S(1)}, u32[]{:S(2)}, u32[]{:S(2)}) %collective-permute-start.12) | collective-permute-done | bytes 98336 | tf_op jit(solution)/shard_map/ppermute | solution.py:242
  96.4 1.2 collective-permute-start.13
  97.6 0.7 collective-permute-done.16
  98.3 0.3 collective-permute-start.17
  98.7 3.5 %collective-permute-done.13 = bf16[48,512]{1,0:T(8,128)(2,1)S(1)} collective-permute-done((bf16[48,512]{1,0:T(8,128)(2,1)S(1)}, bf16[48,512]{1,0:T(8,128)(2,1)S(1)}, u32[]{:S(2)}, u32[]{:S(2)}) %collective-permute-start.13) | collective-permute-done | bytes 49184 | tf_op jit(solution)/shard_map/ppermute | solution.py:242
  102.2 0.0 collective-permute-done.2
  102.2 0.3 add_convert_fusion.1
  102.6 0.8 collective-permute-start.3
  103.4 0.0 collective-permute-done.6
  103.4 0.3 add_convert_fusion
  103.7 0.1 collective-permute-start.7
  103.8 0.0 collective-permute-done.17
  103.9 0.6 maximum_bitcast_fusion.1
  104.5 7.2 %collective-permute-done.3 = bf16[192,1024]{1,0:T(8,128)(2,1)S(1)} collective-permute-done((bf16[192,1024]{1,0:T(8,128)(2,1)S(1)}, bf16[192,1024]{1,0:T(8,128)(2,1)S(1)}, u32[]{:S(2)}, u32[]{:S(2)}) %collective-permute-start.3) | collective-permute-done | bytes 393248 | tf_op jit(solution)/shard_map/ppermute | solution.py:242
  111.7 0.1 add_convert_fusion.5
  111.8 0.1 collective-permute-start.4
  112.0 0.0 collective-permute-done.7
  112.0 0.1 add_convert_fusion.4
  112.1 5.1 %collective-permute-start.8 = (bf16[96,1024]{1,0:T(8,128)(2,1)S(1)}, bf16[96,1024]{1,0:T(8,128)(2,1)S(1)}, u32[]{:S(2)}, u32[]{:S(2)}) collective-permute-start(bf16[96,1024]{1,0:T(8,128)(2,1)S(1)} %slice.129), channel_id=1, source_target_pairs={{0,192},{8,200},{16,208},{24,216},{32,224},{40,232},{48,240},{56,2... | collective-permute-start | bytes 589832 | tf_op jit(solution)/shard_map/ppermute | solution.py:242
  117.2 4.8 %collective-permute-done.4 = bf16[96,1024]{1,0:T(8,128)(2,1)S(1)} collective-permute-done((bf16[96,1024]{1,0:T(8,128)(2,1)S(1)}, bf16[96,1024]{1,0:T(8,128)(2,1)S(1)}, u32[]{:S(2)}, u32[]{:S(2)}) %collective-permute-start.4) | collective-permute-done | bytes 196640 | tf_op jit(solution)/shard_map/ppermute | solution.py:242
  122.1 1.1 collective-permute-start.5
  123.2 1.7 %collective-permute-done.8 = bf16[96,1024]{1,0:T(8,128)(2,1)S(1)} collective-permute-done((bf16[96,1024]{1,0:T(8,128)(2,1)S(1)}, bf16[96,1024]{1,0:T(8,128)(2,1)S(1)}, u32[]{:S(2)}, u32[]{:S(2)}) %collective-permute-start.8) | collective-permute-done | bytes 196640 | tf_op jit(solution)/shard_map/ppermute | solution.py:242
  124.9 1.0 collective-permute-start.9
  125.9 0.0 all-to-all-done.1.recv_ref
  125.9 0.9 copy-done.2
  126.8 2.8 %final.1 = bf16[256,1536]{1,0:T(8,128)(2,1)} custom-call(f32[256,1536]{1,0:T(8,128)} %get-tuple-element.31.pre_ref, bf16[8,384,128]{2,1,0:T(8,128)(2,1)} %copy-done.2), custom_call_target="tpu_custom_call" | custom-call | flops 393216 | bytes 3145728 | tf_op jit(solution)/shard_map/final/pallas_call | solution.py:351
  129.6 0.0 collective-permute-done.5
  129.7 1.3 collective-permute-done.9
  131.0 0.9 copy.7
  (31 shorter events, 0.4 us)
Async XLA Ops:
  2.9 17.1 %all-to-all-start = ((bf16[8,384,128]{2,1,0:T(8,128)(2,1)}), bf16[8,384,128]{2,1,0:T(8,128)(2,1)S(1)}, u32[]{:S(2)}, u32[]{:S(2)}) async-start(bf16[8,384,128]{2,1,0:T(8,128)(2,1)} %pack.1), calls=%async_computation | async-start | bytes 1572864 | tf_op jit(solution)/shard_map/all_to_all | solution.py:288
  20.0 0.9 copy-start.1
  32.9 5.4 %collective-permute-start = (bf16[2560,256]{1,0:T(8,128)(2,1)}, bf16[2560,256]{1,0:T(8,128)(2,1)S(1)}, u32[]{:S(2)}, u32[]{:S(2)}) collective-permute-start(bf16[2560,256]{1,0:T(8,128)(2,1)} %get-tuple-element.28.right_ref), channel_id=1, source_target_pairs={{0,8},{8,0},{16,24},{24,16},{32,40},{40,32},{48,56},{56,48},{64,72... | collective-permute-start | bytes 3932168 | tf_op jit(solution)/shard_map/ppermute | solution.py:242
  37.8 12.5 %collective-permute-start.1 = (bf16[2048,256]{1,0:T(8,128)(2,1)}, bf16[2048,256]{1,0:T(8,128)(2,1)S(1)}, u32[]{:S(2)}, u32[]{:S(2)}) collective-permute-start(bf16[2048,256]{1,0:T(8,128)(2,1)} %inner.1.after_ref.right_ref.inner_ref), channel_id=1, source_target_pairs={{0,8},{8,0},{16,24},{24,16},{32,40},{40,32},{48,56},{56,48},{64,72... | collective-permute-start | bytes 3145736 | tf_op jit(solution)/shard_map/ppermute | solution.py:242
  38.3 1.1 copy-start
  43.5 31.1 %collective-permute-start.10 = (bf16[384,512]{1,0:T(8,128)(2,1)}, bf16[384,512]{1,0:T(8,128)(2,1)}, u32[]{:S(2)}, u32[]{:S(2)}) collective-permute-start(bf16[384,512]{1,0:T(8,128)(2,1)} %get-tuple-element.29.after_ref), channel_id=1, source_target_pairs={{0,64},{8,72},{16,80},{24,88},{32,96},{40,104},{48,112},{56,120},{... | collective-permute-start | bytes 1179656 | tf_op jit(solution)/shard_map/ppermute | solution.py:242
  46.7 29.7 %collective-permute-start.14 = (bf16[384,512]{1,0:T(8,128)(2,1)}, bf16[384,512]{1,0:T(8,128)(2,1)S(1)}, u32[]{:S(2)}, u32[]{:S(2)}) collective-permute-start(bf16[384,512]{1,0:T(8,128)(2,1)} %get-tuple-element.38), channel_id=1, source_target_pairs={{0,192},{8,200},{16,208},{24,216},{32,224},{40,232},{48,240},{56,2... | collective-permute-start | bytes 1179656 | tf_op jit(solution)/shard_map/ppermute | solution.py:242
  50.3 1.0 copy-start.7
  56.4 45.8 %collective-permute-start.2 = (bf16[384,1024]{1,0:T(8,128)(2,1)}, bf16[384,1024]{1,0:T(8,128)(2,1)S(1)}, u32[]{:S(2)}, u32[]{:S(2)}) collective-permute-start(bf16[384,1024]{1,0:T(8,128)(2,1)} %get-tuple-element.30.after_ref), channel_id=1, source_target_pairs={{0,16},{8,24},{16,0},{24,8},{32,48},{40,56},{48,32},{56,40},{64,80... | collective-permute-start | bytes 2359304 | tf_op jit(solution)/shard_map/ppermute | solution.py:242
  57.9 45.5 %collective-permute-start.6 = (bf16[384,1024]{1,0:T(8,128)(2,1)}, bf16[384,1024]{1,0:T(8,128)(2,1)S(1)}, u32[]{:S(2)}, u32[]{:S(2)}) collective-permute-start(bf16[384,1024]{1,0:T(8,128)(2,1)} %get-tuple-element.35), channel_id=1, source_target_pairs={{0,48},{8,56},{16,32},{24,40},{32,16},{40,24},{48,0},{56,8},{64,11... | collective-permute-start | bytes 2359304 | tf_op jit(solution)/shard_map/ppermute | solution.py:242
  69.7 5.0 %copy-start.6 = (bf16[384,512]{1,0:T(8,128)(2,1)S(1)}, bf16[384,512]{1,0:T(8,128)(2,1)}, u32[]{:S(2)}) copy-start(bf16[384,512]{1,0:T(8,128)(2,1)} %get-tuple-element.36) | copy-start | bytes 1179652
  69.7 6.7 %copy-start.5 = (bf16[384,512]{1,0:T(8,128)(2,1)S(1)}, bf16[384,512]{1,0:T(8,128)(2,1)}, u32[]{:S(2)}) copy-start(bf16[384,512]{1,0:T(8,128)(2,1)} %get-tuple-element.37) | copy-start | bytes 1179652
  69.7 56.3 %all-to-all-start.1 = ((bf16[8,384,128]{2,1,0:T(8,128)(2,1)}), bf16[8,384,128]{2,1,0:T(8,128)(2,1)S(1)}, u32[]{:S(2)}, u32[]{:S(2)}) async-start(bf16[8,384,128]{2,1,0:T(8,128)(2,1)} %get-tuple-element.32), calls=%async_computation.1 | async-start | bytes 1572864 | tf_op jit(solution)/shard_map/all_to_all | solution.py:343
  75.7 15.8 %collective-permute-start.11 = (bf16[192,512]{1,0:T(8,128)(2,1)S(1)}, bf16[192,512]{1,0:T(8,128)(2,1)S(1)}, u32[]{:S(2)}, u32[]{:S(2)}) collective-permute-start(bf16[192,512]{1,0:T(8,128)(2,1)S(1)} %slice.133), channel_id=1, source_target_pairs={{0,192},{8,200},{16,208},{24,216},{32,224},{40,232},{48,240},{56,2... | collective-permute-start | bytes 589832 | tf_op jit(solution)/shard_map/ppermute | solution.py:242
  76.5 25.7 %copy-start.4 = (bf16[384,1024]{1,0:T(8,128)(2,1)S(1)}, bf16[384,1024]{1,0:T(8,128)(2,1)}, u32[]{:S(2)}) copy-start(bf16[384,1024]{1,0:T(8,128)(2,1)} %get-tuple-element.33) | copy-start | bytes 2359300
  76.5 15.8 %collective-permute-start.15 = (bf16[192,512]{1,0:T(8,128)(2,1)S(1)}, bf16[192,512]{1,0:T(8,128)(2,1)S(1)}, u32[]{:S(2)}, u32[]{:S(2)}) collective-permute-start(bf16[192,512]{1,0:T(8,128)(2,1)S(1)} %slice.139), channel_id=1, source_target_pairs={{0,64},{8,72},{16,80},{24,88},{32,96},{40,104},{48,112},{56,120},{... | collective-permute-start | bytes 589832 | tf_op jit(solution)/shard_map/ppermute | solution.py:242
  91.6 4.7 %collective-permute-start.12 = (bf16[96,512]{1,0:T(8,128)(2,1)S(1)}, bf16[96,512]{1,0:T(8,128)(2,1)S(1)}, u32[]{:S(2)}, u32[]{:S(2)}) collective-permute-start(bf16[96,512]{1,0:T(8,128)(2,1)S(1)} %slice.135), channel_id=1, source_target_pairs={{0,16},{8,24},{16,0},{24,8},{32,48},{40,56},{48,32},{56,40},{64,80... | collective-permute-start | bytes 294920 | tf_op jit(solution)/shard_map/ppermute | solution.py:242
  92.4 5.9 %collective-permute-start.16 = (bf16[96,512]{1,0:T(8,128)(2,1)S(1)}, bf16[96,512]{1,0:T(8,128)(2,1)S(1)}, u32[]{:S(2)}, u32[]{:S(2)}) collective-permute-start(bf16[96,512]{1,0:T(8,128)(2,1)S(1)} %slice.141), channel_id=1, source_target_pairs={{0,48},{8,56},{16,32},{24,40},{32,16},{40,24},{48,0},{56,8},{64,11... | collective-permute-start | bytes 294920 | tf_op jit(solution)/shard_map/ppermute | solution.py:242
  96.4 5.8 %collective-permute-start.13 = (bf16[48,512]{1,0:T(8,128)(2,1)S(1)}, bf16[48,512]{1,0:T(8,128)(2,1)S(1)}, u32[]{:S(2)}, u32[]{:S(2)}) collective-permute-start(bf16[48,512]{1,0:T(8,128)(2,1)S(1)} %slice.137), channel_id=1, source_target_pairs={{0,48},{8,56},{16,32},{24,40},{32,16},{40,24},{48,0},{56,8},{64,11... | collective-permute-start | bytes 147464 | tf_op jit(solution)/shard_map/ppermute | solution.py:242
  98.3 5.5 %collective-permute-start.17 = (bf16[48,512]{1,0:T(8,128)(2,1)S(1)}, bf16[48,512]{1,0:T(8,128)(2,1)S(1)}, u32[]{:S(2)}, u32[]{:S(2)}) collective-permute-start(bf16[48,512]{1,0:T(8,128)(2,1)S(1)} %slice.143), channel_id=1, source_target_pairs={{0,16},{8,24},{16,0},{24,8},{32,48},{40,56},{48,32},{56,40},{64,80... | collective-permute-start | bytes 147464 | tf_op jit(solution)/shard_map/ppermute | solution.py:242
  102.2 1.1 copy-start.3
  102.6 9.1 %collective-permute-start.3 = (bf16[192,1024]{1,0:T(8,128)(2,1)S(1)}, bf16[192,1024]{1,0:T(8,128)(2,1)S(1)}, u32[]{:S(2)}, u32[]{:S(2)}) collective-permute-start(bf16[192,1024]{1,0:T(8,128)(2,1)S(1)} %slice.121), channel_id=1, source_target_pairs={{0,48},{8,56},{16,32},{24,40},{32,16},{40,24},{48,0},{56,8},{64,11... | collective-permute-start | bytes 1179656 | tf_op jit(solution)/shard_map/ppermute | solution.py:242
  103.7 8.2 %collective-permute-start.7 = (bf16[192,1024]{1,0:T(8,128)(2,1)S(1)}, bf16[192,1024]{1,0:T(8,128)(2,1)S(1)}, u32[]{:S(2)}, u32[]{:S(2)}) collective-permute-start(bf16[192,1024]{1,0:T(8,128)(2,1)S(1)} %slice.127), channel_id=1, source_target_pairs={{0,16},{8,24},{16,0},{24,8},{32,48},{40,56},{48,32},{56,40},{64,80... | collective-permute-start | bytes 1179656 | tf_op jit(solution)/shard_map/ppermute | solution.py:242
  111.8 10.2 %collective-permute-start.4 = (bf16[96,1024]{1,0:T(8,128)(2,1)S(1)}, bf16[96,1024]{1,0:T(8,128)(2,1)S(1)}, u32[]{:S(2)}, u32[]{:S(2)}) collective-permute-start(bf16[96,1024]{1,0:T(8,128)(2,1)S(1)} %slice.123), channel_id=1, source_target_pairs={{0,64},{8,72},{16,80},{24,88},{32,96},{40,104},{48,112},{56,120},{... | collective-permute-start | bytes 589832 | tf_op jit(solution)/shard_map/ppermute | solution.py:242
  112.1 12.7 %collective-permute-start.8 = (bf16[96,1024]{1,0:T(8,128)(2,1)S(1)}, bf16[96,1024]{1,0:T(8,128)(2,1)S(1)}, u32[]{:S(2)}, u32[]{:S(2)}) collective-permute-start(bf16[96,1024]{1,0:T(8,128)(2,1)S(1)} %slice.129), channel_id=1, source_target_pairs={{0,192},{8,200},{16,208},{24,216},{32,224},{40,232},{48,240},{56,2... | collective-permute-start | bytes 589832 | tf_op jit(solution)/shard_map/ppermute | solution.py:242
  122.1 7.5 %collective-permute-start.5 = (bf16[48,1024]{1,0:T(8,128)(2,1)S(1)}, bf16[48,1024]{1,0:T(8,128)(2,1)S(1)}, u32[]{:S(2)}, u32[]{:S(2)}) collective-permute-start(bf16[48,1024]{1,0:T(8,128)(2,1)S(1)} %slice.125), channel_id=1, source_target_pairs={{0,192},{8,200},{16,208},{24,216},{32,224},{40,232},{48,240},{56,2... | collective-permute-start | bytes 294920 | tf_op jit(solution)/shard_map/ppermute | solution.py:242
  124.9 6.0 %collective-permute-start.9 = (bf16[48,1024]{1,0:T(8,128)(2,1)S(1)}, bf16[48,1024]{1,0:T(8,128)(2,1)S(1)}, u32[]{:S(2)}, u32[]{:S(2)}) collective-permute-start(bf16[48,1024]{1,0:T(8,128)(2,1)S(1)} %slice.131), channel_id=1, source_target_pairs={{0,64},{8,72},{16,80},{24,88},{32,96},{40,104},{48,112},{56,120},{... | collective-permute-start | bytes 294920 | tf_op jit(solution)/shard_map/ppermute | solution.py:242
  125.9 0.9 copy-start.2

commit v2 on v1

--- a/solution.py
+++ b/solution.py
@@ -66,16 +66,39 @@
     return lax.dot_general(a, b, (((1,), (1,)), ((), ())), preferred_element_type=F32)
 
 
-def forward_kernel(
-    index_ref, x_ref, recv_ref, cot_ref, w_in_hbm, w_out_hbm,
-    own_ref, send_ref, normed_ref, scale_ref, grad_ref, grad16_ref, slope_ref, silu_ref,
-    w_in, w_out, state, hidden, turned, in_sem, out_sem,
+def norm_state(x_ref, recv_ref, normed_ref):
+    samples, width = x_ref.shape
+    sums = [jnp.zeros((samples, 128), F32)]
+
+    def add_mixed(t, mixed):
+        v = x_ref[:, tile(t)].astype(F32) + mixed
+        normed_ref[:, tile(t)] = v
+        sums[0] = sums[0] + v * v
+
+    unpack(recv_ref, add_mixed)
+    scale = lax.rsqrt(jnp.sum(sums[0], axis=1, keepdims=True) / width + EPS)
+    for t in range(width // 128):
+        normed_ref[:, tile(t)] = normed_ref[:, tile(t)] * scale
+    return scale
+
+
+def main_kernel(
+    index_ref, x_ref, recv_ref, cot_hbm, w_in_hbm, w_out_hbm,
+    own_hbm, send_hbm, inner_hbm, grad16_hbm,
+    w_in, w_out, cot, state, grad16, hidden, values, slope, silu, turned, own, send, inner,
+    in_sem, out_sem, cot_sem, write_sem,
 ):
     samples, width = x_ref.shape
     ff = w_out.shape[1]
     wide = 256
     steps = ff // wide
     half = width // 2
+    writes = []
+
+    def write(source, target, begin, rows):
+        place = pl.ds(begin, rows)
+        writes.append(pltpu.make_async_copy(source.at[place], target.at[place], write_sem.at[len(writes)]))
+        writes[-1].start()
 
     def w_in_copy(j, c):
         cols = pl.ds(c * ff + j * wide, wide)
@@ -86,29 +109,22 @@
         w_in_copy(j, 1).start()
     out_copy = pltpu.make_async_copy(w_out_hbm, w_out, out_sem)
     out_copy.start()
+    cot_copy = pltpu.make_async_copy(cot_hbm, cot, cot_sem)
+    cot_copy.start()
 
     rank = index_ref[0]
 
     def spread(at):
         for b in range(16):
             place = slice(at + 48 * b, at + 48 * b + 48)
-            own_ref[place, :] = turned[pl.ds(pl.multiple_of((rank ^ (2 * b)) * 48, 48), 48), :]
-            send_ref[place, :] = turned[pl.ds(pl.multiple_of((rank ^ (2 * b + 1)) * 48, 48), 48), :]
-
-    def add_mixed(t, mixed):
-        normed_ref[:, tile(t)] = x_ref[:, tile(t)].astype(F32) + mixed
-
-    unpack(recv_ref, add_mixed)
-    squares = jnp.zeros((samples, 128), F32)
-    for t in range(width // 128):
-        v = normed_ref[:, tile(t)]
-        squares = squares + v * v
-    scale = lax.rsqrt(jnp.sum(squares, axis=1, keepdims=True) / width + EPS)
-    scale_ref[...] = jnp.broadcast_to(scale, scale_ref.shape)
-    for t in range(width // 128):
-        v = normed_ref[:, tile(t)] * scale
-        normed_ref[:, tile(t)] = v
-        state[:, tile(t)] = v.astype(BF16)
+            own[place, :] = turned[pl.ds(pl.multiple_of((rank ^ (2 * b)) * 48, 48), 48), :]
+            send[place, :] = turned[pl.ds(pl.multiple_of((rank ^ (2 * b + 1)) * 48, 48), 48), :]
+        write(send, send_hbm, at, half)
+        write(own, own_hbm, at, half)
+
+    norm_state(x_ref, recv_ref, values)
+    for t in range(width // 128):
+        state[:, tile(t)] = values[:, tile(t)].astype(BF16)
 
     for j in range(steps):
         cols = slice(wide * j, wide * j + wide)
@@ -120,51 +136,50 @@
         silu_gate = gate * sigma
         part = (silu_gate * up).astype(BF16)
         hidden[:, cols] = part
-        send_ref[width + wide * j : width + wide * j + wide, :] = part
-        silu_ref[:, cols] = silu_gate
-        slope_ref[:, cols] = up * sigma * (1.0 + gate * (1.0 - sigma))
-
-    for t in range(width // 128):
-        turned[tile(t), :] = state[:, tile(t)].T
-    spread(half)
+        send[width + wide * j : width + wide * j + wide, :] = part
+        silu[:, cols] = silu_gate
+        slope[:, cols] = up * sigma * (1.0 + gate * (1.0 - sigma))
+    write(send, send_hbm, width, ff)
 
     out_copy.wait()
     for d in range(width // wide):
         cols = slice(wide * d, wide * d + wide)
-        grad_ref[:, cols] = nt(hidden[...], w_out[cols, :]) + state[:, cols].astype(F32)
+        values[:, cols] = nt(hidden[...], w_out[cols, :]) + state[:, cols].astype(F32)
+    for t in range(width // 128):
+        turned[tile(t), :] = state[:, tile(t)].T
+    spread(half)
+    cot_copy.wait()
     squares = jnp.zeros((samples, 128), F32)
     products = jnp.zeros((samples, 128), F32)
     for t in range(width // 128):
-        v = grad_ref[:, tile(t)]
+        v = values[:, tile(t)]
         squares = squares + v * v
-        products = products + v * cot_ref[:, tile(t)].astype(F32)
-    scale_two = lax.rsqrt(jnp.sum(squares, axis=1, keepdims=True) / width + EPS)
-    mean = scale_two * jnp.sum(products, axis=1, keepdims=True) / width
-    for t in range(width // 128):
-        out_normed = grad_ref[:, tile(t)] * scale_two
-        g = scale_two * (cot_ref[:, tile(t)].astype(F32) - out_normed * mean)
-        grad_ref[:, tile(t)] = g
-        g16 = g.astype(BF16)
-        grad16_ref[:, tile(t)] = g16
+        products = products + v * cot[:, tile(t)].astype(F32)
+    scale = lax.rsqrt(jnp.sum(squares, axis=1, keepdims=True) / width + EPS)
+    mean = scale * jnp.sum(products, axis=1, keepdims=True) / width
+    for t in range(width // 128):
+        out_normed = values[:, tile(t)] * scale
+        g16 = (scale * (cot[:, tile(t)].astype(F32) - out_normed * mean)).astype(BF16)
+        grad16[:, tile(t)] = g16
         turned[tile(t), :] = g16.T
+    write(grad16, grad16_hbm, 0, samples)
     spread(0)
-
-
-def inner_kernel(grad16_ref, slope_ref, silu_ref, w_out_ref, inner_ref):
-    ff = w_out_ref.shape[1]
-    wide = 256
-    for j in range(ff // wide):
+    for j in range(steps):
         cols = slice(wide * j, wide * j + wide)
-        hidden_grad = nn(grad16_ref[...], w_out_ref[:, cols])
-        inner_ref[cols, :] = (hidden_grad * slope_ref[:, cols]).astype(BF16)
-        inner_ref[ff + wide * j : ff + wide * j + wide, :] = (hidden_grad * silu_ref[:, cols]).astype(BF16)
+        hidden_grad = nn(grad16[...], w_out[:, cols])
+        inner[cols, :] = (hidden_grad * slope[:, cols]).astype(BF16)
+        inner[ff + wide * j : ff + wide * j + wide, :] = (hidden_grad * silu[:, cols]).astype(BF16)
+        write(inner, inner_hbm, wide * j, wide)
+        write(inner, inner_hbm, ff + wide * j, wide)
+    for copy in writes:
+        copy.wait()
 
 
 def input_kernel(
-    inner_ref, w_in_hbm, normed_ref, scale_ref, grad_ref, after_ref, pre_ref, packed_ref, w_in, inner, sem
+    inner_ref, w_in_hbm, x_ref, recv_ref, grad_ref, after_ref, pre_ref, packed_ref, w_in, inner, normed, sem
 ):
     del after_ref
-    samples, width = normed_ref.shape
+    samples, width = x_ref.shape
     wide = 256
 
     def copy(d):
@@ -173,20 +188,20 @@
 
     for d in range(width // wide):
         copy(d).start()
+    scale = norm_state(x_ref, recv_ref, normed)
     for j in range(inner.shape[1] // samples):
         inner[:, samples * j : samples * j + samples] = inner_ref[samples * j : samples * j + samples, :]
     products = jnp.zeros((samples, 128), F32)
     for d in range(width // wide):
         copy(d).wait()
         cols = slice(wide * d, wide * d + wide)
-        g = nt(inner[...], w_in[cols, :]) + grad_ref[:, cols]
+        g = nt(inner[...], w_in[cols, :]) + grad_ref[:, cols].astype(F32)
         pre_ref[:, cols] = g
-        p = g * normed_ref[:, cols]
+        p = g * normed[:, cols]
         products = products + p[:, :128] + p[:, 128:]
     mean = jnp.sum(products, axis=1, keepdims=True) / width
-    scale = scale_ref[:, :1]
-    for t in range(width // 128):
-        pre_ref[:, tile(t)] = scale * (pre_ref[:, tile(t)] - normed_ref[:, tile(t)] * mean)
+    for t in range(width // 128):
+        pre_ref[:, tile(t)] = scale * (pre_ref[:, tile(t)] - normed[:, tile(t)] * mean)
     pack(lambda t: pre_ref[:, tile(t)], packed_ref)
 
 
@@ -256,19 +271,16 @@
     )(own, recv, right, right_recv, after)
 
 
-def reduce_step(scales, step, keep, send):
-    kept, sent = [], []
-    for flavour in range(2):
-        scale = scales[step // 2]
-        got = swap(send[flavour], PARTNERS[flavour][step % 2] * scale)
-        total = keep[flavour].astype(F32) + got.astype(F32)
-        if step == 3:
-            kept.append(total.astype(BF16))
-            continue
-        half = total.shape[0] // 2
-        kept.append(total[:half].astype(BF16))
-        sent.append(total[half:].astype(BF16))
-    return kept, sent
+def reduce_send(scales, step, send):
+    return [swap(send[f], PARTNERS[f][step % 2] * scales[step // 2]) for f in range(2)]
+
+
+def reduce_add(step, keep, got):
+    totals = [k.astype(F32) + g.astype(F32) for k, g in zip(keep, got)]
+    if step == 3:
+        return [t.astype(BF16) for t in totals], []
+    half = totals[0].shape[0] // 2
+    return [t[:half].astype(BF16) for t in totals], [t[half:].astype(BF16) for t in totals]
 
 
 def local(block_input, out_cotangent, w_in, w_out):
@@ -287,71 +299,75 @@
     )(x)
     recv = lax.all_to_all(packed, "token", split_axis=0, concat_axis=0, tiled=True)
 
-    full = shape((samples, width), F32)
-    gates = shape((samples, ff), F32)
-    own, out_send, normed, scale, out_grad, out_grad16, slope, silu = pl.pallas_call(
-        forward_kernel,
-        out_shape=[
-            shape((width, samples)), shape((width + ff, samples)), full, shape((samples, 128), F32), full,
-            shape((samples, width)), gates, gates,
-        ],
-        in_specs=[SMEM, VMEM, VMEM, VMEM, ANY, ANY],
-        out_specs=[VMEM] * 8,
+    flat = shape((samples, width))
+    own, send, inner, out_grad16 = pl.pallas_call(
+        main_kernel,
+        out_shape=[shape((width, samples)), shape((width + ff, samples)), shape((2 * ff, samples)), flat],
+        in_specs=[SMEM, VMEM, VMEM, ANY, ANY, ANY],
+        out_specs=[ANY] * 4,
         scratch_shapes=[
             pltpu.VMEM((width, 2 * ff), BF16),
             pltpu.VMEM((width, ff), BF16),
             pltpu.VMEM((samples, width), BF16),
+            pltpu.VMEM((samples, width), BF16),
+            pltpu.VMEM((samples, width), BF16),
             pltpu.VMEM((samples, ff), BF16),
+            pltpu.VMEM((samples, width), F32),
+            pltpu.VMEM((samples, ff), F32),
+            pltpu.VMEM((samples, ff), F32),
             pltpu.VMEM((width, samples), BF16),
+            pltpu.VMEM((width, samples), BF16),
+            pltpu.VMEM((width + ff, samples), BF16),
+            pltpu.VMEM((2 * ff, samples), BF16),
             pltpu.SemaphoreType.DMA((8,)),
             pltpu.SemaphoreType.DMA,
+            pltpu.SemaphoreType.DMA,
+            pltpu.SemaphoreType.DMA((14,)),
         ],
         compiler_params=params(),
-        cost_estimate=cost(6 * samples * width * ff, 18e6),
-        name="forward",
+        cost_estimate=cost(8 * samples * width * ff, 18e6),
+        name="main",
     )(index, x, recv, cotangent, flat_in, weight_out)
-    out_recv = swap(out_send, 1)
-
-    inner = pl.pallas_call(
-        inner_kernel,
-        out_shape=shape((2 * ff, samples)),
-        in_specs=[VMEM] * 4,
-        out_specs=VMEM,
-        compiler_params=params(),
-        cost_estimate=cost(2 * samples * width * ff, 8e6),
-        name="inner",
-    )(out_grad16, slope, silu, weight_out)
-    inner_recv = swap(inner, 1)
-
-    down = gradients(False, 0, width, ff, own, out_recv, out_send, out_recv, inner, "down_grads")
-    up = gradients(True, width // 2, 0, 2 * ff, own, out_recv, inner, inner_recv, down[1], "in_grads")
+    other, inner_other = swap(send, 1), swap(inner, 1)
+
+    up = gradients(True, width // 2, 0, 2 * ff, own, other, inner, inner_other, index, "in_grads")
+    up_got = reduce_send((2, 8), 0, up[1::2])
+    down = gradients(False, 0, width, ff, own, other, send, other, up[1], "down_grads")
+    down_got = reduce_send((8, 2), 0, down[1::2])
+    up_keep, down_keep = up[0::2], down[0::2]
 
     pre_grad, back = pl.pallas_call(
         input_kernel,
-        out_shape=[full, packed_shape],
+        out_shape=[shape((samples, width), F32), packed_shape],
         in_specs=[VMEM, ANY, VMEM, VMEM, VMEM, ANY],
         out_specs=[VMEM] * 2,
         scratch_shapes=[
             pltpu.VMEM((width, 2 * ff), BF16),
             pltpu.VMEM((samples, 2 * ff), BF16),
+            pltpu.VMEM((samples, width), F32),
             pltpu.SemaphoreType.DMA((width // 256,)),
         ],
         compiler_params=params(),
         cost_estimate=cost(4 * samples * width * ff, 14e6),
         name="input",
-    )(inner, flat_in, normed, scale, out_grad, up[1])
+    )(inner, flat_in, x, recv, out_grad16, down[1])
     returned = lax.all_to_all(back, "token", split_axis=0, concat_axis=0, tiled=True)
 
-    down_keep, down_send = down[0::2], down[1::2]
-    up_keep, up_send = up[0::2], up[1::2]
     for step in range(4):
-        down_keep, down_send = reduce_step((8, 2), step, down_keep, down_send)
-        up_keep, up_send = reduce_step((2, 8), step, up_keep, up_send)
-
-    input_grad = pl.pallas_call(
-        final_kernel, out_shape=shape((samples, width)), in_specs=[VMEM] * 2, out_specs=VMEM,
-        compiler_params=params(), cost_estimate=cost(samples * width, 8 * samples * width), name="final",
-    )(pre_grad, returned)
+        if step == 2:
+            input_grad = pl.pallas_call(
+                final_kernel, out_shape=flat, in_specs=[VMEM] * 2, out_specs=VMEM,
+                compiler_params=params(), cost_estimate=cost(samples * width, 8 * samples * width), name="final",
+            )(pre_grad, returned)
+        up_keep, up_send = reduce_add(step, up_keep, up_got)
+        if step < 3:
+            up_got = reduce_send((2, 8), step + 1, up_send)
+        down_got, up_send = lax.optimization_barrier((down_got, up_send))
+        down_keep, down_send = reduce_add(step, down_keep, down_got)
+        if step < 3:
+            down_got = reduce_send((8, 2), step + 1, down_send)
+            up_got, down_send = lax.optimization_barrier((up_got, down_send))
+
     return (
         input_grad[:, None, :],
         jnp.stack(up_keep, axis=1)[None],

time: 132 us -> 129 us (0.977)
  Pallas kernels: 40.7 us -> 34.2 us
  waiting for transfers between devices: 39 us -> 41.6 us
  starting transfers between devices: 35.3 us -> 37.1 us
    pallas_call x4 -> x3, Pallas kernels: 29.3 us -> 22.7 us  [the longest x1 10.7 us: local(): pl.pallas_call(main_kernel, out_shape=[shape((width, samples)), shape((wi...]
    ppermute x18, waiting for transfers between devices: 36.2 us -> 38.8 us  [swap(): return lax.ppermute(values, 'dp', [(i, i ^ distance) for i in range(32)])]
    ppermute x18, starting transfers between devices: 24.1 us -> 25.9 us  [swap(): return lax.ppermute(values, 'dp', [(i, i ^ distance) for i in range(32)])]
  transfers between devices with their start and end apart: 20 -> 20, of which waited for: 9 -> 8; matrix products, arithmetic and copies ran while one was open for 8% -> 8% of each run, Pallas kernels for 20% -> 13%
where the time goes in v2:
time: 129 us; the launch traced here: 128 us
  waiting for transfers between devices  41.6 us (32%)
  starting transfers between devices  37.1 us (29%)
  Pallas kernels  34.2 us (27%)
  local copies, waits for them, and re-layouts  12.2 us (9%)
  other arithmetic  2.07 us (2%)
    ppermute x18, waiting for transfers between devices, swap(): return lax.ppermute(values, 'dp', [(i, i ^ distance) for i in range(32)])  38.8 us
    ppermute x18, starting transfers between devices, swap(): return lax.ppermute(values, 'dp', [(i, i ^ distance) for i in range(32)])  25.9 us
    unnamed x18, local copies, waits for them, and re-layouts  12.1 us
    pallas_call x1, Pallas kernels, local(): pl.pallas_call(main_kernel, out_shape=[shape((width, samples)), shape((wi...  10.7 us
    pallas_call x2, Pallas kernels, gradients(): pl.pallas_call(functools.partial(grad_kernel, x_first, at, block), out_sh...  9.24 us
    pallas_call x1, Pallas kernels, local(): pl.pallas_call(input_kernel, out_shape=[shape((samples, width), F32), pac...  9.23 us
    all_to_all x1, starting transfers between devices, local(): lax.all_to_all(packed, 'token', split_axis=0, concat_axis=0, tiled=True)  6.27 us
    all_to_all x1, starting transfers between devices, local(): lax.all_to_all(back, 'token', split_axis=0, concat_axis=0, tiled=True)  4.95 us
  transfers between devices with their start and end apart: 20, of which 8 were waited for; matrix products, arithmetic and copies ran while one was open for 8% of the time, Pallas kernels for 13%

profile of v2, /device:TPU:8, one launch (start us, length us, event | category | flops | bytes accessed | tf_op | source)
XLA Modules:
  0.0 128.1 jit_solution(16647549408463255257)
XLA Ops:
  0.6 2.3 %pack.1 = bf16[8,384,128]{2,1,0:T(8,128)(2,1)} custom-call(bf16[256,1536]{1,0:T(8,128)(2,1)} %bitcast.19), custom_call_target="tpu_custom_call" | custom-call | flops 393216 | bytes 1572864 | tf_op jit(solution)/shard_map/pack/pallas_call | solution.py:296
  2.9 6.3 %all-to-all-start = ((bf16[8,384,128]{2,1,0:T(8,128)(2,1)}), bf16[8,384,128]{2,1,0:T(8,128)(2,1)S(1)}, u32[]{:S(2)}, u32[]{:S(2)}) async-start(bf16[8,384,128]{2,1,0:T(8,128)(2,1)} %pack.1), calls=%async_computation | async-start | bytes 1572864 | tf_op jit(solution)/shard_map/all_to_all | solution.py:300
  9.2 8.0 %copy.8 = bf16[192,8,2,1024]{3,1,2,0:T(8,128)(2,1)} copy(bf16[192,8,2,1024]{3,2,1,0:T(2,128)(2,1)} %bitcast.18) | data formatting | bytes 12582912
  17.2 2.8 %all-to-all-done.recv_ref = bf16[8,384,128]{2,1,0:T(8,128)(2,1)S(1)} async-done(((bf16[8,384,128]{2,1,0:T(8,128)(2,1)}), bf16[8,384,128]{2,1,0:T(8,128)(2,1)S(1)}, u32[]{:S(2)}, u32[]{:S(2)}) %all-to-all-start) | async-done | bytes 786464 | tf_op jit(solution)/shard_map/all_to_all | solution.py:300
  20.0 0.9 copy-done.1
  20.9 10.7 %main.1 = (bf16[1536,256]{1,0:T(8,128)(2,1)}, bf16[2560,256]{1,0:T(8,128)(2,1)}, bf16[2048,256]{1,0:T(8,128)(2,1)}, bf16[256,1536]{1,0:T(8,128)(2,1)}) custom-call(s32[1]{0:T(128)} %bitcast.index_ref.after_ref, bf16[256,1536]{1,0:T(8,128)(2,1)} %bitcast.20, bf16[8,384,128]{2,1,0:T(8,128)(2,1)} %copy-done.1, bf16[256,1536]{1,0:T(8,128)(2,1)} %bitcast.24, ...), custom_call_target="tpu_custom_call" | custom-call | flops 3221225472 | bytes 18000000 | tf_op jit(solution)/shard_map/main/pallas_call | solution.py:303
  31.6 0.1 collective-permute-start
  31.7 0.5 collective-permute-start.1
  32.2 4.2 %collective-permute-done.1.right_recv_ref = bf16[2048,256]{1,0:T(8,128)(2,1)S(1)} collective-permute-done((bf16[2048,256]{1,0:T(8,128)(2,1)}, bf16[2048,256]{1,0:T(8,128)(2,1)S(1)}, u32[]{:S(2)}, u32[]{:S(2)}) %collective-permute-start.1) | collective-permute-done | bytes 1048608 | tf_op jit(solution)/shard_map/ppermute | solution.py:257
  36.4 0.0 collective-permute-done.recv_ref.right_recv_ref
  36.4 1.0 copy-done.7
  37.4 0.4 copy-done
  37.8 5.1 %in_grads.1 = (bf16[384,1024]{1,0:T(8,128)(2,1)}, bf16[384,1024]{1,0:T(8,128)(2,1)}, bf16[384,1024]{1,0:T(8,128)(2,1)}, bf16[384,1024]{1,0:T(8,128)(2,1)}) custom-call(bf16[1536,256]{1,0:T(8,128)(2,1)} %get-tuple-element.33.own_ref, bf16[2560,256]{1,0:T(8,128)(2,1)} %copy-done, bf16[2048,256]{1,0:T(8,128)(2,1)} %get-tuple-element.31.right_ref.inner_ref, ...), custom_call_target="tpu_custom_call" | custom-call | flops 1610612736 | bytes 7340032 | tf_op jit(solution)/shard_map/in_grads/pallas_call | solution.py:263
  42.9 2.8 %collective-permute-start.4 = (bf16[384,1024]{1,0:T(8,128)(2,1)}, bf16[384,1024]{1,0:T(8,128)(2,1)S(1)}, u32[]{:S(2)}, u32[]{:S(2)}) collective-permute-start(bf16[384,1024]{1,0:T(8,128)(2,1)} %get-tuple-element.41), channel_id=1, source_target_pairs={{0,48},{8,56},{16,32},{24,40},{32,16},{40,24},{48,0},{56,8},{64,11... | collective-permute-start | bytes 2359304 | tf_op jit(solution)/shard_map/ppermute | solution.py:257
  45.6 0.2 collective-permute-start.2
  45.9 4.1 %down_grads.1 = (bf16[384,512]{1,0:T(8,128)(2,1)}, bf16[384,512]{1,0:T(8,128)(2,1)}, bf16[384,512]{1,0:T(8,128)(2,1)}, bf16[384,512]{1,0:T(8,128)(2,1)}) custom-call(bf16[1536,256]{1,0:T(8,128)(2,1)} %get-tuple-element.33.own_ref, bf16[2560,256]{1,0:T(8,128)(2,1)} %copy-done, bf16[2560,256]{1,0:T(8,128)(2,1)} %get-tuple-element.34.right_ref, ...), custom_call_target="tpu_custom_call" | custom-call | flops 805306368 | bytes 6291456 | tf_op jit(solution)/shard_map/down_grads/pallas_call | solution.py:263
  50.0 3.3 %collective-permute-start.6 = (bf16[384,512]{1,0:T(8,128)(2,1)}, bf16[384,512]{1,0:T(8,128)(2,1)S(1)}, u32[]{:S(2)}, u32[]{:S(2)}) collective-permute-start(bf16[384,512]{1,0:T(8,128)(2,1)} %get-tuple-element.36.after_ref), channel_id=1, source_target_pairs={{0,64},{8,72},{16,80},{24,88},{32,96},{40,104},{48,112},{56,120},{... | collective-permute-start | bytes 1179656 | tf_op jit(solution)/shard_map/ppermute | solution.py:257
  53.3 9.2 %input.1 = (f32[256,1536]{1,0:T(8,128)}, bf16[8,384,128]{2,1,0:T(8,128)(2,1)}) custom-call(bf16[2048,256]{1,0:T(8,128)(2,1)} %get-tuple-element.31.right_ref.inner_ref, bf16[1536,2048]{1,0:T(8,128)(2,1)} %bitcast.17, bf16[256,1536]{1,0:T(8,128)(2,1)} %bitcast.21, bf16[8,384,128]{2,1,0:T(8,128)(2,1)} %copy-done.1, ...), custom_call_target="tpu_custom_call" | custom-call | flops 1610612736 | bytes 14000000 | tf_op jit(solution)/shard_map/input/pallas_call | solution.py:339
  62.5 4.9 %all-to-all-start.1 = ((bf16[8,384,128]{2,1,0:T(8,128)(2,1)}), bf16[8,384,128]{2,1,0:T(8,128)(2,1)S(1)}, u32[]{:S(2)}, u32[]{:S(2)}) async-start(bf16[8,384,128]{2,1,0:T(8,128)(2,1)} %get-tuple-element.38), calls=%async_computation.1 | async-start | bytes 1572864 | tf_op jit(solution)/shard_map/all_to_all | solution.py:354
  67.5 3.6 %collective-permute-start.7 = (bf16[384,512]{1,0:T(8,128)(2,1)}, bf16[384,512]{1,0:T(8,128)(2,1)S(1)}, u32[]{:S(2)}, u32[]{:S(2)}) collective-permute-start(bf16[384,512]{1,0:T(8,128)(2,1)} %get-tuple-element.43), channel_id=1, source_target_pairs={{0,192},{8,200},{16,208},{24,216},{32,224},{40,232},{48,240},{56,2... | collective-permute-start | bytes 1179656 | tf_op jit(solution)/shard_map/ppermute | solution.py:257
  71.0 0.0 collective-permute-done.4
  71.0 0.0 copy-done.4
  71.1 0.3 add_convert_fusion
  71.4 1.9 %collective-permute-start.5 = (bf16[192,1024]{1,0:T(8,128)(2,1)S(1)}, bf16[192,1024]{1,0:T(8,128)(2,1)S(1)}, u32[]{:S(2)}, u32[]{:S(2)}) collective-permute-start(bf16[192,1024]{1,0:T(8,128)(2,1)S(1)} %slice.122), channel_id=1, source_target_pairs={{0,16},{8,24},{16,0},{24,8},{32,48},{40,56},{48,32},{56,40},{64,80... | collective-permute-start | bytes 1179656 | tf_op jit(solution)/shard_map/ppermute | solution.py:257
  73.3 0.0 collective-permute-done.2
  73.3 0.0 copy-done.3
  73.3 0.3 add_convert_fusion.1
  73.6 0.6 collective-permute-start.3
  74.2 18.6 %collective-permute-done.7 = bf16[384,512]{1,0:T(8,128)(2,1)S(1)} collective-permute-done((bf16[384,512]{1,0:T(8,128)(2,1)}, bf16[384,512]{1,0:T(8,128)(2,1)S(1)}, u32[]{:S(2)}, u32[]{:S(2)}) %collective-permute-start.7) | collective-permute-done | bytes 393248 | tf_op jit(solution)/shard_map/ppermute | solution.py:257
  92.8 0.0 collective-permute-done.6
  92.8 0.1 add_convert_fusion.4
  93.0 0.1 add_convert_fusion.5
  93.1 0.1 collective-permute-start.10
  93.2 1.6 %collective-permute-start.11 = (bf16[192,512]{1,0:T(8,128)(2,1)S(1)}, bf16[192,512]{1,0:T(8,128)(2,1)S(1)}, u32[]{:S(2)}, u32[]{:S(2)}) collective-permute-start(bf16[192,512]{1,0:T(8,128)(2,1)S(1)} %slice.124), channel_id=1, source_target_pairs={{0,64},{8,72},{16,80},{24,88},{32,96},{40,104},{48,112},{56,120},{... | collective-permute-start | bytes 589832 | tf_op jit(solution)/shard_map/ppermute | solution.py:257
  94.8 0.0 collective-permute-done.5
  94.8 0.0 collective-permute-done.3
  94.8 0.1 add_convert_fusion.2
  95.0 0.1 add_convert_fusion.3
  95.1 1.5 %collective-permute-start.8 = (bf16[96,1024]{1,0:T(8,128)(2,1)S(1)}, bf16[96,1024]{1,0:T(8,128)(2,1)S(1)}, u32[]{:S(2)}, u32[]{:S(2)}) collective-permute-start(bf16[96,1024]{1,0:T(8,128)(2,1)S(1)} %slice.126), channel_id=1, source_target_pairs={{0,64},{8,72},{16,80},{24,88},{32,96},{40,104},{48,112},{56,120},{... | collective-permute-start | bytes 589832 | tf_op jit(solution)/shard_map/ppermute | solution.py:257
  96.6 4.0 %collective-permute-start.9 = (bf16[96,1024]{1,0:T(8,128)(2,1)S(1)}, bf16[96,1024]{1,0:T(8,128)(2,1)S(1)}, u32[]{:S(2)}, u32[]{:S(2)}) collective-permute-start(bf16[96,1024]{1,0:T(8,128)(2,1)S(1)} %slice.128), channel_id=1, source_target_pairs={{0,192},{8,200},{16,208},{24,216},{32,224},{40,232},{48,240},{56,2... | collective-permute-start | bytes 589832 | tf_op jit(solution)/shard_map/ppermute | solution.py:257
  100.7 9.9 %collective-permute-done.10 = bf16[192,512]{1,0:T(8,128)(2,1)S(1)} collective-permute-done((bf16[192,512]{1,0:T(8,128)(2,1)S(1)}, bf16[192,512]{1,0:T(8,128)(2,1)S(1)}, u32[]{:S(2)}, u32[]{:S(2)}) %collective-permute-start.10) | collective-permute-done | bytes 196640 | tf_op jit(solution)/shard_map/ppermute | solution.py:257
  110.6 0.0 collective-permute-done.11
  110.6 0.1 add_convert_fusion.9
  110.6 0.1 add_convert_fusion.8
  110.7 1.2 collective-permute-start.15
  111.9 0.8 collective-permute-start.14
  112.7 0.9 collective-permute-done.8
  113.5 1.2 collective-permute-done.9
  114.7 0.1 add_convert_fusion.6
  114.8 1.8 %collective-permute-done.15 = bf16[96,512]{1,0:T(8,128)(2,1)S(1)} collective-permute-done((bf16[96,512]{1,0:T(8,128)(2,1)S(1)}, bf16[96,512]{1,0:T(8,128)(2,1)S(1)}, u32[]{:S(2)}, u32[]{:S(2)}) %collective-permute-start.15) | collective-permute-done | bytes 98336 | tf_op jit(solution)/shard_map/ppermute | solution.py:257
  116.6 0.0 collective-permute-done.14
  116.7 0.7 collective-permute-start.17
  117.4 2.5 %collective-permute-start.16 = (bf16[48,512]{1,0:T(8,128)(2,1)S(1)}, bf16[48,512]{1,0:T(8,128)(2,1)S(1)}, u32[]{:S(2)}, u32[]{:S(2)}) collective-permute-start(bf16[48,512]{1,0:T(8,128)(2,1)S(1)} %slice.138), channel_id=1, source_target_pairs={{0,48},{8,56},{16,32},{24,40},{32,16},{40,24},{48,0},{56,8},{64,11... | collective-permute-start | bytes 147464 | tf_op jit(solution)/shard_map/ppermute | solution.py:257
  120.0 0.6 collective-permute-start.12
  120.6 0.0 collective-permute-start.13
  120.6 0.0 all-to-all-done.1.recv_ref
  120.6 0.9 copy-done.2
  121.5 2.8 %final.1 = bf16[256,1536]{1,0:T(8,128)(2,1)} custom-call(f32[256,1536]{1,0:T(8,128)} %get-tuple-element.37.pre_ref, bf16[8,384,128]{2,1,0:T(8,128)(2,1)} %copy-done.2), custom_call_target="tpu_custom_call" | custom-call | flops 393216 | bytes 3145728 | tf_op jit(solution)/shard_map/final/pallas_call | solution.py:358
  124.3 0.0 collective-permute-done.17
  124.3 0.0 collective-permute-done.16
  124.3 0.6 maximum_bitcast_fusion.1
  125.0 2.1 %collective-permute-done.12 = bf16[48,1024]{1,0:T(8,128)(2,1)S(1)} collective-permute-done((bf16[48,1024]{1,0:T(8,128)(2,1)S(1)}, bf16[48,1024]{1,0:T(8,128)(2,1)S(1)}, u32[]{:S(2)}, u32[]{:S(2)}) %collective-permute-start.12) | collective-permute-done | bytes 98336 | tf_op jit(solution)/shard_map/ppermute | solution.py:257
  127.1 0.0 collective-permute-done.13
  127.2 0.9 copy.7
  (28 shorter events, 0.4 us)
Async XLA Ops:
  2.9 17.1 %all-to-all-start = ((bf16[8,384,128]{2,1,0:T(8,128)(2,1)}), bf16[8,384,128]{2,1,0:T(8,128)(2,1)S(1)}, u32[]{:S(2)}, u32[]{:S(2)}) async-start(bf16[8,384,128]{2,1,0:T(8,128)(2,1)} %pack.1), calls=%async_computation | async-start | bytes 1572864 | tf_op jit(solution)/shard_map/all_to_all | solution.py:300
  20.0 0.9 copy-start.1
  31.6 4.8 %collective-permute-start = (bf16[2560,256]{1,0:T(8,128)(2,1)}, bf16[2560,256]{1,0:T(8,128)(2,1)S(1)}, u32[]{:S(2)}, u32[]{:S(2)}) collective-permute-start(bf16[2560,256]{1,0:T(8,128)(2,1)} %get-tuple-element.34.right_ref), channel_id=1, source_target_pairs={{0,8},{8,0},{16,24},{24,16},{32,40},{40,32},{48,56},{56,48},{64,72... | collective-permute-start | bytes 3932168 | tf_op jit(solution)/shard_map/ppermute | solution.py:257
  31.7 4.7 %collective-permute-start.1 = (bf16[2048,256]{1,0:T(8,128)(2,1)}, bf16[2048,256]{1,0:T(8,128)(2,1)S(1)}, u32[]{:S(2)}, u32[]{:S(2)}) collective-permute-start(bf16[2048,256]{1,0:T(8,128)(2,1)} %get-tuple-element.31.right_ref.inner_ref), channel_id=1, source_target_pairs={{0,8},{8,0},{16,24},{24,16},{32,40},{40,32},{48,56},{56,48},{64,72... | collective-permute-start | bytes 3145736 | tf_op jit(solution)/shard_map/ppermute | solution.py:257
  36.4 1.0 copy-start.7
  36.4 1.4 %copy-start = (bf16[2560,256]{1,0:T(8,128)(2,1)}, bf16[2560,256]{1,0:T(8,128)(2,1)S(1)}, u32[]{:S(2)}) copy-start(bf16[2560,256]{1,0:T(8,128)(2,1)S(1)} %collective-permute-done.recv_ref.right_recv_ref) | copy-start | bytes 3932164
  42.9 28.2 %collective-permute-start.4 = (bf16[384,1024]{1,0:T(8,128)(2,1)}, bf16[384,1024]{1,0:T(8,128)(2,1)S(1)}, u32[]{:S(2)}, u32[]{:S(2)}) collective-permute-start(bf16[384,1024]{1,0:T(8,128)(2,1)} %get-tuple-element.41), channel_id=1, source_target_pairs={{0,48},{8,56},{16,32},{24,40},{32,16},{40,24},{48,0},{56,8},{64,11... | collective-permute-start | bytes 2359304 | tf_op jit(solution)/shard_map/ppermute | solution.py:257
  45.6 27.7 %collective-permute-start.2 = (bf16[384,1024]{1,0:T(8,128)(2,1)}, bf16[384,1024]{1,0:T(8,128)(2,1)S(1)}, u32[]{:S(2)}, u32[]{:S(2)}) collective-permute-start(bf16[384,1024]{1,0:T(8,128)(2,1)} %get-tuple-element.35.after_ref), channel_id=1, source_target_pairs={{0,16},{8,24},{16,0},{24,8},{32,48},{40,56},{48,32},{56,40},{64,80... | collective-permute-start | bytes 2359304 | tf_op jit(solution)/shard_map/ppermute | solution.py:257
  50.0 42.8 %collective-permute-start.6 = (bf16[384,512]{1,0:T(8,128)(2,1)}, bf16[384,512]{1,0:T(8,128)(2,1)S(1)}, u32[]{:S(2)}, u32[]{:S(2)}) collective-permute-start(bf16[384,512]{1,0:T(8,128)(2,1)} %get-tuple-element.36.after_ref), channel_id=1, source_target_pairs={{0,64},{8,72},{16,80},{24,88},{32,96},{40,104},{48,112},{56,120},{... | collective-permute-start | bytes 1179656 | tf_op jit(solution)/shard_map/ppermute | solution.py:257
  62.5 8.5 %copy-start.4 = (bf16[384,1024]{1,0:T(8,128)(2,1)S(1)}, bf16[384,1024]{1,0:T(8,128)(2,1)}, u32[]{:S(2)}) copy-start(bf16[384,1024]{1,0:T(8,128)(2,1)} %get-tuple-element.40) | copy-start | bytes 2359300
  62.5 58.1 %all-to-all-start.1 = ((bf16[8,384,128]{2,1,0:T(8,128)(2,1)}), bf16[8,384,128]{2,1,0:T(8,128)(2,1)S(1)}, u32[]{:S(2)}, u32[]{:S(2)}) async-start(bf16[8,384,128]{2,1,0:T(8,128)(2,1)} %get-tuple-element.38), calls=%async_computation.1 | async-start | bytes 1572864 | tf_op jit(solution)/shard_map/all_to_all | solution.py:354
  67.5 25.4 %collective-permute-start.7 = (bf16[384,512]{1,0:T(8,128)(2,1)}, bf16[384,512]{1,0:T(8,128)(2,1)S(1)}, u32[]{:S(2)}, u32[]{:S(2)}) collective-permute-start(bf16[384,512]{1,0:T(8,128)(2,1)} %get-tuple-element.43), channel_id=1, source_target_pairs={{0,192},{8,200},{16,208},{24,216},{32,224},{40,232},{48,240},{56,2... | collective-permute-start | bytes 1179656 | tf_op jit(solution)/shard_map/ppermute | solution.py:257
  71.1 2.2 %copy-start.3 = (bf16[384,1024]{1,0:T(8,128)(2,1)S(1)}, bf16[384,1024]{1,0:T(8,128)(2,1)}, u32[]{:S(2)}) copy-start(bf16[384,1024]{1,0:T(8,128)(2,1)} %get-tuple-element.39) | copy-start | bytes 2359300
  71.4 23.4 %collective-permute-start.5 = (bf16[192,1024]{1,0:T(8,128)(2,1)S(1)}, bf16[192,1024]{1,0:T(8,128)(2,1)S(1)}, u32[]{:S(2)}, u32[]{:S(2)}) collective-permute-start(bf16[192,1024]{1,0:T(8,128)(2,1)S(1)} %slice.122), channel_id=1, source_target_pairs={{0,16},{8,24},{16,0},{24,8},{32,48},{40,56},{48,32},{56,40},{64,80... | collective-permute-start | bytes 1179656 | tf_op jit(solution)/shard_map/ppermute | solution.py:257
  73.3 19.5 %copy-start.6 = (bf16[384,512]{1,0:T(8,128)(2,1)S(1)}, bf16[384,512]{1,0:T(8,128)(2,1)}, u32[]{:S(2)}) copy-start(bf16[384,512]{1,0:T(8,128)(2,1)} %get-tuple-element.45) | copy-start | bytes 1179652
  73.6 19.4 %copy-start.5 = (bf16[384,512]{1,0:T(8,128)(2,1)S(1)}, bf16[384,512]{1,0:T(8,128)(2,1)}, u32[]{:S(2)}) copy-start(bf16[384,512]{1,0:T(8,128)(2,1)} %get-tuple-element.42) | copy-start | bytes 1179652
  73.6 21.2 %collective-permute-start.3 = (bf16[192,1024]{1,0:T(8,128)(2,1)S(1)}, bf16[192,1024]{1,0:T(8,128)(2,1)S(1)}, u32[]{:S(2)}, u32[]{:S(2)}) collective-permute-start(bf16[192,1024]{1,0:T(8,128)(2,1)S(1)} %slice.121), channel_id=1, source_target_pairs={{0,48},{8,56},{16,32},{24,40},{32,16},{40,24},{48,0},{56,8},{64,11... | collective-permute-start | bytes 1179656 | tf_op jit(solution)/shard_map/ppermute | solution.py:257
  93.1 17.5 %collective-permute-start.10 = (bf16[192,512]{1,0:T(8,128)(2,1)S(1)}, bf16[192,512]{1,0:T(8,128)(2,1)S(1)}, u32[]{:S(2)}, u32[]{:S(2)}) collective-permute-start(bf16[192,512]{1,0:T(8,128)(2,1)S(1)} %slice.123), channel_id=1, source_target_pairs={{0,192},{8,200},{16,208},{24,216},{32,224},{40,232},{48,240},{56,2... | collective-permute-start | bytes 589832 | tf_op jit(solution)/shard_map/ppermute | solution.py:257
  93.2 17.4 %collective-permute-start.11 = (bf16[192,512]{1,0:T(8,128)(2,1)S(1)}, bf16[192,512]{1,0:T(8,128)(2,1)S(1)}, u32[]{:S(2)}, u32[]{:S(2)}) collective-permute-start(bf16[192,512]{1,0:T(8,128)(2,1)S(1)} %slice.124), channel_id=1, source_target_pairs={{0,64},{8,72},{16,80},{24,88},{32,96},{40,104},{48,112},{56,120},{... | collective-permute-start | bytes 589832 | tf_op jit(solution)/shard_map/ppermute | solution.py:257
  95.1 18.4 %collective-permute-start.8 = (bf16[96,1024]{1,0:T(8,128)(2,1)S(1)}, bf16[96,1024]{1,0:T(8,128)(2,1)S(1)}, u32[]{:S(2)}, u32[]{:S(2)}) collective-permute-start(bf16[96,1024]{1,0:T(8,128)(2,1)S(1)} %slice.126), channel_id=1, source_target_pairs={{0,64},{8,72},{16,80},{24,88},{32,96},{40,104},{48,112},{56,120},{... | collective-permute-start | bytes 589832 | tf_op jit(solution)/shard_map/ppermute | solution.py:257
  96.6 18.1 %collective-permute-start.9 = (bf16[96,1024]{1,0:T(8,128)(2,1)S(1)}, bf16[96,1024]{1,0:T(8,128)(2,1)S(1)}, u32[]{:S(2)}, u32[]{:S(2)}) collective-permute-start(bf16[96,1024]{1,0:T(8,128)(2,1)S(1)} %slice.128), channel_id=1, source_target_pairs={{0,192},{8,200},{16,208},{24,216},{32,224},{40,232},{48,240},{56,2... | collective-permute-start | bytes 589832 | tf_op jit(solution)/shard_map/ppermute | solution.py:257
  110.7 5.9 %collective-permute-start.15 = (bf16[96,512]{1,0:T(8,128)(2,1)S(1)}, bf16[96,512]{1,0:T(8,128)(2,1)S(1)}, u32[]{:S(2)}, u32[]{:S(2)}) collective-permute-start(bf16[96,512]{1,0:T(8,128)(2,1)S(1)} %slice.132), channel_id=1, source_target_pairs={{0,48},{8,56},{16,32},{24,40},{32,16},{40,24},{48,0},{56,8},{64,11... | collective-permute-start | bytes 294920 | tf_op jit(solution)/shard_map/ppermute | solution.py:257
  111.9 4.8 %collective-permute-start.14 = (bf16[96,512]{1,0:T(8,128)(2,1)S(1)}, bf16[96,512]{1,0:T(8,128)(2,1)S(1)}, u32[]{:S(2)}, u32[]{:S(2)}) collective-permute-start(bf16[96,512]{1,0:T(8,128)(2,1)S(1)} %slice.130), channel_id=1, source_target_pairs={{0,16},{8,24},{16,0},{24,8},{32,48},{40,56},{48,32},{56,40},{64,80... | collective-permute-start | bytes 294920 | tf_op jit(solution)/shard_map/ppermute | solution.py:257
  116.7 7.6 %collective-permute-start.17 = (bf16[48,512]{1,0:T(8,128)(2,1)S(1)}, bf16[48,512]{1,0:T(8,128)(2,1)S(1)}, u32[]{:S(2)}, u32[]{:S(2)}) collective-permute-start(bf16[48,512]{1,0:T(8,128)(2,1)S(1)} %slice.140), channel_id=1, source_target_pairs={{0,16},{8,24},{16,0},{24,8},{32,48},{40,56},{48,32},{56,40},{64,80... | collective-permute-start | bytes 147464 | tf_op jit(solution)/shard_map/ppermute | solution.py:257
  117.4 6.9 %collective-permute-start.16 = (bf16[48,512]{1,0:T(8,128)(2,1)S(1)}, bf16[48,512]{1,0:T(8,128)(2,1)S(1)}, u32[]{:S(2)}, u32[]{:S(2)}) collective-permute-start(bf16[48,512]{1,0:T(8,128)(2,1)S(1)} %slice.138), channel_id=1, source_target_pairs={{0,48},{8,56},{16,32},{24,40},{32,16},{40,24},{48,0},{56,8},{64,11... | collective-permute-start | bytes 147464 | tf_op jit(solution)/shard_map/ppermute | solution.py:257
  120.0 7.2 %collective-permute-start.12 = (bf16[48,1024]{1,0:T(8,128)(2,1)S(1)}, bf16[48,1024]{1,0:T(8,128)(2,1)S(1)}, u32[]{:S(2)}, u32[]{:S(2)}) collective-permute-start(bf16[48,1024]{1,0:T(8,128)(2,1)S(1)} %slice.134), channel_id=1, source_target_pairs={{0,192},{8,200},{16,208},{24,216},{32,224},{40,232},{48,240},{56,2... | collective-permute-start | bytes 294920 | tf_op jit(solution)/shard_map/ppermute | solution.py:257
  120.6 6.5 %collective-permute-start.13 = (bf16[48,1024]{1,0:T(8,128)(2,1)S(1)}, bf16[48,1024]{1,0:T(8,128)(2,1)S(1)}, u32[]{:S(2)}, u32[]{:S(2)}) collective-permute-start(bf16[48,1024]{1,0:T(8,128)(2,1)S(1)} %slice.136), channel_id=1, source_target_pairs={{0,64},{8,72},{16,80},{24,88},{32,96},{40,104},{48,112},{56,120},{... | collective-permute-start | bytes 294920 | tf_op jit(solution)/shard_map/ppermute | solution.py:257
  120.6 0.9 copy-start.2

commit v3 on v2

v3 whole, which is shorter than its diff:
```python
import functools

import jax
import jax.numpy as jnp
from jax import lax
from jax.experimental import pallas as pl
from jax.experimental.pallas import tpu as pltpu
from jax.sharding import PartitionSpec as P

EPS = 1e-06
TOK = 8
F32 = jnp.float32
BF16 = jnp.bfloat16


def low_lanes(rows):
    return lax.broadcasted_iota(jnp.int32, (rows, 128), 1) < 64


def turn(values):
    return pltpu.roll(values, 64, 1)


def pack(pair, first, middle, last, packed_ref):
    samples = packed_ref.shape[1] * 2 // 3
    half = samples // 2
    low, low_half = low_lanes(samples), low_lanes(half)
    even, odd = packed_ref.at[2 * pair], packed_ref.at[2 * pair + 1]
    even[:samples] = first.astype(BF16)
    even[samples:] = jnp.where(low_half, middle[:half], turn(middle[half:])).astype(BF16)
    odd[:samples] = turn(jnp.where(low, last, middle)).astype(BF16)
    odd[samples:] = jnp.where(low_half, turn(last[:half]), last[half:]).astype(BF16)


def unpack(packed_ref, write):
    samples = packed_ref.shape[1] * 2 // 3
    low = low_lanes(samples)
    for pair in range(TOK // 2):
        even, odd = packed_ref.at[2 * pair], packed_ref.at[2 * pair + 1]
        turned = turn(odd[:samples].astype(F32))
        rest = even[samples:].astype(F32)
        rest = jnp.concatenate([rest, turn(rest)], axis=0)
        rest_odd = odd[samples:].astype(F32)
        rest_odd = jnp.concatenate([turn(rest_odd), rest_odd], axis=0)
        write(3 * pair, even[:samples].astype(F32))
        write(3 * pair + 1, jnp.where(low, rest, turned))
        write(3 * pair + 2, jnp.where(low, turned, rest_odd))


def tile(t):
    return slice(128 * t, 128 * t + 128)


def pack_kernel(x_hbm, packed_hbm, x, packed, in_sem, write_sem):
    def read(pair):
        cols = pl.ds(384 * pair, 384)
        return pltpu.make_async_copy(x_hbm.at[:, cols], x.at[:, cols], in_sem.at[pair])

    def write(pair):
        place = pl.ds(2 * pair, 2)
        return pltpu.make_async_copy(packed.at[place], packed_hbm.at[place], write_sem.at[pair])

    for pair in range(TOK // 2):
        read(pair).start()
    for pair in range(TOK // 2):
        read(pair).wait()
        pack(pair, *(x[:, tile(3 * pair + k)].astype(F32) for k in range(3)), packed)
        write(pair).start()
    for pair in range(TOK // 2):
        write(pair).wait()


def nn(a, b):
    return lax.dot_general(a, b, (((1,), (0,)), ((), ())), preferred_element_type=F32)


def nt(a, b):
    return lax.dot_general(a, b, (((1,), (1,)), ((), ())), preferred_element_type=F32)


def main_kernel(
    index_ref, x_hbm, recv_hbm, cot_hbm, w_in_hbm, w_out_hbm,
    own_hbm, send_hbm, grad16_hbm, normed_hbm, scale_hbm,
    x, recv, w_in, w_out, cot, state, grad16, hidden, normed, scales, values, slope, silu, turned, own, send,
    x_sem, recv_sem, in_sem, out_sem, cot_sem, write_sem,
):
    samples, width = x.shape
    ff = w_out.shape[1]
    wide = 256
    steps = ff // wide
    half = width // 2
    writes = []

    def write(source, target, begin, rows):
        place = pl.ds(begin, rows)
        writes.append(pltpu.make_async_copy(source.at[place], target.at[place], write_sem.at[len(writes)]))
        writes[-1].start()

    def w_in_copy(j, c):
        cols = pl.ds(c * ff + j * wide, wide)
        return pltpu.make_async_copy(w_in_hbm.at[:, cols], w_in.at[:, cols], in_sem.at[2 * j + c])

    x_copy = pltpu.make_async_copy(x_hbm, x, x_sem)
    recv_copy = pltpu.make_async_copy(recv_hbm, recv, recv_sem)
    x_copy.start()
    recv_copy.start()
    for j in range(steps):
        w_in_copy(j, 0).start()
        w_in_copy(j, 1).start()
    out_copy = pltpu.make_async_copy(w_out_hbm, w_out, out_sem)
    out_copy.start()
    cot_copy = pltpu.make_async_copy(cot_hbm, cot, cot_sem)
    cot_copy.start()

    rank = index_ref[0]

    def spread(at):
        for b in range(16):
            place = slice(at + 48 * b, at + 48 * b + 48)
            own[place, :] = turned[pl.ds(pl.multiple_of((rank ^ (2 * b)) * 48, 48), 48), :]
            send[place, :] = turned[pl.ds(pl.multiple_of((rank ^ (2 * b + 1)) * 48, 48), 48), :]
        write(send, send_hbm, at, half)
        write(own, own_hbm, at, half)

    x_copy.wait()
    recv_copy.wait()
    sums = [jnp.zeros((samples, 128), F32)]

    def add_mixed(t, mixed):
        v = x[:, tile(t)].astype(F32) + mixed
        normed[:, tile(t)] = v
        sums[0] = sums[0] + v * v

    unpack(recv, add_mixed)
    scale = lax.rsqrt(jnp.sum(sums[0], axis=1, keepdims=True) / width + EPS)
    scales[...] = jnp.broadcast_to(scale, scales.shape)
    for t in range(width // 128):
        v = normed[:, tile(t)] * scale
        normed[:, tile(t)] = v
        state[:, tile(t)] = v.astype(BF16)
    write(normed, normed_hbm, 0, samples)
    write(scales, scale_hbm, 0, samples)

    for j in range(steps):
        cols = slice(wide * j, wide * j + wide)
        w_in_copy(j, 0).wait()
        gate = nn(state[...], w_in[:, cols])
        w_in_copy(j, 1).wait()
        up = nn(state[...], w_in[:, ff + wide * j : ff + wide * j + wide])
        sigma = jax.nn.sigmoid(gate)
        silu_gate = gate * sigma
        part = (silu_gate * up).astype(BF16)
        hidden[:, cols] = part
        send[width + wide * j : width + wide * j + wide, :] = part
        silu[:, cols] = silu_gate
        slope[:, cols] = up * sigma * (1.0 + gate * (1.0 - sigma))
    write(send, send_hbm, width, ff)

    out_copy.wait()
    for d in range(width // wide):
        cols = slice(wide * d, wide * d + wide)
        values[:, cols] = nt(hidden[...], w_out[cols, :]) + state[:, cols].astype(F32)
    for t in range(width // 128):
        turned[tile(t), :] = state[:, tile(t)].T
    spread(half)
    cot_copy.wait()
    squares = jnp.zeros((samples, 128), F32)
    products = jnp.zeros((samples, 128), F32)
    for t in range(width // 128):
        v = values[:, tile(t)]
        squares = squares + v * v
        products = products + v * cot[:, tile(t)].astype(F32)
    scale = lax.rsqrt(jnp.sum(squares, axis=1, keepdims=True) / width + EPS)
    mean = scale * jnp.sum(products, axis=1, keepdims=True) / width
    for t in range(width // 128):
        out_normed = values[:, tile(t)] * scale
        g16 = (scale * (cot[:, tile(t)].astype(F32) - out_normed * mean)).astype(BF16)
        grad16[:, tile(t)] = g16
        turned[tile(t), :] = g16.T
    write(grad16, grad16_hbm, 0, samples)
    spread(0)
    for j in range(steps):
        cols = slice(wide * j, wide * j + wide)
        hidden_grad = nn(grad16[...], w_out[:, cols])
        at = width + ff + wide * j
        send[at : at + wide, :] = (hidden_grad * slope[:, cols]).astype(BF16)
        send[at + ff : at + ff + wide, :] = (hidden_grad * silu[:, cols]).astype(BF16)
        write(send, send_hbm, at, wide)
        write(send, send_hbm, at + ff, wide)
    for copy in writes:
        copy.wait()


def input_kernel(
    block, send_hbm, w_in_hbm, normed_hbm, scale_hbm, grad_hbm, pre_hbm, packed_hbm,
    w_in, inner, normed, scales, grad, pre, packed, w_sem, inner_sem, side_sem, write_sem,
):
    samples, width = normed.shape
    wide = 256
    reads = []

    def read(source, target, sem):
        reads.append(pltpu.make_async_copy(source, target, sem))
        reads[-1].start()

    for j in range(inner.shape[1] // wide):
        read(send_hbm.at[pl.ds(block + wide * j, wide)], inner.at[:, pl.ds(wide * j, wide)], inner_sem.at[j])
    n_inner = len(reads)
    for d in range(width // wide):
        read(w_in_hbm.at[pl.ds(wide * d, wide)], w_in.at[pl.ds(wide * d, wide)], w_sem.at[d])
        if d == 0:
            read(grad_hbm, grad, side_sem.at[0])
            read(normed_hbm, normed, side_sem.at[1])
            read(scale_hbm, scales, side_sem.at[2])
    waits = [reads[: n_inner + 4]] + [[r] for r in reads[n_inner + 4 :]]
    products = jnp.zeros((samples, 128), F32)
    for d in range(width // wide):
        for copy in waits[d]:
            copy.wait()
        cols = slice(wide * d, wide * d + wide)
        g = nt(inner[...], w_in[cols, :]) + grad[:, cols].astype(F32)
        pre[:, cols] = g
        p = g * normed[:, cols]
        products = products + p[:, :128] + p[:, 128:]
    mean = jnp.sum(products, axis=1, keepdims=True) / width
    scale = scales[:, :1]
    writes = []
    for pair in range(TOK // 2):
        tiles = []
        for t in range(3 * pair, 3 * pair + 3):
            tiles.append(scale * (pre[:, tile(t)] - normed[:, tile(t)] * mean))
            pre[:, tile(t)] = tiles[-1]
        pack(pair, *tiles, packed)
        place, cols = pl.ds(2 * pair, 2), pl.ds(384 * pair, 384)
        writes.append(pltpu.make_async_copy(packed.at[place], packed_hbm.at[place], write_sem.at[2 * pair]))
        writes.append(pltpu.make_async_copy(pre.at[:, cols], pre_hbm.at[:, cols], write_sem.at[2 * pair + 1]))
        writes[-2].start()
        writes[-1].start()
    for copy in writes:
        copy.wait()


def final_kernel(pre_ref, recv_ref, out_ref):
    def write(t, returned):
        out_ref[:, tile(t)] = (pre_ref[:, tile(t)] + returned).astype(BF16)

    unpack(recv_ref, write)


KEEP_FIRST = ((0, 3, 1, 2), (0, 1, 3, 2))
PARTNERS = ((1, 3), (3, 1))


def grad_kernel(x_first, at, block, own_hbm, send_hbm, other_hbm, after_hbm, *refs):
    del after_hbm
    outs_hbm, outs = refs[:4], refs[4:8]
    own, other, right, right_other, in_sem, write_sem = refs[8:]
    rows = own.shape[0]
    wide = 256
    per = outs[0].shape[1] // wide
    reads, writes = [], []

    def read(source, begin, target, to, count):
        copy = pltpu.make_async_copy(
            source.at[pl.ds(begin, count)], target.at[pl.ds(to, count)], in_sem.at[len(reads)]
        )
        copy.start()
        reads.append(copy)

    read(own_hbm, at, own, 0, rows)
    read(other_hbm, at, other, 0, rows)
    for k in range(2 * per):
        read(send_hbm, block + wide * k, right, wide * k, wide)
        read(other_hbm, block + wide * k, right_other, wide * k, wide)
    reads[0].wait()
    reads[1].wait()
    for k in range(2 * per):
        flavour, col = divmod(k, per)
        keep, send = outs[2 * flavour], outs[2 * flavour + 1]
        order = KEEP_FIRST[flavour]
        reads[2 + 2 * k].wait()
        reads[3 + 2 * k].wait()
        place, cols = slice(wide * k, wide * k + wide), slice(wide * col, wide * col + wide)
        g = (nn(own[...], right[place, :]) + nn(other[...], right_other[place, :])).astype(BF16)
        for b in range(16):
            rz, rx = order.index(b // 4), order.index(b % 4)
            to = rx * 4 + rz if x_first else rz * 4 + rx
            target = keep if to < 8 else send
            to = (to % 8) * 48
            target[to : to + 48, cols] = g[48 * b : 48 * b + 48]
        for side in range(2):
            n = 2 * flavour + side
            cols = pl.ds(wide * col, wide)
            copy = pltpu.make_async_copy(outs[n].at[:, cols], outs_hbm[n].at[:, cols], write_sem.at[len(writes)])
            copy.start()
            writes.append(copy)
    for copy in writes:
        copy.wait()


def params(mebibytes):
    return pltpu.CompilerParams(vmem_limit_bytes=mebibytes * 1024 * 1024)


VMEM = pl.BlockSpec(memory_space=pltpu.VMEM)
SMEM = pl.BlockSpec(memory_space=pltpu.SMEM)
ANY = pl.BlockSpec(memory_space=pl.ANY)


def cost(flops, moved):
    return pl.CostEstimate(flops=int(flops), bytes_accessed=int(moved), transcendentals=0)


def shape(dims, dtype=BF16):
    return jax.ShapeDtypeStruct(dims, dtype)


def swap(values, distance):
    return lax.ppermute(values, "dp", [(i, i ^ distance) for i in range(32)])


def gradients(x_first, at, block, columns, own, send, other, after, name):
    piece = shape((384, columns // 2))
    rows, samples = own.shape[0] // 2, own.shape[1]
    moved = (2 * rows * samples + 2 * samples * columns + rows * columns) * 2
    return pl.pallas_call(
        functools.partial(grad_kernel, x_first, at, block),
        out_shape=[piece] * 4,
        in_specs=[ANY] * 4,
        out_specs=[ANY] * 4,
        scratch_shapes=[pltpu.VMEM(piece.shape, BF16)] * 4
        + [pltpu.VMEM((rows, samples), BF16)] * 2
        + [pltpu.VMEM((columns, samples), BF16)] * 2
        + [pltpu.SemaphoreType.DMA((2 + columns // 128,)), pltpu.SemaphoreType.DMA((columns // 128,))],
        compiler_params=params(56),
        cost_estimate=cost(2 * rows * 2 * samples * columns, moved),
        name=name,
    )(own, send, other, after)


def reduce_send(scales, step, send):
    return [swap(send[f], PARTNERS[f][step % 2] * scales[step // 2]) for f in range(2)]


def reduce_add(step, keep, got):
    totals = [k.astype(F32) + g.astype(F32) for k, g in zip(keep, got)]
    if step == 3:
        return [t.astype(BF16) for t in totals], []
    half = totals[0].shape[0] // 2
    return [t[:half].astype(BF16) for t in totals], [t[half:].astype(BF16) for t in totals]


def local(block_input, out_cotangent, w_in, w_out):
    samples, _, width = block_input.shape
    ff = w_out.shape[2]
    x = block_input[:, 0]
    cotangent = out_cotangent[:, 0]
    flat_in = w_in[0].reshape(width, 2 * ff)
    weight_out = w_out[0]
    packed_shape = shape((TOK, samples * 3 // 2, 128))
    index = lax.axis_index("dp").astype(jnp.int32).reshape(1)

    packed = pl.pallas_call(
        pack_kernel, out_shape=packed_shape, in_specs=[ANY], out_specs=ANY, compiler_params=params(56),
        scratch_shapes=[
            pltpu.VMEM((samples, width), BF16),
            pltpu.VMEM(packed_shape.shape, BF16),
            pltpu.SemaphoreType.DMA((4,)),
            pltpu.SemaphoreType.DMA((4,)),
        ],
        cost_estimate=cost(samples * width, 4 * samples * width), name="pack",
    )(x)
    recv = lax.all_to_all(packed, "token", split_axis=0, concat_axis=0, tiled=True)

    flat = shape((samples, width))
    full, scales = shape((samples, width), F32), shape((samples, 128), F32)
    own, send, out_grad16, normed, scale = pl.pallas_call(
        main_kernel,
        out_shape=[shape((width, samples)), shape((width + 3 * ff, samples)), flat, full, scales],
        in_specs=[SMEM] + [ANY] * 5,
        out_specs=[ANY] * 5,
        scratch_shapes=[
            pltpu.VMEM((samples, width), BF16),
            pltpu.VMEM(packed_shape.shape, BF16),
            pltpu.VMEM((width, 2 * ff), BF16),
            pltpu.VMEM((width, ff), BF16),
            pltpu.VMEM((samples, width), BF16),
            pltpu.VMEM((samples, width), BF16),
            pltpu.VMEM((samples, width), BF16),
            pltpu.VMEM((samples, ff), BF16),
            pltpu.VMEM((samples, width), F32),
            pltpu.VMEM((samples, 128), F32),
            pltpu.VMEM((samples, width), F32),
            pltpu.VMEM((samples, ff), F32),
            pltpu.VMEM((samples, ff), F32),
            pltpu.VMEM((width, samples), BF16),
            pltpu.VMEM((width, samples), BF16),
            pltpu.VMEM((width + 3 * ff, samples), BF16),
            pltpu.SemaphoreType.DMA,
            pltpu.SemaphoreType.DMA,
            pltpu.SemaphoreType.DMA((8,)),
            pltpu.SemaphoreType.DMA,
            pltpu.SemaphoreType.DMA,
            pltpu.SemaphoreType.DMA((16,)),
        ],
        compiler_params=params(56),
        cost_estimate=cost(8 * samples * width * ff, 18e6),
        name="main",
    )(index, x, recv, cotangent, flat_in, weight_out)
    other = swap(send, 1)

    pre_grad, back = pl.pallas_call(
        functools.partial(input_kernel, width + ff),
        out_shape=[full, packed_shape],
        in_specs=[ANY] * 5,
        out_specs=[ANY] * 2,
        scratch_shapes=[
            pltpu.VMEM((width, 2 * ff), BF16),
            pltpu.VMEM((samples, 2 * ff), BF16),
            pltpu.VMEM((samples, width), F32),
            pltpu.VMEM((samples, 128), F32),
            pltpu.VMEM((samples, width), BF16),
            pltpu.VMEM((samples, width), F32),
            pltpu.VMEM(packed_shape.shape, BF16),
            pltpu.SemaphoreType.DMA((width // 256,)),
            pltpu.SemaphoreType.DMA((8,)),
            pltpu.SemaphoreType.DMA((3,)),
            pltpu.SemaphoreType.DMA((8,)),
        ],
        compiler_params=params(56),
        cost_estimate=cost(4 * samples * width * ff, 14e6),
        name="input",
    )(send, flat_in, normed, scale, out_grad16)

    up = gradients(True, width // 2, width + ff, 2 * ff, own, send, other, back, "in_grads")
    up_got = reduce_send((2, 8), 0, up[1::2])
    down = gradients(False, 0, width, ff, own, send, other, up[1], "down_grads")
    down_got = reduce_send((8, 2), 0, down[1::2])
    up_keep, down_keep = up[0::2], down[0::2]
    returned = lax.all_to_all(back, "token", split_axis=0, concat_axis=0, tiled=True)

    for step in range(4):
        if step == 2:
            input_grad = pl.pallas_call(
                final_kernel, out_shape=flat, in_specs=[VMEM] * 2, out_specs=VMEM,
                compiler_params=params(56), cost_estimate=cost(samples * width, 8 * samples * width), name="final",
            )(pre_grad, returned)
        up_keep, up_send = reduce_add(step, up_keep, up_got)
        if step < 3:
            up_got = reduce_send((2, 8), step + 1, up_send)
        down_got, up_send = lax.optimization_barrier((down_got, up_send))
        down_keep, down_send = reduce_add(step, down_keep, down_got)
        if step < 3:
            down_got = reduce_send((8, 2), step + 1, down_send)
            up_got, down_send = lax.optimization_barrier((up_got, down_send))

    return (
        input_grad[:, None, :],
        jnp.stack(up_keep, axis=1)[None],
        jnp.concatenate(down_keep, axis=1)[None],
    )


def solution(mesh):
    placed = (
        P("dp", "token", None),
        P("dp", "token", None),
        P("token", None, None, None),
        P("token", None, None),
    )
    return jax.shard_map(
        local,
        mesh=mesh,
        in_specs=placed,
        out_specs=(P("dp", "token", None), P("token", "dp", None, None), P("token", "dp", None)),
        check_vma=False,
    )
```

time: 129 us -> 130 us (level)
  waiting for transfers between devices: 41.6 us -> 35.5 us
  Pallas kernels: 34.2 us -> 37.7 us
  starting transfers between devices: 37.1 us -> 40.6 us
    ppermute x18 -> x17, waiting for transfers between devices: 38.8 us -> 32.7 us  [swap(): return lax.ppermute(values, 'dp', [(i, i ^ distance) for i in range(32)])]
    ppermute x18 -> x17, starting transfers between devices: 25.9 us -> 29.5 us  [swap(): return lax.ppermute(values, 'dp', [(i, i ^ distance) for i in range(32)])]
    pallas_call x2, Pallas kernels: 9.24 us -> 11 us  [gradients(): pl.pallas_call(functools.partial(grad_kernel, x_first, at, block), out_sh...]
    unnamed x18 -> x16, local copies, waits for them, and re-layouts: 12.1 us -> 12.1 us
  transfers between devices with their start and end apart: 20 -> 19, of which waited for: 8 -> 11; matrix products, arithmetic and copies ran while one was open for 8% -> 8% of each run, Pallas kernels for 13% -> 13%
where the time goes in v3:
time: 130 us; the launch traced here: 129 us
  starting transfers between devices  40.6 us (31%)
  Pallas kernels  37.7 us (29%)
  waiting for transfers between devices  35.5 us (27%)
  local copies, waits for them, and re-layouts  12.3 us (9%)
  other arithmetic  2.08 us (2%)
    ppermute x17, waiting for transfers between devices, swap(): return lax.ppermute(values, 'dp', [(i, i ^ distance) for i in range(32)])  32.7 us
    ppermute x17, starting transfers between devices, swap(): return lax.ppermute(values, 'dp', [(i, i ^ distance) for i in range(32)])  29.5 us
    unnamed x16, local copies, waits for them, and re-layouts  12.1 us
    pallas_call x1, Pallas kernels, local(): pl.pallas_call(main_kernel, out_shape=[shape((width, samples)), shape((wi...  12 us
    pallas_call x2, Pallas kernels, gradients(): pl.pallas_call(functools.partial(grad_kernel, x_first, at, block), out_sh...  11 us
    pallas_call x1, Pallas kernels, local(): pl.pallas_call(functools.partial(input_kernel, width + ff), out_shape=[fu...  9.87 us
    all_to_all x1, starting transfers between devices, local(): lax.all_to_all(packed, 'token', split_axis=0, concat_axis=0, tiled=True)  6.28 us
    all_to_all x1, starting transfers between devices, local(): lax.all_to_all(back, 'token', split_axis=0, concat_axis=0, tiled=True)  4.8 us
  transfers between devices with their start and end apart: 19, of which 11 were waited for; matrix products, arithmetic and copies ran while one was open for 8% of the time, Pallas kernels for 13%

profile of v3, /device:TPU:8, one launch (start us, length us, event | category | flops | bytes accessed | tf_op | source)
XLA Modules:
  0.0 129.2 jit_solution(9340293639142042268)
XLA Ops:
  0.6 2.1 %pack.1 = bf16[8,384,128]{2,1,0:T(8,128)(2,1)} custom-call(bf16[256,1536]{1,0:T(8,128)(2,1)} %bitcast.19), custom_call_target="tpu_custom_call" | custom-call | flops 393216 | bytes 1572864 | tf_op jit(solution)/shard_map/pack/pallas_call | solution.py:363
  2.7 6.3 %all-to-all-start = ((bf16[8,384,128]{2,1,0:T(8,128)(2,1)}), bf16[8,384,128]{2,1,0:T(8,128)(2,1)S(1)}, u32[]{:S(2)}, u32[]{:S(2)}) async-start(bf16[8,384,128]{2,1,0:T(8,128)(2,1)} %pack.1), calls=%async_computation | async-start | bytes 1572864 | tf_op jit(solution)/shard_map/all_to_all | solution.py:373
  9.0 8.0 %copy.8 = bf16[192,8,2,1024]{3,1,2,0:T(8,128)(2,1)} copy(bf16[192,8,2,1024]{3,2,1,0:T(2,128)(2,1)} %bitcast.18) | data formatting | bytes 12582912
  17.0 2.8 %all-to-all-done.recv_hbm = bf16[8,384,128]{2,1,0:T(8,128)(2,1)S(1)} async-done(((bf16[8,384,128]{2,1,0:T(8,128)(2,1)}), bf16[8,384,128]{2,1,0:T(8,128)(2,1)S(1)}, u32[]{:S(2)}, u32[]{:S(2)}) %all-to-all-start) | async-done | bytes 786464 | tf_op jit(solution)/shard_map/all_to_all | solution.py:373
  19.8 0.9 copy-done.2
  20.7 12.0 %main.1 = (bf16[1536,256]{1,0:T(8,128)(2,1)}, bf16[4608,256]{1,0:T(8,128)(2,1)}, bf16[256,1536]{1,0:T(8,128)(2,1)}, f32[256,1536]{1,0:T(8,128)}, f32[256,128]{1,0:T(8,128)}) custom-call(s32[1]{0:T(128)} %bitcast.index_ref, bf16[256,1536]{1,0:T(8,128)(2,1)} %bitcast.20, bf16[8,384,128]{2,1,0:T(8,128)(2,1)} %copy-done.2, bf16[256,1536]{1,0:T(8,128)(2,1)} %bitcast.23, ...), custom_call_target="tpu_custom_call" | custom-call | flops 3221225472 | bytes 18000000 | tf_op jit(solution)/shard_map/main/pallas_call | solution.py:377
  32.7 0.3 collective-permute-start
  33.0 9.9 %input.1 = (f32[256,1536]{1,0:T(8,128)}, bf16[8,384,128]{2,1,0:T(8,128)(2,1)}) custom-call(bf16[4608,256]{1,0:T(8,128)(2,1)} %get-tuple-element.32.send_hbm, bf16[1536,2048]{1,0:T(8,128)(2,1)} %bitcast.17, f32[256,1536]{1,0:T(8,128)} %get-tuple-element.33.normed_hbm, f32[256,128]{1,0:T(8,128)} %get-tuple-element.34.scale_hbm, ...), custom_call_target="tpu_custom_call" | custom-call | flops 1610612736 | bytes 14000000 | tf_op jit(solution)/shard_map/input/pallas_call | solution.py:412
  42.9 0.0 collective-permute-done.other_hbm
  42.9 0.0 copy-start
  42.9 1.4 %copy-done = bf16[4608,256]{1,0:T(8,128)(2,1)} copy-done((bf16[4608,256]{1,0:T(8,128)(2,1)}, bf16[4608,256]{1,0:T(8,128)(2,1)S(1)}, u32[]{:S(2)}) %copy-start) | copy-done | bytes 2359320
  44.3 6.7 %in_grads.1 = (bf16[384,1024]{1,0:T(8,128)(2,1)}, bf16[384,1024]{1,0:T(8,128)(2,1)}, bf16[384,1024]{1,0:T(8,128)(2,1)}, bf16[384,1024]{1,0:T(8,128)(2,1)}) custom-call(bf16[1536,256]{1,0:T(8,128)(2,1)} %get-tuple-element.38.own_hbm, bf16[4608,256]{1,0:T(8,128)(2,1)} %get-tuple-element.32.send_hbm, bf16[4608,256]{1,0:T(8,128)(2,1)} %copy-done, ...), custom_call_target="tpu_custom_call" | custom-call | flops 1610612736 | bytes 6029312 | tf_op jit(solution)/shard_map/in_grads/pallas_call | solution.py:326
  51.0 2.8 %collective-permute-start.3 = (bf16[384,1024]{1,0:T(8,128)(2,1)}, bf16[384,1024]{1,0:T(8,128)(2,1)S(1)}, u32[]{:S(2)}, u32[]{:S(2)}) collective-permute-start(bf16[384,1024]{1,0:T(8,128)(2,1)} %get-tuple-element.42), channel_id=1, source_target_pairs={{0,48},{8,56},{16,32},{24,40},{32,16},{40,24},{48,0},{56,8},{64,11... | collective-permute-start | bytes 2359304 | tf_op jit(solution)/shard_map/ppermute | solution.py:319
  53.8 0.2 collective-permute-start.1
  54.0 4.8 %all-to-all-start.1 = ((bf16[8,384,128]{2,1,0:T(8,128)(2,1)}), bf16[8,384,128]{2,1,0:T(8,128)(2,1)S(1)}, u32[]{:S(2)}, u32[]{:S(2)}) async-start(bf16[8,384,128]{2,1,0:T(8,128)(2,1)} %get-tuple-element.37.after_hbm), calls=%async_computation.1 | async-start | bytes 1572864 | tf_op jit(solution)/shard_map/all_to_all | solution.py:440
  58.8 4.3 %down_grads.1 = (bf16[384,512]{1,0:T(8,128)(2,1)}, bf16[384,512]{1,0:T(8,128)(2,1)}, bf16[384,512]{1,0:T(8,128)(2,1)}, bf16[384,512]{1,0:T(8,128)(2,1)}) custom-call(bf16[1536,256]{1,0:T(8,128)(2,1)} %get-tuple-element.38.own_hbm, bf16[4608,256]{1,0:T(8,128)(2,1)} %get-tuple-element.32.send_hbm, bf16[4608,256]{1,0:T(8,128)(2,1)} %copy-done, ...), custom_call_target="tpu_custom_call" | custom-call | flops 805306368 | bytes 3407872 | tf_op jit(solution)/shard_map/down_grads/pallas_call | solution.py:326
  63.2 3.4 %collective-permute-start.5 = (bf16[384,512]{1,0:T(8,128)(2,1)}, bf16[384,512]{1,0:T(8,128)(2,1)S(1)}, u32[]{:S(2)}, u32[]{:S(2)}) collective-permute-start(bf16[384,512]{1,0:T(8,128)(2,1)} %get-tuple-element.44), channel_id=1, source_target_pairs={{0,64},{8,72},{16,80},{24,88},{32,96},{40,104},{48,112},{56,120},{... | collective-permute-start | bytes 1179656 | tf_op jit(solution)/shard_map/ppermute | solution.py:319
  66.5 3.6 %collective-permute-start.6 = (bf16[384,512]{1,0:T(8,128)(2,1)}, bf16[384,512]{1,0:T(8,128)(2,1)S(1)}, u32[]{:S(2)}, u32[]{:S(2)}) collective-permute-start(bf16[384,512]{1,0:T(8,128)(2,1)} %get-tuple-element.45), channel_id=1, source_target_pairs={{0,192},{8,200},{16,208},{24,216},{32,224},{40,232},{48,240},{56,2... | collective-permute-start | bytes 1179656 | tf_op jit(solution)/shard_map/ppermute | solution.py:319
  70.1 2.3 %collective-permute-done.3 = bf16[384,1024]{1,0:T(8,128)(2,1)S(1)} collective-permute-done((bf16[384,1024]{1,0:T(8,128)(2,1)}, bf16[384,1024]{1,0:T(8,128)(2,1)S(1)}, u32[]{:S(2)}, u32[]{:S(2)}) %collective-permute-start.3) | collective-permute-done | bytes 786464 | tf_op jit(solution)/shard_map/ppermute | solution.py:319
  72.4 0.0 copy-done.4
  72.4 0.3 add_convert_fusion
  72.8 0.4 collective-permute-start.4
  73.1 0.6 collective-permute-done.1
  73.7 0.0 copy-done.3
  73.7 0.3 add_convert_fusion.1
  74.0 0.0 copy-start.5
  74.0 2.7 %collective-permute-start.2 = (bf16[192,1024]{1,0:T(8,128)(2,1)S(1)}, bf16[192,1024]{1,0:T(8,128)(2,1)S(1)}, u32[]{:S(2)}, u32[]{:S(2)}) collective-permute-start(bf16[192,1024]{1,0:T(8,128)(2,1)S(1)} %slice.121), channel_id=1, source_target_pairs={{0,48},{8,56},{16,32},{24,40},{32,16},{40,24},{48,0},{56,8},{64,11... | collective-permute-start | bytes 1179656 | tf_op jit(solution)/shard_map/ppermute | solution.py:319
  76.7 7.7 %collective-permute-done.5 = bf16[384,512]{1,0:T(8,128)(2,1)S(1)} collective-permute-done((bf16[384,512]{1,0:T(8,128)(2,1)}, bf16[384,512]{1,0:T(8,128)(2,1)S(1)}, u32[]{:S(2)}, u32[]{:S(2)}) %collective-permute-start.5) | collective-permute-done | bytes 393248 | tf_op jit(solution)/shard_map/ppermute | solution.py:319
  84.4 5.7 %collective-permute-done.6 = bf16[384,512]{1,0:T(8,128)(2,1)S(1)} collective-permute-done((bf16[384,512]{1,0:T(8,128)(2,1)}, bf16[384,512]{1,0:T(8,128)(2,1)S(1)}, u32[]{:S(2)}, u32[]{:S(2)}) %collective-permute-start.6) | collective-permute-done | bytes 393248 | tf_op jit(solution)/shard_map/ppermute | solution.py:319
  90.1 0.1 add_convert_fusion.4
  90.3 0.1 add_convert_fusion.5
  90.4 1.2 collective-permute-start.9
  91.6 1.0 collective-permute-start.10
  92.6 0.0 collective-permute-done.4
  92.6 0.0 collective-permute-done.2
  92.6 0.1 add_convert_fusion.2
  92.8 0.1 add_convert_fusion.3
  92.9 2.3 %collective-permute-start.7 = (bf16[96,1024]{1,0:T(8,128)(2,1)S(1)}, bf16[96,1024]{1,0:T(8,128)(2,1)S(1)}, u32[]{:S(2)}, u32[]{:S(2)}) collective-permute-start(bf16[96,1024]{1,0:T(8,128)(2,1)S(1)} %slice.126), channel_id=1, source_target_pairs={{0,64},{8,72},{16,80},{24,88},{32,96},{40,104},{48,112},{56,120},{... | collective-permute-start | bytes 589832 | tf_op jit(solution)/shard_map/ppermute | solution.py:319
  95.2 3.0 %collective-permute-start.8 = (bf16[96,1024]{1,0:T(8,128)(2,1)S(1)}, bf16[96,1024]{1,0:T(8,128)(2,1)S(1)}, u32[]{:S(2)}, u32[]{:S(2)}) collective-permute-start(bf16[96,1024]{1,0:T(8,128)(2,1)S(1)} %slice.128), channel_id=1, source_target_pairs={{0,192},{8,200},{16,208},{24,216},{32,224},{40,232},{48,240},{56,2... | collective-permute-start | bytes 589832 | tf_op jit(solution)/shard_map/ppermute | solution.py:319
  98.2 7.9 %collective-permute-done.9 = bf16[192,512]{1,0:T(8,128)(2,1)S(1)} collective-permute-done((bf16[192,512]{1,0:T(8,128)(2,1)S(1)}, bf16[192,512]{1,0:T(8,128)(2,1)S(1)}, u32[]{:S(2)}, u32[]{:S(2)}) %collective-permute-start.9) | collective-permute-done | bytes 196640 | tf_op jit(solution)/shard_map/ppermute | solution.py:319
  106.1 0.0 collective-permute-done.10
  106.1 0.1 add_convert_fusion.9
  106.2 0.1 add_convert_fusion.8
  106.2 1.1 collective-permute-start.14
  107.3 0.7 collective-permute-start.13
  108.1 2.4 %collective-permute-done.7 = bf16[96,1024]{1,0:T(8,128)(2,1)S(1)} collective-permute-done((bf16[96,1024]{1,0:T(8,128)(2,1)S(1)}, bf16[96,1024]{1,0:T(8,128)(2,1)S(1)}, u32[]{:S(2)}, u32[]{:S(2)}) %collective-permute-start.7) | collective-permute-done | bytes 196640 | tf_op jit(solution)/shard_map/ppermute | solution.py:319
  110.5 0.6 collective-permute-done.8
  111.2 0.1 add_convert_fusion.6
  111.3 0.9 collective-permute-done.14
  112.2 0.0 collective-permute-done.13
  112.2 0.9 collective-permute-start.16
  113.1 2.3 %collective-permute-start.15 = (bf16[48,512]{1,0:T(8,128)(2,1)S(1)}, bf16[48,512]{1,0:T(8,128)(2,1)S(1)}, u32[]{:S(2)}, u32[]{:S(2)}) collective-permute-start(bf16[48,512]{1,0:T(8,128)(2,1)S(1)} %slice.138), channel_id=1, source_target_pairs={{0,48},{8,56},{16,32},{24,40},{32,16},{40,24},{48,0},{56,8},{64,11... | collective-permute-start | bytes 147464 | tf_op jit(solution)/shard_map/ppermute | solution.py:319
  115.5 0.0 all-to-all-done.1.recv_ref
  115.5 0.9 copy-done.1
  116.4 2.8 %final.1 = bf16[256,1536]{1,0:T(8,128)(2,1)} custom-call(f32[256,1536]{1,0:T(8,128)} %get-tuple-element.36.pre_ref, bf16[8,384,128]{2,1,0:T(8,128)(2,1)} %copy-done.1), custom_call_target="tpu_custom_call" | custom-call | flops 393216 | bytes 3145728 | tf_op jit(solution)/shard_map/final/pallas_call | solution.py:444
  119.2 3.5 %collective-permute-start.11 = (bf16[48,1024]{1,0:T(8,128)(2,1)S(1)}, bf16[48,1024]{1,0:T(8,128)(2,1)S(1)}, u32[]{:S(2)}, u32[]{:S(2)}) collective-permute-start(bf16[48,1024]{1,0:T(8,128)(2,1)S(1)} %slice.134), channel_id=1, source_target_pairs={{0,192},{8,200},{16,208},{24,216},{32,224},{40,232},{48,240},{56,2... | collective-permute-start | bytes 294920 | tf_op jit(solution)/shard_map/ppermute | solution.py:319
  122.7 0.2 collective-permute-start.12
  122.9 0.0 collective-permute-done.16
  122.9 0.0 collective-permute-done.15
  122.9 0.6 maximum_bitcast_fusion.1
  123.5 2.3 %collective-permute-done.11 = bf16[48,1024]{1,0:T(8,128)(2,1)S(1)} collective-permute-done((bf16[48,1024]{1,0:T(8,128)(2,1)S(1)}, bf16[48,1024]{1,0:T(8,128)(2,1)S(1)}, u32[]{:S(2)}, u32[]{:S(2)}) %collective-permute-start.11) | collective-permute-done | bytes 98336 | tf_op jit(solution)/shard_map/ppermute | solution.py:319
  125.9 2.3 %collective-permute-done.12 = bf16[48,1024]{1,0:T(8,128)(2,1)S(1)} collective-permute-done((bf16[48,1024]{1,0:T(8,128)(2,1)S(1)}, bf16[48,1024]{1,0:T(8,128)(2,1)S(1)}, u32[]{:S(2)}, u32[]{:S(2)}) %collective-permute-start.12) | collective-permute-done | bytes 98336 | tf_op jit(solution)/shard_map/ppermute | solution.py:319
  128.2 0.1 fusion
  128.3 0.9 copy.7
  (24 shorter events, 0.3 us)
Async XLA Ops:
  2.7 17.1 %all-to-all-start = ((bf16[8,384,128]{2,1,0:T(8,128)(2,1)}), bf16[8,384,128]{2,1,0:T(8,128)(2,1)S(1)}, u32[]{:S(2)}, u32[]{:S(2)}) async-start(bf16[8,384,128]{2,1,0:T(8,128)(2,1)} %pack.1), calls=%async_computation | async-start | bytes 1572864 | tf_op jit(solution)/shard_map/all_to_all | solution.py:373
  19.8 0.9 copy-start.2
  32.7 10.2 %collective-permute-start = (bf16[4608,256]{1,0:T(8,128)(2,1)}, bf16[4608,256]{1,0:T(8,128)(2,1)S(1)}, u32[]{:S(2)}, u32[]{:S(2)}) collective-permute-start(bf16[4608,256]{1,0:T(8,128)(2,1)} %get-tuple-element.32.send_hbm), channel_id=1, source_target_pairs={{0,8},{8,0},{16,24},{24,16},{32,40},{40,32},{48,56},{56,48},{64,72... | collective-permute-start | bytes 7077896 | tf_op jit(solution)/shard_map/ppermute | solution.py:319
  42.9 1.4 %copy-start = (bf16[4608,256]{1,0:T(8,128)(2,1)}, bf16[4608,256]{1,0:T(8,128)(2,1)S(1)}, u32[]{:S(2)}) copy-start(bf16[4608,256]{1,0:T(8,128)(2,1)S(1)} %collective-permute-done.other_hbm) | copy-start | bytes 7077892
  51.0 21.4 %collective-permute-start.3 = (bf16[384,1024]{1,0:T(8,128)(2,1)}, bf16[384,1024]{1,0:T(8,128)(2,1)S(1)}, u32[]{:S(2)}, u32[]{:S(2)}) collective-permute-start(bf16[384,1024]{1,0:T(8,128)(2,1)} %get-tuple-element.42), channel_id=1, source_target_pairs={{0,48},{8,56},{16,32},{24,40},{32,16},{40,24},{48,0},{56,8},{64,11... | collective-permute-start | bytes 2359304 | tf_op jit(solution)/shard_map/ppermute | solution.py:319
  53.8 19.9 %collective-permute-start.1 = (bf16[384,1024]{1,0:T(8,128)(2,1)}, bf16[384,1024]{1,0:T(8,128)(2,1)S(1)}, u32[]{:S(2)}, u32[]{:S(2)}) collective-permute-start(bf16[384,1024]{1,0:T(8,128)(2,1)} %get-tuple-element.40.after_hbm), channel_id=1, source_target_pairs={{0,16},{8,24},{16,0},{24,8},{32,48},{40,56},{48,32},{56,40},{64,80... | collective-permute-start | bytes 2359304 | tf_op jit(solution)/shard_map/ppermute | solution.py:319
  54.0 61.4 %all-to-all-start.1 = ((bf16[8,384,128]{2,1,0:T(8,128)(2,1)}), bf16[8,384,128]{2,1,0:T(8,128)(2,1)S(1)}, u32[]{:S(2)}, u32[]{:S(2)}) async-start(bf16[8,384,128]{2,1,0:T(8,128)(2,1)} %get-tuple-element.37.after_hbm), calls=%async_computation.1 | async-start | bytes 1572864 | tf_op jit(solution)/shard_map/all_to_all | solution.py:440
  58.8 13.6 %copy-start.4 = (bf16[384,1024]{1,0:T(8,128)(2,1)S(1)}, bf16[384,1024]{1,0:T(8,128)(2,1)}, u32[]{:S(2)}) copy-start(bf16[384,1024]{1,0:T(8,128)(2,1)} %get-tuple-element.41) | copy-start | bytes 2359300
  63.2 21.3 %collective-permute-start.5 = (bf16[384,512]{1,0:T(8,128)(2,1)}, bf16[384,512]{1,0:T(8,128)(2,1)S(1)}, u32[]{:S(2)}, u32[]{:S(2)}) collective-permute-start(bf16[384,512]{1,0:T(8,128)(2,1)} %get-tuple-element.44), channel_id=1, source_target_pairs={{0,64},{8,72},{16,80},{24,88},{32,96},{40,104},{48,112},{56,120},{... | collective-permute-start | bytes 1179656 | tf_op jit(solution)/shard_map/ppermute | solution.py:319
  66.5 23.6 %collective-permute-start.6 = (bf16[384,512]{1,0:T(8,128)(2,1)}, bf16[384,512]{1,0:T(8,128)(2,1)S(1)}, u32[]{:S(2)}, u32[]{:S(2)}) collective-permute-start(bf16[384,512]{1,0:T(8,128)(2,1)} %get-tuple-element.45), channel_id=1, source_target_pairs={{0,192},{8,200},{16,208},{24,216},{32,224},{40,232},{48,240},{56,2... | collective-permute-start | bytes 1179656 | tf_op jit(solution)/shard_map/ppermute | solution.py:319
  72.4 1.3 copy-start.3
  72.8 19.8 %collective-permute-start.4 = (bf16[192,1024]{1,0:T(8,128)(2,1)S(1)}, bf16[192,1024]{1,0:T(8,128)(2,1)S(1)}, u32[]{:S(2)}, u32[]{:S(2)}) collective-permute-start(bf16[192,1024]{1,0:T(8,128)(2,1)S(1)} %slice.122), channel_id=1, source_target_pairs={{0,16},{8,24},{16,0},{24,8},{32,48},{40,56},{48,32},{56,40},{64,80... | collective-permute-start | bytes 1179656 | tf_op jit(solution)/shard_map/ppermute | solution.py:319
  73.7 16.5 %copy-start.6 = (bf16[384,512]{1,0:T(8,128)(2,1)S(1)}, bf16[384,512]{1,0:T(8,128)(2,1)}, u32[]{:S(2)}) copy-start(bf16[384,512]{1,0:T(8,128)(2,1)} %get-tuple-element.47) | copy-start | bytes 1179652
  74.0 16.3 %copy-start.5 = (bf16[384,512]{1,0:T(8,128)(2,1)S(1)}, bf16[384,512]{1,0:T(8,128)(2,1)}, u32[]{:S(2)}) copy-start(bf16[384,512]{1,0:T(8,128)(2,1)} %get-tuple-element.43) | copy-start | bytes 1179652
  74.0 18.6 %collective-permute-start.2 = (bf16[192,1024]{1,0:T(8,128)(2,1)S(1)}, bf16[192,1024]{1,0:T(8,128)(2,1)S(1)}, u32[]{:S(2)}, u32[]{:S(2)}) collective-permute-start(bf16[192,1024]{1,0:T(8,128)(2,1)S(1)} %slice.121), channel_id=1, source_target_pairs={{0,48},{8,56},{16,32},{24,40},{32,16},{40,24},{48,0},{56,8},{64,11... | collective-permute-start | bytes 1179656 | tf_op jit(solution)/shard_map/ppermute | solution.py:319
  90.4 15.7 %collective-permute-start.9 = (bf16[192,512]{1,0:T(8,128)(2,1)S(1)}, bf16[192,512]{1,0:T(8,128)(2,1)S(1)}, u32[]{:S(2)}, u32[]{:S(2)}) collective-permute-start(bf16[192,512]{1,0:T(8,128)(2,1)S(1)} %slice.123), channel_id=1, source_target_pairs={{0,192},{8,200},{16,208},{24,216},{32,224},{40,232},{48,240},{56,2... | collective-permute-start | bytes 589832 | tf_op jit(solution)/shard_map/ppermute | solution.py:319
  91.6 14.5 %collective-permute-start.10 = (bf16[192,512]{1,0:T(8,128)(2,1)S(1)}, bf16[192,512]{1,0:T(8,128)(2,1)S(1)}, u32[]{:S(2)}, u32[]{:S(2)}) collective-permute-start(bf16[192,512]{1,0:T(8,128)(2,1)S(1)} %slice.124), channel_id=1, source_target_pairs={{0,64},{8,72},{16,80},{24,88},{32,96},{40,104},{48,112},{56,120},{... | collective-permute-start | bytes 589832 | tf_op jit(solution)/shard_map/ppermute | solution.py:319
  92.9 17.6 %collective-permute-start.7 = (bf16[96,1024]{1,0:T(8,128)(2,1)S(1)}, bf16[96,1024]{1,0:T(8,128)(2,1)S(1)}, u32[]{:S(2)}, u32[]{:S(2)}) collective-permute-start(bf16[96,1024]{1,0:T(8,128)(2,1)S(1)} %slice.126), channel_id=1, source_target_pairs={{0,64},{8,72},{16,80},{24,88},{32,96},{40,104},{48,112},{56,120},{... | collective-permute-start | bytes 589832 | tf_op jit(solution)/shard_map/ppermute | solution.py:319
  95.2 15.9 %collective-permute-start.8 = (bf16[96,1024]{1,0:T(8,128)(2,1)S(1)}, bf16[96,1024]{1,0:T(8,128)(2,1)S(1)}, u32[]{:S(2)}, u32[]{:S(2)}) collective-permute-start(bf16[96,1024]{1,0:T(8,128)(2,1)S(1)} %slice.128), channel_id=1, source_target_pairs={{0,192},{8,200},{16,208},{24,216},{32,224},{40,232},{48,240},{56,2... | collective-permute-start | bytes 589832 | tf_op jit(solution)/shard_map/ppermute | solution.py:319
  106.2 5.9 %collective-permute-start.14 = (bf16[96,512]{1,0:T(8,128)(2,1)S(1)}, bf16[96,512]{1,0:T(8,128)(2,1)S(1)}, u32[]{:S(2)}, u32[]{:S(2)}) collective-permute-start(bf16[96,512]{1,0:T(8,128)(2,1)S(1)} %slice.132), channel_id=1, source_target_pairs={{0,48},{8,56},{16,32},{24,40},{32,16},{40,24},{48,0},{56,8},{64,11... | collective-permute-start | bytes 294920 | tf_op jit(solution)/shard_map/ppermute | solution.py:319
  107.3 4.8 %collective-permute-start.13 = (bf16[96,512]{1,0:T(8,128)(2,1)S(1)}, bf16[96,512]{1,0:T(8,128)(2,1)S(1)}, u32[]{:S(2)}, u32[]{:S(2)}) collective-permute-start(bf16[96,512]{1,0:T(8,128)(2,1)S(1)} %slice.130), channel_id=1, source_target_pairs={{0,16},{8,24},{16,0},{24,8},{32,48},{40,56},{48,32},{56,40},{64,80... | collective-permute-start | bytes 294920 | tf_op jit(solution)/shard_map/ppermute | solution.py:319
  112.2 10.6 %collective-permute-start.16 = (bf16[48,512]{1,0:T(8,128)(2,1)S(1)}, bf16[48,512]{1,0:T(8,128)(2,1)S(1)}, u32[]{:S(2)}, u32[]{:S(2)}) collective-permute-start(bf16[48,512]{1,0:T(8,128)(2,1)S(1)} %slice.140), channel_id=1, source_target_pairs={{0,16},{8,24},{16,0},{24,8},{32,48},{40,56},{48,32},{56,40},{64,80... | collective-permute-start | bytes 147464 | tf_op jit(solution)/shard_map/ppermute | solution.py:319
  113.1 9.7 %collective-permute-start.15 = (bf16[48,512]{1,0:T(8,128)(2,1)S(1)}, bf16[48,512]{1,0:T(8,128)(2,1)S(1)}, u32[]{:S(2)}, u32[]{:S(2)}) collective-permute-start(bf16[48,512]{1,0:T(8,128)(2,1)S(1)} %slice.138), channel_id=1, source_target_pairs={{0,48},{8,56},{16,32},{24,40},{32,16},{40,24},{48,0},{56,8},{64,11... | collective-permute-start | bytes 147464 | tf_op jit(solution)/shard_map/ppermute | solution.py:319
  115.5 0.9 copy-start.1
  119.2 6.7 %collective-permute-start.11 = (bf16[48,1024]{1,0:T(8,128)(2,1)S(1)}, bf16[48,1024]{1,0:T(8,128)(2,1)S(1)}, u32[]{:S(2)}, u32[]{:S(2)}) collective-permute-start(bf16[48,1024]{1,0:T(8,128)(2,1)S(1)} %slice.134), channel_id=1, source_target_pairs={{0,192},{8,200},{16,208},{24,216},{32,224},{40,232},{48,240},{56,2... | collective-permute-start | bytes 294920 | tf_op jit(solution)/shard_map/ppermute | solution.py:319
  122.7 5.5 %collective-permute-start.12 = (bf16[48,1024]{1,0:T(8,128)(2,1)S(1)}, bf16[48,1024]{1,0:T(8,128)(2,1)S(1)}, u32[]{:S(2)}, u32[]{:S(2)}) collective-permute-start(bf16[48,1024]{1,0:T(8,128)(2,1)S(1)} %slice.136), channel_id=1, source_target_pairs={{0,64},{8,72},{16,80},{24,88},{32,96},{40,104},{48,112},{56,120},{... | collective-permute-start | bytes 294920 | tf_op jit(solution)/shard_map/ppermute | solution.py:319

commit v4 on v2

--- a/solution.py
+++ b/solution.py
@@ -214,26 +214,39 @@
 
 KEEP_FIRST = ((0, 3, 1, 2), (0, 1, 3, 2))
 PARTNERS = ((1, 3), (3, 1))
-
-
-def grad_kernel(x_first, at, block, own_ref, recv_ref, right_ref, right_recv_ref, after_ref, *outs):
-    del after_ref
-    rows = own_ref.shape[0] // 2
+SCALES = (2, 2, 8, 8)
+
+
+def grad_kernel(at, block, own_hbm, other_hbm, right_hbm, right_other_hbm, after_hbm, *refs):
+    del after_hbm
+    outs_hbm, outs = refs[:4], refs[4:8]
+    own, other, right, right_other, in_sem, write_sem = refs[8:]
     wide = 256
     per = outs[0].shape[1] // wide
-    for k in range(2 * per):
-        flavour, col = divmod(k, per)
+    sources = ((own_hbm, at, own), (other_hbm, at, other), (right_hbm, block, right), (right_other_hbm, block, right_other))
+    reads, writes = [], []
+    for n, (source, begin, target) in enumerate(sources):
+        reads.append(pltpu.make_async_copy(source.at[pl.ds(begin, target.shape[0])], target, in_sem.at[n]))
+        reads[-1].start()
+    for copy in reads:
+        copy.wait()
+    for flavour in range(2):
         keep, send = outs[2 * flavour], outs[2 * flavour + 1]
         order = KEEP_FIRST[flavour]
-        place = slice(block + wide * k, block + wide * k + wide)
-        g = nn(own_ref[at : at + rows, :], right_ref[place, :])
-        g = (g + nn(recv_ref[at : at + rows, :], right_recv_ref[place, :])).astype(BF16)
-        for b in range(16):
-            rz, rx = order.index(b // 4), order.index(b % 4)
-            to = rx * 4 + rz if x_first else rz * 4 + rx
-            target = keep if to < 8 else send
-            to = (to % 8) * 48
-            target[to : to + 48, wide * col : wide * col + wide] = g[48 * b : 48 * b + 48]
+        for col in range(per):
+            k = flavour * per + col
+            place, cols = slice(wide * k, wide * k + wide), slice(wide * col, wide * col + wide)
+            g = (nn(own[...], right[place, :]) + nn(other[...], right_other[place, :])).astype(BF16)
+            for b in range(16):
+                to = order.index(b % 4) * 4 + order.index(b // 4)
+                target = keep if to < 8 else send
+                to = (to % 8) * 48
+                target[to : to + 48, cols] = g[48 * b : 48 * b + 48]
+        for n in (2 * flavour, 2 * flavour + 1):
+            writes.append(pltpu.make_async_copy(outs[n], outs_hbm[n], write_sem.at[n]))
+            writes[-1].start()
+    for copy in writes:
+        copy.wait()
 
 
 def params():
@@ -257,22 +270,27 @@
     return lax.ppermute(values, "dp", [(i, i ^ distance) for i in range(32)])
 
 
-def gradients(x_first, at, block, columns, own, recv, right, right_recv, after, name):
+def gradients(at, block, columns, own, other, right, right_other, after, name):
     piece = shape((384, columns // 2))
-    moved = (own.size + recv.size + 2 * right.size + 768 * columns) * 2
+    rows, samples = own.shape[0] // 2, own.shape[1]
+    moved = (2 * rows * samples + 2 * samples * columns + rows * columns) * 2
     return pl.pallas_call(
-        functools.partial(grad_kernel, x_first, at, block),
+        functools.partial(grad_kernel, at, block),
         out_shape=[piece] * 4,
-        in_specs=[VMEM] * 4 + [ANY],
-        out_specs=[VMEM] * 4,
+        in_specs=[ANY] * 5,
+        out_specs=[ANY] * 4,
+        scratch_shapes=[pltpu.VMEM(piece.shape, BF16)] * 4
+        + [pltpu.VMEM((rows, samples), BF16)] * 2
+        + [pltpu.VMEM((columns, samples), BF16)] * 2
+        + [pltpu.SemaphoreType.DMA((4,))] * 2,
         compiler_params=params(),
-        cost_estimate=cost(2 * 768 * 512 * columns, moved),
+        cost_estimate=cost(2 * rows * 2 * samples * columns, moved),
         name=name,
-    )(own, recv, right, right_recv, after)
-
-
-def reduce_send(scales, step, send):
-    return [swap(send[f], PARTNERS[f][step % 2] * scales[step // 2]) for f in range(2)]
+    )(own, other, right, right_other, after)
+
+
+def reduce_send(step, send):
+    return [swap(send[f], PARTNERS[f][step % 2] * SCALES[step]) for f in range(2)]
 
 
 def reduce_add(step, keep, got):
@@ -330,11 +348,12 @@
     )(index, x, recv, cotangent, flat_in, weight_out)
     other, inner_other = swap(send, 1), swap(inner, 1)
 
-    up = gradients(True, width // 2, 0, 2 * ff, own, other, inner, inner_other, index, "in_grads")
-    up_got = reduce_send((2, 8), 0, up[1::2])
-    down = gradients(False, 0, width, ff, own, other, send, other, up[1], "down_grads")
-    down_got = reduce_send((8, 2), 0, down[1::2])
-    up_keep, down_keep = up[0::2], down[0::2]
+    half = width // 2
+    down = gradients(0, width, ff, own, other, send, other, inner, "down_grads")
+    gate = gradients(half, 0, ff, own, other, inner, inner_other, down[1], "gate_grads")
+    up = gradients(half, ff, ff, own, other, inner, inner_other, gate[1], "up_grads")
+    kept = [grads[0::2] for grads in (down, gate, up)]
+    got = [reduce_send(0, grads[1::2]) for grads in (down, gate, up)]
 
     pre_grad, back = pl.pallas_call(
         input_kernel,
@@ -350,29 +369,28 @@
         compiler_params=params(),
         cost_estimate=cost(4 * samples * width * ff, 14e6),
         name="input",
-    )(inner, flat_in, x, recv, out_grad16, down[1])
+    )(inner, flat_in, x, recv, out_grad16, up[1])
     returned = lax.all_to_all(back, "token", split_axis=0, concat_axis=0, tiled=True)
 
-    for step in range(4):
-        if step == 2:
-            input_grad = pl.pallas_call(
-                final_kernel, out_shape=flat, in_specs=[VMEM] * 2, out_specs=VMEM,
-                compiler_params=params(), cost_estimate=cost(samples * width, 8 * samples * width), name="final",
-            )(pre_grad, returned)
-        up_keep, up_send = reduce_add(step, up_keep, up_got)
+    input_grad = pl.pallas_call(
+        final_kernel, out_shape=flat, in_specs=[VMEM] * 2, out_specs=VMEM,
+        compiler_params=params(), cost_estimate=cost(samples * width, 8 * samples * width), name="final",
+    )(pre_grad, returned)
+
+    previous = None
+    for which, step in ((0, 0), (1, 0), (0, 1), (2, 0), (1, 1), (0, 2), (2, 1), (1, 2), (0, 3), (2, 2), (1, 3), (2, 3)):
+        arrived = got[which]
+        if previous is not None:
+            arrived, previous = lax.optimization_barrier((arrived, previous))
+        if (which, step) == (0, 3):
+            arrived, input_grad = lax.optimization_barrier((arrived, input_grad))
+        kept[which], sent = reduce_add(step, kept[which], arrived)
+        previous = sent or kept[which]
         if step < 3:
-            up_got = reduce_send((2, 8), step + 1, up_send)
-        down_got, up_send = lax.optimization_barrier((down_got, up_send))
-        down_keep, down_send = reduce_add(step, down_keep, down_got)
-        if step < 3:
-            down_got = reduce_send((8, 2), step + 1, down_send)
-            up_got, down_send = lax.optimization_barrier((up_got, down_send))
-
-    return (
-        input_grad[:, None, :],
-        jnp.stack(up_keep, axis=1)[None],
-        jnp.concatenate(down_keep, axis=1)[None],
-    )
+            got[which] = reduce_send(step + 1, sent)
+
+    down, gate, up = (jnp.concatenate(k, axis=1) for k in kept)
+    return (input_grad[:, None, :], jnp.stack([gate, up], axis=1)[None], down[None])
 
 
 def solution(mesh):

time: 129 us -> 125 us (0.969)
  waiting for transfers between devices: 41.6 us -> 21.1 us
  starting transfers between devices: 37.1 us -> 51.5 us
    ppermute x18 -> x26, waiting for transfers between devices: 38.8 us -> 18.4 us  [swap(): return lax.ppermute(values, 'dp', [(i, i ^ distance) for i in range(32)])]
    ppermute x18 -> x26, starting transfers between devices: 25.9 us -> 40.2 us  [swap(): return lax.ppermute(values, 'dp', [(i, i ^ distance) for i in range(32)])]
    pallas_call x2 -> x3, Pallas kernels: 9.24 us -> 10.2 us  [gradients(): pl.pallas_call(functools.partial(grad_kernel, at, block), out_shape=[piec...]
    unnamed x18 -> x20, local copies, waits for them, and re-layouts: 12.1 us -> 12.8 us
  transfers between devices with their start and end apart: 20 -> 28, of which waited for: 8 -> 6; matrix products, arithmetic and copies ran while one was open for 8% -> 9% of each run, Pallas kernels for 13% -> 18%
where the time goes in v4:
time: 125 us
  starting transfers between devices  51.5 us (41%)
  Pallas kernels  35.1 us (28%)
  waiting for transfers between devices  21.1 us (17%)
  local copies, waits for them, and re-layouts  13 us (10%)
  other arithmetic  2.94 us (2%)
    ppermute x26, starting transfers between devices, swap(): return lax.ppermute(values, 'dp', [(i, i ^ distance) for i in range(32)])  40.2 us
    ppermute x26, waiting for transfers between devices, swap(): return lax.ppermute(values, 'dp', [(i, i ^ distance) for i in range(32)])  18.4 us
    unnamed x20, local copies, waits for them, and re-layouts  12.8 us
    pallas_call x1, Pallas kernels, local(): pl.pallas_call(main_kernel, out_shape=[shape((width, samples)), shape((wi...  10.7 us
    pallas_call x3, Pallas kernels, gradients(): pl.pallas_call(functools.partial(grad_kernel, at, block), out_shape=[piec...  10.2 us
    pallas_call x1, Pallas kernels, local(): pl.pallas_call(input_kernel, out_shape=[shape((samples, width), F32), pac...  9.25 us
    all_to_all x1, starting transfers between devices, local(): lax.all_to_all(packed, 'token', split_axis=0, concat_axis=0, tiled=True)  6.27 us
    all_to_all x1, starting transfers between devices, local(): lax.all_to_all(back, 'token', split_axis=0, concat_axis=0, tiled=True)  4.95 us
  transfers between devices with their start and end apart: 28, of which 6 were waited for; matrix products, arithmetic and copies ran while one was open for 9% of the time, Pallas kernels for 18%

profile of v4, /device:TPU:8, one launch (start us, length us, event | category | flops | bytes accessed | tf_op | source)
XLA Modules:
  0.0 124.7 jit_solution(1450600550112924120)
XLA Ops:
  0.6 2.3 %pack.1 = bf16[8,384,128]{2,1,0:T(8,128)(2,1)} custom-call(bf16[256,1536]{1,0:T(8,128)(2,1)} %bitcast.19), custom_call_target="tpu_custom_call" | custom-call | flops 393216 | bytes 1572864 | tf_op jit(solution)/shard_map/pack/pallas_call | solution.py:314
  2.9 6.3 %all-to-all-start = ((bf16[8,384,128]{2,1,0:T(8,128)(2,1)}), bf16[8,384,128]{2,1,0:T(8,128)(2,1)S(1)}, u32[]{:S(2)}, u32[]{:S(2)}) async-start(bf16[8,384,128]{2,1,0:T(8,128)(2,1)} %pack.1), calls=%async_computation | async-start | bytes 1572864 | tf_op jit(solution)/shard_map/all_to_all | solution.py:318
  9.2 8.1 %copy.8 = bf16[192,8,2,1024]{3,1,2,0:T(8,128)(2,1)} copy(bf16[192,8,2,1024]{3,2,1,0:T(2,128)(2,1)} %bitcast.18) | data formatting | bytes 12582912
  17.2 2.8 %all-to-all-done.recv_ref = bf16[8,384,128]{2,1,0:T(8,128)(2,1)S(1)} async-done(((bf16[8,384,128]{2,1,0:T(8,128)(2,1)}), bf16[8,384,128]{2,1,0:T(8,128)(2,1)S(1)}, u32[]{:S(2)}, u32[]{:S(2)}) %all-to-all-start) | async-done | bytes 786464 | tf_op jit(solution)/shard_map/all_to_all | solution.py:318
  20.0 0.9 copy-done.2
  20.9 10.7 %main.1 = (bf16[1536,256]{1,0:T(8,128)(2,1)}, bf16[2560,256]{1,0:T(8,128)(2,1)}, bf16[2048,256]{1,0:T(8,128)(2,1)}, bf16[256,1536]{1,0:T(8,128)(2,1)}) custom-call(s32[1]{0:T(128)} %bitcast.index_ref, bf16[256,1536]{1,0:T(8,128)(2,1)} %bitcast.20, bf16[8,384,128]{2,1,0:T(8,128)(2,1)} %copy-done.2, bf16[256,1536]{1,0:T(8,128)(2,1)} %bitcast.24, ...), custom_call_target="tpu_custom_call" | custom-call | flops 3221225472 | bytes 18000000 | tf_op jit(solution)/shard_map/main/pallas_call | solution.py:321
  31.5 0.1 collective-permute-start
  31.6 0.5 collective-permute-start.5
  32.1 2.7 %collective-permute-done.other_hbm.right_other_hbm = bf16[2560,256]{1,0:T(8,128)(2,1)S(1)} collective-permute-done((bf16[2560,256]{1,0:T(8,128)(2,1)}, bf16[2560,256]{1,0:T(8,128)(2,1)S(1)}, u32[]{:S(2)}, u32[]{:S(2)}) %collective-permute-start) | collective-permute-done | bytes 1310752 | tf_op jit(solution)/shard_map/ppermute | solution.py:270
  34.9 1.1 copy-done
  35.9 3.4 %down_grads.1 = (bf16[384,512]{1,0:T(8,128)(2,1)}, bf16[384,512]{1,0:T(8,128)(2,1)}, bf16[384,512]{1,0:T(8,128)(2,1)}, bf16[384,512]{1,0:T(8,128)(2,1)}) custom-call(bf16[1536,256]{1,0:T(8,128)(2,1)} %get-tuple-element.46.own_hbm, bf16[2560,256]{1,0:T(8,128)(2,1)} %copy-done, bf16[2560,256]{1,0:T(8,128)(2,1)} %get-tuple-element.47.right_hbm, ...), custom_call_target="tpu_custom_call" | custom-call | flops 805306368 | bytes 3407872 | tf_op jit(solution)/shard_map/down_grads/pallas_call | solution.py:277
  39.4 1.6 %collective-permute-start.1 = (bf16[384,512]{1,0:T(8,128)(2,1)}, bf16[384,512]{1,0:T(8,128)(2,1)}, u32[]{:S(2)}, u32[]{:S(2)}) collective-permute-start(bf16[384,512]{1,0:T(8,128)(2,1)} %get-tuple-element.50.after_hbm), channel_id=1, source_target_pairs={{0,16},{8,24},{16,0},{24,8},{32,48},{40,56},{48,32},{56,40},{64,80... | collective-permute-start | bytes 1179656 | tf_op jit(solution)/shard_map/ppermute | solution.py:270
  41.0 2.1 %collective-permute-start.3 = (bf16[384,512]{1,0:T(8,128)(2,1)}, bf16[384,512]{1,0:T(8,128)(2,1)S(1)}, u32[]{:S(2)}, u32[]{:S(2)}) collective-permute-start(bf16[384,512]{1,0:T(8,128)(2,1)} %get-tuple-element.52), channel_id=1, source_target_pairs={{0,48},{8,56},{16,32},{24,40},{32,16},{40,24},{48,0},{56,8},{64,11... | collective-permute-start | bytes 1179656 | tf_op jit(solution)/shard_map/ppermute | solution.py:270
  43.1 0.0 collective-permute-done.5.right_other_hbm
  43.1 1.0 copy-done.1
  44.0 3.3 %gate_grads.1 = (bf16[384,512]{1,0:T(8,128)(2,1)}, bf16[384,512]{1,0:T(8,128)(2,1)}, bf16[384,512]{1,0:T(8,128)(2,1)}, bf16[384,512]{1,0:T(8,128)(2,1)}) custom-call(bf16[1536,256]{1,0:T(8,128)(2,1)} %get-tuple-element.46.own_hbm, bf16[2560,256]{1,0:T(8,128)(2,1)} %copy-done, bf16[2048,256]{1,0:T(8,128)(2,1)} %get-tuple-element.48.after_hbm.right_hbm.inner_ref, ...), custom_call_target="tpu_custom_call" | custom-call | flops 805306368 | bytes 3407872 | tf_op jit(solution)/shard_map/gate_grads/pallas_call | solution.py:277
  47.4 0.7 collective-permute-start.6
  48.1 0.7 collective-permute-start.7
  48.7 3.4 %up_grads.1 = (bf16[384,512]{1,0:T(8,128)(2,1)}, bf16[384,512]{1,0:T(8,128)(2,1)}, bf16[384,512]{1,0:T(8,128)(2,1)}, bf16[384,512]{1,0:T(8,128)(2,1)}) custom-call(bf16[1536,256]{1,0:T(8,128)(2,1)} %get-tuple-element.46.own_hbm, bf16[2560,256]{1,0:T(8,128)(2,1)} %copy-done, bf16[2048,256]{1,0:T(8,128)(2,1)} %get-tuple-element.48.after_hbm.right_hbm.inner_ref, ...), custom_call_target="tpu_custom_call" | custom-call | flops 805306368 | bytes 3407872 | tf_op jit(solution)/shard_map/up_grads/pallas_call | solution.py:277
  52.1 1.4 %collective-permute-start.12 = (bf16[384,512]{1,0:T(8,128)(2,1)}, bf16[384,512]{1,0:T(8,128)(2,1)S(1)}, u32[]{:S(2)}, u32[]{:S(2)}) collective-permute-start(bf16[384,512]{1,0:T(8,128)(2,1)} %get-tuple-element.62.after_ref), channel_id=1, source_target_pairs={{0,16},{8,24},{16,0},{24,8},{32,48},{40,56},{48,32},{56,40},{64,80... | collective-permute-start | bytes 1179656 | tf_op jit(solution)/shard_map/ppermute | solution.py:270
  53.5 9.3 %input.1 = (f32[256,1536]{1,0:T(8,128)}, bf16[8,384,128]{2,1,0:T(8,128)(2,1)}) custom-call(bf16[2048,256]{1,0:T(8,128)(2,1)} %get-tuple-element.48.after_hbm.right_hbm.inner_ref, bf16[1536,2048]{1,0:T(8,128)(2,1)} %bitcast.17, bf16[256,1536]{1,0:T(8,128)(2,1)} %bitcast.21, bf16[8,384,128]{2,1,0:T(8,128)(2,1)} %copy-done.2, ...), custom_call_target="tpu_custom_call" | custom-call | flops 1610612736 | bytes 14000000 | tf_op jit(solution)/shard_map/input/pallas_call | solution.py:358
  62.8 4.9 %all-to-all-start.1 = ((bf16[8,384,128]{2,1,0:T(8,128)(2,1)}), bf16[8,384,128]{2,1,0:T(8,128)(2,1)S(1)}, u32[]{:S(2)}, u32[]{:S(2)}) async-start(bf16[8,384,128]{2,1,0:T(8,128)(2,1)} %get-tuple-element.79), calls=%async_computation.1 | async-start | bytes 1572864 | tf_op jit(solution)/shard_map/all_to_all | solution.py:373
  67.8 0.0 collective-permute-done.1
  67.8 2.1 %collective-permute-start.13 = (bf16[384,512]{1,0:T(8,128)(2,1)}, bf16[384,512]{1,0:T(8,128)(2,1)S(1)}, u32[]{:S(2)}, u32[]{:S(2)}) collective-permute-start(bf16[384,512]{1,0:T(8,128)(2,1)} %get-tuple-element.63), channel_id=1, source_target_pairs={{0,48},{8,56},{16,32},{24,40},{32,16},{40,24},{48,0},{56,8},{64,11... | collective-permute-start | bytes 1179656 | tf_op jit(solution)/shard_map/ppermute | solution.py:270
  69.9 1.2 add_convert_fusion.5
  71.1 0.0 collective-permute-done.3
  71.1 1.2 collective-permute-start.2
  72.3 0.1 add_convert_fusion.4
  72.5 0.0 collective-permute-done.6
  72.5 0.1 collective-permute-start.4
  72.6 0.0 collective-permute-done.7
  72.6 0.1 add_convert_fusion.3
  72.7 0.1 add_convert_fusion.2
  72.9 2.2 %collective-permute-start.10 = (bf16[192,512]{1,0:T(8,128)(2,1)S(1)}, bf16[192,512]{1,0:T(8,128)(2,1)S(1)}, u32[]{:S(2)}, u32[]{:S(2)}) collective-permute-start(bf16[192,512]{1,0:T(8,128)(2,1)S(1)} %slice.183), channel_id=1, source_target_pairs={{0,48},{8,56},{16,32},{24,40},{32,16},{40,24},{48,0},{56,8},{64,11... | collective-permute-start | bytes 589832 | tf_op jit(solution)/shard_map/ppermute | solution.py:270
  75.0 9.8 %collective-permute-done.2 = bf16[192,512]{1,0:T(8,128)(2,1)S(1)} collective-permute-done((bf16[192,512]{1,0:T(8,128)(2,1)S(1)}, bf16[192,512]{1,0:T(8,128)(2,1)S(1)}, u32[]{:S(2)}, u32[]{:S(2)}) %collective-permute-start.2) | collective-permute-done | bytes 196640 | tf_op jit(solution)/shard_map/ppermute | solution.py:270
  84.8 0.1 add_convert_fusion.11
  84.9 3.4 %collective-permute-start.8 = (bf16[96,512]{1,0:T(8,128)(2,1)S(1)}, bf16[96,512]{1,0:T(8,128)(2,1)S(1)}, u32[]{:S(2)}, u32[]{:S(2)}) collective-permute-start(bf16[96,512]{1,0:T(8,128)(2,1)S(1)} %slice.186), channel_id=1, source_target_pairs={{0,64},{8,72},{16,80},{24,88},{32,96},{40,104},{48,112},{56,120},{... | collective-permute-start | bytes 294920 | tf_op jit(solution)/shard_map/ppermute | solution.py:270
  88.2 0.1 add_convert_fusion.10
  88.3 3.7 %collective-permute-start.9 = (bf16[96,512]{1,0:T(8,128)(2,1)S(1)}, bf16[96,512]{1,0:T(8,128)(2,1)S(1)}, u32[]{:S(2)}, u32[]{:S(2)}) collective-permute-start(bf16[96,512]{1,0:T(8,128)(2,1)S(1)} %slice.188), channel_id=1, source_target_pairs={{0,192},{8,200},{16,208},{24,216},{32,224},{40,232},{48,240},{56,2... | collective-permute-start | bytes 294920 | tf_op jit(solution)/shard_map/ppermute | solution.py:270
  92.0 0.1 add_convert_fusion.1
  92.1 0.1 add_convert_fusion
  92.3 2.2 %collective-permute-start.18 = (bf16[192,512]{1,0:T(8,128)(2,1)S(1)}, bf16[192,512]{1,0:T(8,128)(2,1)S(1)}, u32[]{:S(2)}, u32[]{:S(2)}) collective-permute-start(bf16[192,512]{1,0:T(8,128)(2,1)S(1)} %slice.190), channel_id=1, source_target_pairs={{0,48},{8,56},{16,32},{24,40},{32,16},{40,24},{48,0},{56,8},{64,11... | collective-permute-start | bytes 589832 | tf_op jit(solution)/shard_map/ppermute | solution.py:270
  94.4 1.4 %collective-permute-start.19 = (bf16[192,512]{1,0:T(8,128)(2,1)S(1)}, bf16[192,512]{1,0:T(8,128)(2,1)S(1)}, u32[]{:S(2)}, u32[]{:S(2)}) collective-permute-start(bf16[192,512]{1,0:T(8,128)(2,1)S(1)} %slice.191), channel_id=1, source_target_pairs={{0,16},{8,24},{16,0},{24,8},{32,48},{40,56},{48,32},{56,40},{64,80... | collective-permute-start | bytes 589832 | tf_op jit(solution)/shard_map/ppermute | solution.py:270
  95.9 0.1 add_convert_fusion.9
  95.9 0.1 add_convert_fusion.8
  96.0 1.6 %collective-permute-start.16 = (bf16[96,512]{1,0:T(8,128)(2,1)S(1)}, bf16[96,512]{1,0:T(8,128)(2,1)S(1)}, u32[]{:S(2)}, u32[]{:S(2)}) collective-permute-start(bf16[96,512]{1,0:T(8,128)(2,1)S(1)} %slice.192), channel_id=1, source_target_pairs={{0,64},{8,72},{16,80},{24,88},{32,96},{40,104},{48,112},{56,120},{... | collective-permute-start | bytes 294920 | tf_op jit(solution)/shard_map/ppermute | solution.py:270
  97.6 0.6 collective-permute-start.17
  98.2 3.8 %collective-permute-start.14 = (bf16[48,512]{1,0:T(8,128)(2,1)S(1)}, bf16[48,512]{1,0:T(8,128)(2,1)S(1)}, u32[]{:S(2)}, u32[]{:S(2)}) collective-permute-start(bf16[48,512]{1,0:T(8,128)(2,1)S(1)} %slice.195), channel_id=1, source_target_pairs={{0,192},{8,200},{16,208},{24,216},{32,224},{40,232},{48,240},{56,2... | collective-permute-start | bytes 147464 | tf_op jit(solution)/shard_map/ppermute | solution.py:270
  102.1 1.4 %collective-permute-start.15 = (bf16[48,512]{1,0:T(8,128)(2,1)S(1)}, bf16[48,512]{1,0:T(8,128)(2,1)S(1)}, u32[]{:S(2)}, u32[]{:S(2)}) collective-permute-start(bf16[48,512]{1,0:T(8,128)(2,1)S(1)} %slice.197), channel_id=1, source_target_pairs={{0,64},{8,72},{16,80},{24,88},{32,96},{40,104},{48,112},{56,120},{... | collective-permute-start | bytes 147464 | tf_op jit(solution)/shard_map/ppermute | solution.py:270
  103.4 0.1 add_convert_fusion.7
  103.5 0.1 add_convert_fusion.6
  103.6 1.7 %collective-permute-start.22 = (bf16[96,512]{1,0:T(8,128)(2,1)S(1)}, bf16[96,512]{1,0:T(8,128)(2,1)S(1)}, u32[]{:S(2)}, u32[]{:S(2)}) collective-permute-start(bf16[96,512]{1,0:T(8,128)(2,1)S(1)} %slice.200), channel_id=1, source_target_pairs={{0,64},{8,72},{16,80},{24,88},{32,96},{40,104},{48,112},{56,120},{... | collective-permute-start | bytes 294920 | tf_op jit(solution)/shard_map/ppermute | solution.py:270
  105.3 0.4 collective-permute-start.23
  105.7 0.6 collective-permute-done.17
  106.5 3.2 %collective-permute-start.20 = (bf16[48,512]{1,0:T(8,128)(2,1)S(1)}, bf16[48,512]{1,0:T(8,128)(2,1)S(1)}, u32[]{:S(2)}, u32[]{:S(2)}) collective-permute-start(bf16[48,512]{1,0:T(8,128)(2,1)S(1)} %slice.203), channel_id=1, source_target_pairs={{0,192},{8,200},{16,208},{24,216},{32,224},{40,232},{48,240},{56,2... | collective-permute-start | bytes 147464 | tf_op jit(solution)/shard_map/ppermute | solution.py:270
  109.6 1.3 %collective-permute-start.21 = (bf16[48,512]{1,0:T(8,128)(2,1)S(1)}, bf16[48,512]{1,0:T(8,128)(2,1)S(1)}, u32[]{:S(2)}, u32[]{:S(2)}) collective-permute-start(bf16[48,512]{1,0:T(8,128)(2,1)S(1)} %slice.205), channel_id=1, source_target_pairs={{0,64},{8,72},{16,80},{24,88},{32,96},{40,104},{48,112},{56,120},{... | collective-permute-start | bytes 147464 | tf_op jit(solution)/shard_map/ppermute | solution.py:270
  110.9 0.9 copy-done.3
  111.8 2.8 %final.1 = bf16[256,1536]{1,0:T(8,128)(2,1)} custom-call(f32[256,1536]{1,0:T(8,128)} %get-tuple-element.78.pre_ref, bf16[8,384,128]{2,1,0:T(8,128)(2,1)} %copy-done.3), custom_call_target="tpu_custom_call" | custom-call | flops 393216 | bytes 3145728 | tf_op jit(solution)/shard_map/final/pallas_call | solution.py:375
  114.6 0.6 maximum_bitcast_fusion.3
  115.3 3.0 %collective-permute-start.24 = (bf16[48,512]{1,0:T(8,128)(2,1)S(1)}, bf16[48,512]{1,0:T(8,128)(2,1)S(1)}, u32[]{:S(2)}, u32[]{:S(2)}) collective-permute-start(bf16[48,512]{1,0:T(8,128)(2,1)S(1)} %slice.210), channel_id=1, source_target_pairs={{0,192},{8,200},{16,208},{24,216},{32,224},{40,232},{48,240},{56,2... | collective-permute-start | bytes 147464 | tf_op jit(solution)/shard_map/ppermute | solution.py:270
  118.4 0.1 collective-permute-start.25
  118.6 3.1 %collective-permute-done.24 = bf16[48,512]{1,0:T(8,128)(2,1)S(1)} collective-permute-done((bf16[48,512]{1,0:T(8,128)(2,1)S(1)}, bf16[48,512]{1,0:T(8,128)(2,1)S(1)}, u32[]{:S(2)}, u32[]{:S(2)}) %collective-permute-start.24) | collective-permute-done | bytes 49184 | tf_op jit(solution)/shard_map/ppermute | solution.py:270
  121.7 2.1 %collective-permute-done.25 = bf16[48,512]{1,0:T(8,128)(2,1)S(1)} collective-permute-done((bf16[48,512]{1,0:T(8,128)(2,1)S(1)}, bf16[48,512]{1,0:T(8,128)(2,1)S(1)}, u32[]{:S(2)}, u32[]{:S(2)}) %collective-permute-start.25) | collective-permute-done | bytes 49184 | tf_op jit(solution)/shard_map/ppermute | solution.py:270
  123.8 0.9 copy.7
  (64 shorter events, 0.5 us)
Async XLA Ops:
  2.9 17.1 %all-to-all-start = ((bf16[8,384,128]{2,1,0:T(8,128)(2,1)}), bf16[8,384,128]{2,1,0:T(8,128)(2,1)S(1)}, u32[]{:S(2)}, u32[]{:S(2)}) async-start(bf16[8,384,128]{2,1,0:T(8,128)(2,1)} %pack.1), calls=%async_computation | async-start | bytes 1572864 | tf_op jit(solution)/shard_map/all_to_all | solution.py:318
  20.0 0.9 copy-start.2
  31.5 3.3 %collective-permute-start = (bf16[2560,256]{1,0:T(8,128)(2,1)}, bf16[2560,256]{1,0:T(8,128)(2,1)S(1)}, u32[]{:S(2)}, u32[]{:S(2)}) collective-permute-start(bf16[2560,256]{1,0:T(8,128)(2,1)} %get-tuple-element.47.right_hbm), channel_id=1, source_target_pairs={{0,8},{8,0},{16,24},{24,16},{32,40},{40,32},{48,56},{56,48},{64,72... | collective-permute-start | bytes 3932168 | tf_op jit(solution)/shard_map/ppermute | solution.py:270
  31.6 11.4 %collective-permute-start.5 = (bf16[2048,256]{1,0:T(8,128)(2,1)}, bf16[2048,256]{1,0:T(8,128)(2,1)S(1)}, u32[]{:S(2)}, u32[]{:S(2)}) collective-permute-start(bf16[2048,256]{1,0:T(8,128)(2,1)} %get-tuple-element.48.after_hbm.right_hbm.inner_ref), channel_id=1, source_target_pairs={{0,8},{8,0},{16,24},{24,16},{32,40},{40,32},{48,56},{56,48},{64,72... | collective-permute-start | bytes 3145736 | tf_op jit(solution)/shard_map/ppermute | solution.py:270
  34.9 1.1 copy-start
  39.4 28.4 %collective-permute-start.1 = (bf16[384,512]{1,0:T(8,128)(2,1)}, bf16[384,512]{1,0:T(8,128)(2,1)}, u32[]{:S(2)}, u32[]{:S(2)}) collective-permute-start(bf16[384,512]{1,0:T(8,128)(2,1)} %get-tuple-element.50.after_hbm), channel_id=1, source_target_pairs={{0,16},{8,24},{16,0},{24,8},{32,48},{40,56},{48,32},{56,40},{64,80... | collective-permute-start | bytes 1179656 | tf_op jit(solution)/shard_map/ppermute | solution.py:270
  41.0 30.1 %collective-permute-start.3 = (bf16[384,512]{1,0:T(8,128)(2,1)}, bf16[384,512]{1,0:T(8,128)(2,1)S(1)}, u32[]{:S(2)}, u32[]{:S(2)}) collective-permute-start(bf16[384,512]{1,0:T(8,128)(2,1)} %get-tuple-element.52), channel_id=1, source_target_pairs={{0,48},{8,56},{16,32},{24,40},{32,16},{40,24},{48,0},{56,8},{64,11... | collective-permute-start | bytes 1179656 | tf_op jit(solution)/shard_map/ppermute | solution.py:270
  43.1 1.0 copy-start.1
  47.4 25.1 %collective-permute-start.6 = (bf16[384,512]{1,0:T(8,128)(2,1)}, bf16[384,512]{1,0:T(8,128)(2,1)S(1)}, u32[]{:S(2)}, u32[]{:S(2)}) collective-permute-start(bf16[384,512]{1,0:T(8,128)(2,1)} %get-tuple-element.54.after_hbm), channel_id=1, source_target_pairs={{0,16},{8,24},{16,0},{24,8},{32,48},{40,56},{48,32},{56,40},{64,80... | collective-permute-start | bytes 1179656 | tf_op jit(solution)/shard_map/ppermute | solution.py:270
  48.1 24.5 %collective-permute-start.7 = (bf16[384,512]{1,0:T(8,128)(2,1)}, bf16[384,512]{1,0:T(8,128)(2,1)S(1)}, u32[]{:S(2)}, u32[]{:S(2)}) collective-permute-start(bf16[384,512]{1,0:T(8,128)(2,1)} %get-tuple-element.55), channel_id=1, source_target_pairs={{0,48},{8,56},{16,32},{24,40},{32,16},{40,24},{48,0},{56,8},{64,11... | collective-permute-start | bytes 1179656 | tf_op jit(solution)/shard_map/ppermute | solution.py:270
  52.1 36.2 %collective-permute-start.12 = (bf16[384,512]{1,0:T(8,128)(2,1)}, bf16[384,512]{1,0:T(8,128)(2,1)S(1)}, u32[]{:S(2)}, u32[]{:S(2)}) collective-permute-start(bf16[384,512]{1,0:T(8,128)(2,1)} %get-tuple-element.62.after_ref), channel_id=1, source_target_pairs={{0,16},{8,24},{16,0},{24,8},{32,48},{40,56},{48,32},{56,40},{64,80... | collective-permute-start | bytes 1179656 | tf_op jit(solution)/shard_map/ppermute | solution.py:270
  62.8 9.6 %copy-start.8 = (bf16[384,512]{1,0:T(8,128)(2,1)S(1)}, bf16[384,512]{1,0:T(8,128)(2,1)}, u32[]{:S(2)}) copy-start(bf16[384,512]{1,0:T(8,128)(2,1)} %get-tuple-element.51) | copy-start | bytes 1179652
  62.8 9.8 %copy-start.7 = (bf16[384,512]{1,0:T(8,128)(2,1)S(1)}, bf16[384,512]{1,0:T(8,128)(2,1)}, u32[]{:S(2)}) copy-start(bf16[384,512]{1,0:T(8,128)(2,1)} %get-tuple-element.53) | copy-start | bytes 1179652
  62.8 9.9 %copy-start.6 = (bf16[384,512]{1,0:T(8,128)(2,1)S(1)}, bf16[384,512]{1,0:T(8,128)(2,1)}, u32[]{:S(2)}) copy-start(bf16[384,512]{1,0:T(8,128)(2,1)} %get-tuple-element.57) | copy-start | bytes 1179652
  62.8 48.1 %all-to-all-start.1 = ((bf16[8,384,128]{2,1,0:T(8,128)(2,1)}), bf16[8,384,128]{2,1,0:T(8,128)(2,1)S(1)}, u32[]{:S(2)}, u32[]{:S(2)}) async-start(bf16[8,384,128]{2,1,0:T(8,128)(2,1)} %get-tuple-element.79), calls=%async_computation.1 | async-start | bytes 1572864 | tf_op jit(solution)/shard_map/all_to_all | solution.py:373
  67.8 24.2 %collective-permute-start.13 = (bf16[384,512]{1,0:T(8,128)(2,1)}, bf16[384,512]{1,0:T(8,128)(2,1)S(1)}, u32[]{:S(2)}, u32[]{:S(2)}) collective-permute-start(bf16[384,512]{1,0:T(8,128)(2,1)} %get-tuple-element.63), channel_id=1, source_target_pairs={{0,48},{8,56},{16,32},{24,40},{32,16},{40,24},{48,0},{56,8},{64,11... | collective-permute-start | bytes 1179656 | tf_op jit(solution)/shard_map/ppermute | solution.py:270
  71.1 13.7 %collective-permute-start.2 = (bf16[192,512]{1,0:T(8,128)(2,1)S(1)}, bf16[192,512]{1,0:T(8,128)(2,1)S(1)}, u32[]{:S(2)}, u32[]{:S(2)}) collective-permute-start(bf16[192,512]{1,0:T(8,128)(2,1)S(1)} %slice.181), channel_id=1, source_target_pairs={{0,48},{8,56},{16,32},{24,40},{32,16},{40,24},{48,0},{56,8},{64,11... | collective-permute-start | bytes 589832 | tf_op jit(solution)/shard_map/ppermute | solution.py:270
  72.3 19.6 %copy-start.5 = (bf16[384,512]{1,0:T(8,128)(2,1)S(1)}, bf16[384,512]{1,0:T(8,128)(2,1)}, u32[]{:S(2)}) copy-start(bf16[384,512]{1,0:T(8,128)(2,1)} %get-tuple-element.61) | copy-start | bytes 1179652
  72.5 12.3 %collective-permute-start.4 = (bf16[192,512]{1,0:T(8,128)(2,1)S(1)}, bf16[192,512]{1,0:T(8,128)(2,1)S(1)}, u32[]{:S(2)}, u32[]{:S(2)}) collective-permute-start(bf16[192,512]{1,0:T(8,128)(2,1)S(1)} %slice.182), channel_id=1, source_target_pairs={{0,16},{8,24},{16,0},{24,8},{32,48},{40,56},{48,32},{56,40},{64,80... | collective-permute-start | bytes 589832 | tf_op jit(solution)/shard_map/ppermute | solution.py:270
  72.6 19.5 %copy-start.4 = (bf16[384,512]{1,0:T(8,128)(2,1)S(1)}, bf16[384,512]{1,0:T(8,128)(2,1)}, u32[]{:S(2)}) copy-start(bf16[384,512]{1,0:T(8,128)(2,1)} %get-tuple-element.65) | copy-start | bytes 1179652
  72.9 21.6 %collective-permute-start.10 = (bf16[192,512]{1,0:T(8,128)(2,1)S(1)}, bf16[192,512]{1,0:T(8,128)(2,1)S(1)}, u32[]{:S(2)}, u32[]{:S(2)}) collective-permute-start(bf16[192,512]{1,0:T(8,128)(2,1)S(1)} %slice.183), channel_id=1, source_target_pairs={{0,48},{8,56},{16,32},{24,40},{32,16},{40,24},{48,0},{56,8},{64,11... | collective-permute-start | bytes 589832 | tf_op jit(solution)/shard_map/ppermute | solution.py:270
  84.8 11.1 %collective-permute-start.11 = (bf16[192,512]{1,0:T(8,128)(2,1)S(1)}, bf16[192,512]{1,0:T(8,128)(2,1)S(1)}, u32[]{:S(2)}, u32[]{:S(2)}) collective-permute-start(bf16[192,512]{1,0:T(8,128)(2,1)S(1)} %slice.184), channel_id=1, source_target_pairs={{0,16},{8,24},{16,0},{24,8},{32,48},{40,56},{48,32},{56,40},{64,80... | collective-permute-start | bytes 589832 | tf_op jit(solution)/shard_map/ppermute | solution.py:270
  84.9 12.7 %collective-permute-start.8 = (bf16[96,512]{1,0:T(8,128)(2,1)S(1)}, bf16[96,512]{1,0:T(8,128)(2,1)S(1)}, u32[]{:S(2)}, u32[]{:S(2)}) collective-permute-start(bf16[96,512]{1,0:T(8,128)(2,1)S(1)} %slice.186), channel_id=1, source_target_pairs={{0,64},{8,72},{16,80},{24,88},{32,96},{40,104},{48,112},{56,120},{... | collective-permute-start | bytes 294920 | tf_op jit(solution)/shard_map/ppermute | solution.py:270
  88.3 9.8 %collective-permute-start.9 = (bf16[96,512]{1,0:T(8,128)(2,1)S(1)}, bf16[96,512]{1,0:T(8,128)(2,1)S(1)}, u32[]{:S(2)}, u32[]{:S(2)}) collective-permute-start(bf16[96,512]{1,0:T(8,128)(2,1)S(1)} %slice.188), channel_id=1, source_target_pairs={{0,192},{8,200},{16,208},{24,216},{32,224},{40,232},{48,240},{56,2... | collective-permute-start | bytes 294920 | tf_op jit(solution)/shard_map/ppermute | solution.py:270
  92.3 9.8 %collective-permute-start.18 = (bf16[192,512]{1,0:T(8,128)(2,1)S(1)}, bf16[192,512]{1,0:T(8,128)(2,1)S(1)}, u32[]{:S(2)}, u32[]{:S(2)}) collective-permute-start(bf16[192,512]{1,0:T(8,128)(2,1)S(1)} %slice.190), channel_id=1, source_target_pairs={{0,48},{8,56},{16,32},{24,40},{32,16},{40,24},{48,0},{56,8},{64,11... | collective-permute-start | bytes 589832 | tf_op jit(solution)/shard_map/ppermute | solution.py:270
  94.4 9.0 %collective-permute-start.19 = (bf16[192,512]{1,0:T(8,128)(2,1)S(1)}, bf16[192,512]{1,0:T(8,128)(2,1)S(1)}, u32[]{:S(2)}, u32[]{:S(2)}) collective-permute-start(bf16[192,512]{1,0:T(8,128)(2,1)S(1)} %slice.191), channel_id=1, source_target_pairs={{0,16},{8,24},{16,0},{24,8},{32,48},{40,56},{48,32},{56,40},{64,80... | collective-permute-start | bytes 589832 | tf_op jit(solution)/shard_map/ppermute | solution.py:270
  96.0 9.3 %collective-permute-start.16 = (bf16[96,512]{1,0:T(8,128)(2,1)S(1)}, bf16[96,512]{1,0:T(8,128)(2,1)S(1)}, u32[]{:S(2)}, u32[]{:S(2)}) collective-permute-start(bf16[96,512]{1,0:T(8,128)(2,1)S(1)} %slice.192), channel_id=1, source_target_pairs={{0,64},{8,72},{16,80},{24,88},{32,96},{40,104},{48,112},{56,120},{... | collective-permute-start | bytes 294920 | tf_op jit(solution)/shard_map/ppermute | solution.py:270
  97.6 8.8 %collective-permute-start.17 = (bf16[96,512]{1,0:T(8,128)(2,1)S(1)}, bf16[96,512]{1,0:T(8,128)(2,1)S(1)}, u32[]{:S(2)}, u32[]{:S(2)}) collective-permute-start(bf16[96,512]{1,0:T(8,128)(2,1)S(1)} %slice.194), channel_id=1, source_target_pairs={{0,192},{8,200},{16,208},{24,216},{32,224},{40,232},{48,240},{56,2... | collective-permute-start | bytes 294920 | tf_op jit(solution)/shard_map/ppermute | solution.py:270
  98.2 11.4 %collective-permute-start.14 = (bf16[48,512]{1,0:T(8,128)(2,1)S(1)}, bf16[48,512]{1,0:T(8,128)(2,1)S(1)}, u32[]{:S(2)}, u32[]{:S(2)}) collective-permute-start(bf16[48,512]{1,0:T(8,128)(2,1)S(1)} %slice.195), channel_id=1, source_target_pairs={{0,192},{8,200},{16,208},{24,216},{32,224},{40,232},{48,240},{56,2... | collective-permute-start | bytes 147464 | tf_op jit(solution)/shard_map/ppermute | solution.py:270
  102.1 8.9 %collective-permute-start.15 = (bf16[48,512]{1,0:T(8,128)(2,1)S(1)}, bf16[48,512]{1,0:T(8,128)(2,1)S(1)}, u32[]{:S(2)}, u32[]{:S(2)}) collective-permute-start(bf16[48,512]{1,0:T(8,128)(2,1)S(1)} %slice.197), channel_id=1, source_target_pairs={{0,64},{8,72},{16,80},{24,88},{32,96},{40,104},{48,112},{56,120},{... | collective-permute-start | bytes 147464 | tf_op jit(solution)/shard_map/ppermute | solution.py:270
  103.6 11.7 %collective-permute-start.22 = (bf16[96,512]{1,0:T(8,128)(2,1)S(1)}, bf16[96,512]{1,0:T(8,128)(2,1)S(1)}, u32[]{:S(2)}, u32[]{:S(2)}) collective-permute-start(bf16[96,512]{1,0:T(8,128)(2,1)S(1)} %slice.200), channel_id=1, source_target_pairs={{0,64},{8,72},{16,80},{24,88},{32,96},{40,104},{48,112},{56,120},{... | collective-permute-start | bytes 294920 | tf_op jit(solution)/shard_map/ppermute | solution.py:270
  105.3 10.0 %collective-permute-start.23 = (bf16[96,512]{1,0:T(8,128)(2,1)S(1)}, bf16[96,512]{1,0:T(8,128)(2,1)S(1)}, u32[]{:S(2)}, u32[]{:S(2)}) collective-permute-start(bf16[96,512]{1,0:T(8,128)(2,1)S(1)} %slice.202), channel_id=1, source_target_pairs={{0,192},{8,200},{16,208},{24,216},{32,224},{40,232},{48,240},{56,2... | collective-permute-start | bytes 294920 | tf_op jit(solution)/shard_map/ppermute | solution.py:270
  106.5 12.0 %collective-permute-start.20 = (bf16[48,512]{1,0:T(8,128)(2,1)S(1)}, bf16[48,512]{1,0:T(8,128)(2,1)S(1)}, u32[]{:S(2)}, u32[]{:S(2)}) collective-permute-start(bf16[48,512]{1,0:T(8,128)(2,1)S(1)} %slice.203), channel_id=1, source_target_pairs={{0,192},{8,200},{16,208},{24,216},{32,224},{40,232},{48,240},{56,2... | collective-permute-start | bytes 147464 | tf_op jit(solution)/shard_map/ppermute | solution.py:270
  109.6 8.9 %collective-permute-start.21 = (bf16[48,512]{1,0:T(8,128)(2,1)S(1)}, bf16[48,512]{1,0:T(8,128)(2,1)S(1)}, u32[]{:S(2)}, u32[]{:S(2)}) collective-permute-start(bf16[48,512]{1,0:T(8,128)(2,1)S(1)} %slice.205), channel_id=1, source_target_pairs={{0,64},{8,72},{16,80},{24,88},{32,96},{40,104},{48,112},{56,120},{... | collective-permute-start | bytes 147464 | tf_op jit(solution)/shard_map/ppermute | solution.py:270
  110.9 0.9 copy-start.3
  115.3 6.3 %collective-permute-start.24 = (bf16[48,512]{1,0:T(8,128)(2,1)S(1)}, bf16[48,512]{1,0:T(8,128)(2,1)S(1)}, u32[]{:S(2)}, u32[]{:S(2)}) collective-permute-start(bf16[48,512]{1,0:T(8,128)(2,1)S(1)} %slice.210), channel_id=1, source_target_pairs={{0,192},{8,200},{16,208},{24,216},{32,224},{40,232},{48,240},{56,2... | collective-permute-start | bytes 147464 | tf_op jit(solution)/shard_map/ppermute | solution.py:270
  118.4 5.3 %collective-permute-start.25 = (bf16[48,512]{1,0:T(8,128)(2,1)S(1)}, bf16[48,512]{1,0:T(8,128)(2,1)S(1)}, u32[]{:S(2)}, u32[]{:S(2)}) collective-permute-start(bf16[48,512]{1,0:T(8,128)(2,1)S(1)} %slice.212), channel_id=1, source_target_pairs={{0,64},{8,72},{16,80},{24,88},{32,96},{40,104},{48,112},{56,120},{... | collective-permute-start | bytes 147464 | tf_op jit(solution)/shard_map/ppermute | solution.py:270

commit v5 on v4

--- a/solution.py
+++ b/solution.py
@@ -114,11 +114,19 @@
 
     rank = index_ref[0]
 
+    def block(place, flavour):
+        rx, rz = ((0, 3 - 2 * flavour, 1 + 2 * flavour, 2)[at] for at in divmod(place, 4))
+        return 4 * rz + rx
+
+    core = rank & 1
+
     def spread(at):
-        for b in range(16):
-            place = slice(at + 48 * b, at + 48 * b + 48)
-            own[place, :] = turned[pl.ds(pl.multiple_of((rank ^ (2 * b)) * 48, 48), 48), :]
-            send[place, :] = turned[pl.ds(pl.multiple_of((rank ^ (2 * b + 1)) * 48, 48), 48), :]
+        for p in range(16):
+            place = slice(at + 48 * p, at + 48 * p + 48)
+            mine = (rank ^ (2 * block(p, core))) * 48
+            theirs = (rank ^ (2 * block(p, 1 - core) + 1)) * 48
+            own[place, :] = turned[pl.ds(pl.multiple_of(mine, 48), 48), :]
+            send[place, :] = turned[pl.ds(pl.multiple_of(theirs, 48), 48), :]
         write(send, send_hbm, at, half)
         write(own, own_hbm, at, half)
 
@@ -212,17 +220,16 @@
     unpack(recv_ref, write)
 
 
-KEEP_FIRST = ((0, 3, 1, 2), (0, 1, 3, 2))
 PARTNERS = ((1, 3), (3, 1))
 SCALES = (2, 2, 8, 8)
 
 
 def grad_kernel(at, block, own_hbm, other_hbm, right_hbm, right_other_hbm, after_hbm, *refs):
     del after_hbm
-    outs_hbm, outs = refs[:4], refs[4:8]
-    own, other, right, right_other, in_sem, write_sem = refs[8:]
+    outs_hbm, outs = refs[:2], refs[2:4]
+    own, other, right, right_other, in_sem, write_sem = refs[4:]
+    rows, columns = outs[0].shape
     wide = 256
-    per = outs[0].shape[1] // wide
     sources = ((own_hbm, at, own), (other_hbm, at, other), (right_hbm, block, right), (right_other_hbm, block, right_other))
     reads, writes = [], []
     for n, (source, begin, target) in enumerate(sources):
@@ -230,21 +237,17 @@
         reads[-1].start()
     for copy in reads:
         copy.wait()
-    for flavour in range(2):
-        keep, send = outs[2 * flavour], outs[2 * flavour + 1]
-        order = KEEP_FIRST[flavour]
-        for col in range(per):
-            k = flavour * per + col
-            place, cols = slice(wide * k, wide * k + wide), slice(wide * col, wide * col + wide)
-            g = (nn(own[...], right[place, :]) + nn(other[...], right_other[place, :])).astype(BF16)
-            for b in range(16):
-                to = order.index(b % 4) * 4 + order.index(b // 4)
-                target = keep if to < 8 else send
-                to = (to % 8) * 48
-                target[to : to + 48, cols] = g[48 * b : 48 * b + 48]
-        for n in (2 * flavour, 2 * flavour + 1):
-            writes.append(pltpu.make_async_copy(outs[n], outs_hbm[n], write_sem.at[n]))
-            writes[-1].start()
+    for k in range(columns // wide):
+        cols = slice(wide * k, wide * k + wide)
+        g = (nn(own[...], right[cols, :]) + nn(other[...], right_other[cols, :])).astype(BF16)
+        outs[0][:, cols] = g[:rows]
+        outs[1][:, cols] = g[rows:]
+        if k % 2 == 1:
+            cols = pl.ds(wide * (k - 1), 2 * wide)
+            for n in range(2):
+                copy = pltpu.make_async_copy(outs[n].at[:, cols], outs_hbm[n].at[:, cols], write_sem.at[k - 1 + n])
+                copy.start()
+                writes.append(copy)
     for copy in writes:
         copy.wait()
 
@@ -266,23 +269,23 @@
     return jax.ShapeDtypeStruct(dims, dtype)
 
 
-def swap(values, distance):
-    return lax.ppermute(values, "dp", [(i, i ^ distance) for i in range(32)])
+def swap(values):
+    return lax.ppermute(values, "dp", [(i, i ^ 1) for i in range(32)])
 
 
 def gradients(at, block, columns, own, other, right, right_other, after, name):
-    piece = shape((384, columns // 2))
     rows, samples = own.shape[0] // 2, own.shape[1]
+    piece = shape((rows // 2, columns))
     moved = (2 * rows * samples + 2 * samples * columns + rows * columns) * 2
     return pl.pallas_call(
         functools.partial(grad_kernel, at, block),
-        out_shape=[piece] * 4,
+        out_shape=[piece] * 2,
         in_specs=[ANY] * 5,
-        out_specs=[ANY] * 4,
-        scratch_shapes=[pltpu.VMEM(piece.shape, BF16)] * 4
+        out_specs=[ANY] * 2,
+        scratch_shapes=[pltpu.VMEM(piece.shape, BF16)] * 2
         + [pltpu.VMEM((rows, samples), BF16)] * 2
         + [pltpu.VMEM((columns, samples), BF16)] * 2
-        + [pltpu.SemaphoreType.DMA((4,))] * 2,
+        + [pltpu.SemaphoreType.DMA((4,)), pltpu.SemaphoreType.DMA((columns // 256,))],
         compiler_params=params(),
         cost_estimate=cost(2 * rows * 2 * samples * columns, moved),
         name=name,
@@ -290,15 +293,15 @@
 
 
 def reduce_send(step, send):
-    return [swap(send[f], PARTNERS[f][step % 2] * SCALES[step]) for f in range(2)]
+    return lax.ppermute(send, "dp", [(i, i ^ (PARTNERS[i & 1][step % 2] * SCALES[step])) for i in range(32)])
 
 
 def reduce_add(step, keep, got):
-    totals = [k.astype(F32) + g.astype(F32) for k, g in zip(keep, got)]
+    total = keep.astype(F32) + got.astype(F32)
     if step == 3:
-        return [t.astype(BF16) for t in totals], []
-    half = totals[0].shape[0] // 2
-    return [t[:half].astype(BF16) for t in totals], [t[half:].astype(BF16) for t in totals]
+        return total.astype(BF16), None
+    half = total.shape[0] // 2
+    return total[:half].astype(BF16), total[half:].astype(BF16)
 
 
 def local(block_input, out_cotangent, w_in, w_out):
@@ -346,14 +349,14 @@
         cost_estimate=cost(8 * samples * width * ff, 18e6),
         name="main",
     )(index, x, recv, cotangent, flat_in, weight_out)
-    other, inner_other = swap(send, 1), swap(inner, 1)
+    other, inner_other = swap(send), swap(inner)
 
     half = width // 2
     down = gradients(0, width, ff, own, other, send, other, inner, "down_grads")
     gate = gradients(half, 0, ff, own, other, inner, inner_other, down[1], "gate_grads")
     up = gradients(half, ff, ff, own, other, inner, inner_other, gate[1], "up_grads")
-    kept = [grads[0::2] for grads in (down, gate, up)]
-    got = [reduce_send(0, grads[1::2]) for grads in (down, gate, up)]
+    kept = [grads[0] for grads in (down, gate, up)]
+    got = [reduce_send(0, grads[1]) for grads in (down, gate, up)]
 
     pre_grad, back = pl.pallas_call(
         input_kernel,
@@ -385,12 +388,11 @@
         if (which, step) == (0, 3):
             arrived, input_grad = lax.optimization_barrier((arrived, input_grad))
         kept[which], sent = reduce_add(step, kept[which], arrived)
-        previous = sent or kept[which]
+        previous = kept[which] if sent is None else sent
         if step < 3:
             got[which] = reduce_send(step + 1, sent)
 
-    down, gate, up = (jnp.concatenate(k, axis=1) for k in kept)
-    return (input_grad[:, None, :], jnp.stack([gate, up], axis=1)[None], down[None])
+    return (input_grad[:, None, :], jnp.stack(kept[1:], axis=1)[None], kept[0][None])
 
 
 def solution(mesh):

time: 125 us -> 110 us (0.88)
  starting transfers between devices: 51.5 us -> 38.3 us
  waiting for transfers between devices: 21.1 us -> 17.3 us
  other arithmetic: 2.94 us -> 4.32 us
    ppermute x26 -> x14, starting transfers between devices: 40.2 us -> 27.1 us  [the longest x12 26.5 us: reduce_send(): lax.ppermute(send, 'dp', [(i, i ^ PARTNERS[i & 1][step % 2] * SCALES[step...]
    ppermute x26 -> x14, waiting for transfers between devices: 18.4 us -> 14.5 us  [the longest x12 11.7 us: reduce_send(): lax.ppermute(send, 'dp', [(i, i ^ PARTNERS[i & 1][step % 2] * SCALES[step...]
    another operation x20 -> x10, other arithmetic: 2.18 us -> 3.61 us
    unnamed x20 -> x16, local copies, waits for them, and re-layouts: 12.8 us -> 12.8 us
  transfers between devices with their start and end apart: 28 -> 16, of which waited for: 6 -> 6; matrix products, arithmetic and copies ran while one was open for 9% -> 11% of each run, Pallas kernels for 18% -> 20%
where the time goes in v5:
time: 110 us; the launch traced here: 109 us
  starting transfers between devices  38.3 us (35%)
  Pallas kernels  34.9 us (32%)
  waiting for transfers between devices  17.3 us (16%)
  local copies, waits for them, and re-layouts  12.9 us (12%)
  other arithmetic  4.32 us (4%)
    ppermute x12, starting transfers between devices, reduce_send(): lax.ppermute(send, 'dp', [(i, i ^ PARTNERS[i & 1][step % 2] * SCALES[step...  26.5 us
    unnamed x16, local copies, waits for them, and re-layouts  12.8 us
    ppermute x12, waiting for transfers between devices, reduce_send(): lax.ppermute(send, 'dp', [(i, i ^ PARTNERS[i & 1][step % 2] * SCALES[step...  11.7 us
    pallas_call x1, Pallas kernels, local(): pl.pallas_call(main_kernel, out_shape=[shape((width, samples)), shape((wi...  10.7 us
    pallas_call x3, Pallas kernels, gradients(): pl.pallas_call(functools.partial(grad_kernel, at, block), out_shape=[piec...  9.92 us
    pallas_call x1, Pallas kernels, local(): pl.pallas_call(input_kernel, out_shape=[shape((samples, width), F32), pac...  9.27 us
    all_to_all x1, starting transfers between devices, local(): lax.all_to_all(packed, 'token', split_axis=0, concat_axis=0, tiled=True)  6.27 us
    all_to_all x1, starting transfers between devices, local(): lax.all_to_all(back, 'token', split_axis=0, concat_axis=0, tiled=True)  4.95 us
  transfers between devices with their start and end apart: 16, of which 6 were waited for; matrix products, arithmetic and copies ran while one was open for 11% of the time, Pallas kernels for 20%

profile of v5, /device:TPU:8, one launch (start us, length us, event | category | flops | bytes accessed | tf_op | source)
XLA Modules:
  0.0 108.6 jit_solution(12269406166808482989)
XLA Ops:
  0.6 2.3 %pack.1 = bf16[8,384,128]{2,1,0:T(8,128)(2,1)} custom-call(bf16[256,1536]{1,0:T(8,128)(2,1)} %bitcast.17), custom_call_target="tpu_custom_call" | custom-call | flops 393216 | bytes 1572864 | tf_op jit(solution)/shard_map/pack/pallas_call | solution.py:317
  2.9 6.3 %all-to-all-start = ((bf16[8,384,128]{2,1,0:T(8,128)(2,1)}), bf16[8,384,128]{2,1,0:T(8,128)(2,1)S(1)}, u32[]{:S(2)}, u32[]{:S(2)}) async-start(bf16[8,384,128]{2,1,0:T(8,128)(2,1)} %pack.1), calls=%async_computation | async-start | bytes 1572864 | tf_op jit(solution)/shard_map/all_to_all | solution.py:321
  9.2 8.0 %copy.8 = bf16[192,8,2,1024]{3,1,2,0:T(8,128)(2,1)} copy(bf16[192,8,2,1024]{3,2,1,0:T(2,128)(2,1)} %bitcast.16) | data formatting | bytes 12582912
  17.2 2.8 %all-to-all-done.recv_ref = bf16[8,384,128]{2,1,0:T(8,128)(2,1)S(1)} async-done(((bf16[8,384,128]{2,1,0:T(8,128)(2,1)}), bf16[8,384,128]{2,1,0:T(8,128)(2,1)S(1)}, u32[]{:S(2)}, u32[]{:S(2)}) %all-to-all-start) | async-done | bytes 786464 | tf_op jit(solution)/shard_map/all_to_all | solution.py:321
  20.0 0.0 copy-start.2
  20.0 0.9 copy-done.2
  20.9 10.7 %main.1 = (bf16[1536,256]{1,0:T(8,128)(2,1)}, bf16[2560,256]{1,0:T(8,128)(2,1)}, bf16[2048,256]{1,0:T(8,128)(2,1)}, bf16[256,1536]{1,0:T(8,128)(2,1)}) custom-call(s32[1]{0:T(128)} %bitcast.index_ref, bf16[256,1536]{1,0:T(8,128)(2,1)} %bitcast.18, bf16[8,384,128]{2,1,0:T(8,128)(2,1)} %copy-done.2, bf16[256,1536]{1,0:T(8,128)(2,1)} %bitcast.24, ...), custom_call_target="tpu_custom_call" | custom-call | flops 3221225472 | bytes 18000000 | tf_op jit(solution)/shard_map/main/pallas_call | solution.py:324
  31.5 0.1 collective-permute-start
  31.6 0.5 collective-permute-start.3
  32.1 2.7 %collective-permute-done.other_hbm.right_other_hbm = bf16[2560,256]{1,0:T(8,128)(2,1)S(1)} collective-permute-done((bf16[2560,256]{1,0:T(8,128)(2,1)}, bf16[2560,256]{1,0:T(8,128)(2,1)S(1)}, u32[]{:S(2)}, u32[]{:S(2)}) %collective-permute-start) | collective-permute-done | bytes 1310752 | tf_op jit(solution)/shard_map/ppermute | solution.py:273
  34.9 0.0 copy-start
  34.9 1.1 %copy-done = bf16[2560,256]{1,0:T(8,128)(2,1)} copy-done((bf16[2560,256]{1,0:T(8,128)(2,1)}, bf16[2560,256]{1,0:T(8,128)(2,1)S(1)}, u32[]{:S(2)}) %copy-start) | copy-done | bytes 1310744
  36.0 3.3 %down_grads.1 = (bf16[384,1024]{1,0:T(8,128)(2,1)}, bf16[384,1024]{1,0:T(8,128)(2,1)}) custom-call(bf16[1536,256]{1,0:T(8,128)(2,1)} %get-tuple-element.28.own_hbm, bf16[2560,256]{1,0:T(8,128)(2,1)} %copy-done, bf16[2560,256]{1,0:T(8,128)(2,1)} %get-tuple-element.29.right_hbm, bf16[2560,256]{1,0:T(8,128)(2,1)} %copy-done, ...), custom_call_target="tpu_custom_call" | custom-call | flops 805306368 | bytes 3407872 | tf_op jit(solution)/shard_map/down_grads/pallas_call | solution.py:280
  39.2 1.6 %collective-permute-start.1 = (bf16[384,1024]{1,0:T(8,128)(2,1)}, bf16[384,1024]{1,0:T(8,128)(2,1)S(1)}, u32[]{:S(2)}, u32[]{:S(2)}) collective-permute-start(bf16[384,1024]{1,0:T(8,128)(2,1)} %get-tuple-element.32.after_hbm), channel_id=1, source_target_pairs={{0,16},{8,56},{16,0},{24,40},{32,48},{40,24},{48,32},{56,8},{64,80... | collective-permute-start | bytes 2359304 | tf_op jit(solution)/shard_map/ppermute | solution.py:296
  40.8 0.0 collective-permute-done.3.right_other_hbm
  40.8 0.0 copy-start.1
  40.8 1.0 copy-done.1
  41.8 3.3 %gate_grads.1 = (bf16[384,1024]{1,0:T(8,128)(2,1)}, bf16[384,1024]{1,0:T(8,128)(2,1)}) custom-call(bf16[1536,256]{1,0:T(8,128)(2,1)} %get-tuple-element.28.own_hbm, bf16[2560,256]{1,0:T(8,128)(2,1)} %copy-done, bf16[2048,256]{1,0:T(8,128)(2,1)} %get-tuple-element.30.after_hbm.right_hbm.inner_ref, bf16[2048,256]{1,0:T(8,128)(2,1)} %copy-done.1, ...), custom_call_target="tpu_custom_call" | custom-call | flops 805306368 | bytes 3407872 | tf_op jit(solution)/shard_map/gate_grads/pallas_call | solution.py:280
  45.1 0.0 copy-start.6
  45.1 0.8 collective-permute-start.4
  45.9 3.3 %up_grads.1 = (bf16[384,1024]{1,0:T(8,128)(2,1)}, bf16[384,1024]{1,0:T(8,128)(2,1)}) custom-call(bf16[1536,256]{1,0:T(8,128)(2,1)} %get-tuple-element.28.own_hbm, bf16[2560,256]{1,0:T(8,128)(2,1)} %copy-done, bf16[2048,256]{1,0:T(8,128)(2,1)} %get-tuple-element.30.after_hbm.right_hbm.inner_ref, bf16[2048,256]{1,0:T(8,128)(2,1)} %copy-done.1, ...), custom_call_target="tpu_custom_call" | custom-call | flops 805306368 | bytes 3407872 | tf_op jit(solution)/shard_map/up_grads/pallas_call | solution.py:280
  49.3 1.6 %collective-permute-start.7 = (bf16[384,1024]{1,0:T(8,128)(2,1)}, bf16[384,1024]{1,0:T(8,128)(2,1)S(1)}, u32[]{:S(2)}, u32[]{:S(2)}) collective-permute-start(bf16[384,1024]{1,0:T(8,128)(2,1)} %get-tuple-element.38.after_ref), channel_id=1, source_target_pairs={{0,16},{8,56},{16,0},{24,40},{32,48},{40,24},{48,32},{56,8},{64,80... | collective-permute-start | bytes 2359304 | tf_op jit(solution)/shard_map/ppermute | solution.py:296
  50.9 0.7 collective-permute-done.1
  51.5 0.0 copy-done.6
  51.5 0.3 add_convert_fusion.2
  51.9 2.8 %collective-permute-start.2 = (bf16[192,1024]{1,0:T(8,128)(2,1)S(1)}, bf16[192,1024]{1,0:T(8,128)(2,1)}, u32[]{:S(2)}, u32[]{:S(2)}) collective-permute-start(bf16[192,1024]{1,0:T(8,128)(2,1)S(1)} %slice.91), channel_id=1, source_target_pairs={{0,48},{8,24},{16,32},{24,8},{32,16},{40,56},{48,0},{56,40},{64,11... | collective-permute-start | bytes 1179656 | tf_op jit(solution)/shard_map/ppermute | solution.py:296
  54.7 9.3 %input.1 = (f32[256,1536]{1,0:T(8,128)}, bf16[8,384,128]{2,1,0:T(8,128)(2,1)}) custom-call(bf16[2048,256]{1,0:T(8,128)(2,1)} %get-tuple-element.30.after_hbm.right_hbm.inner_ref, bf16[1536,2048]{1,0:T(8,128)(2,1)} %bitcast.15, bf16[256,1536]{1,0:T(8,128)(2,1)} %bitcast.19, bf16[8,384,128]{2,1,0:T(8,128)(2,1)} %copy-done.2, ...), custom_call_target="tpu_custom_call" | custom-call | flops 1610612736 | bytes 14000000 | tf_op jit(solution)/shard_map/input/pallas_call | solution.py:361
  64.0 0.0 copy-start.5
  64.0 5.0 %all-to-all-start.1 = ((bf16[8,384,128]{2,1,0:T(8,128)(2,1)}), bf16[8,384,128]{2,1,0:T(8,128)(2,1)S(1)}, u32[]{:S(2)}, u32[]{:S(2)}) async-start(bf16[8,384,128]{2,1,0:T(8,128)(2,1)} %get-tuple-element.47), calls=%async_computation.1 | async-start | bytes 1572864 | tf_op jit(solution)/shard_map/all_to_all | solution.py:376
  69.0 0.0 collective-permute-done.4
  69.0 0.0 copy-done.5
  69.0 1.4 %add_convert_fusion.1 = bf16[384,1024]{1,0:T(8,128)(2,1)S(1)} fusion(bf16[384,1024]{1,0:T(8,128)(2,1)} %collective-permute-done.4, bf16[384,1024]{1,0:T(8,128)(2,1)S(1)} %copy-done.5), kind=kLoop, calls=%fused_computation.1 | loop fusion | flops 1572864 | bytes 2359296 | tf_op jit(solution)/shard_map/convert.15
  70.4 0.0 copy-start.4
  70.5 0.6 collective-permute-start.6
  71.0 0.0 collective-permute-done.2
  71.0 1.1 %add_convert_fusion.5 = bf16[192,1024]{1,0:T(8,128)(2,1)S(1)} fusion(bf16[192,1024]{1,0:T(8,128)(2,1)} %collective-permute-done.2, bf16[384,1024]{1,0:T(8,128)(2,1)S(1)} %add_convert_fusion.2), kind=kLoop, calls=%fused_computation.5 | loop fusion | flops 786432 | bytes 1179648 | tf_op jit(solution)/shard_map/convert.14
  72.2 3.4 %collective-permute-start.5 = (bf16[96,1024]{1,0:T(8,128)(2,1)S(1)}, bf16[96,1024]{1,0:T(8,128)(2,1)S(1)}, u32[]{:S(2)}, u32[]{:S(2)}) collective-permute-start(bf16[96,1024]{1,0:T(8,128)(2,1)S(1)} %slice.94), channel_id=1, source_target_pairs={{0,64},{8,200},{16,80},{24,216},{32,96},{40,232},{48,112},{56,248}... | collective-permute-start | bytes 589832 | tf_op jit(solution)/shard_map/ppermute | solution.py:296
  75.5 0.0 collective-permute-done.7
  75.5 0.0 copy-done.4
  75.5 0.3 add_convert_fusion
  75.9 2.8 %collective-permute-start.10 = (bf16[192,1024]{1,0:T(8,128)(2,1)S(1)}, bf16[192,1024]{1,0:T(8,128)(2,1)S(1)}, u32[]{:S(2)}, u32[]{:S(2)}) collective-permute-start(bf16[192,1024]{1,0:T(8,128)(2,1)S(1)} %slice.96), channel_id=1, source_target_pairs={{0,48},{8,24},{16,32},{24,8},{32,16},{40,56},{48,0},{56,40},{64,11... | collective-permute-start | bytes 1179656 | tf_op jit(solution)/shard_map/ppermute | solution.py:296
  78.7 0.8 collective-permute-done.6
  79.5 0.1 add_convert_fusion.4
  79.7 3.4 %collective-permute-start.9 = (bf16[96,1024]{1,0:T(8,128)(2,1)S(1)}, bf16[96,1024]{1,0:T(8,128)(2,1)S(1)}, u32[]{:S(2)}, u32[]{:S(2)}) collective-permute-start(bf16[96,1024]{1,0:T(8,128)(2,1)S(1)} %slice.97), channel_id=1, source_target_pairs={{0,64},{8,200},{16,80},{24,216},{32,96},{40,232},{48,112},{56,248}... | collective-permute-start | bytes 589832 | tf_op jit(solution)/shard_map/ppermute | solution.py:296
  83.0 0.0 collective-permute-done.5
  83.1 4.5 %collective-permute-start.8 = (bf16[48,1024]{1,0:T(8,128)(2,1)S(1)}, bf16[48,1024]{1,0:T(8,128)(2,1)S(1)}, u32[]{:S(2)}, u32[]{:S(2)}) collective-permute-start(bf16[48,1024]{1,0:T(8,128)(2,1)S(1)} %slice.98), channel_id=1, source_target_pairs={{0,192},{8,72},{16,208},{24,88},{32,224},{40,104},{48,240},{56,120... | collective-permute-start | bytes 294920 | tf_op jit(solution)/shard_map/ppermute | solution.py:296
  87.6 0.0 all-to-all-done.1.recv_ref
  87.6 0.0 copy-start.3
  87.6 0.9 copy-done.3
  88.5 2.8 %final.1 = bf16[256,1536]{1,0:T(8,128)(2,1)} custom-call(f32[256,1536]{1,0:T(8,128)} %get-tuple-element.46.pre_ref, bf16[8,384,128]{2,1,0:T(8,128)(2,1)} %copy-done.3), custom_call_target="tpu_custom_call" | custom-call | flops 393216 | bytes 3145728 | tf_op jit(solution)/shard_map/final/pallas_call | solution.py:378
  91.3 0.0 collective-permute-done.10
  91.3 0.1 add_convert_fusion.3
  91.5 0.7 collective-permute-start.12
  92.2 0.0 collective-permute-done.9
  92.3 2.0 %collective-permute-start.11 = (bf16[48,1024]{1,0:T(8,128)(2,1)S(1)}, bf16[48,1024]{1,0:T(8,128)(2,1)S(1)}, u32[]{:S(2)}, u32[]{:S(2)}) collective-permute-start(bf16[48,1024]{1,0:T(8,128)(2,1)S(1)} %slice.102), channel_id=1, source_target_pairs={{0,192},{8,72},{16,208},{24,88},{32,224},{40,104},{48,240},{56,120... | collective-permute-start | bytes 294920 | tf_op jit(solution)/shard_map/ppermute | solution.py:296
  94.3 0.0 collective-permute-done.8
  94.3 0.7 add_convert_fusion.11
  95.0 5.7 %collective-permute-done.12 = bf16[96,1024]{1,0:T(8,128)(2,1)S(1)} collective-permute-done((bf16[96,1024]{1,0:T(8,128)(2,1)S(1)}, bf16[96,1024]{1,0:T(8,128)(2,1)S(1)}, u32[]{:S(2)}, u32[]{:S(2)}) %collective-permute-start.12) | collective-permute-done | bytes 196640 | tf_op jit(solution)/shard_map/ppermute | solution.py:296
  100.7 0.1 add_convert_fusion.6
  100.8 2.3 %collective-permute-start.13 = (bf16[48,1024]{1,0:T(8,128)(2,1)S(1)}, bf16[48,1024]{1,0:T(8,128)(2,1)S(1)}, u32[]{:S(2)}, u32[]{:S(2)}) collective-permute-start(bf16[48,1024]{1,0:T(8,128)(2,1)S(1)} %slice.106), channel_id=1, source_target_pairs={{0,192},{8,72},{16,208},{24,88},{32,224},{40,104},{48,240},{56,120... | collective-permute-start | bytes 294920 | tf_op jit(solution)/shard_map/ppermute | solution.py:296
  103.1 0.0 collective-permute-done.11
  103.2 4.5 %collective-permute-done.13 = bf16[48,1024]{1,0:T(8,128)(2,1)S(1)} collective-permute-done((bf16[48,1024]{1,0:T(8,128)(2,1)S(1)}, bf16[48,1024]{1,0:T(8,128)(2,1)S(1)}, u32[]{:S(2)}, u32[]{:S(2)}) %collective-permute-start.13) | collective-permute-done | bytes 98336 | tf_op jit(solution)/shard_map/ppermute | solution.py:296
  107.7 0.9 copy.7
  (14 shorter events, 0.3 us)
Async XLA Ops:
  2.9 17.1 %all-to-all-start = ((bf16[8,384,128]{2,1,0:T(8,128)(2,1)}), bf16[8,384,128]{2,1,0:T(8,128)(2,1)S(1)}, u32[]{:S(2)}, u32[]{:S(2)}) async-start(bf16[8,384,128]{2,1,0:T(8,128)(2,1)} %pack.1), calls=%async_computation | async-start | bytes 1572864 | tf_op jit(solution)/shard_map/all_to_all | solution.py:321
  20.0 0.9 copy-start.2
  31.5 3.3 %collective-permute-start = (bf16[2560,256]{1,0:T(8,128)(2,1)}, bf16[2560,256]{1,0:T(8,128)(2,1)S(1)}, u32[]{:S(2)}, u32[]{:S(2)}) collective-permute-start(bf16[2560,256]{1,0:T(8,128)(2,1)} %get-tuple-element.29.right_hbm), channel_id=1, source_target_pairs={{0,8},{8,0},{16,24},{24,16},{32,40},{40,32},{48,56},{56,48},{64,72... | collective-permute-start | bytes 3932168 | tf_op jit(solution)/shard_map/ppermute | solution.py:273
  31.6 9.2 %collective-permute-start.3 = (bf16[2048,256]{1,0:T(8,128)(2,1)}, bf16[2048,256]{1,0:T(8,128)(2,1)S(1)}, u32[]{:S(2)}, u32[]{:S(2)}) collective-permute-start(bf16[2048,256]{1,0:T(8,128)(2,1)} %get-tuple-element.30.after_hbm.right_hbm.inner_ref), channel_id=1, source_target_pairs={{0,8},{8,0},{16,24},{24,16},{32,40},{40,32},{48,56},{56,48},{64,72... | collective-permute-start | bytes 3145736 | tf_op jit(solution)/shard_map/ppermute | solution.py:273
  34.9 1.1 %copy-start = (bf16[2560,256]{1,0:T(8,128)(2,1)}, bf16[2560,256]{1,0:T(8,128)(2,1)S(1)}, u32[]{:S(2)}) copy-start(bf16[2560,256]{1,0:T(8,128)(2,1)S(1)} %collective-permute-done.other_hbm.right_other_hbm) | copy-start | bytes 3932164
  39.2 12.3 %collective-permute-start.1 = (bf16[384,1024]{1,0:T(8,128)(2,1)}, bf16[384,1024]{1,0:T(8,128)(2,1)S(1)}, u32[]{:S(2)}, u32[]{:S(2)}) collective-permute-start(bf16[384,1024]{1,0:T(8,128)(2,1)} %get-tuple-element.32.after_hbm), channel_id=1, source_target_pairs={{0,16},{8,56},{16,0},{24,40},{32,48},{40,24},{48,32},{56,8},{64,80... | collective-permute-start | bytes 2359304 | tf_op jit(solution)/shard_map/ppermute | solution.py:296
  40.8 1.0 copy-start.1
  45.1 6.4 %copy-start.6 = (bf16[384,1024]{1,0:T(8,128)(2,1)S(1)}, bf16[384,1024]{1,0:T(8,128)(2,1)}, u32[]{:S(2)}) copy-start(bf16[384,1024]{1,0:T(8,128)(2,1)} %get-tuple-element.31) | copy-start | bytes 2359300
  45.1 23.8 %collective-permute-start.4 = (bf16[384,1024]{1,0:T(8,128)(2,1)}, bf16[384,1024]{1,0:T(8,128)(2,1)}, u32[]{:S(2)}, u32[]{:S(2)}) collective-permute-start(bf16[384,1024]{1,0:T(8,128)(2,1)} %get-tuple-element.34.after_hbm), channel_id=1, source_target_pairs={{0,16},{8,56},{16,0},{24,40},{32,48},{40,24},{48,32},{56,8},{64,80... | collective-permute-start | bytes 2359304 | tf_op jit(solution)/shard_map/ppermute | solution.py:296
  49.3 26.3 %collective-permute-start.7 = (bf16[384,1024]{1,0:T(8,128)(2,1)}, bf16[384,1024]{1,0:T(8,128)(2,1)S(1)}, u32[]{:S(2)}, u32[]{:S(2)}) collective-permute-start(bf16[384,1024]{1,0:T(8,128)(2,1)} %get-tuple-element.38.after_ref), channel_id=1, source_target_pairs={{0,16},{8,56},{16,0},{24,40},{32,48},{40,24},{48,32},{56,8},{64,80... | collective-permute-start | bytes 2359304 | tf_op jit(solution)/shard_map/ppermute | solution.py:296
  51.9 19.1 %collective-permute-start.2 = (bf16[192,1024]{1,0:T(8,128)(2,1)S(1)}, bf16[192,1024]{1,0:T(8,128)(2,1)}, u32[]{:S(2)}, u32[]{:S(2)}) collective-permute-start(bf16[192,1024]{1,0:T(8,128)(2,1)S(1)} %slice.91), channel_id=1, source_target_pairs={{0,48},{8,24},{16,32},{24,8},{32,16},{40,56},{48,0},{56,40},{64,11... | collective-permute-start | bytes 1179656 | tf_op jit(solution)/shard_map/ppermute | solution.py:296
  64.0 5.0 %copy-start.5 = (bf16[384,1024]{1,0:T(8,128)(2,1)S(1)}, bf16[384,1024]{1,0:T(8,128)(2,1)}, u32[]{:S(2)}) copy-start(bf16[384,1024]{1,0:T(8,128)(2,1)} %get-tuple-element.33) | copy-start | bytes 2359300
  64.0 23.6 %all-to-all-start.1 = ((bf16[8,384,128]{2,1,0:T(8,128)(2,1)}), bf16[8,384,128]{2,1,0:T(8,128)(2,1)S(1)}, u32[]{:S(2)}, u32[]{:S(2)}) async-start(bf16[8,384,128]{2,1,0:T(8,128)(2,1)} %get-tuple-element.47), calls=%async_computation.1 | async-start | bytes 1572864 | tf_op jit(solution)/shard_map/all_to_all | solution.py:376
  70.4 5.1 %copy-start.4 = (bf16[384,1024]{1,0:T(8,128)(2,1)S(1)}, bf16[384,1024]{1,0:T(8,128)(2,1)}, u32[]{:S(2)}) copy-start(bf16[384,1024]{1,0:T(8,128)(2,1)} %get-tuple-element.37) | copy-start | bytes 2359300
  70.5 9.1 %collective-permute-start.6 = (bf16[192,1024]{1,0:T(8,128)(2,1)S(1)}, bf16[192,1024]{1,0:T(8,128)(2,1)S(1)}, u32[]{:S(2)}, u32[]{:S(2)}) collective-permute-start(bf16[192,1024]{1,0:T(8,128)(2,1)S(1)} %slice.92), channel_id=1, source_target_pairs={{0,48},{8,24},{16,32},{24,8},{32,16},{40,56},{48,0},{56,40},{64,11... | collective-permute-start | bytes 1179656 | tf_op jit(solution)/shard_map/ppermute | solution.py:296
  72.2 10.9 %collective-permute-start.5 = (bf16[96,1024]{1,0:T(8,128)(2,1)S(1)}, bf16[96,1024]{1,0:T(8,128)(2,1)S(1)}, u32[]{:S(2)}, u32[]{:S(2)}) collective-permute-start(bf16[96,1024]{1,0:T(8,128)(2,1)S(1)} %slice.94), channel_id=1, source_target_pairs={{0,64},{8,200},{16,80},{24,216},{32,96},{40,232},{48,112},{56,248}... | collective-permute-start | bytes 589832 | tf_op jit(solution)/shard_map/ppermute | solution.py:296
  75.9 15.4 %collective-permute-start.10 = (bf16[192,1024]{1,0:T(8,128)(2,1)S(1)}, bf16[192,1024]{1,0:T(8,128)(2,1)S(1)}, u32[]{:S(2)}, u32[]{:S(2)}) collective-permute-start(bf16[192,1024]{1,0:T(8,128)(2,1)S(1)} %slice.96), channel_id=1, source_target_pairs={{0,48},{8,24},{16,32},{24,8},{32,16},{40,56},{48,0},{56,40},{64,11... | collective-permute-start | bytes 1179656 | tf_op jit(solution)/shard_map/ppermute | solution.py:296
  79.7 12.5 %collective-permute-start.9 = (bf16[96,1024]{1,0:T(8,128)(2,1)S(1)}, bf16[96,1024]{1,0:T(8,128)(2,1)S(1)}, u32[]{:S(2)}, u32[]{:S(2)}) collective-permute-start(bf16[96,1024]{1,0:T(8,128)(2,1)S(1)} %slice.97), channel_id=1, source_target_pairs={{0,64},{8,200},{16,80},{24,216},{32,96},{40,232},{48,112},{56,248}... | collective-permute-start | bytes 589832 | tf_op jit(solution)/shard_map/ppermute | solution.py:296
  83.1 11.2 %collective-permute-start.8 = (bf16[48,1024]{1,0:T(8,128)(2,1)S(1)}, bf16[48,1024]{1,0:T(8,128)(2,1)S(1)}, u32[]{:S(2)}, u32[]{:S(2)}) collective-permute-start(bf16[48,1024]{1,0:T(8,128)(2,1)S(1)} %slice.98), channel_id=1, source_target_pairs={{0,192},{8,72},{16,208},{24,88},{32,224},{40,104},{48,240},{56,120... | collective-permute-start | bytes 294920 | tf_op jit(solution)/shard_map/ppermute | solution.py:296
  87.6 0.9 copy-start.3
  91.5 9.3 %collective-permute-start.12 = (bf16[96,1024]{1,0:T(8,128)(2,1)S(1)}, bf16[96,1024]{1,0:T(8,128)(2,1)S(1)}, u32[]{:S(2)}, u32[]{:S(2)}) collective-permute-start(bf16[96,1024]{1,0:T(8,128)(2,1)S(1)} %slice.101), channel_id=1, source_target_pairs={{0,64},{8,200},{16,80},{24,216},{32,96},{40,232},{48,112},{56,248}... | collective-permute-start | bytes 589832 | tf_op jit(solution)/shard_map/ppermute | solution.py:296
  92.3 10.9 %collective-permute-start.11 = (bf16[48,1024]{1,0:T(8,128)(2,1)S(1)}, bf16[48,1024]{1,0:T(8,128)(2,1)S(1)}, u32[]{:S(2)}, u32[]{:S(2)}) collective-permute-start(bf16[48,1024]{1,0:T(8,128)(2,1)S(1)} %slice.102), channel_id=1, source_target_pairs={{0,192},{8,72},{16,208},{24,88},{32,224},{40,104},{48,240},{56,120... | collective-permute-start | bytes 294920 | tf_op jit(solution)/shard_map/ppermute | solution.py:296
  100.8 6.9 %collective-permute-start.13 = (bf16[48,1024]{1,0:T(8,128)(2,1)S(1)}, bf16[48,1024]{1,0:T(8,128)(2,1)S(1)}, u32[]{:S(2)}, u32[]{:S(2)}) collective-permute-start(bf16[48,1024]{1,0:T(8,128)(2,1)S(1)} %slice.106), channel_id=1, source_target_pairs={{0,192},{8,72},{16,208},{24,88},{32,224},{40,104},{48,240},{56,120... | collective-permute-start | bytes 294920 | tf_op jit(solution)/shard_map/ppermute | solution.py:296

commit v6 on v5

--- a/solution.py
+++ b/solution.py
@@ -221,10 +221,10 @@
 
 
 PARTNERS = ((1, 3), (3, 1))
-SCALES = (2, 2, 8, 8)
-
-
-def grad_kernel(at, block, own_hbm, other_hbm, right_hbm, right_other_hbm, after_hbm, *refs):
+X_FIRST, Z_FIRST = (2, 2, 8, 8), (8, 8, 2, 2)
+
+
+def grad_kernel(x_first, at, block, own_hbm, other_hbm, right_hbm, right_other_hbm, after_hbm, *refs):
     del after_hbm
     outs_hbm, outs = refs[:2], refs[2:4]
     own, other, right, right_other, in_sem, write_sem = refs[4:]
@@ -240,12 +240,18 @@
     for k in range(columns // wide):
         cols = slice(wide * k, wide * k + wide)
         g = (nn(own[...], right[cols, :]) + nn(other[...], right_other[cols, :])).astype(BF16)
-        outs[0][:, cols] = g[:rows]
-        outs[1][:, cols] = g[rows:]
-        if k % 2 == 1:
-            cols = pl.ds(wide * (k - 1), 2 * wide)
+        if x_first:
+            outs[0][:, cols] = g[:rows]
+            outs[1][:, cols] = g[rows:]
+        else:
+            for p in range(16):
+                half, to = divmod(4 * (p % 4) + p // 4, 8)
+                outs[half][48 * to : 48 * to + 48, cols] = g[48 * p : 48 * p + 48]
+        if k % 2 == 1 or k == columns // wide - 1:
+            begin = k // 2 * 2
+            cols = pl.ds(wide * begin, wide * (k + 1 - begin))
             for n in range(2):
-                copy = pltpu.make_async_copy(outs[n].at[:, cols], outs_hbm[n].at[:, cols], write_sem.at[k - 1 + n])
+                copy = pltpu.make_async_copy(outs[n].at[:, cols], outs_hbm[n].at[:, cols], write_sem.at[begin + n])
                 copy.start()
                 writes.append(copy)
     for copy in writes:
@@ -273,27 +279,27 @@
     return lax.ppermute(values, "dp", [(i, i ^ 1) for i in range(32)])
 
 
-def gradients(at, block, columns, own, other, right, right_other, after, name):
+def gradients(x_first, at, block, columns, own, other, right, right_other, after, name):
     rows, samples = own.shape[0] // 2, own.shape[1]
     piece = shape((rows // 2, columns))
     moved = (2 * rows * samples + 2 * samples * columns + rows * columns) * 2
     return pl.pallas_call(
-        functools.partial(grad_kernel, at, block),
+        functools.partial(grad_kernel, x_first, at, block),
         out_shape=[piece] * 2,
         in_specs=[ANY] * 5,
         out_specs=[ANY] * 2,
         scratch_shapes=[pltpu.VMEM(piece.shape, BF16)] * 2
         + [pltpu.VMEM((rows, samples), BF16)] * 2
         + [pltpu.VMEM((columns, samples), BF16)] * 2
-        + [pltpu.SemaphoreType.DMA((4,)), pltpu.SemaphoreType.DMA((columns // 256,))],
+        + [pltpu.SemaphoreType.DMA((4,)), pltpu.SemaphoreType.DMA((columns // 256 + 1,))],
         compiler_params=params(),
         cost_estimate=cost(2 * rows * 2 * samples * columns, moved),
         name=name,
     )(own, other, right, right_other, after)
 
 
-def reduce_send(step, send):
-    return lax.ppermute(send, "dp", [(i, i ^ (PARTNERS[i & 1][step % 2] * SCALES[step])) for i in range(32)])
+def reduce_send(scales, step, send):
+    return lax.ppermute(send, "dp", [(i, i ^ (PARTNERS[i & 1][step % 2] * scales[step])) for i in range(32)])
 
 
 def reduce_add(step, keep, got):
@@ -351,12 +357,13 @@
     )(index, x, recv, cotangent, flat_in, weight_out)
     other, inner_other = swap(send), swap(inner)
 
-    half = width // 2
-    down = gradients(0, width, ff, own, other, send, other, inner, "down_grads")
-    gate = gradients(half, 0, ff, own, other, inner, inner_other, down[1], "gate_grads")
-    up = gradients(half, ff, ff, own, other, inner, inner_other, gate[1], "up_grads")
-    kept = [grads[0] for grads in (down, gate, up)]
-    got = [reduce_send(0, grads[1]) for grads in (down, gate, up)]
+    half, split = width // 2, 768
+    down = gradients(True, 0, width, ff, own, other, send, other, inner, "down_grads")
+    low = gradients(False, half, 0, split, own, other, inner, inner_other, down[1], "low_grads")
+    high = gradients(True, half, split, 2 * ff - split, own, other, inner, inner_other, low[1], "high_grads")
+    orders = (X_FIRST, Z_FIRST, X_FIRST)
+    kept = [grads[0] for grads in (down, low, high)]
+    got = [reduce_send(order, 0, grads[1]) for order, grads in zip(orders, (down, low, high))]
 
     pre_grad, back = pl.pallas_call(
         input_kernel,
@@ -372,7 +379,7 @@
         compiler_params=params(),
         cost_estimate=cost(4 * samples * width * ff, 14e6),
         name="input",
-    )(inner, flat_in, x, recv, out_grad16, up[1])
+    )(inner, flat_in, x, recv, out_grad16, high[1])
     returned = lax.all_to_all(back, "token", split_axis=0, concat_axis=0, tiled=True)
 
     input_grad = pl.pallas_call(
@@ -381,18 +388,19 @@
     )(pre_grad, returned)
 
     previous = None
-    for which, step in ((0, 0), (1, 0), (0, 1), (2, 0), (1, 1), (0, 2), (2, 1), (1, 2), (0, 3), (2, 2), (1, 3), (2, 3)):
+    for which, step in ((0, 0), (1, 0), (2, 0), (0, 1), (2, 1), (0, 2), (1, 1), (2, 2), (1, 2), (0, 3), (1, 3), (2, 3)):
         arrived = got[which]
         if previous is not None:
             arrived, previous = lax.optimization_barrier((arrived, previous))
-        if (which, step) == (0, 3):
+        if (which, step) == (2, 2):
             arrived, input_grad = lax.optimization_barrier((arrived, input_grad))
         kept[which], sent = reduce_add(step, kept[which], arrived)
         previous = kept[which] if sent is None else sent
         if step < 3:
-            got[which] = reduce_send(step + 1, sent)
-
-    return (input_grad[:, None, :], jnp.stack(kept[1:], axis=1)[None], kept[0][None])
+            got[which] = reduce_send(orders[which], step + 1, sent)
+
+    in_grad = jnp.concatenate(kept[1:], axis=1).reshape(width // 32, 2, ff)
+    return (input_grad[:, None, :], in_grad[None], kept[0][None])
 
 
 def solution(mesh):

time: 110 us -> 108 us (0.982)
  waiting for transfers between devices: 17.3 us -> 12.8 us
  other arithmetic: 4.32 us -> 6.05 us
  local copies, waits for them, and re-layouts: 12.9 us -> 14.4 us
    ppermute x12, waiting for transfers between devices: 11.7 us -> 7.23 us  [reduce_send(): lax.ppermute(send, 'dp', [(i, i ^ PARTNERS[i & 1][step % 2] * scales[step...]
    another operation x10 -> x9, other arithmetic: 3.61 us -> 5.32 us
    slice x9, local copies, waits for them, and re-layouts: 0.15 us -> 1.69 us  [reduce_add(): return (total[:half].astype(BF16), total[half:].astype(BF16))]
    unnamed x16 -> x17, local copies, waits for them, and re-layouts: 12.8 us -> 11.9 us
  transfers between devices with their start and end apart: 16 -> 16, of which waited for: 6 -> 5; matrix products, arithmetic and copies ran while one was open for 11% -> 15% of each run, Pallas kernels for 20% -> 21%
where the time goes in v6:
time: 108 us
  starting transfers between devices  38.2 us (35%)
  Pallas kernels  35.3 us (33%)
  local copies, waits for them, and re-layouts  14.4 us (13%)
  waiting for transfers between devices  12.8 us (12%)
  other arithmetic  6.05 us (6%)
    ppermute x12, starting transfers between devices, reduce_send(): lax.ppermute(send, 'dp', [(i, i ^ PARTNERS[i & 1][step % 2] * scales[step...  26.4 us
    unnamed x17, local copies, waits for them, and re-layouts  11.9 us
    pallas_call x1, Pallas kernels, local(): pl.pallas_call(main_kernel, out_shape=[shape((width, samples)), shape((wi...  10.7 us
    pallas_call x3, Pallas kernels, gradients(): pl.pallas_call(functools.partial(grad_kernel, x_first, at, block), out_sh...  10.3 us
    pallas_call x1, Pallas kernels, local(): pl.pallas_call(input_kernel, out_shape=[shape((samples, width), F32), pac...  9.31 us
    ppermute x12, waiting for transfers between devices, reduce_send(): lax.ppermute(send, 'dp', [(i, i ^ PARTNERS[i & 1][step % 2] * scales[step...  7.23 us
    all_to_all x1, starting transfers between devices, local(): lax.all_to_all(packed, 'token', split_axis=0, concat_axis=0, tiled=True)  6.27 us
    another operation x9, other arithmetic  5.32 us
  transfers between devices with their start and end apart: 16, of which 5 were waited for; matrix products, arithmetic and copies ran while one was open for 15% of the time, Pallas kernels for 21%

profile of v6, /device:TPU:8, one launch (start us, length us, event | category | flops | bytes accessed | tf_op | source)
XLA Modules:
  0.0 107.6 jit_solution(13434578755286056612)
XLA Ops:
  0.6 2.3 %pack.1 = bf16[8,384,128]{2,1,0:T(8,128)(2,1)} custom-call(bf16[256,1536]{1,0:T(8,128)(2,1)} %bitcast.12), custom_call_target="tpu_custom_call" | custom-call | flops 393216 | bytes 1572864 | tf_op jit(solution)/shard_map/pack/pallas_call | solution.py:323
  2.9 6.3 %all-to-all-start = ((bf16[8,384,128]{2,1,0:T(8,128)(2,1)}), bf16[8,384,128]{2,1,0:T(8,128)(2,1)S(1)}, u32[]{:S(2)}, u32[]{:S(2)}) async-start(bf16[8,384,128]{2,1,0:T(8,128)(2,1)} %pack.1), calls=%async_computation | async-start | bytes 1572864 | tf_op jit(solution)/shard_map/all_to_all | solution.py:327
  9.2 8.0 %copy.7 = bf16[192,8,2,1024]{3,1,2,0:T(8,128)(2,1)} copy(bf16[192,8,2,1024]{3,2,1,0:T(2,128)(2,1)} %bitcast.11) | data formatting | bytes 12582912
  17.2 2.8 %all-to-all-done.recv_ref = bf16[8,384,128]{2,1,0:T(8,128)(2,1)S(1)} async-done(((bf16[8,384,128]{2,1,0:T(8,128)(2,1)}), bf16[8,384,128]{2,1,0:T(8,128)(2,1)S(1)}, u32[]{:S(2)}, u32[]{:S(2)}) %all-to-all-start) | async-done | bytes 786464 | tf_op jit(solution)/shard_map/all_to_all | solution.py:327
  20.0 0.9 copy-done.3
  20.9 10.7 %main.1 = (bf16[1536,256]{1,0:T(8,128)(2,1)}, bf16[2560,256]{1,0:T(8,128)(2,1)}, bf16[2048,256]{1,0:T(8,128)(2,1)}, bf16[256,1536]{1,0:T(8,128)(2,1)}) custom-call(s32[1]{0:T(128)} %bitcast.index_ref, bf16[256,1536]{1,0:T(8,128)(2,1)} %bitcast.13, bf16[8,384,128]{2,1,0:T(8,128)(2,1)} %copy-done.3, bf16[256,1536]{1,0:T(8,128)(2,1)} %bitcast.18, ...), custom_call_target="tpu_custom_call" | custom-call | flops 3221225472 | bytes 18000000 | tf_op jit(solution)/shard_map/main/pallas_call | solution.py:330
  31.5 0.1 collective-permute-start
  31.6 0.5 collective-permute-start.1
  32.1 2.7 %collective-permute-done.other_hbm.right_other_hbm = bf16[2560,256]{1,0:T(8,128)(2,1)S(1)} collective-permute-done((bf16[2560,256]{1,0:T(8,128)(2,1)}, bf16[2560,256]{1,0:T(8,128)(2,1)S(1)}, u32[]{:S(2)}, u32[]{:S(2)}) %collective-permute-start) | collective-permute-done | bytes 1310752 | tf_op jit(solution)/shard_map/ppermute | solution.py:279
  34.9 1.1 copy-done
  35.9 3.3 %down_grads.1 = (bf16[384,1024]{1,0:T(8,128)(2,1)}, bf16[384,1024]{1,0:T(8,128)(2,1)}) custom-call(bf16[1536,256]{1,0:T(8,128)(2,1)} %get-tuple-element.28.own_hbm, bf16[2560,256]{1,0:T(8,128)(2,1)} %copy-done, bf16[2560,256]{1,0:T(8,128)(2,1)} %get-tuple-element.29.right_hbm, bf16[2560,256]{1,0:T(8,128)(2,1)} %copy-done, ...), custom_call_target="tpu_custom_call" | custom-call | flops 805306368 | bytes 3407872 | tf_op jit(solution)/shard_map/down_grads/pallas_call | solution.py:286
  39.2 1.8 %collective-permute-start.4 = (bf16[384,1024]{1,0:T(8,128)(2,1)}, bf16[384,1024]{1,0:T(8,128)(2,1)}, u32[]{:S(2)}, u32[]{:S(2)}) collective-permute-start(bf16[384,1024]{1,0:T(8,128)(2,1)} %get-tuple-element.31.after_hbm), channel_id=1, source_target_pairs={{0,16},{8,56},{16,0},{24,40},{32,48},{40,24},{48,32},{56,8},{64,80... | collective-permute-start | bytes 2359304 | tf_op jit(solution)/shard_map/ppermute | solution.py:302
  41.0 0.0 collective-permute-done.1.right_other_hbm
  41.0 1.0 copy-done.1
  42.0 3.2 %low_grads.1 = (bf16[384,768]{1,0:T(8,128)(2,1)}, bf16[384,768]{1,0:T(8,128)(2,1)}) custom-call(bf16[1536,256]{1,0:T(8,128)(2,1)} %get-tuple-element.28.own_hbm, bf16[2560,256]{1,0:T(8,128)(2,1)} %copy-done, bf16[2048,256]{1,0:T(8,128)(2,1)} %get-tuple-element.30.after_hbm.right_hbm.inner_ref, bf16[2048,256]{1,0:T(8,128)(2,1)} %copy-done.1, ...), custom_call_target="tpu_custom_call" | custom-call | flops 603979776 | bytes 2752512 | tf_op jit(solution)/shard_map/low_grads/pallas_call | solution.py:286
  45.2 0.0 copy-start.6
  45.2 3.8 %high_grads.1 = (bf16[384,1280]{1,0:T(8,128)(2,1)}, bf16[384,1280]{1,0:T(8,128)(2,1)}) custom-call(bf16[1536,256]{1,0:T(8,128)(2,1)} %get-tuple-element.28.own_hbm, bf16[2560,256]{1,0:T(8,128)(2,1)} %copy-done, bf16[2048,256]{1,0:T(8,128)(2,1)} %get-tuple-element.30.after_hbm.right_hbm.inner_ref, bf16[2048,256]{1,0:T(8,128)(2,1)} %copy-done.1, ...), custom_call_target="tpu_custom_call" | custom-call | flops 1006632960 | bytes 4063232 | tf_op jit(solution)/shard_map/high_grads/pallas_call | solution.py:286
  49.0 0.6 collective-permute-start.2
  49.7 0.0 copy-done.6
  49.7 3.3 %collective-permute-start.3 = (bf16[384,768]{1,0:T(8,128)(2,1)S(1)}, bf16[384,768]{1,0:T(8,128)(2,1)}, u32[]{:S(2)}, u32[]{:S(2)}) collective-permute-start(bf16[384,768]{1,0:T(8,128)(2,1)S(1)} %copy-done.6), channel_id=1, source_target_pairs={{0,64},{8,200},{16,80},{24,216},{32,96},{40,232},{48,112},{56,248}... | collective-permute-start | bytes 1769480 | tf_op jit(solution)/shard_map/ppermute | solution.py:302
  52.9 9.3 %input.1 = (f32[256,1536]{1,0:T(8,128)}, bf16[8,384,128]{2,1,0:T(8,128)(2,1)}) custom-call(bf16[2048,256]{1,0:T(8,128)(2,1)} %get-tuple-element.30.after_hbm.right_hbm.inner_ref, bf16[1536,2048]{1,0:T(8,128)(2,1)} %bitcast.10, bf16[256,1536]{1,0:T(8,128)(2,1)} %bitcast.14, bf16[8,384,128]{2,1,0:T(8,128)(2,1)} %copy-done.3, ...), custom_call_target="tpu_custom_call" | custom-call | flops 1610612736 | bytes 14000000 | tf_op jit(solution)/shard_map/input/pallas_call | solution.py:368
  62.3 0.0 copy-start.5
  62.3 5.0 %all-to-all-start.1 = ((bf16[8,384,128]{2,1,0:T(8,128)(2,1)}), bf16[8,384,128]{2,1,0:T(8,128)(2,1)S(1)}, u32[]{:S(2)}, u32[]{:S(2)}) async-start(bf16[8,384,128]{2,1,0:T(8,128)(2,1)} %get-tuple-element.46), calls=%async_computation.1 | async-start | bytes 1572864 | tf_op jit(solution)/shard_map/all_to_all | solution.py:383
  67.2 0.0 collective-permute-done.4
  67.2 0.0 copy-done.5
  67.2 0.0 copy-start.7
  67.2 1.5 %add_convert_fusion.1 = bf16[384,1024]{1,0:T(8,128)(2,1)S(1)} fusion(bf16[384,1024]{1,0:T(8,128)(2,1)} %collective-permute-done.4, bf16[384,1024]{1,0:T(8,128)(2,1)S(1)} %copy-done.5), kind=kLoop, calls=%fused_computation.1 | loop fusion | flops 1572864 | bytes 2359296 | tf_op jit(solution)/shard_map/convert.17
  68.7 0.0 copy-start.4
  68.8 2.8 %collective-permute-start.6 = (bf16[192,1024]{1,0:T(8,128)(2,1)S(1)}, bf16[192,1024]{1,0:T(8,128)(2,1)S(1)}, u32[]{:S(2)}, u32[]{:S(2)}) collective-permute-start(bf16[192,1024]{1,0:T(8,128)(2,1)S(1)} %slice.90), channel_id=1, source_target_pairs={{0,48},{8,24},{16,32},{24,8},{32,16},{40,56},{48,0},{56,40},{64,11... | collective-permute-start | bytes 1179656 | tf_op jit(solution)/shard_map/ppermute | solution.py:302
  71.6 0.0 collective-permute-done.3
  71.6 0.0 copy-done.7
  71.6 1.2 %add_convert_fusion.2 = bf16[384,768]{1,0:T(8,128)(2,1)S(1)} fusion(bf16[384,768]{1,0:T(8,128)(2,1)} %collective-permute-done.3, bf16[384,768]{1,0:T(8,128)(2,1)S(1)} %copy-done.7), kind=kLoop, calls=%fused_computation.2 | loop fusion | flops 1179648 | bytes 1769472 | tf_op jit(solution)/shard_map/convert.16
  72.8 0.8 slice.91
  73.6 0.0 collective-permute-done.2
  73.6 0.0 copy-done.4
  73.6 0.3 add_convert_fusion
  73.9 0.8 slice.93
  74.7 0.5 collective-permute-start.5
  75.2 3.6 %collective-permute-start.8 = (bf16[192,768]{1,0:T(8,128)(2,1)}, bf16[192,768]{1,0:T(8,128)(2,1)}, u32[]{:S(2)}, u32[]{:S(2)}) collective-permute-start(bf16[192,768]{1,0:T(8,128)(2,1)} %slice.91), channel_id=1, source_target_pairs={{0,192},{8,72},{16,208},{24,88},{32,224},{40,104},{48,240},{56,120... | collective-permute-start | bytes 884744 | tf_op jit(solution)/shard_map/ppermute | solution.py:302
  78.8 0.0 collective-permute-done.6
  78.8 0.1 add_convert_fusion.4
  78.9 1.6 %collective-permute-start.9 = (bf16[96,1024]{1,0:T(8,128)(2,1)S(1)}, bf16[96,1024]{1,0:T(8,128)(2,1)}, u32[]{:S(2)}, u32[]{:S(2)}) collective-permute-start(bf16[96,1024]{1,0:T(8,128)(2,1)S(1)} %slice.95), channel_id=1, source_target_pairs={{0,64},{8,200},{16,80},{24,216},{32,96},{40,232},{48,112},{56,248}... | collective-permute-start | bytes 589832 | tf_op jit(solution)/shard_map/ppermute | solution.py:302
  80.5 0.0 all-to-all-done.1.recv_ref
  80.5 0.9 copy-done.2
  81.4 2.8 %final.1 = bf16[256,1536]{1,0:T(8,128)(2,1)} custom-call(f32[256,1536]{1,0:T(8,128)} %get-tuple-element.45.pre_ref, bf16[8,384,128]{2,1,0:T(8,128)(2,1)} %copy-done.2), custom_call_target="tpu_custom_call" | custom-call | flops 393216 | bytes 3145728 | tf_op jit(solution)/shard_map/final/pallas_call | solution.py:385
  84.2 0.8 collective-permute-done.5
  85.0 0.1 add_convert_fusion.3
  85.1 0.8 collective-permute-start.7
  85.9 4.3 %collective-permute-done.9 = bf16[96,1024]{1,0:T(8,128)(2,1)} collective-permute-done((bf16[96,1024]{1,0:T(8,128)(2,1)S(1)}, bf16[96,1024]{1,0:T(8,128)(2,1)}, u32[]{:S(2)}, u32[]{:S(2)}) %collective-permute-start.9) | collective-permute-done | bytes 196640 | tf_op jit(solution)/shard_map/ppermute | solution.py:302
  90.1 1.0 add_convert_fusion.7
  91.1 0.2 collective-permute-start.12
  91.3 0.0 collective-permute-done.8
  91.3 1.0 add_convert_fusion.5
  92.4 3.8 %collective-permute-start.10 = (bf16[96,768]{1,0:T(8,128)(2,1)S(1)}, bf16[96,768]{1,0:T(8,128)(2,1)S(1)}, u32[]{:S(2)}, u32[]{:S(2)}) collective-permute-start(bf16[96,768]{1,0:T(8,128)(2,1)S(1)} %slice.100), channel_id=1, source_target_pairs={{0,16},{8,56},{16,0},{24,40},{32,48},{40,24},{48,32},{56,8},{64,80... | collective-permute-start | bytes 442376 | tf_op jit(solution)/shard_map/ppermute | solution.py:302
  96.2 0.0 collective-permute-done.7
  96.2 0.1 add_convert_fusion.6
  96.3 4.7 %collective-permute-start.13 = (bf16[48,1280]{1,0:T(8,128)(2,1)S(1)}, bf16[48,1280]{1,0:T(8,128)(2,1)S(1)}, u32[]{:S(2)}, u32[]{:S(2)}) collective-permute-start(bf16[48,1280]{1,0:T(8,128)(2,1)S(1)} %slice.103), channel_id=1, source_target_pairs={{0,192},{8,72},{16,208},{24,88},{32,224},{40,104},{48,240},{56,120... | collective-permute-start | bytes 368648 | tf_op jit(solution)/shard_map/ppermute | solution.py:302
  101.0 0.0 collective-permute-done.10
  101.0 2.8 %collective-permute-start.11 = (bf16[48,768]{1,0:T(8,128)(2,1)S(1)}, bf16[48,768]{1,0:T(8,128)(2,1)S(1)}, u32[]{:S(2)}, u32[]{:S(2)}) collective-permute-start(bf16[48,768]{1,0:T(8,128)(2,1)S(1)} %slice.105), channel_id=1, source_target_pairs={{0,48},{8,24},{16,32},{24,8},{32,16},{40,56},{48,0},{56,40},{64,11... | collective-permute-start | bytes 221192 | tf_op jit(solution)/shard_map/ppermute | solution.py:302
  103.8 0.0 collective-permute-done.12
  103.8 0.7 add_convert_fusion.10
  104.5 2.2 %collective-permute-done.11 = bf16[48,768]{1,0:T(8,128)(2,1)S(1)} collective-permute-done((bf16[48,768]{1,0:T(8,128)(2,1)S(1)}, bf16[48,768]{1,0:T(8,128)(2,1)S(1)}, u32[]{:S(2)}, u32[]{:S(2)}) %collective-permute-start.11) | collective-permute-done | bytes 73760 | tf_op jit(solution)/shard_map/ppermute | solution.py:302
  106.7 0.0 collective-permute-done.13
  106.8 0.8 broadcast_in_dim_reshape.3
  (15 shorter events, 0.2 us)
Async XLA Ops:
  2.9 17.1 %all-to-all-start = ((bf16[8,384,128]{2,1,0:T(8,128)(2,1)}), bf16[8,384,128]{2,1,0:T(8,128)(2,1)S(1)}, u32[]{:S(2)}, u32[]{:S(2)}) async-start(bf16[8,384,128]{2,1,0:T(8,128)(2,1)} %pack.1), calls=%async_computation | async-start | bytes 1572864 | tf_op jit(solution)/shard_map/all_to_all | solution.py:327
  20.0 0.9 copy-start.3
  31.5 3.3 %collective-permute-start = (bf16[2560,256]{1,0:T(8,128)(2,1)}, bf16[2560,256]{1,0:T(8,128)(2,1)S(1)}, u32[]{:S(2)}, u32[]{:S(2)}) collective-permute-start(bf16[2560,256]{1,0:T(8,128)(2,1)} %get-tuple-element.29.right_hbm), channel_id=1, source_target_pairs={{0,8},{8,0},{16,24},{24,16},{32,40},{40,32},{48,56},{56,48},{64,72... | collective-permute-start | bytes 3932168 | tf_op jit(solution)/shard_map/ppermute | solution.py:279
  31.6 9.4 %collective-permute-start.1 = (bf16[2048,256]{1,0:T(8,128)(2,1)}, bf16[2048,256]{1,0:T(8,128)(2,1)S(1)}, u32[]{:S(2)}, u32[]{:S(2)}) collective-permute-start(bf16[2048,256]{1,0:T(8,128)(2,1)} %get-tuple-element.30.after_hbm.right_hbm.inner_ref), channel_id=1, source_target_pairs={{0,8},{8,0},{16,24},{24,16},{32,40},{40,32},{48,56},{56,48},{64,72... | collective-permute-start | bytes 3145736 | tf_op jit(solution)/shard_map/ppermute | solution.py:279
  34.9 1.1 copy-start
  39.2 28.0 %collective-permute-start.4 = (bf16[384,1024]{1,0:T(8,128)(2,1)}, bf16[384,1024]{1,0:T(8,128)(2,1)}, u32[]{:S(2)}, u32[]{:S(2)}) collective-permute-start(bf16[384,1024]{1,0:T(8,128)(2,1)} %get-tuple-element.31.after_hbm), channel_id=1, source_target_pairs={{0,16},{8,56},{16,0},{24,40},{32,48},{40,24},{48,32},{56,8},{64,80... | collective-permute-start | bytes 2359304 | tf_op jit(solution)/shard_map/ppermute | solution.py:302
  41.0 1.0 copy-start.1
  45.2 4.4 %copy-start.6 = (bf16[384,768]{1,0:T(8,128)(2,1)S(1)}, bf16[384,768]{1,0:T(8,128)(2,1)}, u32[]{:S(2)}) copy-start(bf16[384,768]{1,0:T(8,128)(2,1)} %get-tuple-element.32.after_hbm) | copy-start | bytes 1769476
  49.0 24.5 %collective-permute-start.2 = (bf16[384,1280]{1,0:T(8,128)(2,1)}, bf16[384,1280]{1,0:T(8,128)(2,1)S(1)}, u32[]{:S(2)}, u32[]{:S(2)}) collective-permute-start(bf16[384,1280]{1,0:T(8,128)(2,1)} %get-tuple-element.34.after_ref), channel_id=1, source_target_pairs={{0,16},{8,56},{16,0},{24,40},{32,48},{40,24},{48,32},{56,8},{64,80... | collective-permute-start | bytes 2949128 | tf_op jit(solution)/shard_map/ppermute | solution.py:302
  49.7 22.0 %collective-permute-start.3 = (bf16[384,768]{1,0:T(8,128)(2,1)S(1)}, bf16[384,768]{1,0:T(8,128)(2,1)}, u32[]{:S(2)}, u32[]{:S(2)}) collective-permute-start(bf16[384,768]{1,0:T(8,128)(2,1)S(1)} %copy-done.6), channel_id=1, source_target_pairs={{0,64},{8,200},{16,80},{24,216},{32,96},{40,232},{48,112},{56,248}... | collective-permute-start | bytes 1769480 | tf_op jit(solution)/shard_map/ppermute | solution.py:302
  62.3 5.0 %copy-start.5 = (bf16[384,1024]{1,0:T(8,128)(2,1)S(1)}, bf16[384,1024]{1,0:T(8,128)(2,1)}, u32[]{:S(2)}) copy-start(bf16[384,1024]{1,0:T(8,128)(2,1)} %get-tuple-element.36) | copy-start | bytes 2359300
  62.3 18.2 %all-to-all-start.1 = ((bf16[8,384,128]{2,1,0:T(8,128)(2,1)}), bf16[8,384,128]{2,1,0:T(8,128)(2,1)S(1)}, u32[]{:S(2)}, u32[]{:S(2)}) async-start(bf16[8,384,128]{2,1,0:T(8,128)(2,1)} %get-tuple-element.46), calls=%async_computation.1 | async-start | bytes 1572864 | tf_op jit(solution)/shard_map/all_to_all | solution.py:383
  67.2 4.4 %copy-start.7 = (bf16[384,768]{1,0:T(8,128)(2,1)S(1)}, bf16[384,768]{1,0:T(8,128)(2,1)}, u32[]{:S(2)}) copy-start(bf16[384,768]{1,0:T(8,128)(2,1)} %get-tuple-element.35) | copy-start | bytes 1769476
  68.7 4.9 %copy-start.4 = (bf16[384,1280]{1,0:T(8,128)(2,1)S(1)}, bf16[384,1280]{1,0:T(8,128)(2,1)}, u32[]{:S(2)}) copy-start(bf16[384,1280]{1,0:T(8,128)(2,1)} %get-tuple-element.33) | copy-start | bytes 2949124
  68.8 10.0 %collective-permute-start.6 = (bf16[192,1024]{1,0:T(8,128)(2,1)S(1)}, bf16[192,1024]{1,0:T(8,128)(2,1)S(1)}, u32[]{:S(2)}, u32[]{:S(2)}) collective-permute-start(bf16[192,1024]{1,0:T(8,128)(2,1)S(1)} %slice.90), channel_id=1, source_target_pairs={{0,48},{8,24},{16,32},{24,8},{32,16},{40,56},{48,0},{56,40},{64,11... | collective-permute-start | bytes 1179656 | tf_op jit(solution)/shard_map/ppermute | solution.py:302
  74.7 10.3 %collective-permute-start.5 = (bf16[192,1280]{1,0:T(8,128)(2,1)}, bf16[192,1280]{1,0:T(8,128)(2,1)S(1)}, u32[]{:S(2)}, u32[]{:S(2)}) collective-permute-start(bf16[192,1280]{1,0:T(8,128)(2,1)} %slice.93), channel_id=1, source_target_pairs={{0,48},{8,24},{16,32},{24,8},{32,16},{40,56},{48,0},{56,40},{64,11... | collective-permute-start | bytes 1474568 | tf_op jit(solution)/shard_map/ppermute | solution.py:302
  75.2 16.1 %collective-permute-start.8 = (bf16[192,768]{1,0:T(8,128)(2,1)}, bf16[192,768]{1,0:T(8,128)(2,1)}, u32[]{:S(2)}, u32[]{:S(2)}) collective-permute-start(bf16[192,768]{1,0:T(8,128)(2,1)} %slice.91), channel_id=1, source_target_pairs={{0,192},{8,72},{16,208},{24,88},{32,224},{40,104},{48,240},{56,120... | collective-permute-start | bytes 884744 | tf_op jit(solution)/shard_map/ppermute | solution.py:302
  78.9 11.2 %collective-permute-start.9 = (bf16[96,1024]{1,0:T(8,128)(2,1)S(1)}, bf16[96,1024]{1,0:T(8,128)(2,1)}, u32[]{:S(2)}, u32[]{:S(2)}) collective-permute-start(bf16[96,1024]{1,0:T(8,128)(2,1)S(1)} %slice.95), channel_id=1, source_target_pairs={{0,64},{8,200},{16,80},{24,216},{32,96},{40,232},{48,112},{56,248}... | collective-permute-start | bytes 589832 | tf_op jit(solution)/shard_map/ppermute | solution.py:302
  80.5 0.9 copy-start.2
  85.1 11.1 %collective-permute-start.7 = (bf16[96,1280]{1,0:T(8,128)(2,1)S(1)}, bf16[96,1280]{1,0:T(8,128)(2,1)S(1)}, u32[]{:S(2)}, u32[]{:S(2)}) collective-permute-start(bf16[96,1280]{1,0:T(8,128)(2,1)S(1)} %slice.96), channel_id=1, source_target_pairs={{0,64},{8,200},{16,80},{24,216},{32,96},{40,232},{48,112},{56,248}... | collective-permute-start | bytes 737288 | tf_op jit(solution)/shard_map/ppermute | solution.py:302
  91.1 12.7 %collective-permute-start.12 = (bf16[48,1024]{1,0:T(8,128)(2,1)S(1)}, bf16[48,1024]{1,0:T(8,128)(2,1)S(1)}, u32[]{:S(2)}, u32[]{:S(2)}) collective-permute-start(bf16[48,1024]{1,0:T(8,128)(2,1)S(1)} %slice.99), channel_id=1, source_target_pairs={{0,192},{8,72},{16,208},{24,88},{32,224},{40,104},{48,240},{56,120... | collective-permute-start | bytes 294920 | tf_op jit(solution)/shard_map/ppermute | solution.py:302
  92.4 8.6 %collective-permute-start.10 = (bf16[96,768]{1,0:T(8,128)(2,1)S(1)}, bf16[96,768]{1,0:T(8,128)(2,1)S(1)}, u32[]{:S(2)}, u32[]{:S(2)}) collective-permute-start(bf16[96,768]{1,0:T(8,128)(2,1)S(1)} %slice.100), channel_id=1, source_target_pairs={{0,16},{8,56},{16,0},{24,40},{32,48},{40,24},{48,32},{56,8},{64,80... | collective-permute-start | bytes 442376 | tf_op jit(solution)/shard_map/ppermute | solution.py:302
  96.3 10.4 %collective-permute-start.13 = (bf16[48,1280]{1,0:T(8,128)(2,1)S(1)}, bf16[48,1280]{1,0:T(8,128)(2,1)S(1)}, u32[]{:S(2)}, u32[]{:S(2)}) collective-permute-start(bf16[48,1280]{1,0:T(8,128)(2,1)S(1)} %slice.103), channel_id=1, source_target_pairs={{0,192},{8,72},{16,208},{24,88},{32,224},{40,104},{48,240},{56,120... | collective-permute-start | bytes 368648 | tf_op jit(solution)/shard_map/ppermute | solution.py:302
  101.0 5.7 %collective-permute-start.11 = (bf16[48,768]{1,0:T(8,128)(2,1)S(1)}, bf16[48,768]{1,0:T(8,128)(2,1)S(1)}, u32[]{:S(2)}, u32[]{:S(2)}) collective-permute-start(bf16[48,768]{1,0:T(8,128)(2,1)S(1)} %slice.105), channel_id=1, source_target_pairs={{0,48},{8,24},{16,32},{24,8},{32,16},{40,56},{48,0},{56,40},{64,11... | collective-permute-start | bytes 221192 | tf_op jit(solution)/shard_map/ppermute | solution.py:302

commit v7 on v6

--- a/solution.py
+++ b/solution.py
@@ -358,10 +358,10 @@
     other, inner_other = swap(send), swap(inner)
 
     half, split = width // 2, 768
-    down = gradients(True, 0, width, ff, own, other, send, other, inner, "down_grads")
-    low = gradients(False, half, 0, split, own, other, inner, inner_other, down[1], "low_grads")
+    down = gradients(False, 0, width, ff, own, other, send, other, inner, "down_grads")
+    low = gradients(True, half, 0, split, own, other, inner, inner_other, down[1], "low_grads")
     high = gradients(True, half, split, 2 * ff - split, own, other, inner, inner_other, low[1], "high_grads")
-    orders = (X_FIRST, Z_FIRST, X_FIRST)
+    orders = (Z_FIRST, X_FIRST, X_FIRST)
     kept = [grads[0] for grads in (down, low, high)]
     got = [reduce_send(order, 0, grads[1]) for order, grads in zip(orders, (down, low, high))]
 
@@ -388,7 +388,7 @@
     )(pre_grad, returned)
 
     previous = None
-    for which, step in ((0, 0), (1, 0), (2, 0), (0, 1), (2, 1), (0, 2), (1, 1), (2, 2), (1, 2), (0, 3), (1, 3), (2, 3)):
+    for which, step in ((0, 0), (1, 0), (2, 0), (1, 1), (2, 1), (0, 1), (1, 2), (0, 2), (2, 2), (1, 3), (0, 3), (2, 3)):
         arrived = got[which]
         if previous is not None:
             arrived, previous = lax.optimization_barrier((arrived, previous))

time: 108 us -> 118 us (1.093)
  the two profiles are of different devices: /device:TPU:8 before, /device:TPU:32 now
where the time goes in v7:
time: 118 us
  starting transfers between devices  40.4 us (34%)
  Pallas kernels  35.3 us (30%)
  waiting for transfers between devices  20 us (17%)
  local copies, waits for them, and re-layouts  16 us (14%)
  other arithmetic  5.16 us (4%)
    ppermute x12, starting transfers between devices, reduce_send(): lax.ppermute(send, 'dp', [(i, i ^ PARTNERS[i & 1][step % 2] * scales[step...  29.5 us
    ppermute x12, waiting for transfers between devices, reduce_send(): lax.ppermute(send, 'dp', [(i, i ^ PARTNERS[i & 1][step % 2] * scales[step...  13.9 us
    unnamed x17, local copies, waits for them, and re-layouts  12.8 us
    pallas_call x1, Pallas kernels, local(): pl.pallas_call(main_kernel, out_shape=[shape((width, samples)), shape((wi...  10.7 us
    pallas_call x3, Pallas kernels, gradients(): pl.pallas_call(functools.partial(grad_kernel, x_first, at, block), out_sh...  10.3 us
    pallas_call x1, Pallas kernels, local(): pl.pallas_call(input_kernel, out_shape=[shape((samples, width), F32), pac...  9.31 us
    all_to_all x1, starting transfers between devices, local(): lax.all_to_all(packed, 'token', split_axis=0, concat_axis=0, tiled=True)  5.93 us
    another operation x9, other arithmetic  4.42 us
  transfers between devices with their start and end apart: 16, of which 6 were waited for; matrix products, arithmetic and copies ran while one was open for 13% of the time, Pallas kernels for 19%

profile of v7, /device:TPU:32, one launch (start us, length us, event | category | flops | bytes accessed | tf_op | source)
XLA Modules:
  0.0 117.7 jit_solution(8951846519927557335)
XLA Ops:
  0.6 2.3 %pack.1 = bf16[8,384,128]{2,1,0:T(8,128)(2,1)} custom-call(bf16[256,1536]{1,0:T(8,128)(2,1)} %bitcast.12), custom_call_target="tpu_custom_call" | custom-call | flops 393216 | bytes 1572864 | tf_op jit(solution)/shard_map/pack/pallas_call | solution.py:323
  2.9 5.9 %all-to-all-start = ((bf16[8,384,128]{2,1,0:T(8,128)(2,1)}), bf16[8,384,128]{2,1,0:T(8,128)(2,1)S(1)}, u32[]{:S(2)}, u32[]{:S(2)}) async-start(bf16[8,384,128]{2,1,0:T(8,128)(2,1)} %pack.1), calls=%async_computation | async-start | bytes 1572864 | tf_op jit(solution)/shard_map/all_to_all | solution.py:327
  8.8 8.0 %copy.7 = bf16[192,8,2,1024]{3,1,2,0:T(8,128)(2,1)} copy(bf16[192,8,2,1024]{3,2,1,0:T(2,128)(2,1)} %bitcast.11) | data formatting | bytes 12582912
  16.8 3.4 %all-to-all-done.recv_ref = bf16[8,384,128]{2,1,0:T(8,128)(2,1)S(1)} async-done(((bf16[8,384,128]{2,1,0:T(8,128)(2,1)}), bf16[8,384,128]{2,1,0:T(8,128)(2,1)S(1)}, u32[]{:S(2)}, u32[]{:S(2)}) %all-to-all-start) | async-done | bytes 786464 | tf_op jit(solution)/shard_map/all_to_all | solution.py:327
  20.2 0.0 copy-start.3
  20.2 0.9 copy-done.3
  21.1 10.7 %main.1 = (bf16[1536,256]{1,0:T(8,128)(2,1)}, bf16[2560,256]{1,0:T(8,128)(2,1)}, bf16[2048,256]{1,0:T(8,128)(2,1)}, bf16[256,1536]{1,0:T(8,128)(2,1)}) custom-call(s32[1]{0:T(128)} %bitcast.index_ref, bf16[256,1536]{1,0:T(8,128)(2,1)} %bitcast.13, bf16[8,384,128]{2,1,0:T(8,128)(2,1)} %copy-done.3, bf16[256,1536]{1,0:T(8,128)(2,1)} %bitcast.18, ...), custom_call_target="tpu_custom_call" | custom-call | flops 3221225472 | bytes 18000000 | tf_op jit(solution)/shard_map/main/pallas_call | solution.py:330
  31.8 0.1 collective-permute-start
  31.9 0.5 collective-permute-start.1
  32.4 2.7 %collective-permute-done.other_hbm.right_other_hbm = bf16[2560,256]{1,0:T(8,128)(2,1)S(1)} collective-permute-done((bf16[2560,256]{1,0:T(8,128)(2,1)}, bf16[2560,256]{1,0:T(8,128)(2,1)S(1)}, u32[]{:S(2)}, u32[]{:S(2)}) %collective-permute-start) | collective-permute-done | bytes 1310752 | tf_op jit(solution)/shard_map/ppermute | solution.py:279
  35.1 1.1 copy-done
  36.2 3.4 %down_grads.1 = (bf16[384,1024]{1,0:T(8,128)(2,1)}, bf16[384,1024]{1,0:T(8,128)(2,1)}) custom-call(bf16[1536,256]{1,0:T(8,128)(2,1)} %get-tuple-element.28.own_hbm, bf16[2560,256]{1,0:T(8,128)(2,1)} %copy-done, bf16[2560,256]{1,0:T(8,128)(2,1)} %get-tuple-element.29.right_hbm, bf16[2560,256]{1,0:T(8,128)(2,1)} %copy-done, ...), custom_call_target="tpu_custom_call" | custom-call | flops 805306368 | bytes 3407872 | tf_op jit(solution)/shard_map/down_grads/pallas_call | solution.py:286
  39.6 3.5 %collective-permute-start.4 = (bf16[384,1024]{1,0:T(8,128)(2,1)}, bf16[384,1024]{1,0:T(8,128)(2,1)S(1)}, u32[]{:S(2)}, u32[]{:S(2)}) collective-permute-start(bf16[384,1024]{1,0:T(8,128)(2,1)} %get-tuple-element.31.after_hbm), channel_id=1, source_target_pairs={{0,64},{8,200},{16,80},{24,216},{32,96},{40,232},{48,112},{56,248}... | collective-permute-start | bytes 2359304 | tf_op jit(solution)/shard_map/ppermute | solution.py:302
  43.1 0.0 collective-permute-done.1.right_other_hbm
  43.1 1.0 copy-done.1
  44.2 3.1 %low_grads.1 = (bf16[384,768]{1,0:T(8,128)(2,1)}, bf16[384,768]{1,0:T(8,128)(2,1)}) custom-call(bf16[1536,256]{1,0:T(8,128)(2,1)} %get-tuple-element.28.own_hbm, bf16[2560,256]{1,0:T(8,128)(2,1)} %copy-done, bf16[2048,256]{1,0:T(8,128)(2,1)} %get-tuple-element.30.after_hbm.right_hbm.inner_ref, bf16[2048,256]{1,0:T(8,128)(2,1)} %copy-done.1, ...), custom_call_target="tpu_custom_call" | custom-call | flops 603979776 | bytes 2752512 | tf_op jit(solution)/shard_map/low_grads/pallas_call | solution.py:286
  47.3 3.7 %high_grads.1 = (bf16[384,1280]{1,0:T(8,128)(2,1)}, bf16[384,1280]{1,0:T(8,128)(2,1)}) custom-call(bf16[1536,256]{1,0:T(8,128)(2,1)} %get-tuple-element.28.own_hbm, bf16[2560,256]{1,0:T(8,128)(2,1)} %copy-done, bf16[2048,256]{1,0:T(8,128)(2,1)} %get-tuple-element.30.after_hbm.right_hbm.inner_ref, bf16[2048,256]{1,0:T(8,128)(2,1)} %copy-done.1, ...), custom_call_target="tpu_custom_call" | custom-call | flops 1006632960 | bytes 4063232 | tf_op jit(solution)/shard_map/high_grads/pallas_call | solution.py:286
  51.1 1.6 %collective-permute-start.2 = (bf16[384,1280]{1,0:T(8,128)(2,1)}, bf16[384,1280]{1,0:T(8,128)(2,1)S(1)}, u32[]{:S(2)}, u32[]{:S(2)}) collective-permute-start(bf16[384,1280]{1,0:T(8,128)(2,1)} %get-tuple-element.34.after_ref), channel_id=1, source_target_pairs={{0,16},{8,56},{16,0},{24,40},{32,48},{40,24},{48,32},{56,8},{64,80... | collective-permute-start | bytes 2949128 | tf_op jit(solution)/shard_map/ppermute | solution.py:302
  52.6 0.5 collective-permute-start.3
  53.2 9.3 %input.1 = (f32[256,1536]{1,0:T(8,128)}, bf16[8,384,128]{2,1,0:T(8,128)(2,1)}) custom-call(bf16[2048,256]{1,0:T(8,128)(2,1)} %get-tuple-element.30.after_hbm.right_hbm.inner_ref, bf16[1536,2048]{1,0:T(8,128)(2,1)} %bitcast.10, bf16[256,1536]{1,0:T(8,128)(2,1)} %bitcast.14, bf16[8,384,128]{2,1,0:T(8,128)(2,1)} %copy-done.3, ...), custom_call_target="tpu_custom_call" | custom-call | flops 1610612736 | bytes 14000000 | tf_op jit(solution)/shard_map/input/pallas_call | solution.py:368
  62.5 0.0 copy-start.5
  62.5 4.3 %all-to-all-start.1 = ((bf16[8,384,128]{2,1,0:T(8,128)(2,1)}), bf16[8,384,128]{2,1,0:T(8,128)(2,1)S(1)}, u32[]{:S(2)}, u32[]{:S(2)}) async-start(bf16[8,384,128]{2,1,0:T(8,128)(2,1)} %get-tuple-element.47), calls=%async_computation.1 | async-start | bytes 1572864 | tf_op jit(solution)/shard_map/all_to_all | solution.py:383
  66.9 0.0 collective-permute-done.4
  66.9 0.9 copy-done.6
  67.7 0.0 copy-done.5
  67.7 1.5 %add_convert_fusion.1 = bf16[384,1024]{1,0:T(8,128)(2,1)S(1)} fusion(bf16[384,1024]{1,0:T(8,128)(2,1)} %copy-done.6, bf16[384,1024]{1,0:T(8,128)(2,1)S(1)} %copy-done.5), kind=kLoop, calls=%fused_computation.1 | loop fusion | flops 1572864 | bytes 2359296 | tf_op jit(solution)/shard_map/convert.17
  69.2 0.0 copy-start.4
  69.3 0.8 slice.90
  70.1 1.8 %collective-permute-done.3 = bf16[384,768]{1,0:T(8,128)(2,1)} collective-permute-done((bf16[384,768]{1,0:T(8,128)(2,1)}, bf16[384,768]{1,0:T(8,128)(2,1)}, u32[]{:S(2)}, u32[]{:S(2)}) %collective-permute-start.3) | collective-permute-done | bytes 589856 | tf_op jit(solution)/shard_map/ppermute | solution.py:302
  71.9 0.0 copy-done.7
  71.9 1.2 %add_convert_fusion.2 = bf16[384,768]{1,0:T(8,128)(2,1)S(1)} fusion(bf16[384,768]{1,0:T(8,128)(2,1)} %collective-permute-done.3, bf16[384,768]{1,0:T(8,128)(2,1)S(1)} %copy-done.7), kind=kLoop, calls=%fused_computation.2 | loop fusion | flops 1179648 | bytes 1769472 | tf_op jit(solution)/shard_map/convert.16
  73.1 2.8 %collective-permute-start.6 = (bf16[192,768]{1,0:T(8,128)(2,1)S(1)}, bf16[192,768]{1,0:T(8,128)(2,1)S(1)}, u32[]{:S(2)}, u32[]{:S(2)}) collective-permute-start(bf16[192,768]{1,0:T(8,128)(2,1)S(1)} %slice.91), channel_id=1, source_target_pairs={{0,48},{8,24},{16,32},{24,8},{32,16},{40,56},{48,0},{56,40},{64,11... | collective-permute-start | bytes 884744 | tf_op jit(solution)/shard_map/ppermute | solution.py:302
  76.0 0.0 collective-permute-done.2
  76.0 0.0 copy-done.4
  76.0 0.3 add_convert_fusion
  76.2 0.8 slice.93
  77.1 0.5 collective-permute-start.5
  77.6 3.6 %collective-permute-start.8 = (bf16[192,1024]{1,0:T(8,128)(2,1)}, bf16[192,1024]{1,0:T(8,128)(2,1)}, u32[]{:S(2)}, u32[]{:S(2)}) collective-permute-start(bf16[192,1024]{1,0:T(8,128)(2,1)} %slice.90), channel_id=1, source_target_pairs={{0,192},{8,72},{16,208},{24,88},{32,224},{40,104},{48,240},{56,120... | collective-permute-start | bytes 1179656 | tf_op jit(solution)/shard_map/ppermute | solution.py:302
  81.2 0.0 collective-permute-done.6
  81.2 0.1 add_convert_fusion.5
  81.2 0.7 slice.95
  81.9 1.5 %collective-permute-start.10 = (bf16[96,768]{1,0:T(8,128)(2,1)}, bf16[96,768]{1,0:T(8,128)(2,1)S(1)}, u32[]{:S(2)}, u32[]{:S(2)}) collective-permute-start(bf16[96,768]{1,0:T(8,128)(2,1)} %slice.95), channel_id=1, source_target_pairs={{0,64},{8,200},{16,80},{24,216},{32,96},{40,232},{48,112},{56,248}... | collective-permute-start | bytes 442376 | tf_op jit(solution)/shard_map/ppermute | solution.py:302
  83.4 0.0 all-to-all-done.1.recv_ref
  83.4 0.9 copy-done.2
  84.3 2.8 %final.1 = bf16[256,1536]{1,0:T(8,128)(2,1)} custom-call(f32[256,1536]{1,0:T(8,128)} %get-tuple-element.46.pre_ref, bf16[8,384,128]{2,1,0:T(8,128)(2,1)} %copy-done.2), custom_call_target="tpu_custom_call" | custom-call | flops 393216 | bytes 3145728 | tf_op jit(solution)/shard_map/final/pallas_call | solution.py:385
  87.1 0.3 collective-permute-done.5
  87.3 0.1 add_convert_fusion.3
  87.5 1.3 %collective-permute-start.7 = (bf16[96,1280]{1,0:T(8,128)(2,1)S(1)}, bf16[96,1280]{1,0:T(8,128)(2,1)S(1)}, u32[]{:S(2)}, u32[]{:S(2)}) collective-permute-start(bf16[96,1280]{1,0:T(8,128)(2,1)S(1)} %slice.96), channel_id=1, source_target_pairs={{0,64},{8,200},{16,80},{24,216},{32,96},{40,232},{48,112},{56,248}... | collective-permute-start | bytes 737288 | tf_op jit(solution)/shard_map/ppermute | solution.py:302
  88.8 9.1 %collective-permute-done.8 = bf16[192,1024]{1,0:T(8,128)(2,1)} collective-permute-done((bf16[192,1024]{1,0:T(8,128)(2,1)}, bf16[192,1024]{1,0:T(8,128)(2,1)}, u32[]{:S(2)}, u32[]{:S(2)}) %collective-permute-start.8) | collective-permute-done | bytes 393248 | tf_op jit(solution)/shard_map/ppermute | solution.py:302
  97.9 1.1 add_convert_fusion.4
  99.0 0.4 collective-permute-start.9
  99.4 0.0 collective-permute-done.10
  99.5 5.3 %collective-permute-start.11 = (bf16[48,768]{1,0:T(8,128)(2,1)S(1)}, bf16[48,768]{1,0:T(8,128)(2,1)S(1)}, u32[]{:S(2)}, u32[]{:S(2)}) collective-permute-start(bf16[48,768]{1,0:T(8,128)(2,1)S(1)} %slice.101), channel_id=1, source_target_pairs={{0,192},{8,72},{16,208},{24,88},{32,224},{40,104},{48,240},{56,120... | collective-permute-start | bytes 221192 | tf_op jit(solution)/shard_map/ppermute | solution.py:302
  104.8 0.0 collective-permute-done.9
  104.8 0.1 add_convert_fusion.7
  104.9 4.8 %collective-permute-start.13 = (bf16[48,1024]{1,0:T(8,128)(2,1)S(1)}, bf16[48,1024]{1,0:T(8,128)(2,1)S(1)}, u32[]{:S(2)}, u32[]{:S(2)}) collective-permute-start(bf16[48,1024]{1,0:T(8,128)(2,1)S(1)} %slice.102), channel_id=1, source_target_pairs={{0,48},{8,24},{16,32},{24,8},{32,16},{40,56},{48,0},{56,40},{64,11... | collective-permute-start | bytes 294920 | tf_op jit(solution)/shard_map/ppermute | solution.py:302
  109.7 0.0 collective-permute-done.7
  109.7 0.1 add_convert_fusion.6
  109.8 3.8 %collective-permute-start.12 = (bf16[48,1280]{1,0:T(8,128)(2,1)S(1)}, bf16[48,1280]{1,0:T(8,128)(2,1)S(1)}, u32[]{:S(2)}, u32[]{:S(2)}) collective-permute-start(bf16[48,1280]{1,0:T(8,128)(2,1)S(1)} %slice.105), channel_id=1, source_target_pairs={{0,192},{8,72},{16,208},{24,88},{32,224},{40,104},{48,240},{56,120... | collective-permute-start | bytes 368648 | tf_op jit(solution)/shard_map/ppermute | solution.py:302
  113.5 0.0 collective-permute-done.11
  113.6 0.0 collective-permute-done.13
  113.6 0.7 add_convert_fusion.10
  114.2 2.6 %collective-permute-done.12 = bf16[48,1280]{1,0:T(8,128)(2,1)S(1)} collective-permute-done((bf16[48,1280]{1,0:T(8,128)(2,1)S(1)}, bf16[48,1280]{1,0:T(8,128)(2,1)S(1)}, u32[]{:S(2)}, u32[]{:S(2)}) %collective-permute-start.12) | collective-permute-done | bytes 122912 | tf_op jit(solution)/shard_map/ppermute | solution.py:302
  116.9 0.8 broadcast_in_dim_reshape.3
  (15 shorter events, 0.2 us)
Async XLA Ops:
  2.9 17.4 %all-to-all-start = ((bf16[8,384,128]{2,1,0:T(8,128)(2,1)}), bf16[8,384,128]{2,1,0:T(8,128)(2,1)S(1)}, u32[]{:S(2)}, u32[]{:S(2)}) async-start(bf16[8,384,128]{2,1,0:T(8,128)(2,1)} %pack.1), calls=%async_computation | async-start | bytes 1572864 | tf_op jit(solution)/shard_map/all_to_all | solution.py:327
  20.2 0.9 copy-start.3
  31.8 3.3 %collective-permute-start = (bf16[2560,256]{1,0:T(8,128)(2,1)}, bf16[2560,256]{1,0:T(8,128)(2,1)S(1)}, u32[]{:S(2)}, u32[]{:S(2)}) collective-permute-start(bf16[2560,256]{1,0:T(8,128)(2,1)} %get-tuple-element.29.right_hbm), channel_id=1, source_target_pairs={{0,8},{8,0},{16,24},{24,16},{32,40},{40,32},{48,56},{56,48},{64,72... | collective-permute-start | bytes 3932168 | tf_op jit(solution)/shard_map/ppermute | solution.py:279
  31.9 11.2 %collective-permute-start.1 = (bf16[2048,256]{1,0:T(8,128)(2,1)}, bf16[2048,256]{1,0:T(8,128)(2,1)S(1)}, u32[]{:S(2)}, u32[]{:S(2)}) collective-permute-start(bf16[2048,256]{1,0:T(8,128)(2,1)} %get-tuple-element.30.after_hbm.right_hbm.inner_ref), channel_id=1, source_target_pairs={{0,8},{8,0},{16,24},{24,16},{32,40},{40,32},{48,56},{56,48},{64,72... | collective-permute-start | bytes 3145736 | tf_op jit(solution)/shard_map/ppermute | solution.py:279
  35.1 1.1 copy-start
  39.6 27.3 %collective-permute-start.4 = (bf16[384,1024]{1,0:T(8,128)(2,1)}, bf16[384,1024]{1,0:T(8,128)(2,1)S(1)}, u32[]{:S(2)}, u32[]{:S(2)}) collective-permute-start(bf16[384,1024]{1,0:T(8,128)(2,1)} %get-tuple-element.31.after_hbm), channel_id=1, source_target_pairs={{0,64},{8,200},{16,80},{24,216},{32,96},{40,232},{48,112},{56,248}... | collective-permute-start | bytes 2359304 | tf_op jit(solution)/shard_map/ppermute | solution.py:302
  43.1 1.0 copy-start.1
  51.1 24.9 %collective-permute-start.2 = (bf16[384,1280]{1,0:T(8,128)(2,1)}, bf16[384,1280]{1,0:T(8,128)(2,1)S(1)}, u32[]{:S(2)}, u32[]{:S(2)}) collective-permute-start(bf16[384,1280]{1,0:T(8,128)(2,1)} %get-tuple-element.34.after_ref), channel_id=1, source_target_pairs={{0,16},{8,56},{16,0},{24,40},{32,48},{40,24},{48,32},{56,8},{64,80... | collective-permute-start | bytes 2949128 | tf_op jit(solution)/shard_map/ppermute | solution.py:302
  52.6 19.2 %collective-permute-start.3 = (bf16[384,768]{1,0:T(8,128)(2,1)}, bf16[384,768]{1,0:T(8,128)(2,1)}, u32[]{:S(2)}, u32[]{:S(2)}) collective-permute-start(bf16[384,768]{1,0:T(8,128)(2,1)} %get-tuple-element.32.after_hbm), channel_id=1, source_target_pairs={{0,16},{8,56},{16,0},{24,40},{32,48},{40,24},{48,32},{56,8},{64,80... | collective-permute-start | bytes 1769480 | tf_op jit(solution)/shard_map/ppermute | solution.py:302
  62.5 5.2 %copy-start.5 = (bf16[384,1024]{1,0:T(8,128)(2,1)S(1)}, bf16[384,1024]{1,0:T(8,128)(2,1)}, u32[]{:S(2)}) copy-start(bf16[384,1024]{1,0:T(8,128)(2,1)} %get-tuple-element.36) | copy-start | bytes 2359300
  62.5 20.9 %all-to-all-start.1 = ((bf16[8,384,128]{2,1,0:T(8,128)(2,1)}), bf16[8,384,128]{2,1,0:T(8,128)(2,1)S(1)}, u32[]{:S(2)}, u32[]{:S(2)}) async-start(bf16[8,384,128]{2,1,0:T(8,128)(2,1)} %get-tuple-element.47), calls=%async_computation.1 | async-start | bytes 1572864 | tf_op jit(solution)/shard_map/all_to_all | solution.py:383
  66.9 0.9 copy-start.6
  67.7 4.2 %copy-start.7 = (bf16[384,768]{1,0:T(8,128)(2,1)S(1)}, bf16[384,768]{1,0:T(8,128)(2,1)}, u32[]{:S(2)}) copy-start(bf16[384,768]{1,0:T(8,128)(2,1)} %get-tuple-element.35) | copy-start | bytes 1769476
  69.2 6.7 %copy-start.4 = (bf16[384,1280]{1,0:T(8,128)(2,1)S(1)}, bf16[384,1280]{1,0:T(8,128)(2,1)}, u32[]{:S(2)}) copy-start(bf16[384,1280]{1,0:T(8,128)(2,1)} %get-tuple-element.33) | copy-start | bytes 2949124
  73.1 8.0 %collective-permute-start.6 = (bf16[192,768]{1,0:T(8,128)(2,1)S(1)}, bf16[192,768]{1,0:T(8,128)(2,1)S(1)}, u32[]{:S(2)}, u32[]{:S(2)}) collective-permute-start(bf16[192,768]{1,0:T(8,128)(2,1)S(1)} %slice.91), channel_id=1, source_target_pairs={{0,48},{8,24},{16,32},{24,8},{32,16},{40,56},{48,0},{56,40},{64,11... | collective-permute-start | bytes 884744 | tf_op jit(solution)/shard_map/ppermute | solution.py:302
  77.1 10.3 %collective-permute-start.5 = (bf16[192,1280]{1,0:T(8,128)(2,1)}, bf16[192,1280]{1,0:T(8,128)(2,1)S(1)}, u32[]{:S(2)}, u32[]{:S(2)}) collective-permute-start(bf16[192,1280]{1,0:T(8,128)(2,1)} %slice.93), channel_id=1, source_target_pairs={{0,48},{8,24},{16,32},{24,8},{32,16},{40,56},{48,0},{56,40},{64,11... | collective-permute-start | bytes 1474568 | tf_op jit(solution)/shard_map/ppermute | solution.py:302
  77.6 20.3 %collective-permute-start.8 = (bf16[192,1024]{1,0:T(8,128)(2,1)}, bf16[192,1024]{1,0:T(8,128)(2,1)}, u32[]{:S(2)}, u32[]{:S(2)}) collective-permute-start(bf16[192,1024]{1,0:T(8,128)(2,1)} %slice.90), channel_id=1, source_target_pairs={{0,192},{8,72},{16,208},{24,88},{32,224},{40,104},{48,240},{56,120... | collective-permute-start | bytes 1179656 | tf_op jit(solution)/shard_map/ppermute | solution.py:302
  81.9 17.5 %collective-permute-start.10 = (bf16[96,768]{1,0:T(8,128)(2,1)}, bf16[96,768]{1,0:T(8,128)(2,1)S(1)}, u32[]{:S(2)}, u32[]{:S(2)}) collective-permute-start(bf16[96,768]{1,0:T(8,128)(2,1)} %slice.95), channel_id=1, source_target_pairs={{0,64},{8,200},{16,80},{24,216},{32,96},{40,232},{48,112},{56,248}... | collective-permute-start | bytes 442376 | tf_op jit(solution)/shard_map/ppermute | solution.py:302
  83.4 0.9 copy-start.2
  87.5 22.2 %collective-permute-start.7 = (bf16[96,1280]{1,0:T(8,128)(2,1)S(1)}, bf16[96,1280]{1,0:T(8,128)(2,1)S(1)}, u32[]{:S(2)}, u32[]{:S(2)}) collective-permute-start(bf16[96,1280]{1,0:T(8,128)(2,1)S(1)} %slice.96), channel_id=1, source_target_pairs={{0,64},{8,200},{16,80},{24,216},{32,96},{40,232},{48,112},{56,248}... | collective-permute-start | bytes 737288 | tf_op jit(solution)/shard_map/ppermute | solution.py:302
  99.0 5.8 %collective-permute-start.9 = (bf16[96,1024]{1,0:T(8,128)(2,1)S(1)}, bf16[96,1024]{1,0:T(8,128)(2,1)S(1)}, u32[]{:S(2)}, u32[]{:S(2)}) collective-permute-start(bf16[96,1024]{1,0:T(8,128)(2,1)S(1)} %slice.99), channel_id=1, source_target_pairs={{0,16},{8,56},{16,0},{24,40},{32,48},{40,24},{48,32},{56,8},{64,80... | collective-permute-start | bytes 589832 | tf_op jit(solution)/shard_map/ppermute | solution.py:302
  99.5 14.1 %collective-permute-start.11 = (bf16[48,768]{1,0:T(8,128)(2,1)S(1)}, bf16[48,768]{1,0:T(8,128)(2,1)S(1)}, u32[]{:S(2)}, u32[]{:S(2)}) collective-permute-start(bf16[48,768]{1,0:T(8,128)(2,1)S(1)} %slice.101), channel_id=1, source_target_pairs={{0,192},{8,72},{16,208},{24,88},{32,224},{40,104},{48,240},{56,120... | collective-permute-start | bytes 221192 | tf_op jit(solution)/shard_map/ppermute | solution.py:302
  104.9 8.7 %collective-permute-start.13 = (bf16[48,1024]{1,0:T(8,128)(2,1)S(1)}, bf16[48,1024]{1,0:T(8,128)(2,1)S(1)}, u32[]{:S(2)}, u32[]{:S(2)}) collective-permute-start(bf16[48,1024]{1,0:T(8,128)(2,1)S(1)} %slice.102), channel_id=1, source_target_pairs={{0,48},{8,24},{16,32},{24,8},{32,16},{40,56},{48,0},{56,40},{64,11... | collective-permute-start | bytes 294920 | tf_op jit(solution)/shard_map/ppermute | solution.py:302
  109.8 7.1 %collective-permute-start.12 = (bf16[48,1280]{1,0:T(8,128)(2,1)S(1)}, bf16[48,1280]{1,0:T(8,128)(2,1)S(1)}, u32[]{:S(2)}, u32[]{:S(2)}) collective-permute-start(bf16[48,1280]{1,0:T(8,128)(2,1)S(1)} %slice.105), channel_id=1, source_target_pairs={{0,192},{8,72},{16,208},{24,88},{32,224},{40,104},{48,240},{56,120... | collective-permute-start | bytes 368648 | tf_op jit(solution)/shard_map/ppermute | solution.py:302

commit v8 on v6

--- a/solution.py
+++ b/solution.py
@@ -84,8 +84,8 @@
 
 def main_kernel(
     index_ref, x_ref, recv_ref, cot_hbm, w_in_hbm, w_out_hbm,
-    own_hbm, send_hbm, inner_hbm, grad16_hbm,
-    w_in, w_out, cot, state, grad16, hidden, values, slope, silu, turned, own, send, inner,
+    own_hbm, send_hbm, inner_hbm, grad16_hbm, w_in,
+    w_out, cot, state, grad16, hidden, values, slope, silu, turned, own, send, inner,
     in_sem, out_sem, cot_sem, write_sem,
 ):
     samples, width = x_ref.shape
@@ -184,24 +184,17 @@
 
 
 def input_kernel(
-    inner_ref, w_in_hbm, x_ref, recv_ref, grad_ref, after_ref, pre_ref, packed_ref, w_in, inner, normed, sem
+    inner_ref, w_in, x_ref, recv_ref, grad_ref, after_ref, pre_ref, packed_ref, inner, normed
 ):
     del after_ref
     samples, width = x_ref.shape
     wide = 256
 
-    def copy(d):
-        rows = pl.ds(d * wide, wide)
-        return pltpu.make_async_copy(w_in_hbm.at[rows], w_in.at[rows], sem.at[d])
-
-    for d in range(width // wide):
-        copy(d).start()
     scale = norm_state(x_ref, recv_ref, normed)
     for j in range(inner.shape[1] // samples):
         inner[:, samples * j : samples * j + samples] = inner_ref[samples * j : samples * j + samples, :]
     products = jnp.zeros((samples, 128), F32)
     for d in range(width // wide):
-        copy(d).wait()
         cols = slice(wide * d, wide * d + wide)
         g = nt(inner[...], w_in[cols, :]) + grad_ref[:, cols].astype(F32)
         pre_ref[:, cols] = g
@@ -327,13 +320,12 @@
     recv = lax.all_to_all(packed, "token", split_axis=0, concat_axis=0, tiled=True)
 
     flat = shape((samples, width))
-    own, send, inner, out_grad16 = pl.pallas_call(
+    own, send, inner, out_grad16, held_in = pl.pallas_call(
         main_kernel,
-        out_shape=[shape((width, samples)), shape((width + ff, samples)), shape((2 * ff, samples)), flat],
+        out_shape=[shape((width, samples)), shape((width + ff, samples)), shape((2 * ff, samples)), flat, pltpu.VMEM((width, 2 * ff), BF16)],
         in_specs=[SMEM, VMEM, VMEM, ANY, ANY, ANY],
-        out_specs=[ANY] * 4,
+        out_specs=[ANY] * 4 + [VMEM],
         scratch_shapes=[
-            pltpu.VMEM((width, 2 * ff), BF16),
             pltpu.VMEM((width, ff), BF16),
             pltpu.VMEM((samples, width), BF16),
             pltpu.VMEM((samples, width), BF16),
@@ -368,18 +360,16 @@
     pre_grad, back = pl.pallas_call(
         input_kernel,
         out_shape=[shape((samples, width), F32), packed_shape],
-        in_specs=[VMEM, ANY, VMEM, VMEM, VMEM, ANY],
+        in_specs=[VMEM] * 5 + [ANY],
         out_specs=[VMEM] * 2,
         scratch_shapes=[
-            pltpu.VMEM((width, 2 * ff), BF16),
             pltpu.VMEM((samples, 2 * ff), BF16),
             pltpu.VMEM((samples, width), F32),
-            pltpu.SemaphoreType.DMA((width // 256,)),
         ],
         compiler_params=params(),
         cost_estimate=cost(4 * samples * width * ff, 14e6),
         name="input",
-    )(inner, flat_in, x, recv, out_grad16, high[1])
+    )(inner, pltpu.with_memory_space_constraint(held_in, pltpu.VMEM), x, recv, out_grad16, high[1])
     returned = lax.all_to_all(back, "token", split_axis=0, concat_axis=0, tiled=True)
 
     input_grad = pl.pallas_call(

time: 108 us -> 112 us (1.037)
  starting transfers between devices: 38.2 us -> 45.5 us
  Pallas kernels: 35.3 us -> 31.9 us
  waiting for transfers between devices: 12.8 us -> 14.6 us
    ppermute x12, starting transfers between devices: 26.4 us -> 33.7 us  [reduce_send(): lax.ppermute(send, 'dp', [(i, i ^ PARTNERS[i & 1][step % 2] * scales[step...]
    pallas_call x1, Pallas kernels: 9.31 us -> 5.74 us  [local(): pl.pallas_call(input_kernel, out_shape=[shape((samples, width), F32), pac...]
    unnamed x17 -> x13, local copies, waits for them, and re-layouts: 11.9 us -> 10.9 us
  transfers between devices with their start and end apart: 16 -> 16, of which waited for: 5 -> 5; matrix products, arithmetic and copies ran while one was open for 15% -> 14% of each run, Pallas kernels for 21% -> 17%
where the time goes in v8:
time: 112 us
  starting transfers between devices  45.5 us (41%)
  Pallas kernels  31.9 us (28%)
  waiting for transfers between devices  14.6 us (13%)
  local copies, waits for them, and re-layouts  14.1 us (13%)
  other arithmetic  5.09 us (5%)
    ppermute x12, starting transfers between devices, reduce_send(): lax.ppermute(send, 'dp', [(i, i ^ PARTNERS[i & 1][step % 2] * scales[step...  33.7 us
    unnamed x13, local copies, waits for them, and re-layouts  10.9 us
    pallas_call x1, Pallas kernels, local(): pl.pallas_call(main_kernel, out_shape=[shape((width, samples)), shape((wi...  10.7 us
    pallas_call x3, Pallas kernels, gradients(): pl.pallas_call(functools.partial(grad_kernel, x_first, at, block), out_sh...  10.4 us
    ppermute x12, waiting for transfers between devices, reduce_send(): lax.ppermute(send, 'dp', [(i, i ^ PARTNERS[i & 1][step % 2] * scales[step...  8.15 us
    all_to_all x1, starting transfers between devices, local(): lax.all_to_all(packed, 'token', split_axis=0, concat_axis=0, tiled=True)  6.27 us
    pallas_call x1, Pallas kernels, local(): pl.pallas_call(input_kernel, out_shape=[shape((samples, width), F32), pac...  5.74 us
    all_to_all x1, starting transfers between devices, local(): lax.all_to_all(back, 'token', split_axis=0, concat_axis=0, tiled=True)  4.94 us
  transfers between devices with their start and end apart: 16, of which 5 were waited for; matrix products, arithmetic and copies ran while one was open for 14% of the time, Pallas kernels for 17%

profile of v8, /device:TPU:8, one launch (start us, length us, event | category | flops | bytes accessed | tf_op | source)
XLA Modules:
  0.0 111.9 jit_solution(221023088341350249)
XLA Ops:
  0.6 2.3 %pack.1 = bf16[8,384,128]{2,1,0:T(8,128)(2,1)} custom-call(bf16[256,1536]{1,0:T(8,128)(2,1)} %bitcast.11), custom_call_target="tpu_custom_call" | custom-call | flops 393216 | bytes 1572864 | tf_op jit(solution)/shard_map/pack/pallas_call | solution.py:316
  2.9 6.3 %all-to-all-start = ((bf16[8,384,128]{2,1,0:T(8,128)(2,1)}), bf16[8,384,128]{2,1,0:T(8,128)(2,1)S(1)}, u32[]{:S(2)}, u32[]{:S(2)}) async-start(bf16[8,384,128]{2,1,0:T(8,128)(2,1)} %pack.1), calls=%async_computation | async-start | bytes 1572864 | tf_op jit(solution)/shard_map/all_to_all | solution.py:320
  9.2 8.0 %copy.7 = bf16[192,8,2,1024]{3,1,2,0:T(8,128)(2,1)} copy(bf16[192,8,2,1024]{3,2,1,0:T(2,128)(2,1)} %bitcast.9) | data formatting | bytes 12582912
  17.2 2.8 %all-to-all-done.recv_ref = bf16[8,384,128]{2,1,0:T(8,128)(2,1)S(1)} async-done(((bf16[8,384,128]{2,1,0:T(8,128)(2,1)}), bf16[8,384,128]{2,1,0:T(8,128)(2,1)S(1)}, u32[]{:S(2)}, u32[]{:S(2)}) %all-to-all-start) | async-done | bytes 786464 | tf_op jit(solution)/shard_map/all_to_all | solution.py:320
  20.0 0.0 copy-start.2
  20.0 0.9 copy-done.2
  20.9 10.7 %main.1 = (bf16[1536,256]{1,0:T(8,128)(2,1)}, bf16[2560,256]{1,0:T(8,128)(2,1)}, bf16[2048,256]{1,0:T(8,128)(2,1)}, bf16[256,1536]{1,0:T(8,128)(2,1)}, bf16[1536,2048]{1,0:T(8,128)(2,1)S(1)}) custom-call(s32[1]{0:T(128)} %bitcast.index_ref, bf16[256,1536]{1,0:T(8,128)(2,1)} %bitcast.12, bf16[8,384,128]{2,1,0:T(8,128)(2,1)} %copy-done.2, ...), custom_call_target="tpu_custom_call" | custom-call | flops 3221225472 | bytes 18000000 | tf_op jit(solution)/shard_map/main/pallas_call | solution.py:323
  31.6 0.1 collective-permute-start
  31.7 0.5 collective-permute-start.1
  32.2 3.6 %collective-permute-done.other_hbm.right_other_hbm = bf16[2560,256]{1,0:T(8,128)(2,1)S(1)} collective-permute-done((bf16[2560,256]{1,0:T(8,128)(2,1)}, bf16[2560,256]{1,0:T(8,128)(2,1)S(1)}, u32[]{:S(2)}, u32[]{:S(2)}) %collective-permute-start) | collective-permute-done | bytes 1310752 | tf_op jit(solution)/shard_map/ppermute | solution.py:272
  35.8 0.0 copy-start
  35.8 1.1 copy-done
  36.9 3.4 %down_grads.1 = (bf16[384,1024]{1,0:T(8,128)(2,1)}, bf16[384,1024]{1,0:T(8,128)(2,1)}) custom-call(bf16[1536,256]{1,0:T(8,128)(2,1)} %get-tuple-element.29.own_hbm, bf16[2560,256]{1,0:T(8,128)(2,1)} %copy-done, bf16[2560,256]{1,0:T(8,128)(2,1)} %get-tuple-element.30.right_hbm, bf16[2560,256]{1,0:T(8,128)(2,1)} %copy-done, ...), custom_call_target="tpu_custom_call" | custom-call | flops 805306368 | bytes 3407872 | tf_op jit(solution)/shard_map/down_grads/pallas_call | solution.py:279
  40.3 1.8 %collective-permute-start.4 = (bf16[384,1024]{1,0:T(8,128)(2,1)}, bf16[384,1024]{1,0:T(8,128)(2,1)}, u32[]{:S(2)}, u32[]{:S(2)}) collective-permute-start(bf16[384,1024]{1,0:T(8,128)(2,1)} %get-tuple-element.32.after_hbm), channel_id=1, source_target_pairs={{0,16},{8,56},{16,0},{24,40},{32,48},{40,24},{48,32},{56,8},{64,80... | collective-permute-start | bytes 2359304 | tf_op jit(solution)/shard_map/ppermute | solution.py:295
  42.0 0.0 collective-permute-done.1.right_other_hbm
  42.0 3.2 %low_grads.1 = (bf16[384,768]{1,0:T(8,128)(2,1)}, bf16[384,768]{1,0:T(8,128)(2,1)}) custom-call(bf16[1536,256]{1,0:T(8,128)(2,1)} %get-tuple-element.29.own_hbm, bf16[2560,256]{1,0:T(8,128)(2,1)} %copy-done, bf16[2048,256]{1,0:T(8,128)(2,1)} %get-tuple-element.31.after_hbm.right_hbm.inner_ref, bf16[2048,256]{1,0:T(8,128)(2,1)} %collective-permute-done.1.right_other_hbm, ...), custom_call_target="tpu_custom_call" | custom-call | flops 603979776 | bytes 2752512 | tf_op jit(solution)/shard_map/low_grads/pallas_call | solution.py:279
  45.2 3.8 %high_grads.1 = (bf16[384,1280]{1,0:T(8,128)(2,1)}, bf16[384,1280]{1,0:T(8,128)(2,1)}) custom-call(bf16[1536,256]{1,0:T(8,128)(2,1)} %get-tuple-element.29.own_hbm, bf16[2560,256]{1,0:T(8,128)(2,1)} %copy-done, bf16[2048,256]{1,0:T(8,128)(2,1)} %get-tuple-element.31.after_hbm.right_hbm.inner_ref, bf16[2048,256]{1,0:T(8,128)(2,1)} %collective-permute-done.1.right_other_hbm, ...), custom_call_target="tpu_custom_call" | custom-call | flops 1006632960 | bytes 4063232 | tf_op jit(solution)/shard_map/high_grads/pallas_call | solution.py:279
  49.0 0.6 collective-permute-start.2
  49.6 3.3 %collective-permute-start.3 = (bf16[384,768]{1,0:T(8,128)(2,1)}, bf16[384,768]{1,0:T(8,128)(2,1)}, u32[]{:S(2)}, u32[]{:S(2)}) collective-permute-start(bf16[384,768]{1,0:T(8,128)(2,1)} %get-tuple-element.33.after_hbm), channel_id=1, source_target_pairs={{0,64},{8,200},{16,80},{24,216},{32,96},{40,232},{48,112},{56,248}... | collective-permute-start | bytes 1769480 | tf_op jit(solution)/shard_map/ppermute | solution.py:295
  52.9 5.7 %input.1 = (f32[256,1536]{1,0:T(8,128)}, bf16[8,384,128]{2,1,0:T(8,128)(2,1)}) custom-call(bf16[2048,256]{1,0:T(8,128)(2,1)} %get-tuple-element.31.after_hbm.right_hbm.inner_ref, bf16[1536,2048]{1,0:T(8,128)(2,1)S(1)} %get-tuple-element.45.w_in, bf16[256,1536]{1,0:T(8,128)(2,1)} %bitcast.13, bf16[8,384,128]{2,1,0:T(8,128)(2,1)} %copy-done.2, ...), custom_call_target="tpu_custom_call" | custom-call | flops 1610612736 | bytes 14000000 | tf_op jit(solution)/shard_map/input/pallas_call | solution.py:360
  58.7 0.0 copy-start.4
  58.7 4.9 %all-to-all-start.1 = ((bf16[8,384,128]{2,1,0:T(8,128)(2,1)}), bf16[8,384,128]{2,1,0:T(8,128)(2,1)S(1)}, u32[]{:S(2)}, u32[]{:S(2)}) async-start(bf16[8,384,128]{2,1,0:T(8,128)(2,1)} %get-tuple-element.48), calls=%async_computation.1 | async-start | bytes 1572864 | tf_op jit(solution)/shard_map/all_to_all | solution.py:373
  63.6 0.0 collective-permute-done.4
  63.6 0.0 copy-done.4
  63.6 0.0 copy-start.5
  63.6 1.5 %add_convert_fusion.1 = bf16[384,1024]{1,0:T(8,128)(2,1)S(1)} fusion(bf16[384,1024]{1,0:T(8,128)(2,1)} %collective-permute-done.4, bf16[384,1024]{1,0:T(8,128)(2,1)S(1)} %copy-done.4), kind=kLoop, calls=%fused_computation.1 | loop fusion | flops 1572864 | bytes 2359296 | tf_op jit(solution)/shard_map/convert.17
  65.1 0.0 copy-start.3
  65.2 2.8 %collective-permute-start.6 = (bf16[192,1024]{1,0:T(8,128)(2,1)S(1)}, bf16[192,1024]{1,0:T(8,128)(2,1)S(1)}, u32[]{:S(2)}, u32[]{:S(2)}) collective-permute-start(bf16[192,1024]{1,0:T(8,128)(2,1)S(1)} %slice.90), channel_id=1, source_target_pairs={{0,48},{8,24},{16,32},{24,8},{32,16},{40,56},{48,0},{56,40},{64,11... | collective-permute-start | bytes 1179656 | tf_op jit(solution)/shard_map/ppermute | solution.py:295
  68.0 0.0 collective-permute-done.3
  68.0 0.0 copy-done.5
  68.0 1.2 %add_convert_fusion.2 = bf16[384,768]{1,0:T(8,128)(2,1)S(1)} fusion(bf16[384,768]{1,0:T(8,128)(2,1)} %collective-permute-done.3, bf16[384,768]{1,0:T(8,128)(2,1)S(1)} %copy-done.5), kind=kLoop, calls=%fused_computation.2 | loop fusion | flops 1179648 | bytes 1769472 | tf_op jit(solution)/shard_map/convert.16
  69.2 0.8 slice.91
  70.0 0.0 collective-permute-done.2
  70.0 0.0 copy-done.3
  70.0 0.3 add_convert_fusion
  70.3 0.8 slice.93
  71.1 2.3 %collective-permute-start.5 = (bf16[192,1280]{1,0:T(8,128)(2,1)}, bf16[192,1280]{1,0:T(8,128)(2,1)S(1)}, u32[]{:S(2)}, u32[]{:S(2)}) collective-permute-start(bf16[192,1280]{1,0:T(8,128)(2,1)} %slice.93), channel_id=1, source_target_pairs={{0,48},{8,24},{16,32},{24,8},{32,16},{40,56},{48,0},{56,40},{64,11... | collective-permute-start | bytes 1474568 | tf_op jit(solution)/shard_map/ppermute | solution.py:295
  73.3 1.8 %collective-permute-start.8 = (bf16[192,768]{1,0:T(8,128)(2,1)}, bf16[192,768]{1,0:T(8,128)(2,1)S(1)}, u32[]{:S(2)}, u32[]{:S(2)}) collective-permute-start(bf16[192,768]{1,0:T(8,128)(2,1)} %slice.91), channel_id=1, source_target_pairs={{0,192},{8,72},{16,208},{24,88},{32,224},{40,104},{48,240},{56,120... | collective-permute-start | bytes 884744 | tf_op jit(solution)/shard_map/ppermute | solution.py:295
  75.1 0.0 collective-permute-done.6
  75.1 0.1 add_convert_fusion.4
  75.3 0.7 slice.95
  76.0 2.6 %collective-permute-start.9 = (bf16[96,1024]{1,0:T(8,128)(2,1)}, bf16[96,1024]{1,0:T(8,128)(2,1)}, u32[]{:S(2)}, u32[]{:S(2)}) collective-permute-start(bf16[96,1024]{1,0:T(8,128)(2,1)} %slice.95), channel_id=1, source_target_pairs={{0,64},{8,200},{16,80},{24,216},{32,96},{40,232},{48,112},{56,248}... | collective-permute-start | bytes 589832 | tf_op jit(solution)/shard_map/ppermute | solution.py:295
  78.6 0.0 all-to-all-done.1.recv_ref
  78.6 0.9 copy-done.1
  79.5 2.8 %final.1 = bf16[256,1536]{1,0:T(8,128)(2,1)} custom-call(f32[256,1536]{1,0:T(8,128)} %get-tuple-element.47.pre_ref, bf16[8,384,128]{2,1,0:T(8,128)(2,1)} %copy-done.1), custom_call_target="tpu_custom_call" | custom-call | flops 393216 | bytes 3145728 | tf_op jit(solution)/shard_map/final/pallas_call | solution.py:375
  82.3 0.0 collective-permute-done.5
  82.3 0.1 add_convert_fusion.3
  82.4 0.4 collective-permute-start.7
  82.8 1.4 %collective-permute-done.9 = bf16[96,1024]{1,0:T(8,128)(2,1)} collective-permute-done((bf16[96,1024]{1,0:T(8,128)(2,1)}, bf16[96,1024]{1,0:T(8,128)(2,1)}, u32[]{:S(2)}, u32[]{:S(2)}) %collective-permute-start.9) | collective-permute-done | bytes 196640 | tf_op jit(solution)/shard_map/ppermute | solution.py:295
  84.3 1.0 add_convert_fusion.7
  85.3 6.2 %collective-permute-start.12 = (bf16[48,1024]{1,0:T(8,128)(2,1)S(1)}, bf16[48,1024]{1,0:T(8,128)(2,1)S(1)}, u32[]{:S(2)}, u32[]{:S(2)}) collective-permute-start(bf16[48,1024]{1,0:T(8,128)(2,1)S(1)} %slice.99), channel_id=1, source_target_pairs={{0,192},{8,72},{16,208},{24,88},{32,224},{40,104},{48,240},{56,120... | collective-permute-start | bytes 294920 | tf_op jit(solution)/shard_map/ppermute | solution.py:295
  91.5 0.0 collective-permute-done.8
  91.5 0.1 add_convert_fusion.5
  91.6 1.1 collective-permute-start.10
  92.6 1.8 %collective-permute-done.7 = bf16[96,1280]{1,0:T(8,128)(2,1)S(1)} collective-permute-done((bf16[96,1280]{1,0:T(8,128)(2,1)S(1)}, bf16[96,1280]{1,0:T(8,128)(2,1)S(1)}, u32[]{:S(2)}, u32[]{:S(2)}) %collective-permute-start.7) | collective-permute-done | bytes 245792 | tf_op jit(solution)/shard_map/ppermute | solution.py:295
  94.4 0.1 add_convert_fusion.6
  94.5 10.8 %collective-permute-start.13 = (bf16[48,1280]{1,0:T(8,128)(2,1)S(1)}, bf16[48,1280]{1,0:T(8,128)(2,1)S(1)}, u32[]{:S(2)}, u32[]{:S(2)}) collective-permute-start(bf16[48,1280]{1,0:T(8,128)(2,1)S(1)} %slice.103), channel_id=1, source_target_pairs={{0,192},{8,72},{16,208},{24,88},{32,224},{40,104},{48,240},{56,120... | collective-permute-start | bytes 368648 | tf_op jit(solution)/shard_map/ppermute | solution.py:295
  105.3 0.0 collective-permute-done.10
  105.3 0.1 collective-permute-start.11
  105.4 0.0 collective-permute-done.12
  105.4 0.7 add_convert_fusion.10
  106.1 4.9 %collective-permute-done.11 = bf16[48,768]{1,0:T(8,128)(2,1)S(1)} collective-permute-done((bf16[48,768]{1,0:T(8,128)(2,1)S(1)}, bf16[48,768]{1,0:T(8,128)(2,1)S(1)}, u32[]{:S(2)}, u32[]{:S(2)}) %collective-permute-start.11) | collective-permute-done | bytes 73760 | tf_op jit(solution)/shard_map/ppermute | solution.py:295
  111.0 0.0 collective-permute-done.13
  111.1 0.8 broadcast_in_dim_reshape.3
  (11 shorter events, 0.2 us)
Async XLA Ops:
  2.9 17.1 %all-to-all-start = ((bf16[8,384,128]{2,1,0:T(8,128)(2,1)}), bf16[8,384,128]{2,1,0:T(8,128)(2,1)S(1)}, u32[]{:S(2)}, u32[]{:S(2)}) async-start(bf16[8,384,128]{2,1,0:T(8,128)(2,1)} %pack.1), calls=%async_computation | async-start | bytes 1572864 | tf_op jit(solution)/shard_map/all_to_all | solution.py:320
  20.0 0.9 copy-start.2
  31.6 4.2 %collective-permute-start = (bf16[2560,256]{1,0:T(8,128)(2,1)}, bf16[2560,256]{1,0:T(8,128)(2,1)S(1)}, u32[]{:S(2)}, u32[]{:S(2)}) collective-permute-start(bf16[2560,256]{1,0:T(8,128)(2,1)} %get-tuple-element.30.right_hbm), channel_id=1, source_target_pairs={{0,8},{8,0},{16,24},{24,16},{32,40},{40,32},{48,56},{56,48},{64,72... | collective-permute-start | bytes 3932168 | tf_op jit(solution)/shard_map/ppermute | solution.py:272
  31.7 10.3 %collective-permute-start.1 = (bf16[2048,256]{1,0:T(8,128)(2,1)}, bf16[2048,256]{1,0:T(8,128)(2,1)}, u32[]{:S(2)}, u32[]{:S(2)}) collective-permute-start(bf16[2048,256]{1,0:T(8,128)(2,1)} %get-tuple-element.31.after_hbm.right_hbm.inner_ref), channel_id=1, source_target_pairs={{0,8},{8,0},{16,24},{24,16},{32,40},{40,32},{48,56},{56,48},{64,72... | collective-permute-start | bytes 3145736 | tf_op jit(solution)/shard_map/ppermute | solution.py:272
  35.8 1.1 copy-start
  40.3 23.3 %collective-permute-start.4 = (bf16[384,1024]{1,0:T(8,128)(2,1)}, bf16[384,1024]{1,0:T(8,128)(2,1)}, u32[]{:S(2)}, u32[]{:S(2)}) collective-permute-start(bf16[384,1024]{1,0:T(8,128)(2,1)} %get-tuple-element.32.after_hbm), channel_id=1, source_target_pairs={{0,16},{8,56},{16,0},{24,40},{32,48},{40,24},{48,32},{56,8},{64,80... | collective-permute-start | bytes 2359304 | tf_op jit(solution)/shard_map/ppermute | solution.py:295
  49.0 21.0 %collective-permute-start.2 = (bf16[384,1280]{1,0:T(8,128)(2,1)}, bf16[384,1280]{1,0:T(8,128)(2,1)S(1)}, u32[]{:S(2)}, u32[]{:S(2)}) collective-permute-start(bf16[384,1280]{1,0:T(8,128)(2,1)} %get-tuple-element.35.after_ref), channel_id=1, source_target_pairs={{0,16},{8,56},{16,0},{24,40},{32,48},{40,24},{48,32},{56,8},{64,80... | collective-permute-start | bytes 2949128 | tf_op jit(solution)/shard_map/ppermute | solution.py:295
  49.6 18.4 %collective-permute-start.3 = (bf16[384,768]{1,0:T(8,128)(2,1)}, bf16[384,768]{1,0:T(8,128)(2,1)}, u32[]{:S(2)}, u32[]{:S(2)}) collective-permute-start(bf16[384,768]{1,0:T(8,128)(2,1)} %get-tuple-element.33.after_hbm), channel_id=1, source_target_pairs={{0,64},{8,200},{16,80},{24,216},{32,96},{40,232},{48,112},{56,248}... | collective-permute-start | bytes 1769480 | tf_op jit(solution)/shard_map/ppermute | solution.py:295
  58.7 4.9 %copy-start.4 = (bf16[384,1024]{1,0:T(8,128)(2,1)S(1)}, bf16[384,1024]{1,0:T(8,128)(2,1)}, u32[]{:S(2)}) copy-start(bf16[384,1024]{1,0:T(8,128)(2,1)} %get-tuple-element.37) | copy-start | bytes 2359300
  58.7 19.9 %all-to-all-start.1 = ((bf16[8,384,128]{2,1,0:T(8,128)(2,1)}), bf16[8,384,128]{2,1,0:T(8,128)(2,1)S(1)}, u32[]{:S(2)}, u32[]{:S(2)}) async-start(bf16[8,384,128]{2,1,0:T(8,128)(2,1)} %get-tuple-element.48), calls=%async_computation.1 | async-start | bytes 1572864 | tf_op jit(solution)/shard_map/all_to_all | solution.py:373
  63.6 4.4 %copy-start.5 = (bf16[384,768]{1,0:T(8,128)(2,1)S(1)}, bf16[384,768]{1,0:T(8,128)(2,1)}, u32[]{:S(2)}) copy-start(bf16[384,768]{1,0:T(8,128)(2,1)} %get-tuple-element.36) | copy-start | bytes 1769476
  65.1 4.9 %copy-start.3 = (bf16[384,1280]{1,0:T(8,128)(2,1)S(1)}, bf16[384,1280]{1,0:T(8,128)(2,1)}, u32[]{:S(2)}) copy-start(bf16[384,1280]{1,0:T(8,128)(2,1)} %get-tuple-element.34) | copy-start | bytes 2949124
  65.2 10.0 %collective-permute-start.6 = (bf16[192,1024]{1,0:T(8,128)(2,1)S(1)}, bf16[192,1024]{1,0:T(8,128)(2,1)S(1)}, u32[]{:S(2)}, u32[]{:S(2)}) collective-permute-start(bf16[192,1024]{1,0:T(8,128)(2,1)S(1)} %slice.90), channel_id=1, source_target_pairs={{0,48},{8,24},{16,32},{24,8},{32,16},{40,56},{48,0},{56,40},{64,11... | collective-permute-start | bytes 1179656 | tf_op jit(solution)/shard_map/ppermute | solution.py:295
  71.1 11.2 %collective-permute-start.5 = (bf16[192,1280]{1,0:T(8,128)(2,1)}, bf16[192,1280]{1,0:T(8,128)(2,1)S(1)}, u32[]{:S(2)}, u32[]{:S(2)}) collective-permute-start(bf16[192,1280]{1,0:T(8,128)(2,1)} %slice.93), channel_id=1, source_target_pairs={{0,48},{8,24},{16,32},{24,8},{32,16},{40,56},{48,0},{56,40},{64,11... | collective-permute-start | bytes 1474568 | tf_op jit(solution)/shard_map/ppermute | solution.py:295
  73.3 18.1 %collective-permute-start.8 = (bf16[192,768]{1,0:T(8,128)(2,1)}, bf16[192,768]{1,0:T(8,128)(2,1)S(1)}, u32[]{:S(2)}, u32[]{:S(2)}) collective-permute-start(bf16[192,768]{1,0:T(8,128)(2,1)} %slice.91), channel_id=1, source_target_pairs={{0,192},{8,72},{16,208},{24,88},{32,224},{40,104},{48,240},{56,120... | collective-permute-start | bytes 884744 | tf_op jit(solution)/shard_map/ppermute | solution.py:295
  76.0 8.3 %collective-permute-start.9 = (bf16[96,1024]{1,0:T(8,128)(2,1)}, bf16[96,1024]{1,0:T(8,128)(2,1)}, u32[]{:S(2)}, u32[]{:S(2)}) collective-permute-start(bf16[96,1024]{1,0:T(8,128)(2,1)} %slice.95), channel_id=1, source_target_pairs={{0,64},{8,200},{16,80},{24,216},{32,96},{40,232},{48,112},{56,248}... | collective-permute-start | bytes 589832 | tf_op jit(solution)/shard_map/ppermute | solution.py:295
  78.6 0.9 copy-start.1
  82.4 12.0 %collective-permute-start.7 = (bf16[96,1280]{1,0:T(8,128)(2,1)S(1)}, bf16[96,1280]{1,0:T(8,128)(2,1)S(1)}, u32[]{:S(2)}, u32[]{:S(2)}) collective-permute-start(bf16[96,1280]{1,0:T(8,128)(2,1)S(1)} %slice.96), channel_id=1, source_target_pairs={{0,64},{8,200},{16,80},{24,216},{32,96},{40,232},{48,112},{56,248}... | collective-permute-start | bytes 737288 | tf_op jit(solution)/shard_map/ppermute | solution.py:295
  85.3 20.2 %collective-permute-start.12 = (bf16[48,1024]{1,0:T(8,128)(2,1)S(1)}, bf16[48,1024]{1,0:T(8,128)(2,1)S(1)}, u32[]{:S(2)}, u32[]{:S(2)}) collective-permute-start(bf16[48,1024]{1,0:T(8,128)(2,1)S(1)} %slice.99), channel_id=1, source_target_pairs={{0,192},{8,72},{16,208},{24,88},{32,224},{40,104},{48,240},{56,120... | collective-permute-start | bytes 294920 | tf_op jit(solution)/shard_map/ppermute | solution.py:295
  91.6 13.7 %collective-permute-start.10 = (bf16[96,768]{1,0:T(8,128)(2,1)S(1)}, bf16[96,768]{1,0:T(8,128)(2,1)S(1)}, u32[]{:S(2)}, u32[]{:S(2)}) collective-permute-start(bf16[96,768]{1,0:T(8,128)(2,1)S(1)} %slice.100), channel_id=1, source_target_pairs={{0,16},{8,56},{16,0},{24,40},{32,48},{40,24},{48,32},{56,8},{64,80... | collective-permute-start | bytes 442376 | tf_op jit(solution)/shard_map/ppermute | solution.py:295
  94.5 16.5 %collective-permute-start.13 = (bf16[48,1280]{1,0:T(8,128)(2,1)S(1)}, bf16[48,1280]{1,0:T(8,128)(2,1)S(1)}, u32[]{:S(2)}, u32[]{:S(2)}) collective-permute-start(bf16[48,1280]{1,0:T(8,128)(2,1)S(1)} %slice.103), channel_id=1, source_target_pairs={{0,192},{8,72},{16,208},{24,88},{32,224},{40,104},{48,240},{56,120... | collective-permute-start | bytes 368648 | tf_op jit(solution)/shard_map/ppermute | solution.py:295
  105.3 5.7 %collective-permute-start.11 = (bf16[48,768]{1,0:T(8,128)(2,1)S(1)}, bf16[48,768]{1,0:T(8,128)(2,1)S(1)}, u32[]{:S(2)}, u32[]{:S(2)}) collective-permute-start(bf16[48,768]{1,0:T(8,128)(2,1)S(1)} %slice.105), channel_id=1, source_target_pairs={{0,48},{8,24},{16,32},{24,8},{32,16},{40,56},{48,0},{56,40},{64,11... | collective-permute-start | bytes 221192 | tf_op jit(solution)/shard_map/ppermute | solution.py:295

commit v9 on v8

--- a/solution.py
+++ b/solution.py
@@ -378,7 +378,7 @@
     )(pre_grad, returned)
 
     previous = None
-    for which, step in ((0, 0), (1, 0), (2, 0), (0, 1), (2, 1), (0, 2), (1, 1), (2, 2), (1, 2), (0, 3), (1, 3), (2, 3)):
+    for which, step in ((0, 0), (1, 0), (2, 0), (0, 1), (2, 1), (1, 1), (2, 2), (0, 2), (1, 2), (0, 3), (1, 3), (2, 3)):
         arrived = got[which]
         if previous is not None:
             arrived, previous = lax.optimization_barrier((arrived, previous))

time: 112 us -> 111 us (level); the launches traced: 112 us -> 110 us
  starting transfers between devices: 45.5 us -> 33.6 us
  waiting for transfers between devices: 14.6 us -> 22.1 us
  other arithmetic: 5.09 us -> 6.3 us
    ppermute x12, starting transfers between devices: 33.7 us -> 21.8 us  [reduce_send(): lax.ppermute(send, 'dp', [(i, i ^ PARTNERS[i & 1][step % 2] * scales[step...]
    ppermute x12, waiting for transfers between devices: 8.15 us -> 15.7 us  [reduce_send(): lax.ppermute(send, 'dp', [(i, i ^ PARTNERS[i & 1][step % 2] * scales[step...]
    another operation x9, other arithmetic: 4.35 us -> 5.56 us
    unnamed x13 -> x15, local copies, waits for them, and re-layouts: 10.9 us -> 11.9 us
  transfers between devices with their start and end apart: 16 -> 16, of which waited for: 5 -> 5; matrix products, arithmetic and copies ran while one was open for 14% -> 15% of each run, Pallas kernels for 17% -> 17%
where the time goes in v9:
time: 111 us; the launch traced here: 110 us
  starting transfers between devices  33.6 us (30%)
  Pallas kernels  31.8 us (29%)
  waiting for transfers between devices  22.1 us (20%)
  local copies, waits for them, and re-layouts  15 us (14%)
  other arithmetic  6.3 us (6%)
    ppermute x12, starting transfers between devices, reduce_send(): lax.ppermute(send, 'dp', [(i, i ^ PARTNERS[i & 1][step % 2] * scales[step...  21.8 us
    ppermute x12, waiting for transfers between devices, reduce_send(): lax.ppermute(send, 'dp', [(i, i ^ PARTNERS[i & 1][step % 2] * scales[step...  15.7 us
    unnamed x15, local copies, waits for them, and re-layouts  11.9 us
    pallas_call x1, Pallas kernels, local(): pl.pallas_call(main_kernel, out_shape=[shape((width, samples)), shape((wi...  10.7 us
    pallas_call x3, Pallas kernels, gradients(): pl.pallas_call(functools.partial(grad_kernel, x_first, at, block), out_sh...  10.3 us
    all_to_all x1, starting transfers between devices, local(): lax.all_to_all(packed, 'token', split_axis=0, concat_axis=0, tiled=True)  6.27 us
    pallas_call x1, Pallas kernels, local(): pl.pallas_call(input_kernel, out_shape=[shape((samples, width), F32), pac...  5.74 us
    another operation x9, other arithmetic  5.56 us
  transfers between devices with their start and end apart: 16, of which 5 were waited for; matrix products, arithmetic and copies ran while one was open for 15% of the time, Pallas kernels for 17%

profile of v9, /device:TPU:8, one launch (start us, length us, event | category | flops | bytes accessed | tf_op | source)
XLA Modules:
  0.0 109.7 jit_solution(5836723346710523771)
XLA Ops:
  0.6 2.3 %pack.1 = bf16[8,384,128]{2,1,0:T(8,128)(2,1)} custom-call(bf16[256,1536]{1,0:T(8,128)(2,1)} %bitcast.11), custom_call_target="tpu_custom_call" | custom-call | flops 393216 | bytes 1572864 | tf_op jit(solution)/shard_map/pack/pallas_call | solution.py:316
  2.9 6.3 %all-to-all-start = ((bf16[8,384,128]{2,1,0:T(8,128)(2,1)}), bf16[8,384,128]{2,1,0:T(8,128)(2,1)S(1)}, u32[]{:S(2)}, u32[]{:S(2)}) async-start(bf16[8,384,128]{2,1,0:T(8,128)(2,1)} %pack.1), calls=%async_computation | async-start | bytes 1572864 | tf_op jit(solution)/shard_map/all_to_all | solution.py:320
  9.2 8.0 %copy.7 = bf16[192,8,2,1024]{3,1,2,0:T(8,128)(2,1)} copy(bf16[192,8,2,1024]{3,2,1,0:T(2,128)(2,1)} %bitcast.9) | data formatting | bytes 12582912
  17.2 2.8 %all-to-all-done.recv_ref = bf16[8,384,128]{2,1,0:T(8,128)(2,1)S(1)} async-done(((bf16[8,384,128]{2,1,0:T(8,128)(2,1)}), bf16[8,384,128]{2,1,0:T(8,128)(2,1)S(1)}, u32[]{:S(2)}, u32[]{:S(2)}) %all-to-all-start) | async-done | bytes 786464 | tf_op jit(solution)/shard_map/all_to_all | solution.py:320
  20.0 0.0 copy-start.2
  20.0 0.9 copy-done.2
  20.9 10.7 %main.1 = (bf16[1536,256]{1,0:T(8,128)(2,1)}, bf16[2560,256]{1,0:T(8,128)(2,1)}, bf16[2048,256]{1,0:T(8,128)(2,1)}, bf16[256,1536]{1,0:T(8,128)(2,1)}, bf16[1536,2048]{1,0:T(8,128)(2,1)S(1)}) custom-call(s32[1]{0:T(128)} %bitcast.index_ref, bf16[256,1536]{1,0:T(8,128)(2,1)} %bitcast.12, bf16[8,384,128]{2,1,0:T(8,128)(2,1)} %copy-done.2, ...), custom_call_target="tpu_custom_call" | custom-call | flops 3221225472 | bytes 18000000 | tf_op jit(solution)/shard_map/main/pallas_call | solution.py:323
  31.6 0.1 collective-permute-start
  31.7 0.5 collective-permute-start.1
  32.2 3.6 %collective-permute-done.other_hbm.right_other_hbm = bf16[2560,256]{1,0:T(8,128)(2,1)S(1)} collective-permute-done((bf16[2560,256]{1,0:T(8,128)(2,1)}, bf16[2560,256]{1,0:T(8,128)(2,1)S(1)}, u32[]{:S(2)}, u32[]{:S(2)}) %collective-permute-start) | collective-permute-done | bytes 1310752 | tf_op jit(solution)/shard_map/ppermute | solution.py:272
  35.8 0.0 copy-start
  35.8 1.1 copy-done
  36.9 3.4 %down_grads.1 = (bf16[384,1024]{1,0:T(8,128)(2,1)}, bf16[384,1024]{1,0:T(8,128)(2,1)}) custom-call(bf16[1536,256]{1,0:T(8,128)(2,1)} %get-tuple-element.29.own_hbm, bf16[2560,256]{1,0:T(8,128)(2,1)} %copy-done, bf16[2560,256]{1,0:T(8,128)(2,1)} %get-tuple-element.30.right_hbm, bf16[2560,256]{1,0:T(8,128)(2,1)} %copy-done, ...), custom_call_target="tpu_custom_call" | custom-call | flops 805306368 | bytes 3407872 | tf_op jit(solution)/shard_map/down_grads/pallas_call | solution.py:279
  40.2 1.8 %collective-permute-start.4 = (bf16[384,1024]{1,0:T(8,128)(2,1)}, bf16[384,1024]{1,0:T(8,128)(2,1)}, u32[]{:S(2)}, u32[]{:S(2)}) collective-permute-start(bf16[384,1024]{1,0:T(8,128)(2,1)} %get-tuple-element.32.after_hbm), channel_id=1, source_target_pairs={{0,16},{8,56},{16,0},{24,40},{32,48},{40,24},{48,32},{56,8},{64,80... | collective-permute-start | bytes 2359304 | tf_op jit(solution)/shard_map/ppermute | solution.py:295
  42.0 0.0 collective-permute-done.1.right_other_hbm
  42.0 3.2 %low_grads.1 = (bf16[384,768]{1,0:T(8,128)(2,1)}, bf16[384,768]{1,0:T(8,128)(2,1)}) custom-call(bf16[1536,256]{1,0:T(8,128)(2,1)} %get-tuple-element.29.own_hbm, bf16[2560,256]{1,0:T(8,128)(2,1)} %copy-done, bf16[2048,256]{1,0:T(8,128)(2,1)} %get-tuple-element.31.after_hbm.right_hbm.inner_ref, bf16[2048,256]{1,0:T(8,128)(2,1)} %collective-permute-done.1.right_other_hbm, ...), custom_call_target="tpu_custom_call" | custom-call | flops 603979776 | bytes 2752512 | tf_op jit(solution)/shard_map/low_grads/pallas_call | solution.py:279
  45.2 3.8 %high_grads.1 = (bf16[384,1280]{1,0:T(8,128)(2,1)}, bf16[384,1280]{1,0:T(8,128)(2,1)}) custom-call(bf16[1536,256]{1,0:T(8,128)(2,1)} %get-tuple-element.29.own_hbm, bf16[2560,256]{1,0:T(8,128)(2,1)} %copy-done, bf16[2048,256]{1,0:T(8,128)(2,1)} %get-tuple-element.31.after_hbm.right_hbm.inner_ref, bf16[2048,256]{1,0:T(8,128)(2,1)} %collective-permute-done.1.right_other_hbm, ...), custom_call_target="tpu_custom_call" | custom-call | flops 1006632960 | bytes 4063232 | tf_op jit(solution)/shard_map/high_grads/pallas_call | solution.py:279
  49.0 0.6 collective-permute-start.2
  49.6 3.3 %collective-permute-start.3 = (bf16[384,768]{1,0:T(8,128)(2,1)}, bf16[384,768]{1,0:T(8,128)(2,1)}, u32[]{:S(2)}, u32[]{:S(2)}) collective-permute-start(bf16[384,768]{1,0:T(8,128)(2,1)} %get-tuple-element.33.after_hbm), channel_id=1, source_target_pairs={{0,64},{8,200},{16,80},{24,216},{32,96},{40,232},{48,112},{56,248}... | collective-permute-start | bytes 1769480 | tf_op jit(solution)/shard_map/ppermute | solution.py:295
  52.9 5.7 %input.1 = (f32[256,1536]{1,0:T(8,128)}, bf16[8,384,128]{2,1,0:T(8,128)(2,1)}) custom-call(bf16[2048,256]{1,0:T(8,128)(2,1)} %get-tuple-element.31.after_hbm.right_hbm.inner_ref, bf16[1536,2048]{1,0:T(8,128)(2,1)S(1)} %get-tuple-element.44.w_in, bf16[256,1536]{1,0:T(8,128)(2,1)} %bitcast.13, bf16[8,384,128]{2,1,0:T(8,128)(2,1)} %copy-done.2, ...), custom_call_target="tpu_custom_call" | custom-call | flops 1610612736 | bytes 14000000 | tf_op jit(solution)/shard_map/input/pallas_call | solution.py:360
  58.6 4.9 %all-to-all-start.1 = ((bf16[8,384,128]{2,1,0:T(8,128)(2,1)}), bf16[8,384,128]{2,1,0:T(8,128)(2,1)S(1)}, u32[]{:S(2)}, u32[]{:S(2)}) async-start(bf16[8,384,128]{2,1,0:T(8,128)(2,1)} %get-tuple-element.47), calls=%async_computation.1 | async-start | bytes 1572864 | tf_op jit(solution)/shard_map/all_to_all | solution.py:373
  63.6 0.0 collective-permute-done.4
  63.6 0.0 copy-done.5
  63.6 0.0 copy-start.6
  63.6 1.5 %add_convert_fusion.1 = bf16[384,1024]{1,0:T(8,128)(2,1)S(1)} fusion(bf16[384,1024]{1,0:T(8,128)(2,1)} %collective-permute-done.4, bf16[384,1024]{1,0:T(8,128)(2,1)S(1)} %copy-done.5), kind=kLoop, calls=%fused_computation.1 | loop fusion | flops 1572864 | bytes 2359296 | tf_op jit(solution)/shard_map/convert.17
  65.1 0.0 copy-start.3
  65.1 2.8 %collective-permute-start.6 = (bf16[192,1024]{1,0:T(8,128)(2,1)S(1)}, bf16[192,1024]{1,0:T(8,128)(2,1)S(1)}, u32[]{:S(2)}, u32[]{:S(2)}) collective-permute-start(bf16[192,1024]{1,0:T(8,128)(2,1)S(1)} %slice.90), channel_id=1, source_target_pairs={{0,48},{8,24},{16,32},{24,8},{32,16},{40,56},{48,0},{56,40},{64,11... | collective-permute-start | bytes 1179656 | tf_op jit(solution)/shard_map/ppermute | solution.py:295
  68.0 0.0 collective-permute-done.3
  68.0 0.0 copy-done.6
  68.0 1.2 %add_convert_fusion.2 = bf16[384,768]{1,0:T(8,128)(2,1)S(1)} fusion(bf16[384,768]{1,0:T(8,128)(2,1)} %collective-permute-done.3, bf16[384,768]{1,0:T(8,128)(2,1)S(1)} %copy-done.6), kind=kLoop, calls=%fused_computation.2 | loop fusion | flops 1179648 | bytes 1769472 | tf_op jit(solution)/shard_map/convert.16
  69.2 0.8 slice.91
  69.9 0.0 collective-permute-done.2
  69.9 1.0 copy-done.4
  70.9 0.0 copy-done.3
  70.9 1.5 %add_convert_fusion = bf16[384,1280]{1,0:T(8,128)(2,1)S(1)} fusion(bf16[384,1280]{1,0:T(8,128)(2,1)} %copy-done.4, bf16[384,1280]{1,0:T(8,128)(2,1)S(1)} %copy-done.3), kind=kLoop, calls=%fused_computation | loop fusion | flops 1966080 | bytes 2949120 | tf_op jit(solution)/shard_map/convert.15
  72.4 0.8 slice.93
  73.2 2.3 %collective-permute-start.5 = (bf16[192,1280]{1,0:T(8,128)(2,1)}, bf16[192,1280]{1,0:T(8,128)(2,1)S(1)}, u32[]{:S(2)}, u32[]{:S(2)}) collective-permute-start(bf16[192,1280]{1,0:T(8,128)(2,1)} %slice.93), channel_id=1, source_target_pairs={{0,48},{8,24},{16,32},{24,8},{32,16},{40,56},{48,0},{56,40},{64,11... | collective-permute-start | bytes 1474568 | tf_op jit(solution)/shard_map/ppermute | solution.py:295
  75.5 1.8 %collective-permute-start.8 = (bf16[192,768]{1,0:T(8,128)(2,1)}, bf16[192,768]{1,0:T(8,128)(2,1)S(1)}, u32[]{:S(2)}, u32[]{:S(2)}) collective-permute-start(bf16[192,768]{1,0:T(8,128)(2,1)} %slice.91), channel_id=1, source_target_pairs={{0,192},{8,72},{16,208},{24,88},{32,224},{40,104},{48,240},{56,120... | collective-permute-start | bytes 884744 | tf_op jit(solution)/shard_map/ppermute | solution.py:295
  77.3 0.0 collective-permute-done.6
  77.3 0.1 add_convert_fusion.4
  77.4 0.7 slice.95
  78.1 2.6 %collective-permute-start.10 = (bf16[96,1024]{1,0:T(8,128)(2,1)}, bf16[96,1024]{1,0:T(8,128)(2,1)}, u32[]{:S(2)}, u32[]{:S(2)}) collective-permute-start(bf16[96,1024]{1,0:T(8,128)(2,1)} %slice.95), channel_id=1, source_target_pairs={{0,64},{8,200},{16,80},{24,216},{32,96},{40,232},{48,112},{56,248}... | collective-permute-start | bytes 589832 | tf_op jit(solution)/shard_map/ppermute | solution.py:295
  80.7 0.0 all-to-all-done.1.recv_ref
  80.7 0.9 copy-done.1
  81.6 2.8 %final.1 = bf16[256,1536]{1,0:T(8,128)(2,1)} custom-call(f32[256,1536]{1,0:T(8,128)} %get-tuple-element.46.pre_ref, bf16[8,384,128]{2,1,0:T(8,128)(2,1)} %copy-done.1), custom_call_target="tpu_custom_call" | custom-call | flops 393216 | bytes 3145728 | tf_op jit(solution)/shard_map/final/pallas_call | solution.py:375
  84.4 0.0 collective-permute-done.5
  84.4 0.1 add_convert_fusion.3
  84.5 0.4 collective-permute-start.7
  84.9 1.8 %collective-permute-done.8 = bf16[192,768]{1,0:T(8,128)(2,1)S(1)} collective-permute-done((bf16[192,768]{1,0:T(8,128)(2,1)}, bf16[192,768]{1,0:T(8,128)(2,1)S(1)}, u32[]{:S(2)}, u32[]{:S(2)}) %collective-permute-start.8) | collective-permute-done | bytes 294944 | tf_op jit(solution)/shard_map/ppermute | solution.py:295
  86.7 0.1 add_convert_fusion.5
  86.8 0.1 collective-permute-start.9
  86.9 9.3 %collective-permute-done.7 = bf16[96,1280]{1,0:T(8,128)(2,1)S(1)} collective-permute-done((bf16[96,1280]{1,0:T(8,128)(2,1)S(1)}, bf16[96,1280]{1,0:T(8,128)(2,1)S(1)}, u32[]{:S(2)}, u32[]{:S(2)}) %collective-permute-start.7) | collective-permute-done | bytes 245792 | tf_op jit(solution)/shard_map/ppermute | solution.py:295
  96.2 0.1 add_convert_fusion.6
  96.3 3.9 %collective-permute-start.13 = (bf16[48,1280]{1,0:T(8,128)(2,1)S(1)}, bf16[48,1280]{1,0:T(8,128)(2,1)S(1)}, u32[]{:S(2)}, u32[]{:S(2)}) collective-permute-start(bf16[48,1280]{1,0:T(8,128)(2,1)S(1)} %slice.102), channel_id=1, source_target_pairs={{0,192},{8,72},{16,208},{24,88},{32,224},{40,104},{48,240},{56,120... | collective-permute-start | bytes 368648 | tf_op jit(solution)/shard_map/ppermute | solution.py:295
  100.2 0.0 collective-permute-done.10
  100.2 1.0 add_convert_fusion.7
  101.2 0.4 collective-permute-start.12
  101.6 0.0 collective-permute-done.9
  101.6 1.9 %collective-permute-start.11 = (bf16[48,768]{1,0:T(8,128)(2,1)S(1)}, bf16[48,768]{1,0:T(8,128)(2,1)S(1)}, u32[]{:S(2)}, u32[]{:S(2)}) collective-permute-start(bf16[48,768]{1,0:T(8,128)(2,1)S(1)} %slice.105), channel_id=1, source_target_pairs={{0,48},{8,24},{16,32},{24,8},{32,16},{40,56},{48,0},{56,40},{64,11... | collective-permute-start | bytes 221192 | tf_op jit(solution)/shard_map/ppermute | solution.py:295
  103.5 4.6 %collective-permute-done.12 = bf16[48,1024]{1,0:T(8,128)(2,1)S(1)} collective-permute-done((bf16[48,1024]{1,0:T(8,128)(2,1)S(1)}, bf16[48,1024]{1,0:T(8,128)(2,1)S(1)}, u32[]{:S(2)}, u32[]{:S(2)}) %collective-permute-start.12) | collective-permute-done | bytes 98336 | tf_op jit(solution)/shard_map/ppermute | solution.py:295
  108.1 0.7 add_convert_fusion.10
  108.8 0.0 collective-permute-done.11
  108.8 0.0 collective-permute-done.13
  108.9 0.8 broadcast_in_dim_reshape.3
  (13 shorter events, 0.2 us)
Async XLA Ops:
  2.9 17.1 %all-to-all-start = ((bf16[8,384,128]{2,1,0:T(8,128)(2,1)}), bf16[8,384,128]{2,1,0:T(8,128)(2,1)S(1)}, u32[]{:S(2)}, u32[]{:S(2)}) async-start(bf16[8,384,128]{2,1,0:T(8,128)(2,1)} %pack.1), calls=%async_computation | async-start | bytes 1572864 | tf_op jit(solution)/shard_map/all_to_all | solution.py:320
  20.0 0.9 copy-start.2
  31.6 4.2 %collective-permute-start = (bf16[2560,256]{1,0:T(8,128)(2,1)}, bf16[2560,256]{1,0:T(8,128)(2,1)S(1)}, u32[]{:S(2)}, u32[]{:S(2)}) collective-permute-start(bf16[2560,256]{1,0:T(8,128)(2,1)} %get-tuple-element.30.right_hbm), channel_id=1, source_target_pairs={{0,8},{8,0},{16,24},{24,16},{32,40},{40,32},{48,56},{56,48},{64,72... | collective-permute-start | bytes 3932168 | tf_op jit(solution)/shard_map/ppermute | solution.py:272
  31.7 10.3 %collective-permute-start.1 = (bf16[2048,256]{1,0:T(8,128)(2,1)}, bf16[2048,256]{1,0:T(8,128)(2,1)}, u32[]{:S(2)}, u32[]{:S(2)}) collective-permute-start(bf16[2048,256]{1,0:T(8,128)(2,1)} %get-tuple-element.31.after_hbm.right_hbm.inner_ref), channel_id=1, source_target_pairs={{0,8},{8,0},{16,24},{24,16},{32,40},{40,32},{48,56},{56,48},{64,72... | collective-permute-start | bytes 3145736 | tf_op jit(solution)/shard_map/ppermute | solution.py:272
  35.8 1.1 copy-start
  40.2 23.3 %collective-permute-start.4 = (bf16[384,1024]{1,0:T(8,128)(2,1)}, bf16[384,1024]{1,0:T(8,128)(2,1)}, u32[]{:S(2)}, u32[]{:S(2)}) collective-permute-start(bf16[384,1024]{1,0:T(8,128)(2,1)} %get-tuple-element.32.after_hbm), channel_id=1, source_target_pairs={{0,16},{8,56},{16,0},{24,40},{32,48},{40,24},{48,32},{56,8},{64,80... | collective-permute-start | bytes 2359304 | tf_op jit(solution)/shard_map/ppermute | solution.py:295
  49.0 20.9 %collective-permute-start.2 = (bf16[384,1280]{1,0:T(8,128)(2,1)}, bf16[384,1280]{1,0:T(8,128)(2,1)S(1)}, u32[]{:S(2)}, u32[]{:S(2)}) collective-permute-start(bf16[384,1280]{1,0:T(8,128)(2,1)} %get-tuple-element.35.after_ref), channel_id=1, source_target_pairs={{0,16},{8,56},{16,0},{24,40},{32,48},{40,24},{48,32},{56,8},{64,80... | collective-permute-start | bytes 2949128 | tf_op jit(solution)/shard_map/ppermute | solution.py:295
  49.6 18.4 %collective-permute-start.3 = (bf16[384,768]{1,0:T(8,128)(2,1)}, bf16[384,768]{1,0:T(8,128)(2,1)}, u32[]{:S(2)}, u32[]{:S(2)}) collective-permute-start(bf16[384,768]{1,0:T(8,128)(2,1)} %get-tuple-element.33.after_hbm), channel_id=1, source_target_pairs={{0,64},{8,200},{16,80},{24,216},{32,96},{40,232},{48,112},{56,248}... | collective-permute-start | bytes 1769480 | tf_op jit(solution)/shard_map/ppermute | solution.py:295
  58.6 4.9 %copy-start.5 = (bf16[384,1024]{1,0:T(8,128)(2,1)S(1)}, bf16[384,1024]{1,0:T(8,128)(2,1)}, u32[]{:S(2)}) copy-start(bf16[384,1024]{1,0:T(8,128)(2,1)} %get-tuple-element.37) | copy-start | bytes 2359300
  58.6 22.1 %all-to-all-start.1 = ((bf16[8,384,128]{2,1,0:T(8,128)(2,1)}), bf16[8,384,128]{2,1,0:T(8,128)(2,1)S(1)}, u32[]{:S(2)}, u32[]{:S(2)}) async-start(bf16[8,384,128]{2,1,0:T(8,128)(2,1)} %get-tuple-element.47), calls=%async_computation.1 | async-start | bytes 1572864 | tf_op jit(solution)/shard_map/all_to_all | solution.py:373
  63.6 4.4 %copy-start.6 = (bf16[384,768]{1,0:T(8,128)(2,1)S(1)}, bf16[384,768]{1,0:T(8,128)(2,1)}, u32[]{:S(2)}) copy-start(bf16[384,768]{1,0:T(8,128)(2,1)} %get-tuple-element.36) | copy-start | bytes 1769476
  65.1 5.8 %copy-start.3 = (bf16[384,1280]{1,0:T(8,128)(2,1)S(1)}, bf16[384,1280]{1,0:T(8,128)(2,1)}, u32[]{:S(2)}) copy-start(bf16[384,1280]{1,0:T(8,128)(2,1)} %get-tuple-element.34) | copy-start | bytes 2949124
  65.1 12.1 %collective-permute-start.6 = (bf16[192,1024]{1,0:T(8,128)(2,1)S(1)}, bf16[192,1024]{1,0:T(8,128)(2,1)S(1)}, u32[]{:S(2)}, u32[]{:S(2)}) collective-permute-start(bf16[192,1024]{1,0:T(8,128)(2,1)S(1)} %slice.90), channel_id=1, source_target_pairs={{0,48},{8,24},{16,32},{24,8},{32,16},{40,56},{48,0},{56,40},{64,11... | collective-permute-start | bytes 1179656 | tf_op jit(solution)/shard_map/ppermute | solution.py:295
  69.9 1.0 copy-start.4
  73.2 11.2 %collective-permute-start.5 = (bf16[192,1280]{1,0:T(8,128)(2,1)}, bf16[192,1280]{1,0:T(8,128)(2,1)S(1)}, u32[]{:S(2)}, u32[]{:S(2)}) collective-permute-start(bf16[192,1280]{1,0:T(8,128)(2,1)} %slice.93), channel_id=1, source_target_pairs={{0,48},{8,24},{16,32},{24,8},{32,16},{40,56},{48,0},{56,40},{64,11... | collective-permute-start | bytes 1474568 | tf_op jit(solution)/shard_map/ppermute | solution.py:295
  75.5 11.2 %collective-permute-start.8 = (bf16[192,768]{1,0:T(8,128)(2,1)}, bf16[192,768]{1,0:T(8,128)(2,1)S(1)}, u32[]{:S(2)}, u32[]{:S(2)}) collective-permute-start(bf16[192,768]{1,0:T(8,128)(2,1)} %slice.91), channel_id=1, source_target_pairs={{0,192},{8,72},{16,208},{24,88},{32,224},{40,104},{48,240},{56,120... | collective-permute-start | bytes 884744 | tf_op jit(solution)/shard_map/ppermute | solution.py:295
  78.1 22.1 %collective-permute-start.10 = (bf16[96,1024]{1,0:T(8,128)(2,1)}, bf16[96,1024]{1,0:T(8,128)(2,1)}, u32[]{:S(2)}, u32[]{:S(2)}) collective-permute-start(bf16[96,1024]{1,0:T(8,128)(2,1)} %slice.95), channel_id=1, source_target_pairs={{0,64},{8,200},{16,80},{24,216},{32,96},{40,232},{48,112},{56,248}... | collective-permute-start | bytes 589832 | tf_op jit(solution)/shard_map/ppermute | solution.py:295
  80.7 0.9 copy-start.1
  84.5 11.7 %collective-permute-start.7 = (bf16[96,1280]{1,0:T(8,128)(2,1)S(1)}, bf16[96,1280]{1,0:T(8,128)(2,1)S(1)}, u32[]{:S(2)}, u32[]{:S(2)}) collective-permute-start(bf16[96,1280]{1,0:T(8,128)(2,1)S(1)} %slice.96), channel_id=1, source_target_pairs={{0,64},{8,200},{16,80},{24,216},{32,96},{40,232},{48,112},{56,248}... | collective-permute-start | bytes 737288 | tf_op jit(solution)/shard_map/ppermute | solution.py:295
  86.8 14.8 %collective-permute-start.9 = (bf16[96,768]{1,0:T(8,128)(2,1)S(1)}, bf16[96,768]{1,0:T(8,128)(2,1)S(1)}, u32[]{:S(2)}, u32[]{:S(2)}) collective-permute-start(bf16[96,768]{1,0:T(8,128)(2,1)S(1)} %slice.98), channel_id=1, source_target_pairs={{0,16},{8,56},{16,0},{24,40},{32,48},{40,24},{48,32},{56,8},{64,80... | collective-permute-start | bytes 442376 | tf_op jit(solution)/shard_map/ppermute | solution.py:295
  96.3 12.5 %collective-permute-start.13 = (bf16[48,1280]{1,0:T(8,128)(2,1)S(1)}, bf16[48,1280]{1,0:T(8,128)(2,1)S(1)}, u32[]{:S(2)}, u32[]{:S(2)}) collective-permute-start(bf16[48,1280]{1,0:T(8,128)(2,1)S(1)} %slice.102), channel_id=1, source_target_pairs={{0,192},{8,72},{16,208},{24,88},{32,224},{40,104},{48,240},{56,120... | collective-permute-start | bytes 368648 | tf_op jit(solution)/shard_map/ppermute | solution.py:295
  101.2 6.9 %collective-permute-start.12 = (bf16[48,1024]{1,0:T(8,128)(2,1)S(1)}, bf16[48,1024]{1,0:T(8,128)(2,1)S(1)}, u32[]{:S(2)}, u32[]{:S(2)}) collective-permute-start(bf16[48,1024]{1,0:T(8,128)(2,1)S(1)} %slice.103), channel_id=1, source_target_pairs={{0,192},{8,72},{16,208},{24,88},{32,224},{40,104},{48,240},{56,120... | collective-permute-start | bytes 294920 | tf_op jit(solution)/shard_map/ppermute | solution.py:295
  101.6 7.1 %collective-permute-start.11 = (bf16[48,768]{1,0:T(8,128)(2,1)S(1)}, bf16[48,768]{1,0:T(8,128)(2,1)S(1)}, u32[]{:S(2)}, u32[]{:S(2)}) collective-permute-start(bf16[48,768]{1,0:T(8,128)(2,1)S(1)} %slice.105), channel_id=1, source_target_pairs={{0,48},{8,24},{16,32},{24,8},{32,16},{40,56},{48,0},{56,40},{64,11... | collective-permute-start | bytes 221192 | tf_op jit(solution)/shard_map/ppermute | solution.py:295

commit v10 on v5

--- a/solution.py
+++ b/solution.py
@@ -84,8 +84,8 @@
 
 def main_kernel(
     index_ref, x_ref, recv_ref, cot_hbm, w_in_hbm, w_out_hbm,
-    own_hbm, send_hbm, inner_hbm, grad16_hbm,
-    w_in, w_out, cot, state, grad16, hidden, values, slope, silu, turned, own, send, inner,
+    own_hbm, send_hbm, inner_hbm, grad16_hbm, w_in,
+    w_out, cot, state, grad16, hidden, values, slope, silu, turned, own, send, inner,
     in_sem, out_sem, cot_sem, write_sem,
 ):
     samples, width = x_ref.shape
@@ -184,24 +184,17 @@
 
 
 def input_kernel(
-    inner_ref, w_in_hbm, x_ref, recv_ref, grad_ref, after_ref, pre_ref, packed_ref, w_in, inner, normed, sem
+    inner_ref, w_in, x_ref, recv_ref, grad_ref, after_ref, pre_ref, packed_ref, inner, normed
 ):
     del after_ref
     samples, width = x_ref.shape
     wide = 256
 
-    def copy(d):
-        rows = pl.ds(d * wide, wide)
-        return pltpu.make_async_copy(w_in_hbm.at[rows], w_in.at[rows], sem.at[d])
-
-    for d in range(width // wide):
-        copy(d).start()
     scale = norm_state(x_ref, recv_ref, normed)
     for j in range(inner.shape[1] // samples):
         inner[:, samples * j : samples * j + samples] = inner_ref[samples * j : samples * j + samples, :]
     products = jnp.zeros((samples, 128), F32)
     for d in range(width // wide):
-        copy(d).wait()
         cols = slice(wide * d, wide * d + wide)
         g = nt(inner[...], w_in[cols, :]) + grad_ref[:, cols].astype(F32)
         pre_ref[:, cols] = g
@@ -321,13 +314,12 @@
     recv = lax.all_to_all(packed, "token", split_axis=0, concat_axis=0, tiled=True)
 
     flat = shape((samples, width))
-    own, send, inner, out_grad16 = pl.pallas_call(
+    own, send, inner, out_grad16, held_in = pl.pallas_call(
         main_kernel,
-        out_shape=[shape((width, samples)), shape((width + ff, samples)), shape((2 * ff, samples)), flat],
+        out_shape=[shape((width, samples)), shape((width + ff, samples)), shape((2 * ff, samples)), flat, pltpu.VMEM((width, 2 * ff), BF16)],
         in_specs=[SMEM, VMEM, VMEM, ANY, ANY, ANY],
-        out_specs=[ANY] * 4,
+        out_specs=[ANY] * 4 + [VMEM],
         scratch_shapes=[
-            pltpu.VMEM((width, 2 * ff), BF16),
             pltpu.VMEM((width, ff), BF16),
             pltpu.VMEM((samples, width), BF16),
             pltpu.VMEM((samples, width), BF16),
@@ -361,18 +353,16 @@
     pre_grad, back = pl.pallas_call(
         input_kernel,
         out_shape=[shape((samples, width), F32), packed_shape],
-        in_specs=[VMEM, ANY, VMEM, VMEM, VMEM, ANY],
+        in_specs=[VMEM] * 5 + [ANY],
         out_specs=[VMEM] * 2,
         scratch_shapes=[
-            pltpu.VMEM((width, 2 * ff), BF16),
             pltpu.VMEM((samples, 2 * ff), BF16),
             pltpu.VMEM((samples, width), F32),
-            pltpu.SemaphoreType.DMA((width // 256,)),
         ],
         compiler_params=params(),
         cost_estimate=cost(4 * samples * width * ff, 14e6),
         name="input",
-    )(inner, flat_in, x, recv, out_grad16, up[1])
+    )(inner, pltpu.with_memory_space_constraint(held_in, pltpu.VMEM), x, recv, out_grad16, up[1])
     returned = lax.all_to_all(back, "token", split_axis=0, concat_axis=0, tiled=True)
 
     input_grad = pl.pallas_call(
@@ -381,11 +371,11 @@
     )(pre_grad, returned)
 
     previous = None
-    for which, step in ((0, 0), (1, 0), (0, 1), (2, 0), (1, 1), (0, 2), (2, 1), (1, 2), (0, 3), (2, 2), (1, 3), (2, 3)):
+    for which, step in ((0, 0), (1, 0), (0, 1), (2, 0), (1, 1), (2, 1), (0, 2), (1, 2), (2, 2), (0, 3), (1, 3), (2, 3)):
         arrived = got[which]
         if previous is not None:
             arrived, previous = lax.optimization_barrier((arrived, previous))
-        if (which, step) == (0, 3):
+        if (which, step) == (2, 2):
             arrived, input_grad = lax.optimization_barrier((arrived, input_grad))
         kept[which], sent = reduce_add(step, kept[which], arrived)
         previous = kept[which] if sent is None else sent

time: 110 us -> 110 us (level)
  starting transfers between devices: 38.3 us -> 43.1 us
  Pallas kernels: 34.9 us -> 31.5 us
  waiting for transfers between devices: 17.3 us -> 14.2 us
  other arithmetic: 4.32 us -> 6.39 us
    ppermute x12, starting transfers between devices: 26.5 us -> 31.3 us  [reduce_send(): lax.ppermute(send, 'dp', [(i, i ^ PARTNERS[i & 1][step % 2] * SCALES[step...]
    ppermute x12, waiting for transfers between devices: 11.7 us -> 7.81 us  [reduce_send(): lax.ppermute(send, 'dp', [(i, i ^ PARTNERS[i & 1][step % 2] * SCALES[step...]
    pallas_call x1, Pallas kernels: 9.27 us -> 5.75 us  [local(): pl.pallas_call(input_kernel, out_shape=[shape((samples, width), F32), pac...]
    another operation x9, other arithmetic: 3.58 us -> 5.65 us
    unnamed x16 -> x14, local copies, waits for them, and re-layouts: 12.8 us -> 11.8 us
  transfers between devices with their start and end apart: 16 -> 16, of which waited for: 6 -> 4; matrix products, arithmetic and copies ran while one was open for 11% -> 13% of each run, Pallas kernels for 20% -> 17%
where the time goes in v10:
time: 110 us; the launch traced here: 108 us
  starting transfers between devices  43.1 us (39%)
  Pallas kernels  31.5 us (29%)
  waiting for transfers between devices  14.2 us (13%)
  local copies, waits for them, and re-layouts  11.9 us (11%)
  other arithmetic  6.39 us (6%)
    ppermute x12, starting transfers between devices, reduce_send(): lax.ppermute(send, 'dp', [(i, i ^ PARTNERS[i & 1][step % 2] * SCALES[step...  31.3 us
    unnamed x14, local copies, waits for them, and re-layouts  11.8 us
    pallas_call x1, Pallas kernels, local(): pl.pallas_call(main_kernel, out_shape=[shape((width, samples)), shape((wi...  10.7 us
    pallas_call x3, Pallas kernels, gradients(): pl.pallas_call(functools.partial(grad_kernel, at, block), out_shape=[piec...  9.97 us
    ppermute x12, waiting for transfers between devices, reduce_send(): lax.ppermute(send, 'dp', [(i, i ^ PARTNERS[i & 1][step % 2] * SCALES[step...  7.81 us
    all_to_all x1, starting transfers between devices, local(): lax.all_to_all(packed, 'token', split_axis=0, concat_axis=0, tiled=True)  6.27 us
    pallas_call x1, Pallas kernels, local(): pl.pallas_call(input_kernel, out_shape=[shape((samples, width), F32), pac...  5.75 us
    another operation x9, other arithmetic  5.65 us
  transfers between devices with their start and end apart: 16, of which 4 were waited for; matrix products, arithmetic and copies ran while one was open for 13% of the time, Pallas kernels for 17%

profile of v10, /device:TPU:8, one launch (start us, length us, event | category | flops | bytes accessed | tf_op | source)
XLA Modules:
  0.0 108.0 jit_solution(13151782129600614779)
XLA Ops:
  0.6 2.3 %pack.1 = bf16[8,384,128]{2,1,0:T(8,128)(2,1)} custom-call(bf16[256,1536]{1,0:T(8,128)(2,1)} %bitcast.16), custom_call_target="tpu_custom_call" | custom-call | flops 393216 | bytes 1572864 | tf_op jit(solution)/shard_map/pack/pallas_call | solution.py:310
  2.9 6.3 %all-to-all-start = ((bf16[8,384,128]{2,1,0:T(8,128)(2,1)}), bf16[8,384,128]{2,1,0:T(8,128)(2,1)S(1)}, u32[]{:S(2)}, u32[]{:S(2)}) async-start(bf16[8,384,128]{2,1,0:T(8,128)(2,1)} %pack.1), calls=%async_computation | async-start | bytes 1572864 | tf_op jit(solution)/shard_map/all_to_all | solution.py:314
  9.2 8.0 %copy.8 = bf16[192,8,2,1024]{3,1,2,0:T(8,128)(2,1)} copy(bf16[192,8,2,1024]{3,2,1,0:T(2,128)(2,1)} %bitcast.14) | data formatting | bytes 12582912
  17.2 2.8 %all-to-all-done.recv_ref = bf16[8,384,128]{2,1,0:T(8,128)(2,1)S(1)} async-done(((bf16[8,384,128]{2,1,0:T(8,128)(2,1)}), bf16[8,384,128]{2,1,0:T(8,128)(2,1)S(1)}, u32[]{:S(2)}, u32[]{:S(2)}) %all-to-all-start) | async-done | bytes 786464 | tf_op jit(solution)/shard_map/all_to_all | solution.py:314
  20.0 0.0 copy-start.1
  20.0 0.9 copy-done.1
  20.9 10.7 %main.1 = (bf16[1536,256]{1,0:T(8,128)(2,1)}, bf16[2560,256]{1,0:T(8,128)(2,1)}, bf16[2048,256]{1,0:T(8,128)(2,1)}, bf16[256,1536]{1,0:T(8,128)(2,1)}, bf16[1536,2048]{1,0:T(8,128)(2,1)S(1)}) custom-call(s32[1]{0:T(128)} %bitcast.index_ref, bf16[256,1536]{1,0:T(8,128)(2,1)} %bitcast.17, bf16[8,384,128]{2,1,0:T(8,128)(2,1)} %copy-done.1, ...), custom_call_target="tpu_custom_call" | custom-call | flops 3221225472 | bytes 18000000 | tf_op jit(solution)/shard_map/main/pallas_call | solution.py:317
  31.6 0.1 collective-permute-start
  31.7 0.5 collective-permute-start.1
  32.2 3.6 %collective-permute-done.other_hbm.right_other_hbm = bf16[2560,256]{1,0:T(8,128)(2,1)S(1)} collective-permute-done((bf16[2560,256]{1,0:T(8,128)(2,1)}, bf16[2560,256]{1,0:T(8,128)(2,1)S(1)}, u32[]{:S(2)}, u32[]{:S(2)}) %collective-permute-start) | collective-permute-done | bytes 1310752 | tf_op jit(solution)/shard_map/ppermute | solution.py:266
  35.8 0.0 copy-start
  35.8 1.1 copy-done
  36.9 3.3 %down_grads.1 = (bf16[384,1024]{1,0:T(8,128)(2,1)}, bf16[384,1024]{1,0:T(8,128)(2,1)}) custom-call(bf16[1536,256]{1,0:T(8,128)(2,1)} %get-tuple-element.29.own_hbm, bf16[2560,256]{1,0:T(8,128)(2,1)} %copy-done, bf16[2560,256]{1,0:T(8,128)(2,1)} %get-tuple-element.30.right_hbm, bf16[2560,256]{1,0:T(8,128)(2,1)} %copy-done, ...), custom_call_target="tpu_custom_call" | custom-call | flops 805306368 | bytes 3407872 | tf_op jit(solution)/shard_map/down_grads/pallas_call | solution.py:273
  40.2 1.6 %collective-permute-start.3 = (bf16[384,1024]{1,0:T(8,128)(2,1)}, bf16[384,1024]{1,0:T(8,128)(2,1)}, u32[]{:S(2)}, u32[]{:S(2)}) collective-permute-start(bf16[384,1024]{1,0:T(8,128)(2,1)} %get-tuple-element.32.after_hbm), channel_id=1, source_target_pairs={{0,16},{8,56},{16,0},{24,40},{32,48},{40,24},{48,32},{56,8},{64,80... | collective-permute-start | bytes 2359304 | tf_op jit(solution)/shard_map/ppermute | solution.py:289
  41.7 0.0 collective-permute-done.1.right_other_hbm
  41.8 3.4 %gate_grads.1 = (bf16[384,1024]{1,0:T(8,128)(2,1)}, bf16[384,1024]{1,0:T(8,128)(2,1)}) custom-call(bf16[1536,256]{1,0:T(8,128)(2,1)} %get-tuple-element.29.own_hbm, bf16[2560,256]{1,0:T(8,128)(2,1)} %copy-done, bf16[2048,256]{1,0:T(8,128)(2,1)} %get-tuple-element.31.after_hbm.right_hbm.inner_ref, bf16[2048,256]{1,0:T(8,128)(2,1)} %collective-permute-done.1.right_other_hbm, ...), custom_call_target="tpu_custom_call" | custom-call | flops 805306368 | bytes 3407872 | tf_op jit(solution)/shard_map/gate_grads/pallas_call | solution.py:273
  45.1 0.8 collective-permute-start.5
  45.9 3.3 %up_grads.1 = (bf16[384,1024]{1,0:T(8,128)(2,1)}, bf16[384,1024]{1,0:T(8,128)(2,1)}) custom-call(bf16[1536,256]{1,0:T(8,128)(2,1)} %get-tuple-element.29.own_hbm, bf16[2560,256]{1,0:T(8,128)(2,1)} %copy-done, bf16[2048,256]{1,0:T(8,128)(2,1)} %get-tuple-element.31.after_hbm.right_hbm.inner_ref, bf16[2048,256]{1,0:T(8,128)(2,1)} %collective-permute-done.1.right_other_hbm, ...), custom_call_target="tpu_custom_call" | custom-call | flops 805306368 | bytes 3407872 | tf_op jit(solution)/shard_map/up_grads/pallas_call | solution.py:273
  49.3 1.6 %collective-permute-start.2 = (bf16[384,1024]{1,0:T(8,128)(2,1)}, bf16[384,1024]{1,0:T(8,128)(2,1)S(1)}, u32[]{:S(2)}, u32[]{:S(2)}) collective-permute-start(bf16[384,1024]{1,0:T(8,128)(2,1)} %get-tuple-element.35.after_ref), channel_id=1, source_target_pairs={{0,16},{8,56},{16,0},{24,40},{32,48},{40,24},{48,32},{56,8},{64,80... | collective-permute-start | bytes 2359304 | tf_op jit(solution)/shard_map/ppermute | solution.py:289
  50.8 5.7 %input.1 = (f32[256,1536]{1,0:T(8,128)}, bf16[8,384,128]{2,1,0:T(8,128)(2,1)}) custom-call(bf16[2048,256]{1,0:T(8,128)(2,1)} %get-tuple-element.31.after_hbm.right_hbm.inner_ref, bf16[1536,2048]{1,0:T(8,128)(2,1)S(1)} %get-tuple-element.46.w_in, bf16[256,1536]{1,0:T(8,128)(2,1)} %bitcast.18, bf16[8,384,128]{2,1,0:T(8,128)(2,1)} %copy-done.1, ...), custom_call_target="tpu_custom_call" | custom-call | flops 1610612736 | bytes 14000000 | tf_op jit(solution)/shard_map/input/pallas_call | solution.py:353
  56.6 0.0 copy-start.5
  56.6 4.9 %all-to-all-start.1 = ((bf16[8,384,128]{2,1,0:T(8,128)(2,1)}), bf16[8,384,128]{2,1,0:T(8,128)(2,1)S(1)}, u32[]{:S(2)}, u32[]{:S(2)}) async-start(bf16[8,384,128]{2,1,0:T(8,128)(2,1)} %get-tuple-element.49), calls=%async_computation.1 | async-start | bytes 1572864 | tf_op jit(solution)/shard_map/all_to_all | solution.py:366
  61.5 0.0 collective-permute-done.3
  61.5 0.0 copy-done.5
  61.5 0.0 copy-start.4
  61.5 1.5 %add_convert_fusion.2 = bf16[384,1024]{1,0:T(8,128)(2,1)S(1)} fusion(bf16[384,1024]{1,0:T(8,128)(2,1)} %collective-permute-done.3, bf16[384,1024]{1,0:T(8,128)(2,1)S(1)} %copy-done.5), kind=kLoop, calls=%fused_computation.2 | loop fusion | flops 1572864 | bytes 2359296 | tf_op jit(solution)/shard_map/convert.17
  63.1 2.2 %collective-permute-start.4 = (bf16[192,1024]{1,0:T(8,128)(2,1)S(1)}, bf16[192,1024]{1,0:T(8,128)(2,1)S(1)}, u32[]{:S(2)}, u32[]{:S(2)}) collective-permute-start(bf16[192,1024]{1,0:T(8,128)(2,1)S(1)} %slice.91), channel_id=1, source_target_pairs={{0,48},{8,24},{16,32},{24,8},{32,16},{40,56},{48,0},{56,40},{64,11... | collective-permute-start | bytes 1179656 | tf_op jit(solution)/shard_map/ppermute | solution.py:289
  65.3 0.0 collective-permute-done.5
  65.3 0.0 copy-done.4
  65.3 1.4 %add_convert_fusion.1 = bf16[384,1024]{1,0:T(8,128)(2,1)S(1)} fusion(bf16[384,1024]{1,0:T(8,128)(2,1)} %collective-permute-done.5, bf16[384,1024]{1,0:T(8,128)(2,1)S(1)} %copy-done.4), kind=kLoop, calls=%fused_computation.1 | loop fusion | flops 1572864 | bytes 2359296 | tf_op jit(solution)/shard_map/convert.15
  66.7 0.0 copy-start.3
  66.8 1.2 %collective-permute-start.7 = (bf16[192,1024]{1,0:T(8,128)(2,1)S(1)}, bf16[192,1024]{1,0:T(8,128)(2,1)S(1)}, u32[]{:S(2)}, u32[]{:S(2)}) collective-permute-start(bf16[192,1024]{1,0:T(8,128)(2,1)S(1)} %slice.92), channel_id=1, source_target_pairs={{0,48},{8,24},{16,32},{24,8},{32,16},{40,56},{48,0},{56,40},{64,11... | collective-permute-start | bytes 1179656 | tf_op jit(solution)/shard_map/ppermute | solution.py:289
  68.0 5.9 %collective-permute-done.4 = bf16[192,1024]{1,0:T(8,128)(2,1)S(1)} collective-permute-done((bf16[192,1024]{1,0:T(8,128)(2,1)S(1)}, bf16[192,1024]{1,0:T(8,128)(2,1)S(1)}, u32[]{:S(2)}, u32[]{:S(2)}) %collective-permute-start.4) | collective-permute-done | bytes 393248 | tf_op jit(solution)/shard_map/ppermute | solution.py:289
  73.9 0.1 add_convert_fusion.5
  74.1 0.0 collective-permute-done.2
  74.1 0.0 copy-done.3
  74.1 0.3 add_convert_fusion
  74.4 2.8 %collective-permute-start.6 = (bf16[192,1024]{1,0:T(8,128)(2,1)S(1)}, bf16[192,1024]{1,0:T(8,128)(2,1)S(1)}, u32[]{:S(2)}, u32[]{:S(2)}) collective-permute-start(bf16[192,1024]{1,0:T(8,128)(2,1)S(1)} %slice.95), channel_id=1, source_target_pairs={{0,48},{8,24},{16,32},{24,8},{32,16},{40,56},{48,0},{56,40},{64,11... | collective-permute-start | bytes 1179656 | tf_op jit(solution)/shard_map/ppermute | solution.py:289
  77.3 3.3 %collective-permute-start.10 = (bf16[96,1024]{1,0:T(8,128)(2,1)S(1)}, bf16[96,1024]{1,0:T(8,128)(2,1)}, u32[]{:S(2)}, u32[]{:S(2)}) collective-permute-start(bf16[96,1024]{1,0:T(8,128)(2,1)S(1)} %slice.93), channel_id=1, source_target_pairs={{0,64},{8,200},{16,80},{24,216},{32,96},{40,232},{48,112},{56,248}... | collective-permute-start | bytes 589832 | tf_op jit(solution)/shard_map/ppermute | solution.py:289
  80.5 0.0 collective-permute-done.7
  80.5 0.1 add_convert_fusion.4
  80.7 0.9 collective-permute-start.9
  81.6 0.0 all-to-all-done.1.recv_ref
  81.6 0.0 copy-start.2
  81.6 0.9 copy-done.2
  82.5 2.8 %final.1 = bf16[256,1536]{1,0:T(8,128)(2,1)} custom-call(f32[256,1536]{1,0:T(8,128)} %get-tuple-element.48.pre_ref, bf16[8,384,128]{2,1,0:T(8,128)(2,1)} %copy-done.2), custom_call_target="tpu_custom_call" | custom-call | flops 393216 | bytes 3145728 | tf_op jit(solution)/shard_map/final/pallas_call | solution.py:368
  85.3 0.0 collective-permute-done.6
  85.3 0.1 add_convert_fusion.3
  85.5 2.2 %collective-permute-start.8 = (bf16[96,1024]{1,0:T(8,128)(2,1)S(1)}, bf16[96,1024]{1,0:T(8,128)(2,1)S(1)}, u32[]{:S(2)}, u32[]{:S(2)}) collective-permute-start(bf16[96,1024]{1,0:T(8,128)(2,1)S(1)} %slice.98), channel_id=1, source_target_pairs={{0,64},{8,200},{16,80},{24,216},{32,96},{40,232},{48,112},{56,248}... | collective-permute-start | bytes 589832 | tf_op jit(solution)/shard_map/ppermute | solution.py:289
  87.7 0.0 collective-permute-done.10
  87.7 1.0 add_convert_fusion.8
  88.7 4.0 %collective-permute-start.12 = (bf16[48,1024]{1,0:T(8,128)(2,1)S(1)}, bf16[48,1024]{1,0:T(8,128)(2,1)S(1)}, u32[]{:S(2)}, u32[]{:S(2)}) collective-permute-start(bf16[48,1024]{1,0:T(8,128)(2,1)S(1)} %slice.101), channel_id=1, source_target_pairs={{0,192},{8,72},{16,208},{24,88},{32,224},{40,104},{48,240},{56,120... | collective-permute-start | bytes 294920 | tf_op jit(solution)/shard_map/ppermute | solution.py:289
  92.7 0.0 collective-permute-done.9
  92.7 1.0 add_convert_fusion.7
  93.7 4.4 %collective-permute-start.11 = (bf16[48,1024]{1,0:T(8,128)(2,1)S(1)}, bf16[48,1024]{1,0:T(8,128)(2,1)S(1)}, u32[]{:S(2)}, u32[]{:S(2)}) collective-permute-start(bf16[48,1024]{1,0:T(8,128)(2,1)S(1)} %slice.102), channel_id=1, source_target_pairs={{0,192},{8,72},{16,208},{24,88},{32,224},{40,104},{48,240},{56,120... | collective-permute-start | bytes 294920 | tf_op jit(solution)/shard_map/ppermute | solution.py:289
  98.1 0.0 collective-permute-done.8
  98.1 6.3 %collective-permute-start.13 = (bf16[48,1024]{1,0:T(8,128)(2,1)S(1)}, bf16[48,1024]{1,0:T(8,128)(2,1)S(1)}, u32[]{:S(2)}, u32[]{:S(2)}) collective-permute-start(bf16[48,1024]{1,0:T(8,128)(2,1)S(1)} %slice.106), channel_id=1, source_target_pairs={{0,192},{8,72},{16,208},{24,88},{32,224},{40,104},{48,240},{56,120... | collective-permute-start | bytes 294920 | tf_op jit(solution)/shard_map/ppermute | solution.py:289
  104.5 0.0 collective-permute-done.12
  104.5 0.7 add_convert_fusion.11
  105.2 0.0 collective-permute-done.11
  105.2 1.9 %collective-permute-done.13 = bf16[48,1024]{1,0:T(8,128)(2,1)S(1)} collective-permute-done((bf16[48,1024]{1,0:T(8,128)(2,1)S(1)}, bf16[48,1024]{1,0:T(8,128)(2,1)S(1)}, u32[]{:S(2)}, u32[]{:S(2)}) %collective-permute-start.13) | collective-permute-done | bytes 98336 | tf_op jit(solution)/shard_map/ppermute | solution.py:289
  107.1 0.9 copy.7
  (13 shorter events, 0.3 us)
Async XLA Ops:
  2.9 17.1 %all-to-all-start = ((bf16[8,384,128]{2,1,0:T(8,128)(2,1)}), bf16[8,384,128]{2,1,0:T(8,128)(2,1)S(1)}, u32[]{:S(2)}, u32[]{:S(2)}) async-start(bf16[8,384,128]{2,1,0:T(8,128)(2,1)} %pack.1), calls=%async_computation | async-start | bytes 1572864 | tf_op jit(solution)/shard_map/all_to_all | solution.py:314
  20.0 0.9 copy-start.1
  31.6 4.2 %collective-permute-start = (bf16[2560,256]{1,0:T(8,128)(2,1)}, bf16[2560,256]{1,0:T(8,128)(2,1)S(1)}, u32[]{:S(2)}, u32[]{:S(2)}) collective-permute-start(bf16[2560,256]{1,0:T(8,128)(2,1)} %get-tuple-element.30.right_hbm), channel_id=1, source_target_pairs={{0,8},{8,0},{16,24},{24,16},{32,40},{40,32},{48,56},{56,48},{64,72... | collective-permute-start | bytes 3932168 | tf_op jit(solution)/shard_map/ppermute | solution.py:266
  31.7 10.0 %collective-permute-start.1 = (bf16[2048,256]{1,0:T(8,128)(2,1)}, bf16[2048,256]{1,0:T(8,128)(2,1)}, u32[]{:S(2)}, u32[]{:S(2)}) collective-permute-start(bf16[2048,256]{1,0:T(8,128)(2,1)} %get-tuple-element.31.after_hbm.right_hbm.inner_ref), channel_id=1, source_target_pairs={{0,8},{8,0},{16,24},{24,16},{32,40},{40,32},{48,56},{56,48},{64,72... | collective-permute-start | bytes 3145736 | tf_op jit(solution)/shard_map/ppermute | solution.py:266
  35.8 1.1 copy-start
  40.2 21.4 %collective-permute-start.3 = (bf16[384,1024]{1,0:T(8,128)(2,1)}, bf16[384,1024]{1,0:T(8,128)(2,1)}, u32[]{:S(2)}, u32[]{:S(2)}) collective-permute-start(bf16[384,1024]{1,0:T(8,128)(2,1)} %get-tuple-element.32.after_hbm), channel_id=1, source_target_pairs={{0,16},{8,56},{16,0},{24,40},{32,48},{40,24},{48,32},{56,8},{64,80... | collective-permute-start | bytes 2359304 | tf_op jit(solution)/shard_map/ppermute | solution.py:289
  45.1 20.1 %collective-permute-start.5 = (bf16[384,1024]{1,0:T(8,128)(2,1)}, bf16[384,1024]{1,0:T(8,128)(2,1)}, u32[]{:S(2)}, u32[]{:S(2)}) collective-permute-start(bf16[384,1024]{1,0:T(8,128)(2,1)} %get-tuple-element.33.after_hbm), channel_id=1, source_target_pairs={{0,16},{8,56},{16,0},{24,40},{32,48},{40,24},{48,32},{56,8},{64,80... | collective-permute-start | bytes 2359304 | tf_op jit(solution)/shard_map/ppermute | solution.py:289
  49.3 24.8 %collective-permute-start.2 = (bf16[384,1024]{1,0:T(8,128)(2,1)}, bf16[384,1024]{1,0:T(8,128)(2,1)S(1)}, u32[]{:S(2)}, u32[]{:S(2)}) collective-permute-start(bf16[384,1024]{1,0:T(8,128)(2,1)} %get-tuple-element.35.after_ref), channel_id=1, source_target_pairs={{0,16},{8,56},{16,0},{24,40},{32,48},{40,24},{48,32},{56,8},{64,80... | collective-permute-start | bytes 2359304 | tf_op jit(solution)/shard_map/ppermute | solution.py:289
  56.6 4.9 %copy-start.5 = (bf16[384,1024]{1,0:T(8,128)(2,1)S(1)}, bf16[384,1024]{1,0:T(8,128)(2,1)}, u32[]{:S(2)}) copy-start(bf16[384,1024]{1,0:T(8,128)(2,1)} %get-tuple-element.36) | copy-start | bytes 2359300
  56.6 25.0 %all-to-all-start.1 = ((bf16[8,384,128]{2,1,0:T(8,128)(2,1)}), bf16[8,384,128]{2,1,0:T(8,128)(2,1)S(1)}, u32[]{:S(2)}, u32[]{:S(2)}) async-start(bf16[8,384,128]{2,1,0:T(8,128)(2,1)} %get-tuple-element.49), calls=%async_computation.1 | async-start | bytes 1572864 | tf_op jit(solution)/shard_map/all_to_all | solution.py:366
  61.5 3.7 %copy-start.4 = (bf16[384,1024]{1,0:T(8,128)(2,1)S(1)}, bf16[384,1024]{1,0:T(8,128)(2,1)}, u32[]{:S(2)}) copy-start(bf16[384,1024]{1,0:T(8,128)(2,1)} %get-tuple-element.37) | copy-start | bytes 2359300
  63.1 10.8 %collective-permute-start.4 = (bf16[192,1024]{1,0:T(8,128)(2,1)S(1)}, bf16[192,1024]{1,0:T(8,128)(2,1)S(1)}, u32[]{:S(2)}, u32[]{:S(2)}) collective-permute-start(bf16[192,1024]{1,0:T(8,128)(2,1)S(1)} %slice.91), channel_id=1, source_target_pairs={{0,48},{8,24},{16,32},{24,8},{32,16},{40,56},{48,0},{56,40},{64,11... | collective-permute-start | bytes 1179656 | tf_op jit(solution)/shard_map/ppermute | solution.py:289
  66.7 7.4 %copy-start.3 = (bf16[384,1024]{1,0:T(8,128)(2,1)S(1)}, bf16[384,1024]{1,0:T(8,128)(2,1)}, u32[]{:S(2)}) copy-start(bf16[384,1024]{1,0:T(8,128)(2,1)} %get-tuple-element.34) | copy-start | bytes 2359300
  66.8 13.8 %collective-permute-start.7 = (bf16[192,1024]{1,0:T(8,128)(2,1)S(1)}, bf16[192,1024]{1,0:T(8,128)(2,1)S(1)}, u32[]{:S(2)}, u32[]{:S(2)}) collective-permute-start(bf16[192,1024]{1,0:T(8,128)(2,1)S(1)} %slice.92), channel_id=1, source_target_pairs={{0,48},{8,24},{16,32},{24,8},{32,16},{40,56},{48,0},{56,40},{64,11... | collective-permute-start | bytes 1179656 | tf_op jit(solution)/shard_map/ppermute | solution.py:289
  74.4 10.9 %collective-permute-start.6 = (bf16[192,1024]{1,0:T(8,128)(2,1)S(1)}, bf16[192,1024]{1,0:T(8,128)(2,1)S(1)}, u32[]{:S(2)}, u32[]{:S(2)}) collective-permute-start(bf16[192,1024]{1,0:T(8,128)(2,1)S(1)} %slice.95), channel_id=1, source_target_pairs={{0,48},{8,24},{16,32},{24,8},{32,16},{40,56},{48,0},{56,40},{64,11... | collective-permute-start | bytes 1179656 | tf_op jit(solution)/shard_map/ppermute | solution.py:289
  77.3 10.4 %collective-permute-start.10 = (bf16[96,1024]{1,0:T(8,128)(2,1)S(1)}, bf16[96,1024]{1,0:T(8,128)(2,1)}, u32[]{:S(2)}, u32[]{:S(2)}) collective-permute-start(bf16[96,1024]{1,0:T(8,128)(2,1)S(1)} %slice.93), channel_id=1, source_target_pairs={{0,64},{8,200},{16,80},{24,216},{32,96},{40,232},{48,112},{56,248}... | collective-permute-start | bytes 589832 | tf_op jit(solution)/shard_map/ppermute | solution.py:289
  80.7 12.0 %collective-permute-start.9 = (bf16[96,1024]{1,0:T(8,128)(2,1)S(1)}, bf16[96,1024]{1,0:T(8,128)(2,1)}, u32[]{:S(2)}, u32[]{:S(2)}) collective-permute-start(bf16[96,1024]{1,0:T(8,128)(2,1)S(1)} %slice.97), channel_id=1, source_target_pairs={{0,64},{8,200},{16,80},{24,216},{32,96},{40,232},{48,112},{56,248}... | collective-permute-start | bytes 589832 | tf_op jit(solution)/shard_map/ppermute | solution.py:289
  81.6 0.9 copy-start.2
  85.5 12.6 %collective-permute-start.8 = (bf16[96,1024]{1,0:T(8,128)(2,1)S(1)}, bf16[96,1024]{1,0:T(8,128)(2,1)S(1)}, u32[]{:S(2)}, u32[]{:S(2)}) collective-permute-start(bf16[96,1024]{1,0:T(8,128)(2,1)S(1)} %slice.98), channel_id=1, source_target_pairs={{0,64},{8,200},{16,80},{24,216},{32,96},{40,232},{48,112},{56,248}... | collective-permute-start | bytes 589832 | tf_op jit(solution)/shard_map/ppermute | solution.py:289
  88.7 15.8 %collective-permute-start.12 = (bf16[48,1024]{1,0:T(8,128)(2,1)S(1)}, bf16[48,1024]{1,0:T(8,128)(2,1)S(1)}, u32[]{:S(2)}, u32[]{:S(2)}) collective-permute-start(bf16[48,1024]{1,0:T(8,128)(2,1)S(1)} %slice.101), channel_id=1, source_target_pairs={{0,192},{8,72},{16,208},{24,88},{32,224},{40,104},{48,240},{56,120... | collective-permute-start | bytes 294920 | tf_op jit(solution)/shard_map/ppermute | solution.py:289
  93.7 11.4 %collective-permute-start.11 = (bf16[48,1024]{1,0:T(8,128)(2,1)S(1)}, bf16[48,1024]{1,0:T(8,128)(2,1)S(1)}, u32[]{:S(2)}, u32[]{:S(2)}) collective-permute-start(bf16[48,1024]{1,0:T(8,128)(2,1)S(1)} %slice.102), channel_id=1, source_target_pairs={{0,192},{8,72},{16,208},{24,88},{32,224},{40,104},{48,240},{56,120... | collective-permute-start | bytes 294920 | tf_op jit(solution)/shard_map/ppermute | solution.py:289
  98.1 8.9 %collective-permute-start.13 = (bf16[48,1024]{1,0:T(8,128)(2,1)S(1)}, bf16[48,1024]{1,0:T(8,128)(2,1)S(1)}, u32[]{:S(2)}, u32[]{:S(2)}) collective-permute-start(bf16[48,1024]{1,0:T(8,128)(2,1)S(1)} %slice.106), channel_id=1, source_target_pairs={{0,192},{8,72},{16,208},{24,88},{32,224},{40,104},{48,240},{56,120... | collective-permute-start | bytes 294920 | tf_op jit(solution)/shard_map/ppermute | solution.py:289
